TPU v7x, 32 devices: a whole 2x2x4 slice. The times are simulated.
32 devices in a mesh: fsdp: 8 (over z, y), seq: 4 (over x, core).
Axes of the slice: x: 2, y: 2, z: 4, core: 2. Of those that a mesh axis runs over, the one named last changes fastest.
Arguments:
- images: bfloat16 [16, 1376, 1024], P('fsdp', 'seq'), may hold values from -6 to 6
- cotangent: bfloat16 [16, 1376, 1024], P('fsdp', 'seq'), may hold values from -6 to 6
- valid_count: int32 [16], P('fsdp'), may hold values from 1370 to 1373
- first_gain: bfloat16 [1024], P('fsdp'), may hold values from 0.25 to 1.75
- first_shift: bfloat16 [1024], P('fsdp'), may hold values from -3 to 3
- triple_weight: bfloat16 [1024, 3072], P('fsdp'), may hold values from -0.25 to 0.25
- query_bias: bfloat16 [1024], P('fsdp'), may hold values from -3 to 3
- value_bias: bfloat16 [1024], P('fsdp'), may hold values from -3 to 3
- output_weight: bfloat16 [1024, 1024], P('fsdp'), may hold values from -0.75 to 0.75
- output_bias: bfloat16 [1024], P('fsdp'), may hold values from -3 to 3
- attend_scale: bfloat16 [1024], P('fsdp'), may hold values from 0.5 to 1.5
- second_gain: bfloat16 [1024], P('fsdp'), may hold values from 0.25 to 1.75
- second_shift: bfloat16 [1024], P('fsdp'), may hold values from -3 to 3
- expand_weight: bfloat16 [1024, 4096], P('fsdp'), may hold values from -0.1875 to 0.1875
- expand_bias: bfloat16 [4096], P('fsdp'), may hold values from -3 to 3
- reduce_weight: bfloat16 [4096, 1024], P('fsdp'), may hold values from -0.09375 to 0.09375
- reduce_bias: bfloat16 [1024], P('fsdp'), may hold values from -3 to 3
- feed_scale: bfloat16 [1024], P('fsdp'), may hold values from 0.5 to 1.5
Outputs:
- outputs: bfloat16 [16, 1376, 1024], P('fsdp', 'seq')
- grad_images: float32 [16, 1376, 1024], P('fsdp', 'seq')
- grad_first_gain: float32 [1024], P('fsdp')
- grad_first_shift: float32 [1024], P('fsdp')
- grad_triple_weight: float32 [1024, 3072], P('fsdp')
- grad_query_bias: float32 [1024], P('fsdp')
- grad_value_bias: float32 [1024], P('fsdp')
- grad_output_weight: float32 [1024, 1024], P('fsdp')
- grad_output_bias: float32 [1024], P('fsdp')
- grad_attend_scale: float32 [1024], P('fsdp')
- grad_second_gain: float32 [1024], P('fsdp')
- grad_second_shift: float32 [1024], P('fsdp')
- grad_expand_weight: float32 [1024, 4096], P('fsdp')
- grad_expand_bias: float32 [4096], P('fsdp')
- grad_reduce_weight: float32 [4096, 1024], P('fsdp')
- grad_reduce_bias: float32 [1024], P('fsdp')
- grad_feed_scale: float32 [1024], P('fsdp')
Inputs may be any that keep to these rules, and one draw needn't show every extreme that they name: `valid_count`: the number of live tokens of each image; its positions from there to 1376 are padding, masked as keys.
All inputs are finite; a program needn't handle non-finite values.
Results may differ from a plain program's by a relative error of at most 0.018.
Values may be sent and summed in bfloat16 or wider, within the bound.
No kernel may reach another device: no remote copies, remote signals or barrier semaphores. Data moves between devices by JAX's collectives and lax.ppermute only.
A program may use at most 256 MiB of HBM per device.

v0:
```python
import jax
import jax.numpy as jnp
from jax import lax
from jax.sharding import PartitionSpec as P

HEAD_DIM = 64


EPSILON = 1e-06


def layer_norm(inputs, gain, shift):
    average = jnp.mean(inputs, -1, keepdims=True)
    centered = inputs - average
    variance = jnp.mean(centered * centered, -1, keepdims=True)
    return centered * lax.rsqrt(variance + EPSILON) * gain + shift


def exact_gelu(values):
    return jax.nn.gelu(values, approximate=False)


def to_float(array):
    return array.astype(jnp.float32)


def matmul(left, right):
    return jnp.dot(left, right, preferred_element_type=jnp.float32)


def matmul_left_t(left, right):
    return lax.dot_general(
        left, right, (((0,), (0,)), ((), ())), preferred_element_type=jnp.float32
    )


def matmul_right_t(left, right):
    return lax.dot_general(
        left, right, (((1,), (1,)), ((), ())), preferred_element_type=jnp.float32
    )


def column_total(array):
    return matmul(jnp.ones((1, array.shape[0]), jnp.bfloat16), array)[0]


def masked_scores(queries, key_rows, live_count, factor):
    scores = (
        jnp.einsum("qhd,khd->hqk", queries, key_rows, preferred_element_type=jnp.float32) * factor
    )
    live_keys = lax.broadcasted_iota(jnp.int32, (1, 1, key_rows.shape[0]), 2) < live_count
    return jnp.where(live_keys, scores, -1e30)


def attend_forward(bundle):
    packed, live_count = bundle
    length, triple_count, local_width = packed.shape
    head_count = local_width // HEAD_DIM
    unpacked = packed.reshape(length, triple_count, head_count, HEAD_DIM)
    factor = HEAD_DIM ** (-0.5)
    scores = masked_scores(unpacked[:, 0], unpacked[:, 1], live_count, factor)
    highest = jnp.max(scores, -1, keepdims=True)
    powers = jnp.exp(scores - highest)
    row_total = jnp.sum(powers, -1, keepdims=True)
    weights_low = (powers / row_total).astype(jnp.bfloat16)
    mixed_rows = jnp.einsum(
        "hqk,khd->qhd", weights_low, unpacked[:, 2], preferred_element_type=jnp.float32
    )
    logsum = highest + jnp.log(row_total)
    return (mixed_rows.reshape(length, local_width).astype(jnp.bfloat16), logsum)


def attend_backward(bundle):
    packed, grad_mixed, logsum, live_count = bundle
    length, triple_count, local_width = packed.shape
    head_count = local_width // HEAD_DIM
    unpacked = packed.reshape(length, triple_count, head_count, HEAD_DIM)
    factor = HEAD_DIM ** (-0.5)
    scores = masked_scores(unpacked[:, 0], unpacked[:, 1], live_count, factor)
    probs = jnp.exp(scores - logsum)
    grad_heads = grad_mixed.reshape(length, head_count, HEAD_DIM)
    grad_probs = jnp.einsum(
        "qhd,khd->hqk", grad_heads, unpacked[:, 2], preferred_element_type=jnp.float32
    )
    grad_values = jnp.einsum(
        "hqk,qhd->khd", probs.astype(jnp.bfloat16), grad_heads, preferred_element_type=jnp.float32
    )
    inner = jnp.sum(probs * grad_probs, -1, keepdims=True)
    grad_scores = (probs * (grad_probs - inner)).astype(jnp.bfloat16)
    grad_queries = (
        jnp.einsum("hqk,khd->qhd", grad_scores, unpacked[:, 1], preferred_element_type=jnp.float32)
        * factor
    )
    grad_keys = (
        jnp.einsum("hqk,qhd->khd", grad_scores, unpacked[:, 0], preferred_element_type=jnp.float32)
        * factor
    )
    stacked = jnp.stack([grad_queries, grad_keys, grad_values], 1)
    return stacked.reshape(length, triple_count, local_width).astype(jnp.bfloat16)


def shards(
    images,
    cotangent,
    valid_count,
    first_gain,
    first_shift,
    triple_weight,
    query_bias,
    value_bias,
    output_weight,
    output_bias,
    attend_scale,
    second_gain,
    second_shift,
    expand_weight,
    expand_bias,
    reduce_weight,
    reduce_bias,
    feed_scale,
):
    image_count, local_len, width = images.shape
    gathered = (
        lax.all_gather(first_gain, "fsdp", axis=0, tiled=True),
        lax.all_gather(first_shift, "fsdp", axis=0, tiled=True),
        lax.all_gather(triple_weight, "fsdp", axis=0, tiled=True),
        lax.all_gather(query_bias, "fsdp", axis=0, tiled=True),
        lax.all_gather(value_bias, "fsdp", axis=0, tiled=True),
        lax.all_gather(output_weight, "fsdp", axis=0, tiled=True),
        lax.all_gather(output_bias, "fsdp", axis=0, tiled=True),
        lax.all_gather(attend_scale, "fsdp", axis=0, tiled=True),
        lax.all_gather(second_gain, "fsdp", axis=0, tiled=True),
        lax.all_gather(second_shift, "fsdp", axis=0, tiled=True),
        lax.all_gather(expand_weight, "fsdp", axis=0, tiled=True),
        lax.all_gather(expand_bias, "fsdp", axis=0, tiled=True),
        lax.all_gather(reduce_weight, "fsdp", axis=0, tiled=True),
        lax.all_gather(reduce_bias, "fsdp", axis=0, tiled=True),
        lax.all_gather(feed_scale, "fsdp", axis=0, tiled=True),
    )
    inputs = images.astype(jnp.float32).reshape(-1, width)
    first_normed = layer_norm(inputs, to_float(gathered[0]), to_float(gathered[1])).astype(
        jnp.bfloat16
    )
    joint_bias = to_float(jnp.concatenate([gathered[3], jnp.zeros_like(gathered[3]), gathered[4]]))
    triple = (matmul(first_normed, gathered[2]) + joint_bias).astype(jnp.bfloat16)
    triple = triple.reshape(image_count, local_len, 3, width)
    by_heads = lax.all_to_all(triple, "seq", split_axis=3, concat_axis=1, tiled=True)
    attended, logsums = lax.map(attend_forward, (by_heads, valid_count))
    by_tokens = lax.all_to_all(attended, "seq", split_axis=1, concat_axis=2, tiled=True)
    attended_rows = by_tokens.reshape(-1, width)
    branch_attend = matmul(attended_rows, gathered[5]) + to_float(gathered[6])
    residual = inputs + to_float(gathered[7]) * branch_attend
    second_normed = layer_norm(residual, to_float(gathered[8]), to_float(gathered[9])).astype(
        jnp.bfloat16
    )
    expanded = matmul(second_normed, gathered[10]) + to_float(gathered[11])
    activated = exact_gelu(expanded).astype(jnp.bfloat16)
    branch_feed = matmul(activated, gathered[12]) + to_float(gathered[13])
    outputs = residual + to_float(gathered[14]) * branch_feed
    weights = (
        lax.all_gather(first_gain, "fsdp", axis=0, tiled=True),
        lax.all_gather(first_shift, "fsdp", axis=0, tiled=True),
        lax.all_gather(triple_weight, "fsdp", axis=0, tiled=True),
        lax.all_gather(query_bias, "fsdp", axis=0, tiled=True),
        lax.all_gather(value_bias, "fsdp", axis=0, tiled=True),
        lax.all_gather(output_weight, "fsdp", axis=0, tiled=True),
        lax.all_gather(output_bias, "fsdp", axis=0, tiled=True),
        lax.all_gather(attend_scale, "fsdp", axis=0, tiled=True),
        lax.all_gather(second_gain, "fsdp", axis=0, tiled=True),
        lax.all_gather(second_shift, "fsdp", axis=0, tiled=True),
        lax.all_gather(expand_weight, "fsdp", axis=0, tiled=True),
        lax.all_gather(expand_bias, "fsdp", axis=0, tiled=True),
        lax.all_gather(reduce_weight, "fsdp", axis=0, tiled=True),
        lax.all_gather(reduce_bias, "fsdp", axis=0, tiled=True),
        lax.all_gather(feed_scale, "fsdp", axis=0, tiled=True),
    )
    upstream = cotangent.astype(jnp.float32).reshape(-1, width)
    grad_feed_scale = jnp.sum(upstream * branch_feed, 0)
    grad_feed = (to_float(weights[14]) * upstream).astype(jnp.bfloat16)
    grad_reduce_bias = column_total(grad_feed)
    grad_reduce_weight = matmul_left_t(activated, grad_feed)
    grad_activated = matmul_right_t(grad_feed, weights[12])
    unused, gelu_pull = jax.vjp(exact_gelu, expanded)
    grad_expanded = gelu_pull(grad_activated)[0].astype(jnp.bfloat16)
    grad_expand_bias = column_total(grad_expanded)
    grad_expand_weight = matmul_left_t(second_normed, grad_expanded)
    grad_second_normed = matmul_right_t(grad_expanded, weights[10])
    unused, second_pull = jax.vjp(layer_norm, residual, to_float(weights[8]), to_float(weights[9]))
    grad_residual_norm, grad_second_gain, grad_second_shift = second_pull(grad_second_normed)
    grad_residual = upstream + grad_residual_norm
    grad_attend_scale = jnp.sum(grad_residual * branch_attend, 0)
    grad_attend = (to_float(weights[7]) * grad_residual).astype(jnp.bfloat16)
    grad_output_bias = column_total(grad_attend)
    grad_output_weight = matmul_left_t(attended_rows, grad_attend)
    grad_attended = matmul_right_t(grad_attend, weights[5]).astype(jnp.bfloat16)
    grad_attended = grad_attended.reshape(image_count, local_len, width)
    grad_by_heads = lax.all_to_all(grad_attended, "seq", split_axis=2, concat_axis=1, tiled=True)
    grad_triple_heads = lax.map(attend_backward, (by_heads, grad_by_heads, logsums, valid_count))
    grad_triple = lax.all_to_all(grad_triple_heads, "seq", split_axis=1, concat_axis=3, tiled=True)
    grad_triple = grad_triple.reshape(-1, 3 * width)
    column_sums = column_total(grad_triple)
    grad_query_bias = column_sums[:width]
    grad_value_bias = column_sums[2 * width :]
    grad_triple_weight = matmul_left_t(first_normed, grad_triple)
    grad_first_normed = matmul_right_t(grad_triple, weights[2])
    unused, first_pull = jax.vjp(layer_norm, inputs, to_float(weights[0]), to_float(weights[1]))
    grad_inputs_norm, grad_first_gain, grad_first_shift = first_pull(grad_first_normed)
    grad_images = grad_residual + grad_inputs_norm
    owned = (
        lax.psum_scatter(
            grad_first_gain.astype(jnp.bfloat16), "fsdp", scatter_dimension=0, tiled=True
        ).astype(jnp.float32),
        lax.psum_scatter(
            grad_first_shift.astype(jnp.bfloat16), "fsdp", scatter_dimension=0, tiled=True
        ).astype(jnp.float32),
        lax.psum_scatter(
            grad_triple_weight.astype(jnp.bfloat16), "fsdp", scatter_dimension=0, tiled=True
        ).astype(jnp.float32),
        lax.psum_scatter(
            grad_query_bias.astype(jnp.bfloat16), "fsdp", scatter_dimension=0, tiled=True
        ).astype(jnp.float32),
        lax.psum_scatter(
            grad_value_bias.astype(jnp.bfloat16), "fsdp", scatter_dimension=0, tiled=True
        ).astype(jnp.float32),
        lax.psum_scatter(
            grad_output_weight.astype(jnp.bfloat16), "fsdp", scatter_dimension=0, tiled=True
        ).astype(jnp.float32),
        lax.psum_scatter(
            grad_output_bias.astype(jnp.bfloat16), "fsdp", scatter_dimension=0, tiled=True
        ).astype(jnp.float32),
        lax.psum_scatter(
            grad_attend_scale.astype(jnp.bfloat16), "fsdp", scatter_dimension=0, tiled=True
        ).astype(jnp.float32),
        lax.psum_scatter(
            grad_second_gain.astype(jnp.bfloat16), "fsdp", scatter_dimension=0, tiled=True
        ).astype(jnp.float32),
        lax.psum_scatter(
            grad_second_shift.astype(jnp.bfloat16), "fsdp", scatter_dimension=0, tiled=True
        ).astype(jnp.float32),
        lax.psum_scatter(
            grad_expand_weight.astype(jnp.bfloat16), "fsdp", scatter_dimension=0, tiled=True
        ).astype(jnp.float32),
        lax.psum_scatter(
            grad_expand_bias.astype(jnp.bfloat16), "fsdp", scatter_dimension=0, tiled=True
        ).astype(jnp.float32),
        lax.psum_scatter(
            grad_reduce_weight.astype(jnp.bfloat16), "fsdp", scatter_dimension=0, tiled=True
        ).astype(jnp.float32),
        lax.psum_scatter(
            grad_reduce_bias.astype(jnp.bfloat16), "fsdp", scatter_dimension=0, tiled=True
        ).astype(jnp.float32),
        lax.psum_scatter(
            grad_feed_scale.astype(jnp.bfloat16), "fsdp", scatter_dimension=0, tiled=True
        ).astype(jnp.float32),
    )
    summed = lax.psum(
        (
            owned[0],
            owned[1],
            owned[2],
            owned[3],
            owned[4],
            owned[5],
            owned[6],
            owned[7],
            owned[8],
            owned[9],
            owned[10],
            owned[11],
            owned[12],
            owned[13],
            owned[14],
        ),
        "seq",
    )
    return (
        outputs.reshape(image_count, local_len, width).astype(jnp.bfloat16),
        grad_images.reshape(image_count, local_len, width),
        summed[0],
        summed[1],
        summed[2],
        summed[3],
        summed[4],
        summed[5],
        summed[6],
        summed[7],
        summed[8],
        summed[9],
        summed[10],
        summed[11],
        summed[12],
        summed[13],
        summed[14],
    )


def solution(mesh):
    placed = (
        P("fsdp", "seq", None),
        P("fsdp", "seq", None),
        P("fsdp"),
        P("fsdp"),
        P("fsdp"),
        P("fsdp", None),
        P("fsdp"),
        P("fsdp"),
        P("fsdp", None),
        P("fsdp"),
        P("fsdp"),
        P("fsdp"),
        P("fsdp"),
        P("fsdp", None),
        P("fsdp"),
        P("fsdp", None),
        P("fsdp"),
        P("fsdp"),
    )
    return jax.shard_map(
        shards,
        mesh=mesh,
        in_specs=placed,
        out_specs=(
            P("fsdp", "seq", None),
            P("fsdp", "seq", None),
            P("fsdp"),
            P("fsdp"),
            P("fsdp", None),
            P("fsdp"),
            P("fsdp"),
            P("fsdp", None),
            P("fsdp"),
            P("fsdp"),
            P("fsdp"),
            P("fsdp"),
            P("fsdp", None),
            P("fsdp"),
            P("fsdp", None),
            P("fsdp"),
            P("fsdp"),
        ),
        check_vma=False,
    )
```

profile of v0, /device:TPU:0, one launch (start us, length us, event | category | flops | bytes accessed | tf_op | source)
XLA Modules:
  0.0 1119.9 jit_solution(14954223214425034258)
XLA Ops:
  11.6 22.3 %all-gather.1 = bf16[8,1,128]{2,1,0:T(2,128)(2,1)S(1)} all-gather(bf16[1,1,128]{2,1,0:T(2,128)(2,1)S(1)} %bitcast.244), channel_id=1, replica_groups=mesh['fsdp'=8,'seq'=4] {'fsdp'}, dimensions={0}, use_global_device_ids=true | all-gather | bytes 2304 | tf_op jit(solution)/shard_map/all_gather | solution.py:124
  34.0 16.5 %all-gather.2 = bf16[8,1,128]{2,1,0:T(2,128)(2,1)S(1)} all-gather(bf16[1,1,128]{2,1,0:T(2,128)(2,1)S(1)} %bitcast.245), channel_id=1, replica_groups=mesh['fsdp'=8,'seq'=4] {'fsdp'}, dimensions={0}, use_global_device_ids=true | all-gather | bytes 2304 | tf_op jit(solution)/shard_map/all_gather | solution.py:125
  50.4 18.3 %all-gather.3 = bf16[8,1,128]{2,1,0:T(2,128)(2,1)S(1)} all-gather(bf16[1,1,128]{2,1,0:T(2,128)(2,1)S(1)} %bitcast.246), channel_id=1, replica_groups=mesh['fsdp'=8,'seq'=4] {'fsdp'}, dimensions={0}, use_global_device_ids=true | all-gather | bytes 2304 | tf_op jit(solution)/shard_map/all_gather | solution.py:127
  68.8 16.5 %all-gather.4 = bf16[8,1,128]{2,1,0:T(2,128)(2,1)S(1)} all-gather(bf16[1,1,128]{2,1,0:T(2,128)(2,1)S(1)} %bitcast.247), channel_id=1, replica_groups=mesh['fsdp'=8,'seq'=4] {'fsdp'}, dimensions={0}, use_global_device_ids=true | all-gather | bytes 2304 | tf_op jit(solution)/shard_map/all_gather | solution.py:128
  85.3 26.9 %all-gather.16.cloned.1.call-done = bf16[1024,3072]{1,0:T(8,128)(2,1)} async-done(((bf16[128,3072]{1,0:T(8,128)(2,1)}), bf16[1024,3072]{1,0:T(8,128)(2,1)}) %all-gather.16.cloned.1.call-update) | async-done | bytes 6291472 | tf_op jit(solution)/shard_map/all_gather | solution.py:126
  121.6 13.1 %reshape.362 = bf16[2,344,3,1024]{3,2,1,0:T(4,128)(2,1)} reshape(bf16[688,3072]{1,0:T(8,128)(2,1)} %add_convert_fusion.1) | data formatting | bytes 8454144 | tf_op jit(solution)/shard_map/reshape | solution.py:146
  134.7 16.7 %copy.95 = bf16[2,344,3,1024]{1,0,2,3:T(2,128)(2,1)} copy(bf16[2,344,3,1024]{3,2,1,0:T(4,128)(2,1)} %reshape.362) | data formatting | bytes 8454144 | tf_op jit(solution)/shard_map/reshape | solution.py:146
  157.0 53.2 %all-to-all-done = bf16[2,344,3,1024]{1,0,2,3:T(2,128)(2,1)} async-done(((bf16[2,344,3,1024]{1,0,2,3:T(2,128)(2,1)}), bf16[2,344,3,1024]{1,0,2,3:T(2,128)(2,1)}, u32[]{:S(2)}, u32[]{:S(2)}) %all-to-all-start) | async-done | bytes 4227104 | tf_op jit(solution)/shard_map/all_to_all | solution.py:147
  210.3 13.2 %copy.116 = bf16[2,344,3,4,256]{4,3,1,2,0:T(4,128)(2,1)} copy(bf16[2,344,3,4,256]{1,0,2,4,3:T(2,128)(2,1)} %bitcast.30) | data formatting | bytes 8454144 | tf_op jit(solution)/shard_map/all_to_all | solution.py:147
  234.8 83.0 %while.22 = (s32[]{:T(128)}, bf16[2,1376,256]{1,2,0:T(8,128)(2,1)S(1)}, f32[2,4,1376,1]{2,1,3,0:T(4,128)S(1)}, bf16[2,1376,3,256]{1,3,2,0:T(8,128)(2,1)}, s32[2]{0:T(128)S(1)}, /*index=5*/s32[]{:T(128)}) while((s32[]{:T(128)}, bf16[2,1376,256]{1,2,0:T(8,128)(2,1)S(1)}, f32[2,4,1376,1]{2,1,3,0:T(4,128)S(1)}, ...), condition=%wide.region_5.6_spmd, body=%wide.region_2.5_spmd.sunk | while | flops 1999753216 | bytes 99600328 | solution.py:148
  291.8 13.2 %fusion.90 = f32[4,1376]{1,0:T(4,128)S(1)} fusion(f32[4,1376,1376]{1,2,0:T(8,128)} %get-tuple-element.274, f32[4,1376]{1,0:T(4,128)S(1)} %get-tuple-element.275), kind=kLoop, calls=%fused_computation.4.clone.1 | loop fusion | flops 15141504 | bytes 30338048 | tf_op jit(solution)/shard_map/while/body/eval_jaxpr/reduce_sum | solution.py:64
  325.0 17.9 %all-gather.5 = bf16[8,1,128]{2,1,0:T(2,128)(2,1)S(1)} all-gather(bf16[1,1,128]{2,1,0:T(2,128)(2,1)S(1)} %bitcast.248), channel_id=1, replica_groups=mesh['fsdp'=8,'seq'=4] {'fsdp'}, dimensions={0}, use_global_device_ids=true | all-gather | bytes 2304 | tf_op jit(solution)/shard_map/all_gather | solution.py:130
  343.0 16.7 %all-gather = bf16[8,1,128]{2,1,0:T(2,128)(2,1)S(1)} all-gather(bf16[1,1,128]{2,1,0:T(2,128)(2,1)S(1)} %bitcast.249), channel_id=1, replica_groups=mesh['fsdp'=8,'seq'=4] {'fsdp'}, dimensions={0}, use_global_device_ids=true | all-gather | bytes 2304 | tf_op jit(solution)/shard_map/all_gather | solution.py:131
  359.7 18.2 %all-gather.7 = bf16[8,1,128]{2,1,0:T(2,128)(2,1)S(1)} all-gather(bf16[1,1,128]{2,1,0:T(2,128)(2,1)S(1)} %bitcast.250), channel_id=1, replica_groups=mesh['fsdp'=8,'seq'=4] {'fsdp'}, dimensions={0}, use_global_device_ids=true | all-gather | bytes 2304 | tf_op jit(solution)/shard_map/all_gather | solution.py:132
  377.9 16.6 %all-gather.8 = bf16[8,1,128]{2,1,0:T(2,128)(2,1)S(1)} all-gather(bf16[1,1,128]{2,1,0:T(2,128)(2,1)S(1)} %bitcast.251), channel_id=1, replica_groups=mesh['fsdp'=8,'seq'=4] {'fsdp'}, dimensions={0}, use_global_device_ids=true | all-gather | bytes 2304 | tf_op jit(solution)/shard_map/all_gather | solution.py:133
  394.5 17.9 %all-gather.6 = bf16[8,1,128]{2,1,0:T(2,128)(2,1)S(1)} all-gather(bf16[1,1,128]{2,1,0:T(2,128)(2,1)S(1)} %bitcast.252), channel_id=1, replica_groups=mesh['fsdp'=8,'seq'=4] {'fsdp'}, dimensions={0}, use_global_device_ids=true | all-gather | bytes 2304 | tf_op jit(solution)/shard_map/all_gather | solution.py:138
  412.3 26.2 %all-gather.9 = bf16[8,1,512]{2,1,0:T(2,128)(2,1)S(1)} all-gather(bf16[1,1,512]{2,1,0:T(2,128)(2,1)S(1)} %reshape.341), channel_id=1, replica_groups=mesh['fsdp'=8,'seq'=4] {'fsdp'}, dimensions={0}, use_global_device_ids=true | all-gather | bytes 9216 | tf_op jit(solution)/shard_map/all_gather | solution.py:135
  448.5 12.8 %fusion.42 = f32[688,4096]{1,0:T(8,128)} fusion(bf16[1024,4096]{1,0:T(8,128)(2,1)} %all-gather.20.cloned.1.call-done, f32[688,1024]{1,0:T(8,128)S(1)} %get-tuple-element.194, f32[1024]{0:T(1024)S(1)} %bitcast.241, f32[1024]{0:T(1024)S(1)} %bitcast.229, f32[688]{0:T(1024)S(1)} %fusion.28, f32[688]{0:T(1024)S(1)} %broadcast_multiply_fusion), kind=kOutput, calls=%fused_computation.121 | convolution fusion | flops 5774884864 | bytes 22492544 | tf_op jit(solution)/shard_map/dot_general | solution.py:28
  461.3 35.5 %add_convert_fusion = (bf16[688,4096]{1,0:T(8,128)(2,1)S(1)}, f32[688,4096]{1,0:T(8,128)}) fusion(f32[688,4096]{1,0:T(8,128)} %fusion.42, f32[4096]{0:T(1024)S(1)} %bitcast.216, bf16[688,1024]{1,0:T(8,128)(2,1)} %fusion.22, bf16[4096,1024]{1,0:T(8,128)(2,1)} %all-gather.22.cloned.1.call-done), kind=kOutput, calls=%fused_computation.38 | convolution fusion | flops 5977079808 | bytes 37994496 | tf_op jit(solution)/shard_map/dot_general | solution.py:38
  558.0 197.5 %while.23 = (s32[]{:T(128)}, bf16[2,1376,3,256]{1,3,2,0:T(8,128)(2,1)}, bf16[2,1376,3,256]{1,3,2,0:T(8,128)(2,1)}, s32[2]{0:T(128)S(1)}, f32[2,4,1376,1]{2,1,3,0...) while((s32[]{:T(128)}, bf16[2,1376,3,256]{1,3,2,0:T(8,128)(2,1)}, ...), condition=%wide.region_12.13_spmd, body=%wide.region_10.12_spmd.sunk | while | flops 4923301888 | bytes 259874352 | solution.py:198
  575.1 21.8 %multiply_reduce_fusion.9 = (f32[4,1376]{1,0:T(4,128)S(1)}, f32[4,1376,1376]{1,2,0:T(8,128)}) fusion(f32[4,1376,1376]{1,2,0:T(8,128)} %fusion.97, f32[4,1376]{1,0:T(4,128)S(1)} %dynamic-slice_bitcast_fusion.2, bf16[1376,3,4,64]{0,3,2,1:T(8,128)(2,1)S(1)} %bitcast.190, pred[1376]{0:T(1024)(128)(4,1)S(1)} %iota_compare_fusion.5), kind=kOutput, calls=%fused_computation.19.clone.1 | convolution fusion | flops 1007270528 | bytes 62076416 | tf_op jit(solution)/shard_map/while/body/eval_jaxpr/qhd,khd->hqk/dot_general | solution.py:49
  596.9 25.9 %multiply_convert_fusion.4 = bf16[4,1376,1376]{1,2,0:T(8,128)(2,1)} fusion(f32[4,1376,1376]{1,2,0:T(8,128)} %get-tuple-element.282, f32[4,1376,1376]{1,2,0:T(8,128)} %fusion.97, f32[4,1376]{1,0:T(4,128)S(1)} %get-tuple-element.283), kind=kLoop, calls=%fused_computation.18.clone.1 | loop fusion | flops 22720512 | bytes 75757056 | tf_op jit(solution)/shard_map/while/body/eval_jaxpr/convert_element_type | solution.py:89
  622.8 13.7 %fusion.98 = bf16[4,64,1376]{2,1,0:T(8,128)(2,1)} fusion(bf16[1376,4,64]{0,2,1:T(8,128)(2,1)S(1)} %bitcast.194, f32[4,1376,1376]{1,2,0:T(8,128)} %get-tuple-element.282), kind=kOutput, calls=%fused_computation.24.clone.1 | convolution fusion | flops 977334272 | bytes 31703040 | tf_op jit(solution)/shard_map/while/body/eval_jaxpr/hqk,qhd->khd/dot_general | solution.py:85
  673.7 21.8 %multiply_reduce_fusion.9 = (f32[4,1376]{1,0:T(4,128)S(1)}, f32[4,1376,1376]{1,2,0:T(8,128)}) fusion(f32[4,1376,1376]{1,2,0:T(8,128)} %fusion.97, f32[4,1376]{1,0:T(4,128)S(1)} %dynamic-slice_bitcast_fusion.2, bf16[1376,3,4,64]{0,3,2,1:T(8,128)(2,1)S(1)} %bitcast.190, pred[1376]{0:T(1024)(128)(4,1)S(1)} %iota_compare_fusion.5), kind=kOutput, calls=%fused_computation.19.clone.1 | convolution fusion | flops 1007270528 | bytes 62076416 | tf_op jit(solution)/shard_map/while/body/eval_jaxpr/qhd,khd->hqk/dot_general | solution.py:49
  695.4 25.8 %multiply_convert_fusion.4 = bf16[4,1376,1376]{1,2,0:T(8,128)(2,1)} fusion(f32[4,1376,1376]{1,2,0:T(8,128)} %get-tuple-element.282, f32[4,1376,1376]{1,2,0:T(8,128)} %fusion.97, f32[4,1376]{1,0:T(4,128)S(1)} %get-tuple-element.283), kind=kLoop, calls=%fused_computation.18.clone.1 | loop fusion | flops 22720512 | bytes 75757056 | tf_op jit(solution)/shard_map/while/body/eval_jaxpr/convert_element_type | solution.py:89
  721.3 13.5 %fusion.98 = bf16[4,64,1376]{2,1,0:T(8,128)(2,1)} fusion(bf16[1376,4,64]{0,2,1:T(8,128)(2,1)S(1)} %bitcast.194, f32[4,1376,1376]{1,2,0:T(8,128)} %get-tuple-element.282), kind=kOutput, calls=%fused_computation.24.clone.1 | convolution fusion | flops 977334272 | bytes 31703040 | tf_op jit(solution)/shard_map/while/body/eval_jaxpr/hqk,qhd->khd/dot_general | solution.py:85
  773.9 48.1 %all-to-all-done.3 = bf16[2,1376,3,256]{3,0,2,1:T(2,128)(2,1)} async-done(((bf16[2,1376,3,256]{3,0,2,1:T(2,128)(2,1)}), bf16[2,1376,3,256]{3,0,2,1:T(2,128)(2,1)}, u32[]{:S(2)}, u32[]{:S(2)}) %all-to-all-start.3) | async-done | bytes 4227104 | tf_op jit(solution)/shard_map/all_to_all | solution.py:199
  848.5 16.8 %all-gather.10 = bf16[8,1,128]{2,1,0:T(2,128)(2,1)S(1)} all-gather(bf16[1,1,128]{2,1,0:T(2,128)(2,1)S(1)} %bitcast.253), channel_id=1, replica_groups=mesh['fsdp'=8,'seq'=4] {'fsdp'}, dimensions={0}, use_global_device_ids=true | all-gather | bytes 2304 | tf_op jit(solution)/shard_map/all_gather | solution.py:137
  886.3 15.2 %fusion.23 = (bf16[1024]{0:T(1024)(128)(2,1)S(1)}, bf16[1024]{0:T(1024)(128)(2,1)S(1)}, f32[688,1024]{1,0:T(8,128)}, bf16[688,1024]{1,0:T(8,128)(2,1)}) fusion(bf16[2,344,1024]{2,1,0:T(8,128)(2,1)S(1)} %copy-done.9, f32[1024]{0:T(1024)S(1)} %bitcast.243, f32[688,1024]{1,0:T(8,128)} %get-tuple-element.195, f32[1024]{0:T(1024)S(1)} %bitcast.240, ...), kind=kOutput, calls=%fused_computation.65 | convolution fusion | flops 5781223424 | bytes 30954880 | tf_op jit(solution)/shard_map/dot_general | solution.py:28
  901.5 37.1 %all-reduce.12 = (bf16[1024]{0:T(1024)(128)(2,1)S(1)}, bf16[1024]{0:T(1024)(128)(2,1)S(1)}, bf16[1024]{0:T(1024)(128)(2,1)S(1)}, bf16[1024]{0:T(1024)(128)(2,1)S...) all-reduce(bf16[1024]{0:T(1024)(128)(2,1)S(1)} %get-tuple-element.1, ...), channel_id=2, replica_groups=mesh['fsdp'=8,'seq'=4] {'fsdp'}, use_global_device_ids=true, to_apply=%region_16.17.clone | all-reduce | flops 14336 | bytes 57344
  939.1 62.1 %reduce-scatter.5.cloned.1.call-done = bf16[128,3072]{1,0:T(8,128)(2,1)} async-done(((bf16[1024,3072]{1,0:T(8,128)(2,1)}), bf16[128,3072]{1,0:T(8,128)(2,1)}) %reduce-scatter.5.cloned.1.call-update) | async-done | bytes 786448 | tf_op jit(solution)/shard_map/reduce_scatter | solution.py:216
  1001.2 111.5 %all-reduce.14 = (f32[128]{0:T(128)}, f32[128]{0:T(128)}, f32[128,3072]{1,0:T(8,128)}, f32[128]{0:T(128)}, f32[128]{0:T(128)}, /*index=5*/f32[128,1024]{1,0:T(8,...) all-reduce(f32[128]{0:T(128)S(1)} %get-tuple-element.207, ...), channel_id=1, replica_groups=mesh['fsdp'=8,'seq'=4] {'seq'}, use_global_device_ids=true, to_apply=%region_17.18 | all-reduce | flops 1574656 | bytes 9451520 | tf_op jit(solution)/shard_map/psum | solution.py:256
  (259 shorter events, 317.9 us)
Async XLA Ops:
  7.2 26.7 %copy-start.43 = (bf16[128]{0:T(256)(128)(2,1)S(1)}, bf16[128]{0:T(256)(128)(2,1)}, u32[]{:S(2)}) copy-start(bf16[128]{0:T(256)(128)(2,1)} %param.26) | copy-start | bytes 772
  7.2 43.2 %copy-start.44 = (bf16[128]{0:T(256)(128)(2,1)S(1)}, bf16[128]{0:T(256)(128)(2,1)}, u32[]{:S(2)}) copy-start(bf16[128]{0:T(256)(128)(2,1)} %param.28) | copy-start | bytes 772
  7.2 61.5 %copy-start.45 = (bf16[128]{0:T(256)(128)(2,1)S(1)}, bf16[128]{0:T(256)(128)(2,1)}, u32[]{:S(2)}) copy-start(bf16[128]{0:T(256)(128)(2,1)} %param.29) | copy-start | bytes 772
  7.2 105.0 %all-gather.16.cloned.1.call-start = ((), (), s32[]{:S(2)}) async-start(), calls=%async_computation.8 | async-start | bytes 7077888 | tf_op jit(solution)/shard_map/all_gather | solution.py:126
  8.0 434.2 %all-gather.18.cloned.1.call-start = ((), (), s32[]{:S(2)}) async-start(), calls=%async_computation.9 | async-start | bytes 2359296 | tf_op jit(solution)/shard_map/all_gather | solution.py:129
  8.7 439.7 %all-gather.20.cloned.1.call-start = ((), (), s32[]{:S(2)}) async-start(), calls=%async_computation.10 | async-start | bytes 9437184 | tf_op jit(solution)/shard_map/all_gather | solution.py:134
  9.7 111.9 %copy-start.20 = (f32[2,344]{1,0:T(2,128)}, f32[2,344]{1,0:T(2,128)S(1)}, u32[]{:S(2)}) copy-start(f32[2,344]{1,0:T(2,128)S(1)} %broadcast_multiply_fusion.1) | copy-start | bytes 8260
  9.8 111.8 %copy-start.28 = (f32[688]{0:T(1024)}, f32[688]{0:T(1024)S(1)}, u32[]{:S(2)}) copy-start(f32[688]{0:T(1024)S(1)} %div.51) | copy-start | bytes 8260
  11.0 110.6 %copy-start.30 = (f32[688]{0:T(1024)}, f32[688]{0:T(1024)S(1)}, u32[]{:S(2)}) copy-start(f32[688]{0:T(1024)S(1)} %rsqrt.25) | copy-start | bytes 8260
  33.9 87.7 %copy-start.22 = (f32[8,1,128]{2,1,0:T(1,128)}, f32[8,1,128]{2,1,0:T(1,128)S(1)}, u32[]{:S(2)}) copy-start(f32[8,1,128]{2,1,0:T(1,128)S(1)} %convert_element_type.258) | copy-start | bytes 12292
  50.4 71.2 %copy-start.32 = (f32[8,1,128]{2,1,0:T(1,128)}, f32[8,1,128]{2,1,0:T(1,128)S(1)}, u32[]{:S(2)}) copy-start(f32[8,1,128]{2,1,0:T(1,128)S(1)} %convert_element_type.259) | copy-start | bytes 12292
  151.5 58.8 %all-to-all-start = ((bf16[2,344,3,1024]{1,0,2,3:T(2,128)(2,1)}), bf16[2,344,3,1024]{1,0,2,3:T(2,128)(2,1)}, u32[]{:S(2)}, u32[]{:S(2)}) async-start(bf16[2,344,3,1024]{1,0,2,3:T(2,128)(2,1)} %copy.95), calls=%async_computation | async-start | bytes 9437184 | tf_op jit(solution)/shard_map/all_to_all | solution.py:147
  156.4 304.8 %all-gather.22.cloned.1.call-start = ((), (), s32[]{:S(2)}) async-start(), calls=%async_computation.11 | async-start | bytes 9437184 | tf_op jit(solution)/shard_map/all_gather | solution.py:136
  318.5 24.5 %copy-start.47 = (bf16[128]{0:T(256)(128)(2,1)S(1)}, bf16[128]{0:T(256)(128)(2,1)}, u32[]{:S(2)}) copy-start(bf16[128]{0:T(256)(128)(2,1)} %param.32) | copy-start | bytes 772
  318.5 41.2 %copy-start.48 = (bf16[128]{0:T(256)(128)(2,1)S(1)}, bf16[128]{0:T(256)(128)(2,1)}, u32[]{:S(2)}) copy-start(bf16[128]{0:T(256)(128)(2,1)} %param.33) | copy-start | bytes 772
  318.5 59.4 %copy-start.49 = (bf16[128]{0:T(256)(128)(2,1)S(1)}, bf16[128]{0:T(256)(128)(2,1)}, u32[]{:S(2)}) copy-start(bf16[128]{0:T(256)(128)(2,1)} %param.34) | copy-start | bytes 772
  318.5 76.0 %copy-start.50 = (bf16[128]{0:T(256)(128)(2,1)S(1)}, bf16[128]{0:T(256)(128)(2,1)}, u32[]{:S(2)}) copy-start(bf16[128]{0:T(256)(128)(2,1)} %param.39) | copy-start | bytes 772
  318.5 120.0 %copy-start.7 = (bf16[2,344,1024]{2,1,0:T(8,128)(2,1)S(1)}, bf16[2,344,1024]{2,1,0:T(8,128)(2,1)}, u32[]{:S(2)}) copy-start(bf16[2,344,1024]{2,1,0:T(8,128)(2,1)} %param.23) | copy-start | bytes 4227076
  321.4 118.6 %all-to-all-start.1 = ((bf16[2,1376,256]{2,0,1:T(2,128)(2,1)}), bf16[2,1376,256]{2,0,1:T(2,128)(2,1)S(1)}, u32[]{:S(2)}, u32[]{:S(2)}) async-start(bf16[2,1376,256]{2,0,1:T(2,128)(2,1)} %copy.99), calls=%async_computation.1 | async-start | bytes 2818048 | tf_op jit(solution)/shard_map/all_to_all | solution.py:149
  324.9 544.9 %reduce-scatter.7.cloned.1.call-start = ((), (), s32[]{:S(2)}) async-start(), calls=%async_computation.13 | async-start | bytes 2359296 | tf_op jit(solution)/shard_map/reduce_scatter | solution.py:225
  342.9 99.2 %copy-start.37 = (f32[8,1,128]{2,1,0:T(1,128)}, f32[8,1,128]{2,1,0:T(1,128)S(1)}, u32[]{:S(2)}) copy-start(f32[8,1,128]{2,1,0:T(1,128)S(1)} %convert_element_type.260) | copy-start | bytes 12292
  412.3 26.2 %copy-start.24 = (f32[8,1,128]{2,1,0:T(1,128)}, f32[8,1,128]{2,1,0:T(1,128)S(1)}, u32[]{:S(2)}) copy-start(f32[8,1,128]{2,1,0:T(1,128)S(1)} %convert_element_type.261) | copy-start | bytes 12292
  447.8 62.9 %copy-start.1 = (f32[688,1024]{1,0:T(8,128)}, f32[688,1024]{1,0:T(8,128)S(1)}, u32[]{:S(2)}) copy-start(f32[688,1024]{1,0:T(8,128)S(1)} %get-tuple-element.194) | copy-start | bytes 8454148
  461.3 35.5 %copy-start.52 = (bf16[1024,4096]{1,0:T(8,128)(2,1)S(1)}, bf16[1024,4096]{1,0:T(8,128)(2,1)}, u32[]{:S(2)}) copy-start(bf16[1024,4096]{1,0:T(8,128)(2,1)} %all-gather.20.cloned.1.call-done) | copy-start | bytes 25165828
  510.6 428.5 %reduce-scatter.9.cloned.1.call-start = ((), (), s32[]{:S(2)}) async-start(), calls=%async_computation.14 | async-start | bytes 9437184 | tf_op jit(solution)/shard_map/reduce_scatter | solution.py:240
  530.5 24.0 %all-to-all-start.2 = ((bf16[2,344,1024]{1,0,2:T(2,128)(2,1)}), bf16[2,344,1024]{1,0,2:T(2,128)(2,1)S(1)}, u32[]{:S(2)}, u32[]{:S(2)}) async-start(bf16[2,344,1024]{1,0,2:T(2,128)(2,1)} %copy.102), calls=%async_computation.2 | async-start | bytes 3145728 | tf_op jit(solution)/shard_map/all_to_all | solution.py:197
  534.1 405.0 %reduce-scatter.11.cloned.1.call-start = ((), (), s32[]{:S(2)}) async-start(), calls=%async_computation.15 | async-start | bytes 9437184 | tf_op jit(solution)/shard_map/reduce_scatter | solution.py:246
  768.1 53.9 %all-to-all-start.3 = ((bf16[2,1376,3,256]{3,0,2,1:T(2,128)(2,1)}), bf16[2,1376,3,256]{3,0,2,1:T(2,128)(2,1)}, u32[]{:S(2)}, u32[]{:S(2)}) async-start(bf16[2,1376,3,256]{3,0,2,1:T(2,128)(2,1)} %copy.107), calls=%async_computation.3 | async-start | bytes 8454144 | tf_op jit(solution)/shard_map/all_to_all | solution.py:199
  773.2 228.0 %reduce-scatter.5.cloned.1.call-start = ((), (), s32[]{:S(2)}) async-start(), calls=%async_computation.12 | async-start | bytes 7077888 | tf_op jit(solution)/shard_map/reduce_scatter | solution.py:216
  845.9 19.4 %copy-start.9 = (bf16[2,344,1024]{2,1,0:T(8,128)(2,1)S(1)}, bf16[2,344,1024]{2,1,0:T(8,128)(2,1)}, u32[]{:S(2)}) copy-start(bf16[2,344,1024]{2,1,0:T(8,128)(2,1)} %param.23) | copy-start | bytes 4227076
  845.9 19.4 %copy-start.25 = (f32[8,1,128]{2,1,0:T(1,128)S(1)}, f32[8,1,128]{2,1,0:T(1,128)}, u32[]{:S(2)}) copy-start(f32[8,1,128]{2,1,0:T(1,128)} %copy-done.24) | copy-start | bytes 12292
  886.3 114.9 %copy-start.19 = (bf16[128,1024]{1,0:T(8,128)(2,1)S(1)}, bf16[128,1024]{1,0:T(8,128)(2,1)}, u32[]{:S(2)}) copy-start(bf16[128,1024]{1,0:T(8,128)(2,1)} %reduce-scatter.7.cloned.1.call-done) | copy-start | bytes 786436
  (39 other events, 179.0 us)
Sparse Core Ops, SparseCore 0:
  10.3 101.8 all-gather.15
  114.3 47.4 all-gather.17
  164.0 123.4 all-gather.19
  289.4 123.2 all-gather.21
  510.7 65.5 reduce-scatter.6
  579.8 147.9 reduce-scatter.8
  731.9 148.0 reduce-scatter.10
  883.6 117.6 reduce-scatter.4
where the time goes:
time: 1130 us; the launch traced here: 1120 us
  blocking collectives  353 us (31%)
  matrix products  322 us (28%)
  waiting for transfers between devices  193 us (17%)
  local copies, waits for them, and re-layouts  115 us (10%)
  other arithmetic  103 us (9%)
  starting transfers between devices  18 us (2%)
  between operations  16.4 us (1%)
    psum x1, blocking collectives, shards(): lax.psum((owned[0], owned[1], owned[2], owned[3], owned[4], owned[5], own...  112 us
    dot_general x4, matrix products, masked_scores(): jnp.einsum('qhd,khd->hqk', queries, key_rows, preferred_element_type=jnp....  69.1 us
    reduce_scatter x1, waiting for transfers between devices, shards(): lax.psum_scatter(grad_triple_weight.astype(jnp.bfloat16), 'fsdp', scatter...  62.1 us
    dot_general x4, matrix products, matmul_right_t(): lax.dot_general(left, right, (((1,), (1,)), ((), ())), preferred_element_...  54.8 us
    all_to_all x1, waiting for transfers between devices, shards(): lax.all_to_all(triple, 'seq', split_axis=3, concat_axis=1, tiled=True)  53.2 us
    convert_element_type x2, other arithmetic, attend_backward(): grad_scores = (probs * (grad_probs - inner)).astype(jnp.bfloat16)  51.7 us
    dot_general x8, matrix products, matmul(): return jnp.dot(left, right, preferred_element_type=jnp.float32)  50.2 us
    all_to_all x1, waiting for transfers between devices, shards(): lax.all_to_all(grad_triple_heads, 'seq', split_axis=1, concat_axis=3, til...  48.1 us
  transfers between devices with their start and end apart: 12, of which 4 were waited for; matrix products, arithmetic and copies ran while one was open for 43% of the time, Pallas kernels for 0%

commit v1 on v0

v1 whole, which is shorter than its diff:
```python
import functools

import jax
import jax.numpy as jnp
from jax import lax
from jax.experimental import pallas as pl
from jax.experimental.pallas import tpu as pltpu
from jax.sharding import Mesh, PartitionSpec as P

HEAD_DIM = 64
EPSILON = 1e-06
BF = jnp.bfloat16
F32 = jnp.float32
MASKED = -1e30


def dot(left, right):
    return lax.dot_general(left, right, (((1,), (0,)), ((), ())), preferred_element_type=F32)


def dot_left_t(left, right):
    return lax.dot_general(left, right, (((0,), (0,)), ((), ())), preferred_element_type=F32)


def dot_right_t(left, right):
    return lax.dot_general(left, right, (((1,), (1,)), ((), ())), preferred_element_type=F32)


def column_total(array):
    return dot(jnp.ones((8, array.shape[0]), BF), array)[0]


def normalize(rows):
    average = jnp.mean(rows, -1, keepdims=True)
    centered = rows - average
    variance = jnp.mean(centered * centered, -1, keepdims=True)
    factor = lax.rsqrt(variance + EPSILON)
    return centered * factor, factor


def normalize_back(normal, factor, weighted):
    return factor * (
        weighted
        - jnp.mean(weighted, -1, keepdims=True)
        - normal * jnp.mean(weighted * normal, -1, keepdims=True)
    )


def spans(total, step):
    return [(start, min(step, total - start)) for start in range(0, total, step)]


def merge(ref, out):
    pieces, _, rows, _ = ref.shape
    for piece in range(pieces):
        out[pl.ds(piece * rows, rows), :] = ref[piece, 0].astype(F32)


def lane_parts(block, heads, head):
    lane = lax.broadcasted_iota(jnp.int32, (1, block), 1)
    if heads == 1:
        return lane < HEAD_DIM, lane - HEAD_DIM
    if head == 0:
        return lane < HEAD_DIM, lane - HEAD_DIM
    return lane >= HEAD_DIM, lane


def split_three(values):
    high = values.astype(BF).astype(F32)
    rest = values - high
    middle = rest.astype(BF).astype(F32)
    return high, middle, rest - middle


def dead_column(limit_ref, length):
    image = pl.program_id(0)
    row = lax.broadcasted_iota(jnp.int32, (length, 1), 0)
    dead = (row >= limit_ref[image, 0]) & (row < limit_ref[image, 1])
    return jnp.where(dead, MASKED, 0.0)


def attend_forward_kernel(limit_ref, q_ref, k_ref, v_ref, out_ref, log_ref, q_s, k_s, v_s, o_s):
    pieces, _, rows, block = q_ref.shape
    length = pieces * rows
    heads = max(block // HEAD_DIM, 1)
    merge(q_ref, q_s)
    merge(k_ref, k_s)
    merge(v_ref, v_s)
    dead = dead_column(limit_ref, length)
    aug = []
    for head in range(heads):
        own, spare = lane_parts(2 * HEAD_DIM, heads, head)
        q = jnp.where(own, q_s[...] * 0.125, jnp.where(spare == 0, 1.0, 0.0)).astype(BF)
        k = jnp.where(own, k_s[...], jnp.where(spare == 0, dead, 0.0)).astype(BF)
        v = jnp.where(own, v_s[...], jnp.where(spare == 0, 1.0, 0.0)).astype(BF)
        aug.append((q, k, v))
    for start, size in spans(length, 352):
        results = []
        for head in range(heads):
            q, k, v = aug[head]
            scores = dot_right_t(q[start : start + size], k)
            top = jnp.max(scores, -1, keepdims=True)
            powers = jnp.exp(scores - top).astype(BF)
            mixed = dot(powers, v)
            own, spare = lane_parts(2 * HEAD_DIM, heads, head)
            at = HEAD_DIM if head == 0 else 0
            total = mixed[:, at : at + 1]
            results.append((mixed / total, top + jnp.log(total)))
        own, _ = lane_parts(2 * HEAD_DIM, heads, 0)
        if heads == 1:
            o_s[pl.ds(start, size), :] = results[0][0]
            log_ref[0, 0, pl.ds(start, size), :] = jnp.broadcast_to(
                results[0][1], (size, 2 * HEAD_DIM)
            )
        else:
            o_s[pl.ds(start, size), :] = jnp.where(own, results[0][0], results[1][0])
            log_ref[0, 0, pl.ds(start, size), :] = jnp.where(own, results[1][1], results[0][1])
    for piece in range(pieces):
        out_ref[piece, 0] = o_s[pl.ds(piece * rows, rows), :].astype(BF)


def attend_backward_kernel(
    limit_ref, q_ref, k_ref, v_ref, o_ref, g_ref, log_ref, dq_ref, dk_ref, dv_ref,
    q_s, k_s, v_s, o_s, g_s, dq_s, dk_s, dv_s,
):
    pieces, _, rows, block = q_ref.shape
    length = pieces * rows
    heads = max(block // HEAD_DIM, 1)
    merge(q_ref, q_s)
    merge(k_ref, k_s)
    merge(v_ref, v_s)
    merge(o_ref, o_s)
    merge(g_ref, g_s)
    dead = dead_column(limit_ref, length)
    product = o_s[...] * g_s[...]
    for head in range(heads):
        own, spare = lane_parts(2 * HEAD_DIM, heads, head)
        log_parts = split_three(log_ref[0, 0])
        inner = jnp.sum(jnp.where(own, product, 0.0), -1, keepdims=True)
        inner_parts = split_three(inner)
        zero = jnp.zeros((length, 2 * HEAD_DIM), F32)
        q_tail, k_tail, v_tail, g_tail = zero, zero, zero, zero
        for place in range(3):
            q_tail = jnp.where(spare == place, -log_parts[place], q_tail)
            g_tail = jnp.where(spare == place, -inner_parts[place], g_tail)
            k_tail = jnp.where(spare == place, 1.0, k_tail)
            v_tail = jnp.where(spare == place, 1.0, v_tail)
        q_tail = jnp.where(spare == 3, 1.0, q_tail)
        k_tail = jnp.where(spare == 3, dead, k_tail)
        q = jnp.where(own, q_s[...] * 0.125, q_tail).astype(BF)
        k = jnp.where(own, k_s[...], k_tail).astype(BF)
        v = jnp.where(own, v_s[...], v_tail).astype(BF)
        g = jnp.where(own, g_s[...], g_tail).astype(BF)
        k_t = jnp.where(own, k_s[...] * 0.125, 0.0).T.astype(BF)
        dk = dv = None
        for start, size in spans(length, 512):
            q_part, g_part = q[start : start + size], g[start : start + size]
            probs = jnp.exp(dot_right_t(k, q_part))
            slopes = (probs * dot_right_t(v, g_part)).astype(BF)
            probs = probs.astype(BF)
            dv_part = dot(probs, g_part)
            dk_part = dot(slopes, q_part)
            dv = dv_part if dv is None else dv + dv_part
            dk = dk_part if dk is None else dk + dk_part
            dq_part = dot(k_t, slopes).T
            if head == 0:
                dq_s[pl.ds(start, size), :] = dq_part
            else:
                dq_s[pl.ds(start, size), :] += dq_part
        if head == 0:
            dk_s[...] = dk
            dv_s[...] = dv
        else:
            dk_s[...] = jnp.where(own, dk, dk_s[...])
            dv_s[...] = jnp.where(own, dv, dv_s[...])
    for piece in range(pieces):
        part = pl.ds(piece * rows, rows)
        dq_ref[piece, 0] = dq_s[part, :].astype(BF)
        dk_ref[piece, 0] = dk_s[part, :].astype(BF)
        dv_ref[piece, 0] = dv_s[part, :].astype(BF)


def attend_specs(pieces, rows, first):
    def at(limit_index):
        return pl.BlockSpec(
            (pieces, 1, rows, 2 * HEAD_DIM),
            lambda image, pair, limits: (0, image, 0, limit_index + pair),
        )

    return at(first)


def attend_forward(triple, limits):
    pieces, images, rows, columns = triple.shape
    head_width = columns // 3
    length = pieces * rows
    pairs = head_width // (2 * HEAD_DIM)
    wide = pltpu.VMEM((length, 2 * HEAD_DIM), F32)
    spec = functools.partial(attend_specs, pieces, rows)
    heads = images * head_width // HEAD_DIM
    return pl.pallas_call(
        attend_forward_kernel,
        grid_spec=pltpu.PrefetchScalarGridSpec(
            num_scalar_prefetch=1,
            grid=(images, pairs),
            in_specs=[spec(0), spec(pairs), spec(2 * pairs)],
            out_specs=[
                spec(0),
                pl.BlockSpec((1, 1, length, 2 * HEAD_DIM), lambda i, p, limits: (i, p, 0, 0)),
            ],
            scratch_shapes=[wide] * 4,
        ),
        out_shape=[
            jax.ShapeDtypeStruct((pieces, images, rows, head_width), BF),
            jax.ShapeDtypeStruct((images, pairs, length, 2 * HEAD_DIM), F32),
        ],
        compiler_params=pltpu.CompilerParams(vmem_limit_bytes=50 * 2**20),
        cost_estimate=pl.CostEstimate(
            flops=heads * length * length * 1024,
            bytes_accessed=4 * triple.size,
            transcendentals=heads * length * length,
        ),
        name="attend_forward",
    )(limits, triple, triple, triple)


def attend_backward(triple, attended, grad, logs, limits):
    pieces, images, rows, columns = triple.shape
    head_width = columns // 3
    length = pieces * rows
    pairs = head_width // (2 * HEAD_DIM)
    wide = pltpu.VMEM((length, 2 * HEAD_DIM), F32)
    spec = functools.partial(attend_specs, pieces, rows)
    shape = jax.ShapeDtypeStruct((pieces, images, rows, head_width), BF)
    heads = images * head_width // HEAD_DIM
    return pl.pallas_call(
        attend_backward_kernel,
        grid_spec=pltpu.PrefetchScalarGridSpec(
            num_scalar_prefetch=1,
            grid=(images, pairs),
            in_specs=[
                spec(0),
                spec(pairs),
                spec(2 * pairs),
                spec(0),
                spec(0),
                pl.BlockSpec((1, 1, length, 2 * HEAD_DIM), lambda i, p, limits: (i, p, 0, 0)),
            ],
            out_specs=[spec(0)] * 3,
            scratch_shapes=[wide] * 8,
        ),
        out_shape=[shape] * 3,
        compiler_params=pltpu.CompilerParams(vmem_limit_bytes=56 * 2**20),
        cost_estimate=pl.CostEstimate(
            flops=heads * length * length * 2560,
            bytes_accessed=8 * triple.size,
            transcendentals=heads * length * length,
        ),
        name="attend_backward",
    )(limits, triple, triple, triple, attended, grad, logs)


def gelu_parts(values):
    size = jnp.abs(values) * 0.7071067811865476
    bell = jnp.exp(-size * size)
    t = 1.0 / (1.0 + 0.3275911 * size)
    tail = t * (
        0.254829592
        + t * (-0.284496736 + t * (1.421413741 + t * (-1.453152027 + t * 1.061405429)))
    )
    tail = 0.5 * tail * bell
    return jnp.where(values >= 0.0, 1.0 - tail, tail), 0.3989422804014327 * bell


def expand_kernel(rows_ref, weight_ref, bias_ref, active_ref, slope_ref):
    count = rows_ref.shape[0]
    for start, size in spans(count, 352):
        expanded = dot(rows_ref[start : start + size, :], weight_ref[...]) + bias_ref[...]
        below, density = gelu_parts(expanded)
        active_ref[start : start + size, :] = (expanded * below).astype(BF)
        slope_ref[start : start + size, :] = (below + expanded * density).astype(BF)


def expand_rows(rows, weight, bias):
    count, width = rows.shape
    units = weight.shape[1]
    tile = 256
    shape = jax.ShapeDtypeStruct((count, units), BF)
    return pl.pallas_call(
        expand_kernel,
        grid=(units // tile,),
        in_specs=[
            pl.BlockSpec((count, width), lambda i: (0, 0)),
            pl.BlockSpec((width, tile), lambda i: (0, i)),
            pl.BlockSpec((1, tile), lambda i: (0, i)),
        ],
        out_specs=[pl.BlockSpec((count, tile), lambda i: (0, i))] * 2,
        out_shape=[shape] * 2,
        compiler_params=pltpu.CompilerParams(vmem_limit_bytes=48 * 2**20),
        cost_estimate=pl.CostEstimate(
            flops=4 * count * units * width,
            bytes_accessed=2 * (count * width + width * units + 2 * count * units),
            transcendentals=2 * count * units,
        ),
        name="expand_rows",
    )(rows, weight, bias)


def far_send(array, shift):
    count = lax.axis_size("far")
    return lax.ppermute(array, "far", [(i, (i + shift) % count) for i in range(count)])


def far_gather(array):
    count = lax.axis_size("far")
    return [array] + [far_send(array, count - r) for r in range(1, count)]


def far_exchange(slots):
    count = len(slots)
    out = [slots[0]] + [None] * (count - 1)
    for r in range(1, count):
        out[count - r] = far_send(slots[r], r)
    return out


def far_sum(slots):
    arrived = far_exchange(slots)
    return sum(part.astype(F32) for part in arrived)


def other_core(array):
    return lax.ppermute(array, "core", [(0, 1), (1, 0)])


def fsdp_gather(array):
    return lax.all_gather(array, "fsdp", axis=0, tiled=True)


def fsdp_scatter(array):
    return lax.psum_scatter(array, "fsdp", scatter_dimension=0, tiled=True)


def core_join(mine, axis, core):
    other = other_core(mine)
    return jnp.stack(
        [jnp.where(core == 0, mine, other), jnp.where(core == 0, other, mine)], axis
    )


def shards(
    images,
    cotangent,
    valid_count,
    first_gain,
    first_shift,
    triple_weight,
    query_bias,
    value_bias,
    output_weight,
    output_bias,
    attend_scale,
    second_gain,
    second_shift,
    expand_weight,
    expand_bias,
    reduce_weight,
    reduce_bias,
    feed_scale,
):
    image_count, local_len, width = images.shape
    own_rows = image_count * local_len
    far_count, fsdp_count = lax.axis_size("far"), lax.axis_size("fsdp")
    far, core = lax.axis_index("far"), lax.axis_index("core")
    seq_count = 2 * far_count
    shard = width // fsdp_count
    units = expand_weight.shape[1]
    unit_part = units // (2 * fsdp_count)
    near_heads = width // HEAD_DIM // seq_count
    head_width = near_heads * HEAD_DIM

    def my_heads(array, axis):
        shape = array.shape
        array = array.reshape(
            shape[:axis] + (far_count, near_heads, 2, HEAD_DIM) + shape[axis + 1 :]
        )
        array = lax.dynamic_index_in_dim(array, far, axis, False)
        array = lax.dynamic_index_in_dim(array, core, axis + 1, False)
        return array.reshape(shape[:axis] + (head_width,) + shape[axis + 1 :])

    triple_mine = my_heads(triple_weight.reshape(shard, 3, width), 2).reshape(shard, 3 * head_width)
    bias_mine = lax.dynamic_index_in_dim(expand_bias.reshape(2, unit_part), core, 0, False)
    bias_columns = unit_part // shard
    vectors = [
        first_gain, first_shift, query_bias, value_bias, output_bias, attend_scale,
        second_gain, second_shift, reduce_bias, feed_scale,
    ]
    vector_count = len(vectors)
    packed = jnp.concatenate(
        [triple_mine, jnp.stack(vectors, 1), bias_mine.reshape(shard, bias_columns)], 1
    )
    packed = jnp.pad(packed, ((0, 0), (0, -packed.shape[1] % 128)))
    packed = fsdp_gather(packed)
    triple_whole = packed[:, : 3 * head_width]
    small = packed[:, 3 * head_width : 3 * head_width + vector_count + bias_columns]
    small = small.astype(F32).T
    (gain_1, shift_1, bias_q, bias_v, bias_o, scale_a, gain_2, shift_2, bias_r, scale_f) = [
        small[i] for i in range(vector_count)
    ]
    bias_e = (
        small[vector_count:]
        .reshape(bias_columns, fsdp_count, shard)
        .transpose(1, 2, 0)
        .reshape(1, fsdp_count * unit_part)
    )

    split_output = shard % (2 * HEAD_DIM) == 0
    if split_output:
        output_mine = lax.dynamic_index_in_dim(
            output_weight.reshape(shard // (2 * HEAD_DIM), 2, HEAD_DIM, width), core, 1, False
        ).reshape(shard // 2, width)
        output_whole = fsdp_gather(output_mine)
    else:
        output_whole = lax.dynamic_index_in_dim(
            fsdp_gather(output_weight).reshape(-1, 2, HEAD_DIM, width), core, 1, False
        )
    output_whole = output_whole.reshape(far_count, head_width, width)
    output_whole = jnp.roll(output_whole, -far, 0).reshape(width // 2, width)
    expand_mine = lax.dynamic_index_in_dim(
        expand_weight.reshape(shard, fsdp_count, 2, unit_part), core, 2, False
    ).reshape(shard, units // 2)
    expand_whole = fsdp_gather(expand_mine)
    reduce_mine = lax.dynamic_index_in_dim(
        reduce_weight.reshape(2, unit_part, width), core, 0, False
    )
    reduce_whole = fsdp_gather(reduce_mine)

    mine = images.reshape(own_rows, width)
    slots = far_gather(mine)
    tokens = []
    for slot in slots:
        tokens += [slot, other_core(slot)]
    tokens = jnp.stack(tokens, 0).reshape(seq_count * own_rows, width)
    normal_1, factor_1 = normalize(tokens.astype(F32))
    first_normed = (normal_1 * gain_1 + shift_1).astype(BF)
    joint_bias = jnp.concatenate(
        [my_heads(bias_q, 0), jnp.zeros((head_width,), F32), my_heads(bias_v, 0)]
    )
    triple = (dot(first_normed, triple_whole) + joint_bias).astype(BF)

    last_slot = ((far_count - 1 - far) % far_count) * 2 + (1 - core)
    dead_from = last_slot * local_len + valid_count - (seq_count - 1) * local_len
    limits = jnp.stack(
        [dead_from, jnp.broadcast_to((last_slot + 1) * local_len, dead_from.shape)], 1
    ).astype(jnp.int32)

    direct = local_len % 8 == 0 and head_width % (2 * HEAD_DIM) == 0

    def to_kernel(array):
        array = array.reshape(seq_count, image_count, local_len, -1)
        if direct:
            return array
        parts = array.shape[-1] // head_width
        array = array.transpose(1, 0, 2, 3).reshape(
            1, image_count, seq_count * local_len, parts, head_width
        )
        lanes = -head_width % (2 * HEAD_DIM)
        array = jnp.pad(array, ((0, 0),) * 4 + ((0, lanes),))
        return array.reshape(1, image_count, seq_count * local_len, -1)

    def from_kernel(array):
        if direct:
            return array.reshape(seq_count * own_rows, -1)
        array = array[..., :head_width].reshape(image_count, seq_count, local_len, head_width)
        return array.transpose(1, 0, 2, 3).reshape(seq_count * own_rows, head_width)

    triple_in = to_kernel(triple)
    attended_in, logs = attend_forward(triple_in, limits)
    attended = from_kernel(attended_in).reshape(far_count, 2 * own_rows, head_width)
    attended = far_exchange([attended[r] for r in range(far_count)])
    attended_rows = jnp.concatenate(attended, 1)

    branch = dot(attended_rows, output_whole)
    branch_attend = (
        branch[:own_rows] + other_core(branch[own_rows:].astype(BF)).astype(F32) + bias_o
    )
    inputs = mine.astype(F32)
    residual = inputs + scale_a * branch_attend
    normal_2, factor_2 = normalize(residual)
    second_mine = (normal_2 * gain_2 + shift_2).astype(BF)
    second_normed = jnp.concatenate([second_mine, other_core(second_mine)], 0)
    activated, slope = expand_rows(second_normed, expand_whole, bias_e)
    branch = dot(activated, reduce_whole)
    branch_feed = (
        branch[:own_rows] + other_core(branch[own_rows:].astype(BF)).astype(F32) + bias_r
    )
    outputs = residual + scale_f * branch_feed

    cotangent = cotangent.reshape(own_rows, width)
    upstream = cotangent.astype(F32)
    both = jnp.concatenate([cotangent, other_core(cotangent)], 0)
    grad_feed = (scale_f * both.astype(F32)).astype(BF)
    grad_feed_scale = jnp.sum(upstream * branch_feed, 0)
    grad_reduce_bias = column_total(grad_feed[:own_rows])
    grad_reduce_weight = fsdp_scatter(dot_left_t(activated, grad_feed).astype(BF))
    grad_expanded = (dot_right_t(grad_feed, reduce_whole) * slope.astype(F32)).astype(BF)
    grad_expand_bias = column_total(grad_expanded)
    grad_expand_weight = fsdp_scatter(dot_left_t(second_normed, grad_expanded).astype(BF))
    partial = dot_right_t(grad_expanded, expand_whole)
    upper = partial[:own_rows] + other_core(partial[own_rows:].astype(BF)).astype(F32)
    grad_second_gain = jnp.sum(upper * normal_2, 0)
    grad_second_shift = jnp.sum(upper, 0)
    grad_residual = upstream + normalize_back(normal_2, factor_2, upper * gain_2)
    grad_attend_scale = jnp.sum(grad_residual * branch_attend, 0)
    grad_attend = (scale_a * grad_residual).astype(BF)
    grad_output_bias = column_total(grad_attend)
    grad_attend = jnp.concatenate([grad_attend, other_core(grad_attend)], 0)
    grad_attended = dot_right_t(grad_attend, output_whole).astype(BF)
    grad_attended = far_exchange(
        [grad_attended[:, r * head_width : (r + 1) * head_width] for r in range(far_count)]
    )
    grad_attended = to_kernel(jnp.stack(grad_attended, 0))
    grad_output_weight = dot_left_t(attended_rows, grad_attend).astype(BF)
    grad_output_weight = jnp.roll(
        grad_output_weight.reshape(far_count, head_width, width), far, 0
    ).reshape(width // 2, width)

    pieces = attend_backward(triple_in, attended_in, grad_attended, logs, limits)
    grad_triple = jnp.concatenate([from_kernel(piece) for piece in pieces], 1)

    partial = dot_right_t(grad_triple, triple_whole)
    grad_first_gain = jnp.sum(partial * normal_1, 0)
    grad_first_shift = jnp.sum(partial, 0)
    partial = partial.astype(BF).reshape(far_count, 2, own_rows, width)
    partial = partial[:, 0].astype(F32) + other_core(partial[:, 1]).astype(F32)
    partial = partial.astype(BF)
    upper = far_sum([partial[r] for r in range(far_count)])
    normal, factor = normalize(inputs)
    grad_images = grad_residual + normalize_back(normal, factor, upper * gain_1)

    column_sums = column_total(grad_triple)

    def place_heads(vector):
        here = jnp.arange(far_count)[:, None, None, None] == far
        here = here & (jnp.arange(2)[None, None, :, None] == core)
        vector = vector.reshape(1, near_heads, 1, HEAD_DIM)
        return jnp.where(here, vector, 0.0).reshape(width)

    def place_units(vector):
        vector = vector.reshape(fsdp_count, shard, bias_columns)
        vector = vector.transpose(2, 0, 1).reshape(1, bias_columns, width)
        vector = jnp.where(jnp.arange(2)[:, None, None] == core, vector, 0.0)
        return [vector[i, j] for i in range(2) for j in range(bias_columns)]

    sums = [
        grad_first_gain, grad_first_shift,
        place_heads(column_sums[:head_width]), place_heads(column_sums[2 * head_width :]),
        grad_output_bias, grad_attend_scale, grad_second_gain, grad_second_shift,
        grad_reduce_bias, grad_feed_scale,
    ] + place_units(grad_expand_bias)
    sums = jnp.stack(sums, 0).astype(BF).T
    sums = jnp.pad(sums, ((0, 0), (0, -sums.shape[1] % 128)))
    grad_packed = jnp.concatenate([dot_left_t(first_normed, grad_triple).astype(BF), sums], 1)
    grad_packed = fsdp_scatter(grad_packed)
    grad_packed = lax.all_gather(grad_packed, ("far", "core"), axis=0, tiled=False)
    grad_packed = grad_packed.astype(F32)
    grad_triple_weight = (
        grad_packed[:, :, : 3 * head_width]
        .reshape(far_count, 2, shard, 3, near_heads, HEAD_DIM)
        .transpose(2, 3, 0, 4, 1, 5)
        .reshape(shard, 3 * width)
    )
    sums = jnp.sum(grad_packed[:, :, 3 * head_width :], 0).T

    def far_total(array):
        total = array.astype(F32)
        for r in range(1, far_count):
            total = total + far_send(array, r).astype(F32)
        return total

    if split_output:
        grad_output_weight = far_total(fsdp_scatter(grad_output_weight)).astype(BF)
        grad_output_weight = core_join(
            grad_output_weight.reshape(-1, HEAD_DIM, width), 1, core
        ).reshape(shard, width)
    else:
        spread = grad_output_weight.reshape(-1, 1, HEAD_DIM, width)
        spread = jnp.where(jnp.arange(2)[None, :, None, None] == core, spread, 0)
        spread = fsdp_scatter(spread.reshape(width, width))
        grad_output_weight = far_total(spread)
        grad_output_weight = grad_output_weight + other_core(grad_output_weight)
    grad_expand_weight = core_join(
        far_total(grad_expand_weight).astype(BF).reshape(shard, fsdp_count, unit_part), 2, core
    ).reshape(shard, units)
    grad_reduce_weight = core_join(far_total(grad_reduce_weight).astype(BF), 0, core).reshape(
        2 * unit_part, width
    )
    grad_expand_bias = (
        sums[10 : 10 + 2 * bias_columns]
        .reshape(2, bias_columns, shard)
        .transpose(0, 2, 1)
        .reshape(2 * unit_part)
    )
    return (
        outputs.reshape(image_count, local_len, width).astype(BF),
        grad_images.reshape(image_count, local_len, width),
        sums[0],
        sums[1],
        grad_triple_weight,
        sums[2],
        sums[3],
        grad_output_weight.astype(F32),
        sums[4],
        sums[5],
        sums[6],
        sums[7],
        grad_expand_weight.astype(F32),
        grad_expand_bias,
        grad_reduce_weight.astype(F32),
        sums[8],
        sums[9],
    )


def solution(mesh):
    fsdp, seq = mesh.devices.shape
    split = Mesh(mesh.devices.reshape(fsdp, seq // 2, 2), ("fsdp", "far", "core"))
    tokens = P("fsdp", ("far", "core"), None)
    row, matrix = P("fsdp"), P("fsdp", None)
    return jax.shard_map(
        shards,
        mesh=split,
        in_specs=(
            tokens, tokens, row, row, row, matrix, row, row, matrix,
            row, row, row, row, matrix, row, matrix, row, row,
        ),
        out_specs=(
            tokens, tokens, row, row, matrix, row, row, matrix,
            row, row, row, row, matrix, row, matrix, row, row,
        ),
        check_vma=False,
    )
```

time: 1130 us -> 673 us (0.60)
  blocking collectives: 353 us -> 17.2 us
  matrix products: 322 us -> 84.2 us
  waiting for transfers between devices: 193 us -> 326 us
  Pallas kernels: 0 us -> 93.1 us
  local copies, waits for them, and re-layouts: 115 us -> 53.8 us
  other arithmetic: 103 us -> 63.2 us
    dot_general x30 -> x15, matrix products: 322 us -> 84.2 us  [the longest x4 33.6 us: dot_left_t(): lax.dot_general(left, right, (((0,), (0,)), ((), ())), preferred_element_...]
    all_gather x11 -> x1, blocking collectives: 204 us -> 17.2 us  [shards(): lax.all_gather(grad_packed, ('far', 'core'), axis=0, tiled=False)]
    psum x1 -> x0, blocking collectives: 112 us -> none  [shards(): lax.psum((owned[0], owned[1], owned[2], owned[3], owned[4], owned[5], own...]
    reduce_scatter x4, waiting for transfers between devices: 62.1 us -> 168 us  [fsdp_scatter(): return lax.psum_scatter(array, 'fsdp', scatter_dimension=0, tiled=True)]
    all_to_all x4 -> x0, waiting for transfers between devices: 101 us -> none  [the longest x1 53.2 us: shards(): lax.all_to_all(triple, 'seq', split_axis=3, concat_axis=1, tiled=True)]
    pallas_call x0 -> x3, Pallas kernels: none -> 93.1 us  [the longest x1 46.3 us: attend_backward(): pl.pallas_call(attend_backward_kernel, grid_spec=pltpu.PrefetchScalarGrid...]
    ppermute x0 -> x19, waiting for transfers between devices: none -> 75.4 us  [the longest x7 69.4 us: far_send(): lax.ppermute(array, 'far', [(i, (i + shift) % count) for i in range(count)])]
    all_gather x4, waiting for transfers between devices: 26.9 us -> 82.1 us  [fsdp_gather(): return lax.all_gather(array, 'fsdp', axis=0, tiled=True)]
  transfers between devices with their start and end apart: 12 -> 27, of which waited for: 4 -> 13; matrix products, arithmetic and copies ran while one was open for 43% -> 23% of each run, Pallas kernels for 0% -> 14%
where the time goes in v1:
time: 673 us; the launch traced here: 668 us
  waiting for transfers between devices  326 us (48%)
  Pallas kernels  93.1 us (14%)
  matrix products  84.2 us (13%)
  other arithmetic  63.2 us (9%)
  local copies, waits for them, and re-layouts  53.8 us (8%)
  blocking collectives  17.2 us (3%)
  between operations  15.4 us (2%)
  starting transfers between devices  15.1 us (2%)
    reduce_scatter x4, waiting for transfers between devices, fsdp_scatter(): return lax.psum_scatter(array, 'fsdp', scatter_dimension=0, tiled=True)  168 us
    all_gather x4, waiting for transfers between devices, fsdp_gather(): return lax.all_gather(array, 'fsdp', axis=0, tiled=True)  82.1 us
    ppermute x7, waiting for transfers between devices, far_send(): lax.ppermute(array, 'far', [(i, (i + shift) % count) for i in range(count)])  69.4 us
    pallas_call x1, Pallas kernels, attend_backward(): pl.pallas_call(attend_backward_kernel, grid_spec=pltpu.PrefetchScalarGrid...  46.3 us
    dot_general x4, matrix products, dot_left_t(): lax.dot_general(left, right, (((0,), (0,)), ((), ())), preferred_element_...  33.6 us
    dot_general x4, matrix products, dot_right_t(): lax.dot_general(left, right, (((1,), (1,)), ((), ())), preferred_element_...  32 us
    pallas_call x1, Pallas kernels, attend_forward(): pl.pallas_call(attend_forward_kernel, grid_spec=pltpu.PrefetchScalarGridS...  28.2 us
    pallas_call x1, Pallas kernels, expand_rows(): pl.pallas_call(expand_kernel, grid=(units // tile,), in_specs=[pl.BlockSp...  18.7 us
  transfers between devices with their start and end apart: 27, of which 13 were waited for; matrix products, arithmetic and copies ran while one was open for 23% of the time, Pallas kernels for 14%

profile of v1, /device:TPU:0, one launch (start us, length us, event | category | flops | bytes accessed | tf_op | source)
XLA Modules:
  0.0 667.8 jit_solution(3198571697708009008)
XLA Ops:
  22.0 31.0 %collective-permute-done.1 = bf16[688,1024]{1,0:T(8,128)(2,1)} collective-permute-done((bf16[688,1024]{1,0:T(8,128)(2,1)S(1)}, bf16[688,1024]{1,0:T(8,128)(2,1)}, u32[]{:S(2)}, u32[]{:S(2)}) %collective-permute-start.1) | collective-permute-done | bytes 1409056 | tf_op jit(solution)/shard_map/ppermute | solution.py:311
  59.3 4.5 multiply_reduce_fusion.1
  65.6 7.7 %add_convert_fusion = bf16[2752,1024]{1,0:T(8,128)(2,1)S(1)} fusion(f32[1024]{0:T(1024)S(1)} %bitcast.206, f32[1024]{0:T(1024)S(1)} %bitcast.193, f32[2752]{0:T(1024)S(1)} %rsqrt.31, f32[2752]{0:T(1024)S(1)} %div.35, bf16[1,688,1024]{2,1,0:T(8,128)(2,1)} %bitcast.19, bf16[1,688,1024]{2,1,0:T(8,128)(2,1)} %bitcast.18, bf16[1,688,1024]{2,1,0:T(8,128)(2,1)} %bitcast.17, ...), kind=kLoop, calls=%fused_computation.4 | loop fusion | flops 25362432 | bytes 11302400 | tf_op jit(solution)/shard_map/convert_element_type | solution.py:445
  73.3 6.2 add_convert_fusion.1
  79.6 28.2 %attend_forward.1 = (bf16[4,2,344,256]{3,2,1,0:T(8,128)(2,1)S(1)}, f32[2,2,1376,128]{3,2,1,0:T(8,128)}) custom-call(s32[2,2]{1,0:T(2,128)S(1)} %stack.123.limit_ref, bf16[4,2,344,768]{3,2,1,0:T(8,128)(2,1)} %bitcast.220, bf16[4,2,344,768]{3,2,1,0:T(8,128)(2,1)} %bitcast.221, bf16[4,2,344,768]{3,2,1,0:T(8,128)(2,1)} %bitcast.222), custom_call_target="tpu_custom_call" | custom-call | flops 15510536192 | bytes 8454144 | tf_op jit(solution)/shard_map/attend_forward/pallas_call | solution.py:201
  112.3 14.5 %collective-permute-done.3 = bf16[1376,256]{1,0:T(8,128)(2,1)S(1)} collective-permute-done((bf16[1376,256]{1,0:T(8,128)(2,1)S(1)}, bf16[1376,256]{1,0:T(8,128)(2,1)S(1)}, u32[]{:S(2)}, u32[]{:S(2)}) %collective-permute-start.3) | collective-permute-done | bytes 704544 | tf_op jit(solution)/shard_map/ppermute | solution.py:311
  126.8 4.1 fusion.33
  133.6 3.9 collective-permute-done.4
  146.2 4.2 multiply_convert_fusion.1
  152.4 26.5 %all-gather.10.cloned.1.call-done.weight_ref = bf16[1024,2048]{1,0:T(8,128)(2,1)} async-done(((bf16[128,2048]{1,0:T(8,128)(2,1)}), bf16[1024,2048]{1,0:T(8,128)(2,1)}) %all-gather.10.cloned.1.call-update) | async-done | bytes 4194320 | tf_op jit(solution)/shard_map/all_gather | solution.py:337
  179.0 18.7 %expand_rows.1 = (bf16[1376,2048]{1,0:T(8,128)(2,1)}, bf16[1376,2048]{1,0:T(8,128)(2,1)}) custom-call(bf16[1376,1024]{1,0:T(8,128)(2,1)S(1)} %pad_maximum_fusion.2.rows_ref, bf16[1024,2048]{1,0:T(8,128)(2,1)} %all-gather.10.cloned.1.call-done.weight_ref, f32[1,2048]{1,0:T(1,128)S(1)} %reshape.370.bias_ref), custom_call_target="tpu_custom_call" | custom-call | flops 11542724608 | bytes 18284544 | tf_op jit(solution)/shard_map/expand_rows/pallas_call | solution.py:289
  197.7 55.6 %all-gather.14.cloned.1.call-done = bf16[1,2048,1024]{2,1,0:T(8,128)(2,1)} async-done(((bf16[1,256,1024]{2,1,0:T(8,128)(2,1)}), bf16[1,2048,1024]{2,1,0:T(8,128)(2,1)}) %all-gather.14.cloned.1.call-update) | async-done | bytes 4194320 | tf_op jit(solution)/shard_map/all_gather | solution.py:337
  253.2 9.9 %multiply_convert_fusion = bf16[1376,2048]{1,0:T(8,128)(2,1)S(1)} fusion(bf16[1376,2048]{1,0:T(8,128)(2,1)} %get-tuple-element.27, bf16[1376,1024]{1,0:T(8,128)(2,1)} %multiply_convert_fusion.1, bf16[1,2048,1024]{2,1,0:T(8,128)(2,1)} %all-gather.14.cloned.1.call-done), kind=kOutput, calls=%fused_computation.3 | convolution fusion | flops 5779816448 | bytes 18284544 | tf_op jit(solution)/shard_map/dot_general | solution.py:26
  263.2 6.1 fusion.55
  270.8 6.1 fusion.4
  280.8 4.3 multiply_reduce_fusion.2
  285.2 7.3 %fusion.16 = (bf16[1024]{0:T(1024)(128)(2,1)}, bf16[688,1024]{1,0:T(8,128)(2,1)}, bf16[1024]{0:T(1024)(128)(2,1)}, f32[688,1024]{1,0:T(8,128)S(1)}) fusion(bf16[688,1024]{1,0:T(8,128)(2,1)} %collective-permute-done.6, f32[1376,1024]{1,0:T(8,128)} %copy-done.17, f32[1024]{0:T(1024)S(1)} %bitcast.208, bf16[2,344,1024]{2,1,0:T(8,128)(2,1)} %param.21, ...), kind=kLoop, calls=%fused_computation.35 | loop fusion | flops 16906240 | bytes 21166848 | tf_op jit(solution)/shard_map/reduce_sum | solution.py:503
  307.8 11.6 %collective-permute-done.10 = bf16[1376,256]{1,0:T(8,128)(2,1)} collective-permute-done((bf16[1376,256]{1,0:T(8,128)(2,1)S(1)}, bf16[1376,256]{1,0:T(8,128)(2,1)}, u32[]{:S(2)}, u32[]{:S(2)}) %collective-permute-start.10) | collective-permute-done | bytes 704544 | tf_op jit(solution)/shard_map/ppermute | solution.py:311
  321.8 46.3 %attend_backward.1 = (bf16[4,2,344,256]{3,2,1,0:T(8,128)(2,1)}, bf16[4,2,344,256]{3,2,1,0:T(8,128)(2,1)}, bf16[4,2,344,256]{3,2,1,0:T(8,128)(2,1)}) custom-call(s32[2,2]{1,0:T(2,128)} %copy-done.3, bf16[4,2,344,768]{3,2,1,0:T(8,128)(2,1)} %bitcast.223, bf16[4,2,344,768]{3,2,1,0:T(8,128)(2,1)} %bitcast.224, bf16[4,2,344,768]{3,2,1,0:T(8,128)(2,1)} %bitcast.225, ...), custom_call_target="tpu_custom_call" | custom-call | flops 38776340480 | bytes 16908288 | tf_op jit(solution)/shard_map/attend_backward/pallas_call | solution.py:236
  368.1 13.0 %fusion.52 = (bf16[1024]{0:T(1024)(128)(2,1)S(1)}, bf16[1024]{0:T(1024)(128)(2,1)S(1)}, bf16[2752,1024]{1,0:T(8,128)(2,1)}) fusion(f32[2752]{0:T(1024)S(1)} %copy-done.29, f32[2752]{0:T(1024)S(1)} %copy-done.27, bf16[1,688,1024]{2,1,0:T(8,128)(2,1)} %bitcast.19, bf16[1,688,1024]{2,1,0:T(8,128)(2,1)} %bitcast.18, bf16[1,688,1024]{2,1,0:T(8,128)(2,1)} %bitcast.17, ...), kind=kOutput, calls=%fused_computation.164 | convolution fusion | flops 4380653568 | bytes 17100800 | tf_op jit(solution)/shard_map/dot_general | solution.py:26
  382.5 8.1 %convolution_convert_fusion.3 = bf16[1024,768]{0,1:T(8,128)(2,1)S(1)} fusion(bf16[2752,1024]{1,0:T(8,128)(2,1)} %copy-done.15, bf16[2752,256]{1,0:T(8,128)(2,1)} %bitcast.233, bf16[2752,256]{1,0:T(8,128)(2,1)} %bitcast.230, bf16[2752,256]{1,0:T(8,128)(2,1)S(1)} %bitcast.228), kind=kOutput, calls=%fused_computation.68 | convolution fusion | flops 4341989376 | bytes 11436032 | tf_op jit(solution)/shard_map/dot_general | solution.py:22
  393.3 11.3 %convolution_convert_fusion = bf16[2048,1024]{1,0:T(8,128)(2,1)} fusion(bf16[1376,2048]{1,0:T(8,128)(2,1)} %get-tuple-element.26, bf16[1376,1024]{1,0:T(8,128)(2,1)} %multiply_convert_fusion.1), kind=kOutput, calls=%fused_computation.17 | convolution fusion | flops 5773459456 | bytes 12648448 | tf_op jit(solution)/shard_map/dot_general | solution.py:22
  404.7 11.0 %convolution_convert_fusion.1 = bf16[1024,2048]{1,0:T(8,128)(2,1)} fusion(bf16[1376,2048]{1,0:T(8,128)(2,1)} %copy-done.16, bf16[688,1024]{1,0:T(8,128)(2,1)} %collective-permute-done.5, bf16[688,1024]{1,0:T(8,128)(2,1)} %add_convert_fusion.3), kind=kOutput, calls=%fused_computation.18 | convolution fusion | flops 5779095552 | bytes 12648448 | tf_op jit(solution)/shard_map/dot_general | solution.py:22
  415.7 3.6 slice_bitcast_fusion
  421.9 4.5 collective-permute-done.13
  427.5 5.7 fusion.1
  438.1 19.6 %reduce-scatter.13.cloned.1.call-done = bf16[128,896]{1,0:T(8,128)(2,1)} async-done(((bf16[1024,896]{1,0:T(8,128)(2,1)}), bf16[128,896]{1,0:T(8,128)(2,1)}) %reduce-scatter.13.cloned.1.call-update) | async-done | bytes 229392 | tf_op jit(solution)/shard_map/reduce_scatter | solution.py:341
  457.7 17.2 %all-gather.2 = bf16[512,896]{1,0:T(8,128)(2,1)S(1)} all-gather(bf16[128,896]{1,0:T(8,128)(2,1)} %reduce-scatter.13.cloned.1.call-done), channel_id=4, replica_groups=mesh['fsdp'=8,'far'=2,'core'=2] {'far','core'}, dimensions={0}, use_global_device_ids=true | all-gather | bytes 1146880 | tf_op jit(solution)/shard_map/all_gather | solution.py:565
  487.2 60.9 %reduce-scatter.11.cloned.1.call-done = bf16[256,1024]{1,0:T(8,128)(2,1)} async-done(((bf16[2048,1024]{1,0:T(8,128)(2,1)}), bf16[256,1024]{1,0:T(8,128)(2,1)}) %reduce-scatter.11.cloned.1.call-update) | async-done | bytes 524304 | tf_op jit(solution)/shard_map/reduce_scatter | solution.py:341
  552.4 87.6 %reduce-scatter.9.cloned.1.call-done = bf16[128,2048]{1,0:T(8,128)(2,1)} async-done(((bf16[1024,2048]{1,0:T(8,128)(2,1)}), bf16[128,2048]{1,0:T(8,128)(2,1)}) %reduce-scatter.9.cloned.1.call-update) | async-done | bytes 524304 | tf_op jit(solution)/shard_map/reduce_scatter | solution.py:341
  641.7 4.4 fusion.15
  646.1 7.8 %collective-permute-done.15 = bf16[128,2048]{1,0:T(8,128)(2,1)S(1)} collective-permute-done((bf16[128,2048]{1,0:T(8,128)(2,1)}, bf16[128,2048]{1,0:T(8,128)(2,1)S(1)}, u32[]{:S(2)}, u32[]{:S(2)}) %collective-permute-start.15) | collective-permute-done | bytes 524320 | tf_op jit(solution)/shard_map/ppermute | solution.py:311
  (277 shorter events, 101.1 us)
Async XLA Ops:
  7.2 56.6 %all-gather.8.cloned.1.call-start = ((), (), s32[]{:S(2)}) async-start(), calls=%async_computation.4 | async-start | bytes 2064384 | tf_op jit(solution)/shard_map/all_gather | solution.py:337
  12.2 98.5 %all-gather.12.cloned.1.call-start = ((), (), s32[]{:S(2)}) async-start(), calls=%async_computation.9 | async-start | bytes 1179648 | tf_op jit(solution)/shard_map/all_gather | solution.py:337
  13.0 166.0 %all-gather.10.cloned.1.call-start = ((), (), s32[]{:S(2)}) async-start(), calls=%async_computation.5 | async-start | bytes 4718592 | tf_op jit(solution)/shard_map/all_gather | solution.py:337
  18.9 234.3 %all-gather.14.cloned.1.call-start = ((), (), s32[]{:S(2)}) async-start(), calls=%async_computation.10 | async-start | bytes 4718592 | tf_op jit(solution)/shard_map/all_gather | solution.py:337
  19.0 34.0 %collective-permute-start.1 = (bf16[688,1024]{1,0:T(8,128)(2,1)S(1)}, bf16[688,1024]{1,0:T(8,128)(2,1)}, u32[]{:S(2)}, u32[]{:S(2)}) collective-permute-start(bf16[688,1024]{1,0:T(8,128)(2,1)S(1)} %bitcast.158), channel_id=1, source_target_pairs={{0,2},{2,0},{1,3},{3,1},{4,6},{6,4},{5,7},{7,5},{8,10},{10,8},{9,1... | collective-permute-start | bytes 4227080 | tf_op jit(solution)/shard_map/ppermute | solution.py:311
  22.0 32.6 %collective-permute-start = (bf16[688,1024]{1,0:T(8,128)(2,1)S(1)}, bf16[688,1024]{1,0:T(8,128)(2,1)}, u32[]{:S(2)}, u32[]{:S(2)}) collective-permute-start(bf16[688,1024]{1,0:T(8,128)(2,1)S(1)} %bitcast.159), channel_id=1, source_target_pairs={{0,1},{1,0},{2,3},{3,2},{4,5},{5,4},{6,7},{7,6},{8,9},{9,8},{10,11... | collective-permute-start | bytes 4227080 | tf_op jit(solution)/shard_map/ppermute | solution.py:333
  53.0 3.5 collective-permute-start.2
  53.8 366.4 %reduce-scatter.7.cloned.1.call-start = ((), (), s32[]{:S(2)}) async-start(), calls=%async_computation.6 | async-start | bytes 1179648 | tf_op jit(solution)/shard_map/reduce_scatter | solution.py:341
  108.9 17.9 %collective-permute-start.3 = (bf16[1376,256]{1,0:T(8,128)(2,1)S(1)}, bf16[1376,256]{1,0:T(8,128)(2,1)S(1)}, u32[]{:S(2)}, u32[]{:S(2)}) collective-permute-start(bf16[1376,256]{1,0:T(8,128)(2,1)S(1)} %bitcast.191), channel_id=1, source_target_pairs={{0,2},{2,0},{1,3},{3,1},{4,6},{6,4},{5,7},{7,5},{8,10},{10,8},{9,1... | collective-permute-start | bytes 2113544 | tf_op jit(solution)/shard_map/ppermute | solution.py:311
  133.0 4.5 collective-permute-start.4
  133.1 13.1 %collective-permute-start.7 = (bf16[688,1024]{1,0:T(8,128)(2,1)}, bf16[688,1024]{1,0:T(8,128)(2,1)}, u32[]{:S(2)}, u32[]{:S(2)}) collective-permute-start(bf16[688,1024]{1,0:T(8,128)(2,1)} %bitcast.39), channel_id=1, source_target_pairs={{0,1},{1,0},{2,3},{3,2},{4,5},{5,4},{6,7},{7,6},{8,9},{9,8},{10,11... | collective-permute-start | bytes 4227080 | tf_op jit(solution)/shard_map/ppermute | solution.py:333
  144.8 5.6 collective-permute-start.5
  270.8 10.0 %collective-permute-start.8 = (bf16[688,1024]{1,0:T(8,128)(2,1)}, bf16[688,1024]{1,0:T(8,128)(2,1)}, u32[]{:S(2)}, u32[]{:S(2)}) collective-permute-start(bf16[688,1024]{1,0:T(8,128)(2,1)} %slice.334), channel_id=1, source_target_pairs={{0,1},{1,0},{2,3},{3,2},{4,5},{5,4},{6,7},{7,6},{8,9},{9,8},{10,11... | collective-permute-start | bytes 4227080 | tf_op jit(solution)/shard_map/ppermute | solution.py:333
  280.3 4.8 collective-permute-start.6
  294.4 3.8 collective-permute-start.9
  301.4 18.1 %collective-permute-start.10 = (bf16[1376,256]{1,0:T(8,128)(2,1)S(1)}, bf16[1376,256]{1,0:T(8,128)(2,1)}, u32[]{:S(2)}, u32[]{:S(2)}) collective-permute-start(bf16[1376,256]{1,0:T(8,128)(2,1)S(1)} %get-tuple-element.164), channel_id=1, source_target_pairs={{0,2},{2,0},{1,3},{3,1},{4,6},{6,4},{5,7},{7,5},{8,10},{10,8},{9,1... | collective-permute-start | bytes 2113544 | tf_op jit(solution)/shard_map/ppermute | solution.py:311
  307.8 150.0 %reduce-scatter.13.cloned.1.call-start = ((), (), s32[]{:S(2)}) async-start(), calls=%async_computation.11 | async-start | bytes 2064384 | tf_op jit(solution)/shard_map/reduce_scatter | solution.py:341
  321.8 46.3 %copy-start.27 = (f32[2752]{0:T(1024)S(1)}, f32[2752]{0:T(1024)}, u32[]{:S(2)}) copy-start(f32[2752]{0:T(1024)} %copy-done.26) | copy-start | bytes 33028
  321.8 46.3 %copy-start.29 = (f32[2752]{0:T(1024)S(1)}, f32[2752]{0:T(1024)}, u32[]{:S(2)}) copy-start(f32[2752]{0:T(1024)} %copy-done.28) | copy-start | bytes 33028
  321.8 46.3 %copy-start.38 = (bf16[1024,896]{0,1:T(8,128)(2,1)S(1)}, bf16[1024,896]{0,1:T(8,128)(2,1)}, u32[]{:S(2)}) copy-start(bf16[1024,896]{0,1:T(8,128)(2,1)} %all-gather.8.cloned.1.call-done) | copy-start | bytes 5505028
  393.2 154.8 %reduce-scatter.11.cloned.1.call-start = ((), (), s32[]{:S(2)}) async-start(), calls=%async_computation.8 | async-start | bytes 4718592 | tf_op jit(solution)/shard_map/reduce_scatter | solution.py:341
  404.7 235.3 %reduce-scatter.9.cloned.1.call-start = ((), (), s32[]{:S(2)}) async-start(), calls=%async_computation.7 | async-start | bytes 4718592 | tf_op jit(solution)/shard_map/reduce_scatter | solution.py:341
  419.4 8.1 %collective-permute-start.11 = (bf16[2,688,1024]{2,1,0:T(8,128)(2,1)}, bf16[2,688,1024]{2,1,0:T(8,128)(2,1)}, u32[]{:S(2)}, u32[]{:S(2)}) collective-permute-start(bf16[2,688,1024]{2,1,0:T(8,128)(2,1)} %slice_bitcast_fusion), channel_id=1, source_target_pairs={{0,1},{1,0},{2,3},{3,2},{4,5},{5,4},{6,7},{7,6},{8,9},{9,8},{10,11... | collective-permute-start | bytes 8454152 | tf_op jit(solution)/shard_map/ppermute | solution.py:333
  420.3 6.2 collective-permute-start.13
  427.4 9.8 %collective-permute-start.14 = (bf16[1,64,1024]{2,1,0:T(8,128)(2,1)S(1)}, bf16[1,64,1024]{2,1,0:T(8,128)(2,1)S(1)}, u32[]{:S(2)}, u32[]{:S(2)}) collective-permute-start(bf16[1,64,1024]{2,1,0:T(8,128)(2,1)S(1)} %fusion.34), channel_id=1, source_target_pairs={{0,1},{1,0},{2,3},{3,2},{4,5},{5,4},{6,7},{7,6},{8,9},{9,8},{10,11... | collective-permute-start | bytes 393224 | tf_op jit(solution)/shard_map/ppermute | solution.py:333
  435.7 113.9 %collective-permute-start.12 = (bf16[688,1024]{1,0:T(8,128)(2,1)}, bf16[688,1024]{1,0:T(8,128)(2,1)}, u32[]{:S(2)}, u32[]{:S(2)}) collective-permute-start(bf16[688,1024]{1,0:T(8,128)(2,1)} %slice_bitcast_fusion.2), channel_id=1, source_target_pairs={{0,2},{2,0},{1,3},{3,1},{4,6},{6,4},{5,7},{7,5},{8,10},{10,8},{9,1... | collective-permute-start | bytes 4227080 | tf_op jit(solution)/shard_map/ppermute | solution.py:311
  482.1 67.4 %copy-start.24 = (f32[1,1024]{1,0:T(1,128)S(1)}, f32[1,1024]{1,0:T(1,128)}, u32[]{:S(2)}) copy-start(f32[1,1024]{1,0:T(1,128)} %copy-done.23) | copy-start | bytes 12292
  548.1 93.4 %copy-start.21 = (bf16[256,1024]{1,0:T(8,128)(2,1)S(1)}, bf16[256,1024]{1,0:T(8,128)(2,1)}, u32[]{:S(2)}) copy-start(bf16[256,1024]{1,0:T(8,128)(2,1)} %reduce-scatter.11.cloned.1.call-done) | copy-start | bytes 1572868
  548.1 93.4 %collective-permute-start.17 = (bf16[256,1024]{1,0:T(8,128)(2,1)}, bf16[256,1024]{1,0:T(8,128)(2,1)S(1)}, u32[]{:S(2)}, u32[]{:S(2)}) collective-permute-start(bf16[256,1024]{1,0:T(8,128)(2,1)} %reduce-scatter.11.cloned.1.call-done), channel_id=1, source_target_pairs={{0,2},{2,0},{1,3},{3,1},{4,6},{6,4},{5,7},{7,5},{8,10},{10,8},{9,1... | collective-permute-start | bytes 1572872 | tf_op jit(solution)/shard_map/ppermute | solution.py:311
  640.0 13.9 %collective-permute-start.15 = (bf16[128,2048]{1,0:T(8,128)(2,1)}, bf16[128,2048]{1,0:T(8,128)(2,1)S(1)}, u32[]{:S(2)}, u32[]{:S(2)}) collective-permute-start(bf16[128,2048]{1,0:T(8,128)(2,1)} %reduce-scatter.9.cloned.1.call-done), channel_id=1, source_target_pairs={{0,2},{2,0},{1,3},{3,1},{4,6},{6,4},{5,7},{7,5},{8,10},{10,8},{9,1... | collective-permute-start | bytes 1572872 | tf_op jit(solution)/shard_map/ppermute | solution.py:311
  641.7 12.6 %collective-permute-start.18 = (bf16[256,1024]{1,0:T(8,128)(2,1)S(1)}, bf16[256,1024]{1,0:T(8,128)(2,1)S(1)}, u32[]{:S(2)}, u32[]{:S(2)}) collective-permute-start(bf16[256,1024]{1,0:T(8,128)(2,1)S(1)} %add_convert_fusion.4), channel_id=1, source_target_pairs={{0,1},{1,0},{2,3},{3,2},{4,5},{5,4},{6,7},{7,6},{8,9},{9,8},{10,11... | collective-permute-start | bytes 1572872 | tf_op jit(solution)/shard_map/ppermute | solution.py:333
  654.2 2.0 collective-permute-start.16
  (49 other events, 439.9 us)
Sparse Core Ops, SparseCore 0:
  12.3 50.6 all-gather.7
  65.7 38.3 all-gather.11
  106.8 72.1 all-gather.9
  181.5 71.6 all-gather.13
  307.9 60.8 reduce-scatter.6
  393.4 64.3 reduce-scatter.12
  461.4 86.6 reduce-scatter.10
  552.1 87.8 reduce-scatter.8

commit v2 on v1

--- a/solution.py
+++ b/solution.py
@@ -120,7 +120,7 @@
 
 
 def attend_backward_kernel(
-    limit_ref, q_ref, k_ref, v_ref, o_ref, g_ref, log_ref, dq_ref, dk_ref, dv_ref,
+    limit_ref, q_ref, k_ref, v_ref, o_ref, g_ref, log_ref, grad_ref,
     q_s, k_s, v_s, o_s, g_s, dq_s, dk_s, dv_s,
 ):
     pieces, _, rows, block = q_ref.shape
@@ -173,11 +173,12 @@
         else:
             dk_s[...] = jnp.where(own, dk, dk_s[...])
             dv_s[...] = jnp.where(own, dv, dv_s[...])
+    stride = grad_ref.shape[3] // 3
     for piece in range(pieces):
         part = pl.ds(piece * rows, rows)
-        dq_ref[piece, 0] = dq_s[part, :].astype(BF)
-        dk_ref[piece, 0] = dk_s[part, :].astype(BF)
-        dv_ref[piece, 0] = dv_s[part, :].astype(BF)
+        for which, grad in enumerate((dq_s, dk_s, dv_s)):
+            at = pl.multiple_of(which * stride + pl.program_id(1) * block, block)
+            grad_ref[piece, 0, :, pl.ds(at, block)] = grad[part, :].astype(BF)
 
 
 def attend_specs(pieces, rows, first):
@@ -231,7 +232,6 @@
     pairs = head_width // (2 * HEAD_DIM)
     wide = pltpu.VMEM((length, 2 * HEAD_DIM), F32)
     spec = functools.partial(attend_specs, pieces, rows)
-    shape = jax.ShapeDtypeStruct((pieces, images, rows, head_width), BF)
     heads = images * head_width // HEAD_DIM
     return pl.pallas_call(
         attend_backward_kernel,
@@ -246,10 +246,12 @@
                 spec(0),
                 pl.BlockSpec((1, 1, length, 2 * HEAD_DIM), lambda i, p, limits: (i, p, 0, 0)),
             ],
-            out_specs=[spec(0)] * 3,
+            out_specs=pl.BlockSpec(
+                (pieces, 1, rows, columns), lambda image, pair, limits: (0, image, 0, 0)
+            ),
             scratch_shapes=[wide] * 8,
         ),
-        out_shape=[shape] * 3,
+        out_shape=jax.ShapeDtypeStruct(triple.shape, BF),
         compiler_params=pltpu.CompilerParams(vmem_limit_bytes=56 * 2**20),
         cost_estimate=pl.CostEstimate(
             flops=heads * length * length * 2560,
@@ -258,6 +260,88 @@
         ),
         name="attend_backward",
     )(limits, triple, triple, triple, attended, grad, logs)
+
+
+def project_kernel(rows_ref, gain_ref, shift_ref, weight_ref, bias_ref, normed_ref, triple_ref):
+    normal, _ = normalize(rows_ref[0].astype(F32))
+    normed = (normal * gain_ref[...] + shift_ref[...]).astype(BF)
+    normed_ref[0] = normed
+    triple_ref[0] = (dot(normed, weight_ref[...]) + bias_ref[...]).astype(BF)
+
+
+def project(tokens, gain, shift, weight, bias):
+    pieces, rows, width = tokens.shape
+    columns = weight.shape[1]
+
+    def whole(array):
+        return pl.BlockSpec(array.shape, lambda i: (0, 0))
+
+    def piece(columns):
+        return pl.BlockSpec((1, rows, columns), lambda i: (i, 0, 0))
+
+    return pl.pallas_call(
+        project_kernel,
+        grid=(pieces,),
+        in_specs=[piece(width), whole(gain), whole(shift), whole(weight), whole(bias)],
+        out_specs=[piece(width), piece(columns)],
+        out_shape=[
+            jax.ShapeDtypeStruct((pieces, rows, width), BF),
+            jax.ShapeDtypeStruct((pieces, rows, columns), BF),
+        ],
+        compiler_params=pltpu.CompilerParams(vmem_limit_bytes=40 * 2**20),
+        cost_estimate=pl.CostEstimate(
+            flops=2 * pieces * rows * width * columns,
+            bytes_accessed=2 * pieces * rows * (2 * width + columns),
+            transcendentals=0,
+        ),
+        name="project",
+    )(tokens, gain, shift, weight, bias)
+
+
+def project_back_kernel(grad_ref, rows_ref, weight_ref, part_ref, gain_ref, shift_ref, total_ref):
+    @pl.when(pl.program_id(0) == 0)
+    def _():
+        gain_ref[...] = jnp.zeros_like(gain_ref)
+        shift_ref[...] = jnp.zeros_like(shift_ref)
+        total_ref[...] = jnp.zeros_like(total_ref)
+
+    normal, _ = normalize(rows_ref[0].astype(F32))
+    part = dot_right_t(grad_ref[0], weight_ref[...])
+    part_ref[0] = part.astype(BF)
+    gain_ref[...] += jnp.sum(part * normal, 0, keepdims=True)
+    shift_ref[...] += jnp.sum(part, 0, keepdims=True)
+    total_ref[...] += jnp.sum(grad_ref[0].astype(F32), 0, keepdims=True)
+
+
+def project_back(grad, tokens, weight):
+    pieces, rows, width = tokens.shape
+    columns = weight.shape[1]
+
+    def piece(columns):
+        return pl.BlockSpec((1, rows, columns), lambda i: (i, 0, 0))
+
+    def whole(shape):
+        return pl.BlockSpec(shape, lambda i: (0, 0))
+
+    return pl.pallas_call(
+        project_back_kernel,
+        grid=(pieces,),
+        in_specs=[piece(columns), piece(width), whole(weight.shape)],
+        out_specs=[piece(width), whole((1, width)), whole((1, width)), whole((1, columns))],
+        out_shape=[
+            jax.ShapeDtypeStruct((pieces, rows, width), BF),
+            jax.ShapeDtypeStruct((1, width), F32),
+            jax.ShapeDtypeStruct((1, width), F32),
+            jax.ShapeDtypeStruct((1, columns), F32),
+        ],
+        compiler_params=pltpu.CompilerParams(vmem_limit_bytes=40 * 2**20),
+        cost_estimate=pl.CostEstimate(
+            flops=2 * pieces * rows * width * columns,
+            bytes_accessed=2 * pieces * rows * (2 * width + columns),
+            transcendentals=0,
+        ),
+        name="project_back",
+    )(grad, tokens, weight)
 
 
 def gelu_parts(values):
@@ -339,6 +423,51 @@
 
 def fsdp_scatter(array):
     return lax.psum_scatter(array, "fsdp", scatter_dimension=0, tiled=True)
+
+
+def ring_send(array, step):
+    count = lax.axis_size("fsdp")
+    order = list(range(0, count, 2)) + list(range(1, count, 2))[::-1]
+    pairs = [(order[i], order[(i + step) % count]) for i in range(count)]
+    return lax.ppermute(array, "fsdp", pairs)
+
+
+def ring_index(offset):
+    count, index = lax.axis_size("fsdp"), lax.axis_index("fsdp")
+    place = jnp.where(index % 2 == 0, index // 2, count - 1 - index // 2)
+    place = (place + offset + count) % count
+    return jnp.where(place < count // 2, 2 * place, 2 * (count - 1 - place) + 1)
+
+
+def ring_gather(array):
+    count = lax.axis_size("fsdp")
+    out = jnp.zeros((count,) + array.shape, array.dtype)
+    out = lax.dynamic_update_index_in_dim(out, array, ring_index(0), 0)
+    up = down = array
+    for step in range(1, count // 2 + 1):
+        up = ring_send(up, 1)
+        out = lax.dynamic_update_index_in_dim(out, up, ring_index(-step), 0)
+        if step <= (count - 1) // 2:
+            down = ring_send(down, -1)
+            out = lax.dynamic_update_index_in_dim(out, down, ring_index(step), 0)
+    return out
+
+
+def ring_scatter(array):
+    count = lax.axis_size("fsdp")
+
+    def block(offset):
+        return lax.dynamic_index_in_dim(array, ring_index(offset), 0, False).astype(F32)
+
+    total = block(0)
+    for direction, hops in ((1, count // 2), (-1, (count - 1) // 2)):
+        moving = block(direction * hops)
+        for step in range(1, hops + 1):
+            moving = ring_send(moving.astype(BF), direction).astype(F32)
+            if step < hops:
+                moving = moving + block(direction * (hops - step))
+        total = total + moving
+    return total
 
 
 def core_join(mine, axis, core):
@@ -400,7 +529,7 @@
         [triple_mine, jnp.stack(vectors, 1), bias_mine.reshape(shard, bias_columns)], 1
     )
     packed = jnp.pad(packed, ((0, 0), (0, -packed.shape[1] % 128)))
-    packed = fsdp_gather(packed)
+    packed = ring_gather(packed).reshape(width, -1)
     triple_whole = packed[:, : 3 * head_width]
     small = packed[:, 3 * head_width : 3 * head_width + vector_count + bias_columns]
     small = small.astype(F32).T
@@ -419,7 +548,7 @@
         output_mine = lax.dynamic_index_in_dim(
             output_weight.reshape(shard // (2 * HEAD_DIM), 2, HEAD_DIM, width), core, 1, False
         ).reshape(shard // 2, width)
-        output_whole = fsdp_gather(output_mine)
+        output_whole = ring_gather(output_mine)
     else:
         output_whole = lax.dynamic_index_in_dim(
             fsdp_gather(output_weight).reshape(-1, 2, HEAD_DIM, width), core, 1, False
@@ -435,18 +564,24 @@
     )
     reduce_whole = fsdp_gather(reduce_mine)
 
-    mine = images.reshape(own_rows, width)
-    slots = far_gather(mine)
-    tokens = []
-    for slot in slots:
-        tokens += [slot, other_core(slot)]
-    tokens = jnp.stack(tokens, 0).reshape(seq_count * own_rows, width)
-    normal_1, factor_1 = normalize(tokens.astype(F32))
-    first_normed = (normal_1 * gain_1 + shift_1).astype(BF)
+    groups = 2 if image_count % 2 == 0 else 1
+    group_images = image_count // groups
+    rows = group_images * local_len
     joint_bias = jnp.concatenate(
         [my_heads(bias_q, 0), jnp.zeros((head_width,), F32), my_heads(bias_v, 0)]
     )
-    triple = (dot(first_normed, triple_whole) + joint_bias).astype(BF)
+    tokens, normed, triples = [], [], []
+    for group in range(groups):
+        mine = images[group * group_images : (group + 1) * group_images].reshape(rows, width)
+        slots = []
+        for slot in far_gather(mine):
+            slots += [slot, other_core(slot)]
+        tokens.append(jnp.stack(slots, 0))
+        first_normed, triple = project(
+            tokens[-1], gain_1[None], shift_1[None], triple_whole, joint_bias[None]
+        )
+        normed.append(first_normed)
+        triples.append(triple)
 
     last_slot = ((far_count - 1 - far) % far_count) * 2 + (1 - core)
     dead_from = last_slot * local_len + valid_count - (seq_count - 1) * local_len
@@ -457,34 +592,40 @@
     direct = local_len % 8 == 0 and head_width % (2 * HEAD_DIM) == 0
 
     def to_kernel(array):
-        array = array.reshape(seq_count, image_count, local_len, -1)
+        array = array.reshape(seq_count, group_images, local_len, -1)
         if direct:
             return array
         parts = array.shape[-1] // head_width
         array = array.transpose(1, 0, 2, 3).reshape(
-            1, image_count, seq_count * local_len, parts, head_width
+            1, group_images, seq_count * local_len, parts, head_width
         )
         lanes = -head_width % (2 * HEAD_DIM)
         array = jnp.pad(array, ((0, 0),) * 4 + ((0, lanes),))
-        return array.reshape(1, image_count, seq_count * local_len, -1)
-
-    def from_kernel(array):
+        return array.reshape(1, group_images, seq_count * local_len, -1)
+
+    def from_kernel(array, parts):
         if direct:
-            return array.reshape(seq_count * own_rows, -1)
-        array = array[..., :head_width].reshape(image_count, seq_count, local_len, head_width)
-        return array.transpose(1, 0, 2, 3).reshape(seq_count * own_rows, head_width)
-
-    triple_in = to_kernel(triple)
-    attended_in, logs = attend_forward(triple_in, limits)
-    attended = from_kernel(attended_in).reshape(far_count, 2 * own_rows, head_width)
-    attended = far_exchange([attended[r] for r in range(far_count)])
-    attended_rows = jnp.concatenate(attended, 1)
-
-    branch = dot(attended_rows, output_whole)
-    branch_attend = (
-        branch[:own_rows] + other_core(branch[own_rows:].astype(BF)).astype(F32) + bias_o
-    )
-    inputs = mine.astype(F32)
+            return array.reshape(seq_count, rows, -1)
+        array = array.reshape(group_images, seq_count, local_len, parts, -1)
+        array = array[..., :head_width].transpose(1, 0, 2, 3, 4)
+        return array.reshape(seq_count, rows, parts * head_width)
+
+    kernel_in, kernel_out, kernel_logs, attended_rows, branch_parts = [], [], [], [], []
+    for group in range(groups):
+        picked = limits[group * group_images : (group + 1) * group_images]
+        kernel_in.append(to_kernel(triples[group]))
+        attended, logs = attend_forward(kernel_in[-1], picked)
+        kernel_out.append(attended)
+        kernel_logs.append(logs)
+        attended = from_kernel(attended, 1).reshape(far_count, 2 * rows, head_width)
+        attended = far_exchange([attended[r] for r in range(far_count)])
+        attended_rows.append(jnp.concatenate(attended, 1))
+        branch = dot(attended_rows[-1], output_whole)
+        branch_parts.append(
+            branch[:rows] + other_core(branch[rows:].astype(BF)).astype(F32) + bias_o
+        )
+    branch_attend = jnp.concatenate(branch_parts, 0)
+    inputs = images.reshape(own_rows, width).astype(F32)
     residual = inputs + scale_a * branch_attend
     normal_2, factor_2 = normalize(residual)
     second_mine = (normal_2 * gain_2 + shift_2).astype(BF)
@@ -502,10 +643,18 @@
     grad_feed = (scale_f * both.astype(F32)).astype(BF)
     grad_feed_scale = jnp.sum(upstream * branch_feed, 0)
     grad_reduce_bias = column_total(grad_feed[:own_rows])
-    grad_reduce_weight = fsdp_scatter(dot_left_t(activated, grad_feed).astype(BF))
+    grad_reduce_weight = dot_left_t(activated, grad_feed).astype(BF)
     grad_expanded = (dot_right_t(grad_feed, reduce_whole) * slope.astype(F32)).astype(BF)
+    grad_expanded, grad_reduce_weight = lax.optimization_barrier(
+        (grad_expanded, grad_reduce_weight)
+    )
+    grad_reduce_weight = fsdp_scatter(grad_reduce_weight)
     grad_expand_bias = column_total(grad_expanded)
-    grad_expand_weight = fsdp_scatter(dot_left_t(second_normed, grad_expanded).astype(BF))
+    grad_expand_weight = dot_left_t(second_normed, grad_expanded).astype(BF)
+    grad_expanded, grad_expand_weight = lax.optimization_barrier(
+        (grad_expanded, grad_expand_weight)
+    )
+    grad_expand_weight = fsdp_scatter(grad_expand_weight)
     partial = dot_right_t(grad_expanded, expand_whole)
     upper = partial[:own_rows] + other_core(partial[own_rows:].astype(BF)).astype(F32)
     grad_second_gain = jnp.sum(upper * normal_2, 0)
@@ -516,29 +665,61 @@
     grad_output_bias = column_total(grad_attend)
     grad_attend = jnp.concatenate([grad_attend, other_core(grad_attend)], 0)
     grad_attended = dot_right_t(grad_attend, output_whole).astype(BF)
-    grad_attended = far_exchange(
-        [grad_attended[:, r * head_width : (r + 1) * head_width] for r in range(far_count)]
-    )
-    grad_attended = to_kernel(jnp.stack(grad_attended, 0))
-    grad_output_weight = dot_left_t(attended_rows, grad_attend).astype(BF)
+    grad_attended = grad_attended.reshape(2, groups, rows, far_count, head_width)
+    grad_sides = grad_attend.reshape(2, groups, rows, width)
+    grad_output_weight = sum(
+        dot_left_t(attended_rows[group], grad_sides[:, group].reshape(2 * rows, width))
+        for group in range(groups)
+    ).astype(BF)
     grad_output_weight = jnp.roll(
         grad_output_weight.reshape(far_count, head_width, width), far, 0
     ).reshape(width // 2, width)
 
-    pieces = attend_backward(triple_in, attended_in, grad_attended, logs, limits)
-    grad_triple = jnp.concatenate([from_kernel(piece) for piece in pieces], 1)
-
-    partial = dot_right_t(grad_triple, triple_whole)
-    grad_first_gain = jnp.sum(partial * normal_1, 0)
-    grad_first_shift = jnp.sum(partial, 0)
-    partial = partial.astype(BF).reshape(far_count, 2, own_rows, width)
-    partial = partial[:, 0].astype(F32) + other_core(partial[:, 1]).astype(F32)
-    partial = partial.astype(BF)
-    upper = far_sum([partial[r] for r in range(far_count)])
+    grad_heads = [
+        to_kernel(
+            jnp.stack(
+                far_exchange(
+                    [
+                        grad_attended[:, group, :, r].reshape(2 * rows, head_width)
+                        for r in range(far_count)
+                    ]
+                ),
+                0,
+            )
+        )
+        for group in range(groups)
+    ]
+    upper_parts, grad_triples = [], []
+    grad_first_gain = grad_first_shift = column_sums = 0.0
+    for group in range(groups):
+        picked = limits[group * group_images : (group + 1) * group_images]
+        grad_triple = from_kernel(
+            attend_backward(
+                kernel_in[group], kernel_out[group], grad_heads[group], kernel_logs[group], picked
+            ),
+            3,
+        )
+        grad_triples.append(grad_triple)
+        partial, gain_part, shift_part, total_part = project_back(
+            grad_triple, tokens[group], triple_whole
+        )
+        grad_first_gain = grad_first_gain + gain_part[0]
+        grad_first_shift = grad_first_shift + shift_part[0]
+        column_sums = column_sums + total_part[0]
+        partial = partial.reshape(far_count, 2, rows, width)
+        partial = partial[:, 0].astype(F32) + other_core(partial[:, 1]).astype(F32)
+        partial = partial.astype(BF)
+        upper_parts.append(far_sum([partial[r] for r in range(far_count)]))
+    grad_triple_weight = sum(
+        dot_left_t(
+            normed[group].reshape(seq_count * rows, width),
+            grad_triples[group].reshape(seq_count * rows, 3 * head_width),
+        )
+        for group in range(groups)
+    ).astype(BF)
+    upper = jnp.concatenate(upper_parts, 0)
     normal, factor = normalize(inputs)
     grad_images = grad_residual + normalize_back(normal, factor, upper * gain_1)
-
-    column_sums = column_total(grad_triple)
 
     def place_heads(vector):
         here = jnp.arange(far_count)[:, None, None, None] == far
@@ -560,17 +741,17 @@
     ] + place_units(grad_expand_bias)
     sums = jnp.stack(sums, 0).astype(BF).T
     sums = jnp.pad(sums, ((0, 0), (0, -sums.shape[1] % 128)))
-    grad_packed = jnp.concatenate([dot_left_t(first_normed, grad_triple).astype(BF), sums], 1)
-    grad_packed = fsdp_scatter(grad_packed)
-    grad_packed = lax.all_gather(grad_packed, ("far", "core"), axis=0, tiled=False)
-    grad_packed = grad_packed.astype(F32)
+    grad_packed = jnp.concatenate([grad_triple_weight, sums], 1)
+    grad_packed = ring_scatter(grad_packed.reshape(fsdp_count, shard, -1)).astype(BF)
+    grad_packed = jnp.roll(jnp.stack(far_gather(grad_packed), 0), far, 0)
+    grad_packed = core_join(grad_packed, 1, core).astype(F32)
     grad_triple_weight = (
-        grad_packed[:, :, : 3 * head_width]
+        grad_packed[:, :, :, : 3 * head_width]
         .reshape(far_count, 2, shard, 3, near_heads, HEAD_DIM)
         .transpose(2, 3, 0, 4, 1, 5)
         .reshape(shard, 3 * width)
     )
-    sums = jnp.sum(grad_packed[:, :, 3 * head_width :], 0).T
+    sums = jnp.sum(grad_packed[:, :, :, 3 * head_width :], (0, 1)).T
 
     def far_total(array):
         total = array.astype(F32)
@@ -579,7 +760,10 @@
         return total
 
     if split_output:
-        grad_output_weight = far_total(fsdp_scatter(grad_output_weight)).astype(BF)
+        grad_output_weight = ring_scatter(
+            grad_output_weight.reshape(fsdp_count, shard // 2, width)
+        ).astype(BF)
+        grad_output_weight = far_total(grad_output_weight).astype(BF)
         grad_output_weight = core_join(
             grad_output_weight.reshape(-1, HEAD_DIM, width), 1, core
         ).reshape(shard, width)

time: 673 us -> 579 us (0.86)
  waiting for transfers between devices: 326 us -> 146 us
  local copies, waits for them, and re-layouts: 53.8 us -> 105 us
  starting transfers between devices: 15.1 us -> 60.5 us
  Pallas kernels: 93.1 us -> 116 us
  blocking collectives: 17.2 us -> 0 us
  matrix products: 84.2 us -> 70.4 us
    reduce_scatter x4 -> x2, waiting for transfers between devices: 168 us -> 0.01 us  [fsdp_scatter(): return lax.psum_scatter(array, 'fsdp', scatter_dimension=0, tiled=True)]
    ppermute x0 -> x28, waiting for transfers between devices: none -> 78.5 us  [ring_send(): return lax.ppermute(array, 'fsdp', pairs)]
    all_gather x4 -> x2, waiting for transfers between devices: 82.1 us -> 22.3 us  [fsdp_gather(): return lax.all_gather(array, 'fsdp', axis=0, tiled=True)]
    ppermute x0 -> x28, starting transfers between devices: none -> 42.9 us  [ring_send(): return lax.ppermute(array, 'fsdp', pairs)]
    ppermute x7 -> x12, waiting for transfers between devices: 69.4 us -> 44.5 us  [far_send(): lax.ppermute(array, 'far', [(i, (i + shift) % count) for i in range(count)])]
    reshape x0 -> x3, local copies, waits for them, and re-layouts: none -> 21 us  [the longest x1 15.5 us: shards(): grad_attended.reshape(2, groups, rows, far_count, head_width)]
    all_gather x1 -> x0, blocking collectives: 17.2 us -> none  [shards(): lax.all_gather(grad_packed, ('far', 'core'), axis=0, tiled=False)]
    pallas_call x0 -> x4, Pallas kernels: none -> 16.3 us  [the longest x2 8.72 us: project(): pl.pallas_call(project_kernel, grid=(pieces,), in_specs=[piece(width), wh...]
  transfers between devices with their start and end apart: 27 -> 61, of which waited for: 13 -> 27; matrix products, arithmetic and copies ran while one was open for 23% -> 34% of each run, Pallas kernels for 14% -> 20%
where the time goes in v2:
time: 579 us; the launch traced here: 575 us
  waiting for transfers between devices  146 us (25%)
  Pallas kernels  116 us (20%)
  local copies, waits for them, and re-layouts  105 us (18%)
  matrix products  70.4 us (12%)
  starting transfers between devices  60.5 us (10%)
  other arithmetic  60.4 us (10%)
  between operations  15.9 us (3%)
    ppermute x28, waiting for transfers between devices, ring_send(): return lax.ppermute(array, 'fsdp', pairs)  78.5 us
    pallas_call x2, Pallas kernels, attend_backward(): pl.pallas_call(attend_backward_kernel, grid_spec=pltpu.PrefetchScalarGrid...  51.3 us
    ppermute x12, waiting for transfers between devices, far_send(): lax.ppermute(array, 'far', [(i, (i + shift) % count) for i in range(count)])  44.5 us
    ppermute x28, starting transfers between devices, ring_send(): return lax.ppermute(array, 'fsdp', pairs)  42.9 us
    dot_general x6, matrix products, dot_left_t(): lax.dot_general(left, right, (((0,), (0,)), ((), ())), preferred_element_...  32.4 us
    pallas_call x2, Pallas kernels, attend_forward(): pl.pallas_call(attend_forward_kernel, grid_spec=pltpu.PrefetchScalarGridS...  29.3 us
    unnamed x170, local copies, waits for them, and re-layouts  26.3 us
    dot_general x3, matrix products, dot_right_t(): lax.dot_general(left, right, (((1,), (1,)), ((), ())), preferred_element_...  24.6 us
  transfers between devices with their start and end apart: 61, of which 27 were waited for; matrix products, arithmetic and copies ran while one was open for 34% of the time, Pallas kernels for 20%

profile of v2, /device:TPU:0, one launch (start us, length us, event | category | flops | bytes accessed | tf_op | source)
XLA Modules:
  0.0 574.7 jit_solution(8251186238353937006)
XLA Ops:
  38.8 4.4 collective-permute-done.13
  52.7 10.1 %collective-permute-done.15 = bf16[64,1024]{1,0:T(8,128)(2,1)S(1)} collective-permute-done((bf16[64,1024]{1,0:T(8,128)(2,1)}, bf16[64,1024]{1,0:T(8,128)(2,1)S(1)}, u32[]{:S(2)}, u32[]{:S(2)}) %collective-permute-start.15) | collective-permute-done | bytes 131104 | tf_op jit(solution)/shard_map/ppermute | solution.py:432
  72.9 14.4 %collective-permute-done.3 = bf16[128,896]{0,1:T(8,128)(2,1)} collective-permute-done((bf16[128,896]{0,1:T(8,128)(2,1)}, bf16[128,896]{0,1:T(8,128)(2,1)}, u32[]{:S(2)}, u32[]{:S(2)}) %collective-permute-start.3) | collective-permute-done | bytes 229408 | tf_op jit(solution)/shard_map/ppermute | solution.py:432
  92.1 7.3 %collective-permute-done.4 = bf16[128,896]{0,1:T(8,128)(2,1)S(1)} collective-permute-done((bf16[128,896]{0,1:T(8,128)(2,1)S(1)}, bf16[128,896]{0,1:T(8,128)(2,1)S(1)}, u32[]{:S(2)}, u32[]{:S(2)}) %collective-permute-start.4) | collective-permute-done | bytes 229408 | tf_op jit(solution)/shard_map/ppermute | solution.py:432
  101.2 7.7 %collective-permute-done.5 = bf16[128,896]{0,1:T(8,128)(2,1)} collective-permute-done((bf16[128,896]{0,1:T(8,128)(2,1)}, bf16[128,896]{0,1:T(8,128)(2,1)}, u32[]{:S(2)}, u32[]{:S(2)}) %collective-permute-start.5) | collective-permute-done | bytes 229408 | tf_op jit(solution)/shard_map/ppermute | solution.py:432
  110.9 8.1 %collective-permute-done.6 = bf16[128,896]{0,1:T(8,128)(2,1)S(1)} collective-permute-done((bf16[128,896]{0,1:T(8,128)(2,1)}, bf16[128,896]{0,1:T(8,128)(2,1)S(1)}, u32[]{:S(2)}, u32[]{:S(2)}) %collective-permute-start.6) | collective-permute-done | bytes 229408 | tf_op jit(solution)/shard_map/ppermute | solution.py:432
  133.6 4.4 project.3
  140.8 14.4 %attend_forward.3 = (bf16[4,1,344,256]{3,2,1,0:T(8,128)(2,1)S(1)}, f32[1,2,1376,128]{3,2,1,0:T(8,128)S(1)}) custom-call(s32[1,2]{1,0:T(1,128)S(1)} %get-tuple-element.223.limit_ref, bf16[4,1,344,768]{3,2,1,0:T(8,128)(2,1)} %bitcast.275, bf16[4,1,344,768]{3,2,1,0:T(8,128)(2,1)} %bitcast.276, bf16[4,1,344,768]{3,2,1,0:T(8,128)(2,1)} %bitcast.277), custom_call_target="tpu_custom_call" | custom-call | flops 7755268096 | bytes 4227072 | tf_op jit(solution)/shard_map/attend_forward/pallas_call | solution.py:202
  158.7 4.4 project.2
  165.9 14.8 %attend_forward.2 = (bf16[4,1,344,256]{3,2,1,0:T(8,128)(2,1)S(1)}, f32[1,2,1376,128]{3,2,1,0:T(8,128)S(1)}) custom-call(s32[1,2]{1,0:T(1,128)S(1)} %get-tuple-element.222.limit_ref, bf16[4,1,344,768]{3,2,1,0:T(8,128)(2,1)} %bitcast.281, bf16[4,1,344,768]{3,2,1,0:T(8,128)(2,1)} %bitcast.282, bf16[4,1,344,768]{3,2,1,0:T(8,128)(2,1)} %bitcast.283), custom_call_target="tpu_custom_call" | custom-call | flops 7755268096 | bytes 4227072 | tf_op jit(solution)/shard_map/attend_forward/pallas_call | solution.py:202
  203.0 4.2 add_convert_fusion.2
  207.9 4.2 multiply_convert_fusion.1
  214.1 19.0 %expand_rows.1 = (bf16[1376,2048]{1,0:T(8,128)(2,1)}, bf16[1376,2048]{1,0:T(8,128)(2,1)}) custom-call(bf16[1376,1024]{1,0:T(8,128)(2,1)S(1)} %pad_maximum_fusion.3.rows_ref, bf16[1024,2048]{1,0:T(8,128)(2,1)} %all-gather.4.cloned.1.call-done.weight_ref, f32[1,2048]{1,0:T(1,128)S(1)} %reshape.470.bias_ref), custom_call_target="tpu_custom_call" | custom-call | flops 11542724608 | bytes 18284544 | tf_op jit(solution)/shard_map/expand_rows/pallas_call | solution.py:373
  233.2 11.1 %convolution_convert_fusion.1 = bf16[2048,1024]{1,0:T(8,128)(2,1)} fusion(bf16[1376,2048]{1,0:T(8,128)(2,1)} %get-tuple-element.44, bf16[1376,1024]{1,0:T(8,128)(2,1)S(1)} %copy-done.38), kind=kOutput, calls=%fused_computation.7 | convolution fusion | flops 5773459456 | bytes 12648448 | tf_op jit(solution)/shard_map/dot_general | solution.py:22
  244.3 22.3 %all-gather.6.cloned.1.call-done = bf16[1,2048,1024]{2,1,0:T(8,128)(2,1)} async-done(((bf16[1,256,1024]{2,1,0:T(8,128)(2,1)}), bf16[1,2048,1024]{2,1,0:T(8,128)(2,1)}) %all-gather.6.cloned.1.call-update) | async-done | bytes 4194320 | tf_op jit(solution)/shard_map/all_gather | solution.py:421
  266.6 10.8 %multiply_convert_fusion = bf16[1376,2048]{1,0:T(8,128)(2,1)} fusion(bf16[1376,2048]{1,0:T(8,128)(2,1)} %get-tuple-element.45, bf16[1376,1024]{1,0:T(8,128)(2,1)S(1)} %copy-done.39, bf16[1,2048,1024]{2,1,0:T(8,128)(2,1)} %all-gather.6.cloned.1.call-done), kind=kOutput, calls=%fused_computation | convolution fusion | flops 5779816448 | bytes 18284544 | tf_op jit(solution)/shard_map/dot_general | solution.py:26
  277.5 11.3 %convolution_convert_fusion = bf16[1024,2048]{1,0:T(8,128)(2,1)} fusion(bf16[1376,2048]{1,0:T(8,128)(2,1)} %multiply_convert_fusion, bf16[688,1024]{1,0:T(8,128)(2,1)} %collective-permute-done.24, bf16[688,1024]{1,0:T(8,128)(2,1)} %get-tuple-element.161), kind=kOutput, calls=%fused_computation.6 | convolution fusion | flops 5779095552 | bytes 12648448 | tf_op jit(solution)/shard_map/dot_general | solution.py:22
  288.8 9.8 %fusion.73 = f32[1376,1024]{1,0:T(8,128)S(1)} fusion(bf16[1376,2048]{1,0:T(8,128)(2,1)} %multiply_convert_fusion, bf16[1024,2048]{1,0:T(8,128)(2,1)} %all-gather.4.cloned.1.call-done.weight_ref), kind=kOutput, calls=%fused_computation.243 | convolution fusion | flops 5771362304 | bytes 15466496 | tf_op jit(solution)/shard_map/dot_general | solution.py:26
  298.9 6.1 %fusion.2 = f32[1376,1024]{1,0:T(8,128)S(1)} fusion(bf16[1376,2048]{1,0:T(8,128)(2,1)S(1)} %bitcast.363, bf16[1,2048,1024]{2,1,0:T(8,128)(2,1)S(1)} %copy-done.73), kind=kOutput, calls=%fused_computation.4 | convolution fusion | flops 5771362304 | bytes 15466496 | tf_op jit(solution)/shard_map/dot_general | solution.py:18
  308.7 5.3 fusion.7
  325.3 4.0 convolution_convert_fusion.2
  329.3 15.5 %reshape.473 = bf16[2,2,344,2,256]{4,3,2,1,0:T(2,128)(2,1)S(1)} reshape(bf16[1376,512]{1,0:T(8,128)(2,1)} %convolution_convert_fusion.2) | data formatting | bytes 2818048 | tf_op jit(solution)/shard_map/reshape | solution.py:668
  357.1 4.0 collective-permute-start.45
  371.4 25.7 %attend_backward.3 = bf16[4,1,344,768]{3,2,1,0:T(8,128)(2,1)} custom-call(s32[1,2]{1,0:T(1,128)} %copy-done.13, bf16[4,1,344,768]{3,2,1,0:T(8,128)(2,1)} %bitcast.278, bf16[4,1,344,768]{3,2,1,0:T(8,128)(2,1)} %bitcast.279, bf16[4,1,344,768]{3,2,1,0:T(8,128)(2,1)} %bitcast.280, bf16[4,1,344,256]{3,2,1,0:T(8,128)(2,1)} %copy-done.10, ...), custom_call_target="tpu_custom_call" | custom-call | flops 19388170240 | bytes 8454144 | tf_op jit(solution)/shard_map/attend_backward/pallas_call | solution.py:236
  403.4 25.6 %attend_backward.2 = bf16[4,1,344,768]{3,2,1,0:T(8,128)(2,1)} custom-call(s32[1,2]{1,0:T(1,128)} %copy-done.12, bf16[4,1,344,768]{3,2,1,0:T(8,128)(2,1)} %bitcast.284, bf16[4,1,344,768]{3,2,1,0:T(8,128)(2,1)} %bitcast.285, bf16[4,1,344,768]{3,2,1,0:T(8,128)(2,1)} %bitcast.286, bf16[4,1,344,256]{3,2,1,0:T(8,128)(2,1)} %copy-done.11, ...), custom_call_target="tpu_custom_call" | custom-call | flops 19388170240 | bytes 8454144 | tf_op jit(solution)/shard_map/attend_backward/pallas_call | solution.py:236
  436.8 5.2 fusion.74
  458.1 5.4 collective-permute-done.35
  477.4 4.7 collective-permute-done.37
  506.7 10.4 %collective-permute-done.34 = bf16[344,1024]{1,0:T(8,128)(2,1)} collective-permute-done((bf16[344,1024]{1,0:T(8,128)(2,1)}, bf16[344,1024]{1,0:T(8,128)(2,1)}, u32[]{:S(2)}, u32[]{:S(2)}) %collective-permute-start.34) | collective-permute-done | bytes 704544 | tf_op jit(solution)/shard_map/ppermute | solution.py:395
  518.6 13.2 %collective-permute-done.31 = bf16[344,1024]{1,0:T(8,128)(2,1)} collective-permute-done((bf16[344,1024]{1,0:T(8,128)(2,1)}, bf16[344,1024]{1,0:T(8,128)(2,1)}, u32[]{:S(2)}, u32[]{:S(2)}) %collective-permute-start.31) | collective-permute-done | bytes 704544 | tf_op jit(solution)/shard_map/ppermute | solution.py:395
  540.7 10.5 %collective-permute-done.55 = bf16[256,1024]{1,0:T(8,128)(2,1)} collective-permute-done((bf16[256,1024]{1,0:T(8,128)(2,1)}, bf16[256,1024]{1,0:T(8,128)(2,1)}, u32[]{:S(2)}, u32[]{:S(2)}) %collective-permute-start.55) | collective-permute-done | bytes 524320 | tf_op jit(solution)/shard_map/ppermute | solution.py:395
  552.5 4.7 fusion.20
  (454 shorter events, 235.9 us)
Async XLA Ops:
  7.2 206.9 %all-gather.4.cloned.1.call-start = ((), (), s32[]{:S(2)}) async-start(), calls=%async_computation.2 | async-start | bytes 4718592 | tf_op jit(solution)/shard_map/all_gather | solution.py:421
  8.9 23.8 %collective-permute-start.12 = (bf16[64,1024]{1,0:T(8,128)(2,1)}, bf16[64,1024]{1,0:T(8,128)(2,1)}, u32[]{:S(2)}, u32[]{:S(2)}) collective-permute-start(bf16[64,1024]{1,0:T(8,128)(2,1)} %dynamic-slice_bitcast_fusion.4), channel_id=1, source_target_pairs={{0,4},{8,0},{16,8},{24,16},{28,24},{20,28},{12,20},{4,12},{1,5},{9... | collective-permute-start | bytes 393224 | tf_op jit(solution)/shard_map/ppermute | solution.py:432
  11.9 19.2 %collective-permute-start.11 = (bf16[64,1024]{1,0:T(8,128)(2,1)}, bf16[64,1024]{1,0:T(8,128)(2,1)}, u32[]{:S(2)}, u32[]{:S(2)}) collective-permute-start(bf16[64,1024]{1,0:T(8,128)(2,1)} %dynamic-slice_bitcast_fusion.4), channel_id=1, source_target_pairs={{0,8},{8,16},{16,24},{24,28},{28,20},{20,12},{12,4},{4,0},{1,9},{9... | collective-permute-start | bytes 393224 | tf_op jit(solution)/shard_map/ppermute | solution.py:432
  16.8 17.6 %collective-permute-start = (bf16[128,896]{0,1:T(8,128)(2,1)}, bf16[128,896]{0,1:T(8,128)(2,1)}, u32[]{:S(2)}, u32[]{:S(2)}) collective-permute-start(bf16[128,896]{0,1:T(8,128)(2,1)} %get-tuple-element.214), channel_id=1, source_target_pairs={{0,8},{8,16},{16,24},{24,28},{28,20},{20,12},{12,4},{4,0},{1,9},{9... | collective-permute-start | bytes 688136 | tf_op jit(solution)/shard_map/ppermute | solution.py:432
  18.9 18.7 %collective-permute-start.1 = (bf16[128,896]{0,1:T(8,128)(2,1)}, bf16[128,896]{0,1:T(8,128)(2,1)}, u32[]{:S(2)}, u32[]{:S(2)}) collective-permute-start(bf16[128,896]{0,1:T(8,128)(2,1)} %get-tuple-element.214), channel_id=1, source_target_pairs={{0,4},{8,0},{16,8},{24,16},{28,24},{20,28},{12,20},{4,12},{1,5},{9... | collective-permute-start | bytes 688136 | tf_op jit(solution)/shard_map/ppermute | solution.py:432
  24.8 241.8 %all-gather.6.cloned.1.call-start = ((), (), s32[]{:S(2)}) async-start(), calls=%async_computation.5 | async-start | bytes 4718592 | tf_op jit(solution)/shard_map/all_gather | solution.py:421
  26.6 83.7 %collective-permute-start.8 = (bf16[344,1024]{1,0:T(8,128)(2,1)}, bf16[344,1024]{1,0:T(8,128)(2,1)}, u32[]{:S(2)}, u32[]{:S(2)}) collective-permute-start(bf16[344,1024]{1,0:T(8,128)(2,1)} %get-tuple-element.182), channel_id=1, source_target_pairs={{0,2},{2,0},{1,3},{3,1},{4,6},{6,4},{5,7},{7,5},{8,10},{10,8},{9,1... | collective-permute-start | bytes 2113544 | tf_op jit(solution)/shard_map/ppermute | solution.py:395
  31.1 125.8 %collective-permute-start.7 = (bf16[344,1024]{1,0:T(8,128)(2,1)}, bf16[344,1024]{1,0:T(8,128)(2,1)}, u32[]{:S(2)}, u32[]{:S(2)}) collective-permute-start(bf16[344,1024]{1,0:T(8,128)(2,1)} %get-tuple-element.182), channel_id=1, source_target_pairs={{0,1},{1,0},{2,3},{3,2},{4,5},{5,4},{6,7},{7,6},{8,9},{9,8},{10,11... | collective-permute-start | bytes 2113544 | tf_op jit(solution)/shard_map/ppermute | solution.py:417
  32.7 77.6 %collective-permute-start.20 = (bf16[344,1024]{1,0:T(8,128)(2,1)}, bf16[344,1024]{1,0:T(8,128)(2,1)}, u32[]{:S(2)}, u32[]{:S(2)}) collective-permute-start(bf16[344,1024]{1,0:T(8,128)(2,1)} %get-tuple-element.183), channel_id=1, source_target_pairs={{0,2},{2,0},{1,3},{3,1},{4,6},{6,4},{5,7},{7,5},{8,10},{10,8},{9,1... | collective-permute-start | bytes 2113544 | tf_op jit(solution)/shard_map/ppermute | solution.py:395
  43.2 29.5 %collective-permute-start.2 = (bf16[128,896]{0,1:T(8,128)(2,1)}, bf16[128,896]{0,1:T(8,128)(2,1)S(1)}, u32[]{:S(2)}, u32[]{:S(2)}) collective-permute-start(bf16[128,896]{0,1:T(8,128)(2,1)} %collective-permute-done), channel_id=1, source_target_pairs={{0,8},{8,16},{16,24},{24,28},{28,20},{20,12},{12,4},{4,0},{1,9},{9... | collective-permute-start | bytes 688136 | tf_op jit(solution)/shard_map/ppermute | solution.py:432
  69.7 17.6 %collective-permute-start.3 = (bf16[128,896]{0,1:T(8,128)(2,1)}, bf16[128,896]{0,1:T(8,128)(2,1)}, u32[]{:S(2)}, u32[]{:S(2)}) collective-permute-start(bf16[128,896]{0,1:T(8,128)(2,1)} %collective-permute-done.1), channel_id=1, source_target_pairs={{0,4},{8,0},{16,8},{24,16},{28,24},{20,28},{12,20},{4,12},{1,5},{9... | collective-permute-start | bytes 688136 | tf_op jit(solution)/shard_map/ppermute | solution.py:432
  72.7 15.8 %collective-permute-start.17 = (bf16[64,1024]{1,0:T(8,128)(2,1)S(1)}, bf16[64,1024]{1,0:T(8,128)(2,1)}, u32[]{:S(2)}, u32[]{:S(2)}) collective-permute-start(bf16[64,1024]{1,0:T(8,128)(2,1)S(1)} %collective-permute-done.15), channel_id=1, source_target_pairs={{0,8},{8,16},{16,24},{24,28},{28,20},{20,12},{12,4},{4,0},{1,9},{9... | collective-permute-start | bytes 393224 | tf_op jit(solution)/shard_map/ppermute | solution.py:432
  88.5 20.3 %collective-permute-start.5 = (bf16[128,896]{0,1:T(8,128)(2,1)}, bf16[128,896]{0,1:T(8,128)(2,1)}, u32[]{:S(2)}, u32[]{:S(2)}) collective-permute-start(bf16[128,896]{0,1:T(8,128)(2,1)} %collective-permute-done.3), channel_id=1, source_target_pairs={{0,4},{8,0},{16,8},{24,16},{28,24},{20,28},{12,20},{4,12},{1,5},{9... | collective-permute-start | bytes 688136 | tf_op jit(solution)/shard_map/ppermute | solution.py:432
  99.4 32.2 %collective-permute-start.19 = (bf16[344,1024]{1,0:T(8,128)(2,1)}, bf16[344,1024]{1,0:T(8,128)(2,1)}, u32[]{:S(2)}, u32[]{:S(2)}) collective-permute-start(bf16[344,1024]{1,0:T(8,128)(2,1)} %get-tuple-element.183), channel_id=1, source_target_pairs={{0,1},{1,0},{2,3},{3,2},{4,5},{5,4},{6,7},{7,6},{8,9},{9,8},{10,11... | collective-permute-start | bytes 2113544 | tf_op jit(solution)/shard_map/ppermute | solution.py:417
  110.3 46.6 %collective-permute-start.9 = (bf16[344,1024]{1,0:T(8,128)(2,1)}, bf16[344,1024]{1,0:T(8,128)(2,1)}, u32[]{:S(2)}, u32[]{:S(2)}) collective-permute-start(bf16[344,1024]{1,0:T(8,128)(2,1)} %collective-permute-done.8), channel_id=1, source_target_pairs={{0,1},{1,0},{2,3},{3,2},{4,5},{5,4},{6,7},{7,6},{8,9},{9,8},{10,11... | collective-permute-start | bytes 2113544 | tf_op jit(solution)/shard_map/ppermute | solution.py:417
  110.4 21.2 %collective-permute-start.21 = (bf16[344,1024]{1,0:T(8,128)(2,1)}, bf16[344,1024]{1,0:T(8,128)(2,1)}, u32[]{:S(2)}, u32[]{:S(2)}) collective-permute-start(bf16[344,1024]{1,0:T(8,128)(2,1)} %collective-permute-done.20), channel_id=1, source_target_pairs={{0,1},{1,0},{2,3},{3,2},{4,5},{5,4},{6,7},{7,6},{8,9},{9,8},{10,11... | collective-permute-start | bytes 2113544 | tf_op jit(solution)/shard_map/ppermute | solution.py:417
  155.4 27.9 %collective-permute-start.22 = (bf16[688,256]{1,0:T(8,128)(2,1)S(1)}, bf16[688,256]{1,0:T(8,128)(2,1)S(1)}, u32[]{:S(2)}, u32[]{:S(2)}) collective-permute-start(bf16[688,256]{1,0:T(8,128)(2,1)S(1)} %bitcast.343), channel_id=1, source_target_pairs={{0,2},{2,0},{1,3},{3,1},{4,6},{6,4},{5,7},{7,5},{8,10},{10,8},{9,1... | collective-permute-start | bytes 1056776 | tf_op jit(solution)/shard_map/ppermute | solution.py:395
  191.6 344.5 %reduce-scatter.5.cloned.1.call-start = ((), (), s32[]{:S(2)}) async-start(), calls=%async_computation.4 | async-start | bytes 4718592 | tf_op jit(solution)/shard_map/reduce_scatter | solution.py:425
  191.7 16.2 %collective-permute-start.26 = (bf16[688,1024]{1,0:T(8,128)(2,1)}, bf16[688,1024]{1,0:T(8,128)(2,1)}, u32[]{:S(2)}, u32[]{:S(2)}) collective-permute-start(bf16[688,1024]{1,0:T(8,128)(2,1)} %bitcast.56), channel_id=1, source_target_pairs={{0,1},{1,0},{2,3},{3,2},{4,5},{5,4},{6,7},{7,6},{8,9},{9,8},{10,11... | collective-permute-start | bytes 4227080 | tf_op jit(solution)/shard_map/ppermute | solution.py:417
  277.4 262.8 %reduce-scatter.3.cloned.1.call-start = ((), (), s32[]{:S(2)}) async-start(), calls=%async_computation.3 | async-start | bytes 4718592 | tf_op jit(solution)/shard_map/reduce_scatter | solution.py:425
  350.7 15.1 %collective-permute-start.48 = (bf16[64,1024]{1,0:T(8,128)(2,1)S(1)}, bf16[64,1024]{1,0:T(8,128)(2,1)S(1)}, u32[]{:S(2)}, u32[]{:S(2)}) collective-permute-start(bf16[64,1024]{1,0:T(8,128)(2,1)S(1)} %get-tuple-element.194), channel_id=1, source_target_pairs={{0,4},{8,0},{16,8},{24,16},{28,24},{20,28},{12,20},{4,12},{1,5},{9... | collective-permute-start | bytes 393224 | tf_op jit(solution)/shard_map/ppermute | solution.py:432
  354.1 16.4 %collective-permute-start.32 = (bf16[688,256]{1,0:T(8,128)(2,1)S(1)}, bf16[688,256]{1,0:T(8,128)(2,1)S(1)}, u32[]{:S(2)}, u32[]{:S(2)}) collective-permute-start(bf16[688,256]{1,0:T(8,128)(2,1)S(1)} %bitcast.335), channel_id=1, source_target_pairs={{0,2},{2,0},{1,3},{3,1},{4,6},{6,4},{5,7},{7,5},{8,10},{10,8},{9,1... | collective-permute-start | bytes 1056776 | tf_op jit(solution)/shard_map/ppermute | solution.py:395
  364.6 37.8 %collective-permute-start.29 = (bf16[688,256]{1,0:T(8,128)(2,1)S(1)}, bf16[688,256]{1,0:T(8,128)(2,1)S(1)}, u32[]{:S(2)}, u32[]{:S(2)}) collective-permute-start(bf16[688,256]{1,0:T(8,128)(2,1)S(1)} %bitcast.336), channel_id=1, source_target_pairs={{0,2},{2,0},{1,3},{3,1},{4,6},{6,4},{5,7},{7,5},{8,10},{10,8},{9,1... | collective-permute-start | bytes 1056776 | tf_op jit(solution)/shard_map/ppermute | solution.py:395
  366.8 88.2 %collective-permute-start.46 = (bf16[64,1024]{1,0:T(8,128)(2,1)}, bf16[64,1024]{1,0:T(8,128)(2,1)}, u32[]{:S(2)}, u32[]{:S(2)}) collective-permute-start(bf16[64,1024]{1,0:T(8,128)(2,1)} %get-tuple-element.191), channel_id=1, source_target_pairs={{0,8},{8,16},{16,24},{24,28},{28,20},{20,12},{12,4},{4,0},{1,9},{9... | collective-permute-start | bytes 393224 | tf_op jit(solution)/shard_map/ppermute | solution.py:432
  370.0 85.5 %collective-permute-start.49 = (bf16[64,1024]{1,0:T(8,128)(2,1)}, bf16[64,1024]{1,0:T(8,128)(2,1)}, u32[]{:S(2)}, u32[]{:S(2)}) collective-permute-start(bf16[64,1024]{1,0:T(8,128)(2,1)} %get-tuple-element.192), channel_id=1, source_target_pairs={{0,4},{8,0},{16,8},{24,16},{28,24},{20,28},{12,20},{4,12},{1,5},{9... | collective-permute-start | bytes 393224 | tf_op jit(solution)/shard_map/ppermute | solution.py:432
  452.6 19.3 %collective-permute-start.39 = (bf16[128,896]{1,0:T(8,128)(2,1)S(1)}, bf16[128,896]{1,0:T(8,128)(2,1)S(1)}, u32[]{:S(2)}, u32[]{:S(2)}) collective-permute-start(bf16[128,896]{1,0:T(8,128)(2,1)S(1)} %get-tuple-element.176), channel_id=1, source_target_pairs={{0,4},{8,0},{16,8},{24,16},{28,24},{20,28},{12,20},{4,12},{1,5},{9... | collective-permute-start | bytes 688136 | tf_op jit(solution)/shard_map/ppermute | solution.py:432
  454.9 41.7 %collective-permute-start.33 = (bf16[2,344,1024]{2,1,0:T(8,128)(2,1)S(1)}, bf16[2,344,1024]{2,1,0:T(8,128)(2,1)S(1)}, u32[]{:S(2)}, u32[]{:S(2)}) collective-permute-start(bf16[2,344,1024]{2,1,0:T(8,128)(2,1)S(1)} %slice_bitcast_fusion), channel_id=1, source_target_pairs={{0,1},{1,0},{2,3},{3,2},{4,5},{5,4},{6,7},{7,6},{8,9},{9,8},{10,11... | collective-permute-start | bytes 4227080 | tf_op jit(solution)/shard_map/ppermute | solution.py:417
  455.0 44.7 %collective-permute-start.30 = (bf16[2,344,1024]{2,1,0:T(8,128)(2,1)S(1)}, bf16[2,344,1024]{2,1,0:T(8,128)(2,1)S(1)}, u32[]{:S(2)}, u32[]{:S(2)}) collective-permute-start(bf16[2,344,1024]{2,1,0:T(8,128)(2,1)S(1)} %slice_bitcast_fusion.2), channel_id=1, source_target_pairs={{0,1},{1,0},{2,3},{3,2},{4,5},{5,4},{6,7},{7,6},{8,9},{9,8},{10,11... | collective-permute-start | bytes 4227080 | tf_op jit(solution)/shard_map/ppermute | solution.py:417
  498.1 18.9 %collective-permute-start.34 = (bf16[344,1024]{1,0:T(8,128)(2,1)}, bf16[344,1024]{1,0:T(8,128)(2,1)}, u32[]{:S(2)}, u32[]{:S(2)}) collective-permute-start(bf16[344,1024]{1,0:T(8,128)(2,1)} %slice_bitcast_fusion.4), channel_id=1, source_target_pairs={{0,2},{2,0},{1,3},{3,1},{4,6},{6,4},{5,7},{7,5},{8,10},{10,8},{9,1... | collective-permute-start | bytes 2113544 | tf_op jit(solution)/shard_map/ppermute | solution.py:395
  501.3 30.5 %collective-permute-start.31 = (bf16[344,1024]{1,0:T(8,128)(2,1)}, bf16[344,1024]{1,0:T(8,128)(2,1)}, u32[]{:S(2)}, u32[]{:S(2)}) collective-permute-start(bf16[344,1024]{1,0:T(8,128)(2,1)} %slice_bitcast_fusion.6), channel_id=1, source_target_pairs={{0,2},{2,0},{1,3},{3,1},{4,6},{6,4},{5,7},{7,5},{8,10},{10,8},{9,1... | collective-permute-start | bytes 2113544 | tf_op jit(solution)/shard_map/ppermute | solution.py:395
  536.1 15.1 %collective-permute-start.55 = (bf16[256,1024]{1,0:T(8,128)(2,1)}, bf16[256,1024]{1,0:T(8,128)(2,1)}, u32[]{:S(2)}, u32[]{:S(2)}) collective-permute-start(bf16[256,1024]{1,0:T(8,128)(2,1)} %reduce-scatter.5.cloned.1.call-done), channel_id=1, source_target_pairs={{0,2},{2,0},{1,3},{3,1},{4,6},{6,4},{5,7},{7,5},{8,10},{10,8},{9,1... | collective-permute-start | bytes 1572872 | tf_op jit(solution)/shard_map/ppermute | solution.py:395
  540.2 20.9 %collective-permute-start.53 = (bf16[128,2048]{1,0:T(8,128)(2,1)}, bf16[128,2048]{1,0:T(8,128)(2,1)S(1)}, u32[]{:S(2)}, u32[]{:S(2)}) collective-permute-start(bf16[128,2048]{1,0:T(8,128)(2,1)} %reduce-scatter.3.cloned.1.call-done), channel_id=1, source_target_pairs={{0,2},{2,0},{1,3},{3,1},{4,6},{6,4},{5,7},{7,5},{8,10},{10,8},{9,1... | collective-permute-start | bytes 1572872 | tf_op jit(solution)/shard_map/ppermute | solution.py:395
  (110 other events, 1213.0 us)
Sparse Core Ops, SparseCore 0:
  24.9 95.1 all-gather.3
  191.7 74.7 all-gather.5
  277.5 89.1 reduce-scatter.4
  370.7 95.0 reduce-scatter.2

commit v3 on v2

--- a/solution.py
+++ b/solution.py
@@ -357,25 +357,29 @@
 
 
 def expand_kernel(rows_ref, weight_ref, bias_ref, active_ref, slope_ref):
-    count = rows_ref.shape[0]
+    count, width = rows_ref.shape
+    weight = weight_ref[...].reshape(width, weight_ref.shape[2])
     for start, size in spans(count, 352):
-        expanded = dot(rows_ref[start : start + size, :], weight_ref[...]) + bias_ref[...]
+        expanded = dot(rows_ref[start : start + size, :], weight) + bias_ref[...]
         below, density = gelu_parts(expanded)
         active_ref[start : start + size, :] = (expanded * below).astype(BF)
         slope_ref[start : start + size, :] = (below + expanded * density).astype(BF)
 
 
-def expand_rows(rows, weight, bias):
+def expand_rows(rows, feed_weights, bias):
     count, width = rows.shape
-    units = weight.shape[1]
+    devices = feed_weights.shape[0]
+    shard = width // devices
+    units = bias.shape[1]
     tile = 256
+    across = width // tile
     shape = jax.ShapeDtypeStruct((count, units), BF)
     return pl.pallas_call(
         expand_kernel,
         grid=(units // tile,),
         in_specs=[
             pl.BlockSpec((count, width), lambda i: (0, 0)),
-            pl.BlockSpec((width, tile), lambda i: (0, i)),
+            pl.BlockSpec((devices, shard, tile), lambda i: (0, i // across, i % across)),
             pl.BlockSpec((1, tile), lambda i: (0, i)),
         ],
         out_specs=[pl.BlockSpec((count, tile), lambda i: (0, i))] * 2,
@@ -387,7 +391,49 @@
             transcendentals=2 * count * units,
         ),
         name="expand_rows",
-    )(rows, weight, bias)
+    )(rows, feed_weights, bias)
+
+
+def feed_grads_kernel(rows_ref, active_ref, expanded_ref, feed_ref, out_ref):
+    shard, width = rows_ref.shape[1], out_ref.shape[2]
+    blocks = expanded_ref.shape[1] // width
+    for block in range(blocks):
+        out_ref[0, block * shard : (block + 1) * shard, :] = dot_left_t(
+            rows_ref[...], expanded_ref[:, block * width : (block + 1) * width]
+        ).astype(BF)
+    out_ref[0, blocks * shard :, :] = dot_left_t(active_ref[...], feed_ref[...]).astype(BF)
+
+
+def feed_grads(rows, active, grad_expanded, grad_feed, devices):
+    count, width = rows.shape
+    units = active.shape[1]
+    shard, unit_part = width // devices, units // devices
+    blocks = units // width
+    if shard % 128 != 0 or unit_part % 128 != 0:
+        expand = dot_left_t(rows, grad_expanded).astype(BF).reshape(devices, shard, blocks, width)
+        expand = expand.transpose(0, 2, 1, 3).reshape(devices, blocks * shard, width)
+        reduce = dot_left_t(active, grad_feed).astype(BF).reshape(devices, unit_part, width)
+        return jnp.concatenate([expand, reduce], 1)
+    height = blocks * shard + unit_part
+    return pl.pallas_call(
+        feed_grads_kernel,
+        grid=(devices,),
+        in_specs=[
+            pl.BlockSpec((count, shard), lambda i: (0, i)),
+            pl.BlockSpec((count, unit_part), lambda i: (0, i)),
+            pl.BlockSpec((count, units), lambda i: (0, 0)),
+            pl.BlockSpec((count, width), lambda i: (0, 0)),
+        ],
+        out_specs=pl.BlockSpec((1, height, width), lambda i: (i, 0, 0)),
+        out_shape=jax.ShapeDtypeStruct((devices, height, width), BF),
+        compiler_params=pltpu.CompilerParams(vmem_limit_bytes=52 * 2**20),
+        cost_estimate=pl.CostEstimate(
+            flops=4 * count * units * width,
+            bytes_accessed=2 * (2 * count * (width + units) + 2 * width * units),
+            transcendentals=0,
+        ),
+        name="feed_grads",
+    )(rows, active, grad_expanded, grad_feed)
 
 
 def far_send(array, shift):
@@ -468,6 +514,10 @@
                 moving = moving + block(direction * (hops - step))
         total = total + moving
     return total
+
+
+def after(array, *earlier):
+    return lax.optimization_barrier((array,) + earlier)[0]
 
 
 def core_join(mine, axis, core):
@@ -555,14 +605,24 @@
         )
     output_whole = output_whole.reshape(far_count, head_width, width)
     output_whole = jnp.roll(output_whole, -far, 0).reshape(width // 2, width)
+    blocks = units // 2 // width
     expand_mine = lax.dynamic_index_in_dim(
         expand_weight.reshape(shard, fsdp_count, 2, unit_part), core, 2, False
-    ).reshape(shard, units // 2)
-    expand_whole = fsdp_gather(expand_mine)
+    ).reshape(shard, blocks, width)
     reduce_mine = lax.dynamic_index_in_dim(
         reduce_weight.reshape(2, unit_part, width), core, 0, False
     )
-    reduce_whole = fsdp_gather(reduce_mine)
+    feed_mine = jnp.concatenate([expand_mine[:, i] for i in range(blocks)] + [reduce_mine], 0)
+    height = blocks * shard + unit_part
+    feed_mine = lax.dynamic_slice_in_dim(
+        feed_mine, far * (height // far_count), height // far_count, 0
+    )
+    feed_weights = lax.all_gather(after(feed_mine, packed), ("fsdp", "far"), axis=0, tiled=True)
+    feed_weights = feed_weights.reshape(fsdp_count, height, width)
+    expand_blocks = [
+        feed_weights[:, i * shard : (i + 1) * shard].reshape(width, width) for i in range(blocks)
+    ]
+    reduce_whole = feed_weights[:, blocks * shard :].reshape(units // 2, width)
 
     groups = 2 if image_count % 2 == 0 else 1
     group_images = image_count // groups
@@ -630,7 +690,7 @@
     normal_2, factor_2 = normalize(residual)
     second_mine = (normal_2 * gain_2 + shift_2).astype(BF)
     second_normed = jnp.concatenate([second_mine, other_core(second_mine)], 0)
-    activated, slope = expand_rows(second_normed, expand_whole, bias_e)
+    activated, slope = expand_rows(second_normed, feed_weights, bias_e)
     branch = dot(activated, reduce_whole)
     branch_feed = (
         branch[:own_rows] + other_core(branch[own_rows:].astype(BF)).astype(F32) + bias_r
@@ -643,19 +703,20 @@
     grad_feed = (scale_f * both.astype(F32)).astype(BF)
     grad_feed_scale = jnp.sum(upstream * branch_feed, 0)
     grad_reduce_bias = column_total(grad_feed[:own_rows])
-    grad_reduce_weight = dot_left_t(activated, grad_feed).astype(BF)
     grad_expanded = (dot_right_t(grad_feed, reduce_whole) * slope.astype(F32)).astype(BF)
-    grad_expanded, grad_reduce_weight = lax.optimization_barrier(
-        (grad_expanded, grad_reduce_weight)
-    )
-    grad_reduce_weight = fsdp_scatter(grad_reduce_weight)
+    feed_sums = feed_grads(second_normed, activated, grad_expanded, grad_feed, fsdp_count)
+    grad_expanded, feed_sums = lax.optimization_barrier((grad_expanded, feed_sums))
+    feed_sums = lax.psum_scatter(
+        feed_sums.reshape(fsdp_count * height, width),
+        ("fsdp", "far"),
+        scatter_dimension=0,
+        tiled=True,
+    )
+    partial = sum(
+        dot_right_t(grad_expanded[:, i * width : (i + 1) * width], expand_blocks[i])
+        for i in range(blocks)
+    )
     grad_expand_bias = column_total(grad_expanded)
-    grad_expand_weight = dot_left_t(second_normed, grad_expanded).astype(BF)
-    grad_expanded, grad_expand_weight = lax.optimization_barrier(
-        (grad_expanded, grad_expand_weight)
-    )
-    grad_expand_weight = fsdp_scatter(grad_expand_weight)
-    partial = dot_right_t(grad_expanded, expand_whole)
     upper = partial[:own_rows] + other_core(partial[own_rows:].astype(BF)).astype(F32)
     grad_second_gain = jnp.sum(upper * normal_2, 0)
     grad_second_shift = jnp.sum(upper, 0)
@@ -693,12 +754,17 @@
     grad_first_gain = grad_first_shift = column_sums = 0.0
     for group in range(groups):
         picked = limits[group * group_images : (group + 1) * group_images]
+        grad_heads_in = grad_heads[group]
+        if group > 0:
+            grad_heads_in = after(grad_heads_in, partial)
         grad_triple = from_kernel(
             attend_backward(
-                kernel_in[group], kernel_out[group], grad_heads[group], kernel_logs[group], picked
+                kernel_in[group], kernel_out[group], grad_heads_in, kernel_logs[group], picked
             ),
             3,
         )
+        if group > 0:
+            grad_triple = after(grad_triple, *moved)
         grad_triples.append(grad_triple)
         partial, gain_part, shift_part, total_part = project_back(
             grad_triple, tokens[group], triple_whole
@@ -709,7 +775,8 @@
         partial = partial.reshape(far_count, 2, rows, width)
         partial = partial[:, 0].astype(F32) + other_core(partial[:, 1]).astype(F32)
         partial = partial.astype(BF)
-        upper_parts.append(far_sum([partial[r] for r in range(far_count)]))
+        moved = far_exchange([partial[r] for r in range(far_count)])
+        upper_parts.append(sum(part.astype(F32) for part in moved))
     grad_triple_weight = sum(
         dot_left_t(
             normed[group].reshape(seq_count * rows, width),
@@ -773,12 +840,15 @@
         spread = fsdp_scatter(spread.reshape(width, width))
         grad_output_weight = far_total(spread)
         grad_output_weight = grad_output_weight + other_core(grad_output_weight)
-    grad_expand_weight = core_join(
-        far_total(grad_expand_weight).astype(BF).reshape(shard, fsdp_count, unit_part), 2, core
-    ).reshape(shard, units)
-    grad_reduce_weight = core_join(far_total(grad_reduce_weight).astype(BF), 0, core).reshape(
-        2 * unit_part, width
-    )
+    feed_sums = jnp.roll(jnp.stack(far_gather(core_join(feed_sums, 0, core)), 0), far, 0)
+    feed_sums = feed_sums.transpose(1, 0, 2, 3).reshape(2, height, width).astype(F32)
+    grad_expand_weight = (
+        feed_sums[:, : blocks * shard]
+        .reshape(2, blocks, shard, -1, unit_part)
+        .transpose(2, 1, 3, 0, 4)
+        .reshape(shard, units)
+    )
+    grad_reduce_weight = feed_sums[:, blocks * shard :].reshape(2 * unit_part, width)
     grad_expand_bias = (
         sums[10 : 10 + 2 * bias_columns]
         .reshape(2, bias_columns, shard)
@@ -798,9 +868,9 @@
         sums[5],
         sums[6],
         sums[7],
-        grad_expand_weight.astype(F32),
+        grad_expand_weight,
         grad_expand_bias,
-        grad_reduce_weight.astype(F32),
+        grad_reduce_weight,
         sums[8],
         sums[9],
     )

time: 579 us -> 593 us (1.024)
  matrix products: 70.4 us -> 48.5 us
  Pallas kernels: 116 us -> 136 us
  waiting for transfers between devices: 146 us -> 166 us
  starting transfers between devices: 60.5 us -> 53.3 us
    ppermute x12 -> x11, waiting for transfers between devices: 44.5 us -> 94.5 us  [far_send(): lax.ppermute(array, 'far', [(i, (i + shift) % count) for i in range(count)])]
    all_gather x2 -> x1, waiting for transfers between devices: 22.3 us -> 0.01 us  [shards(): lax.all_gather(after(feed_mine, packed), ('fsdp', 'far'), axis=0, tiled=T...]
    pallas_call x0 -> x1, Pallas kernels: none -> 20.2 us  [feed_grads(): pl.pallas_call(feed_grads_kernel, grid=(devices,), in_specs=[pl.BlockSpec...]
    dot_general x6 -> x4, matrix products: 32.4 us -> 12.4 us  [dot_left_t(): lax.dot_general(left, right, (((0,), (0,)), ((), ())), preferred_element_...]
    reshape x1, local copies, waits for them, and re-layouts: 15.5 us -> 4.26 us  [shards(): grad_attended.reshape(2, groups, rows, far_count, head_width)]
    ppermute x28, waiting for transfers between devices: 78.5 us -> 69.2 us  [ring_send(): return lax.ppermute(array, 'fsdp', pairs)]
    slice x0 -> x3, local copies, waits for them, and re-layouts: none -> 6.89 us  [the longest x1 2.8 us: shards(): reduce_whole = feed_weights[:, blocks * shard:].reshape(units // 2, width)]
    unnamed x170 -> x149, local copies, waits for them, and re-layouts: 26.3 us -> 28.6 us
  transfers between devices with their start and end apart: 61 -> 57, of which waited for: 27 -> 26; matrix products, arithmetic and copies ran while one was open for 34% -> 24% of each run, Pallas kernels for 20% -> 17%
where the time goes in v3:
time: 593 us; the launch traced here: 586 us
  waiting for transfers between devices  166 us (28%)
  Pallas kernels  136 us (23%)
  local copies, waits for them, and re-layouts  104 us (18%)
  other arithmetic  62 us (10%)
  starting transfers between devices  53.3 us (9%)
  matrix products  48.5 us (8%)
  between operations  15.9 us (3%)
    ppermute x11, waiting for transfers between devices, far_send(): lax.ppermute(array, 'far', [(i, (i + shift) % count) for i in range(count)])  94.5 us
    ppermute x28, waiting for transfers between devices, ring_send(): return lax.ppermute(array, 'fsdp', pairs)  69.2 us
    pallas_call x2, Pallas kernels, attend_backward(): pl.pallas_call(attend_backward_kernel, grid_spec=pltpu.PrefetchScalarGrid...  51.3 us
    ppermute x28, starting transfers between devices, ring_send(): return lax.ppermute(array, 'fsdp', pairs)  37.5 us
    pallas_call x2, Pallas kernels, attend_forward(): pl.pallas_call(attend_forward_kernel, grid_spec=pltpu.PrefetchScalarGridS...  29.4 us
    unnamed x149, local copies, waits for them, and re-layouts  28.6 us
    dot_general x4, matrix products, dot_right_t(): lax.dot_general(left, right, (((1,), (1,)), ((), ())), preferred_element_...  22.6 us
    pallas_call x1, Pallas kernels, feed_grads(): pl.pallas_call(feed_grads_kernel, grid=(devices,), in_specs=[pl.BlockSpec...  20.2 us
  transfers between devices with their start and end apart: 57, of which 26 were waited for; matrix products, arithmetic and copies ran while one was open for 24% of the time, Pallas kernels for 17%

profile of v3, /device:TPU:0, one launch (start us, length us, event | category | flops | bytes accessed | tf_op | source)
XLA Modules:
  0.0 586.2 jit_solution(16348981855304588621)
XLA Ops:
  65.2 7.3 %collective-permute-done.13 = bf16[64,1024]{1,0:T(8,128)(2,1)S(1)} collective-permute-done((bf16[64,1024]{1,0:T(8,128)(2,1)}, bf16[64,1024]{1,0:T(8,128)(2,1)S(1)}, u32[]{:S(2)}, u32[]{:S(2)}) %collective-permute-start.13) | collective-permute-done | bytes 131104 | tf_op jit(solution)/shard_map/ppermute | solution.py:478
  76.1 6.7 %collective-permute-done.14 = bf16[64,1024]{1,0:T(8,128)(2,1)S(1)} collective-permute-done((bf16[64,1024]{1,0:T(8,128)(2,1)S(1)}, bf16[64,1024]{1,0:T(8,128)(2,1)S(1)}, u32[]{:S(2)}, u32[]{:S(2)}) %collective-permute-start.14) | collective-permute-done | bytes 131104 | tf_op jit(solution)/shard_map/ppermute | solution.py:478
  88.5 9.7 %collective-permute-done.16 = bf16[64,1024]{1,0:T(8,128)(2,1)S(1)} collective-permute-done((bf16[64,1024]{1,0:T(8,128)(2,1)S(1)}, bf16[64,1024]{1,0:T(8,128)(2,1)S(1)}, u32[]{:S(2)}, u32[]{:S(2)}) %collective-permute-start.16) | collective-permute-done | bytes 131104 | tf_op jit(solution)/shard_map/ppermute | solution.py:478
  100.3 5.2 collective-permute-done.17
  115.2 4.3 project.3
  122.4 14.8 %attend_forward.3 = (bf16[4,1,344,256]{3,2,1,0:T(8,128)(2,1)S(1)}, f32[1,2,1376,128]{3,2,1,0:T(8,128)S(1)}) custom-call(s32[1,2]{1,0:T(1,128)S(1)} %get-tuple-element.231.limit_ref, bf16[4,1,344,768]{3,2,1,0:T(8,128)(2,1)} %bitcast.278, bf16[4,1,344,768]{3,2,1,0:T(8,128)(2,1)} %bitcast.279, bf16[4,1,344,768]{3,2,1,0:T(8,128)(2,1)} %bitcast.280), custom_call_target="tpu_custom_call" | custom-call | flops 7755268096 | bytes 4227072 | tf_op jit(solution)/shard_map/attend_forward/pallas_call | solution.py:202
  141.3 4.5 project.2
  148.8 14.6 %attend_forward.2 = (bf16[4,1,344,256]{3,2,1,0:T(8,128)(2,1)S(1)}, f32[1,2,1376,128]{3,2,1,0:T(8,128)S(1)}) custom-call(s32[1,2]{1,0:T(1,128)S(1)} %get-tuple-element.230.limit_ref, bf16[4,1,344,768]{3,2,1,0:T(8,128)(2,1)} %bitcast.284, bf16[4,1,344,768]{3,2,1,0:T(8,128)(2,1)} %bitcast.285, bf16[4,1,344,768]{3,2,1,0:T(8,128)(2,1)} %bitcast.286), custom_call_target="tpu_custom_call" | custom-call | flops 7755268096 | bytes 4227072 | tf_op jit(solution)/shard_map/attend_forward/pallas_call | solution.py:202
  166.0 7.9 %collective-permute-done.10 = bf16[688,256]{1,0:T(8,128)(2,1)S(1)} collective-permute-done((bf16[688,256]{1,0:T(8,128)(2,1)S(1)}, bf16[688,256]{1,0:T(8,128)(2,1)S(1)}, u32[]{:S(2)}, u32[]{:S(2)}) %collective-permute-start.10) | collective-permute-done | bytes 352288 | tf_op jit(solution)/shard_map/ppermute | solution.py:441
  185.5 5.0 add_convert_fusion.1
  207.4 19.1 %expand_rows.1 = (bf16[1376,2048]{1,0:T(8,128)(2,1)}, bf16[1376,2048]{1,0:T(8,128)(2,1)}) custom-call(bf16[1376,1024]{1,0:T(8,128)(2,1)S(1)} %copy-done.4, bf16[8,512,1024]{2,1,0:T(8,128)(2,1)} %bitcast.303, f32[1,2048]{1,0:T(1,128)S(1)} %reshape.487.bias_ref), custom_call_target="tpu_custom_call" | custom-call | flops 11542724608 | bytes 18284544 | tf_op jit(solution)/shard_map/expand_rows/pallas_call | solution.py:377
  226.5 9.7 %multiply_convert_fusion.expanded_ref = bf16[1376,2048]{1,0:T(8,128)(2,1)} fusion(bf16[1376,2048]{1,0:T(8,128)(2,1)} %get-tuple-element.47, bf16[1376,1024]{1,0:T(8,128)(2,1)S(1)} %copy-done.39, bf16[2048,1024]{1,0:T(8,128)(2,1)S(1)} %bitcast.321), kind=kOutput, calls=%fused_computation | convolution fusion | flops 5779816448 | bytes 18284544 | tf_op jit(solution)/shard_map/dot_general | solution.py:26
  236.2 20.2 %feed_grads.1 = bf16[8,512,1024]{2,1,0:T(8,128)(2,1)} custom-call(bf16[1376,1024]{1,0:T(8,128)(2,1)} %pad_maximum_fusion.3.rows_ref, bf16[1376,2048]{1,0:T(8,128)(2,1)} %get-tuple-element.46.active_ref, bf16[1376,2048]{1,0:T(8,128)(2,1)} %multiply_convert_fusion.expanded_ref, bf16[1376,1024]{1,0:T(8,128)(2,1)} %multiply_convert_fusion.1.feed_ref), custom_call_target="tpu_custom_call" | custom-call | flops 11542724608 | bytes 25296896 | tf_op jit(solution)/shard_map/feed_grads/pallas_call | solution.py:418
  256.4 4.9 fusion.17
  266.5 6.1 %fusion.80 = f32[1376,1024]{1,0:T(8,128)S(1)} fusion(bf16[1376,2048]{1,0:T(8,128)(2,1)S(1)} %bitcast.373, bf16[2048,1024]{1,0:T(8,128)(2,1)S(1)} %bitcast.322), kind=kOutput, calls=%fused_computation.254 | convolution fusion | flops 5771362304 | bytes 15466496 | tf_op jit(solution)/shard_map/dot_general | solution.py:18
  275.7 4.6 multiply_reduce_fusion
  280.5 6.5 %fusion.2 = (bf16[1024]{0:T(1024)(128)(2,1)S(1)}, bf16[688,1024]{1,0:T(8,128)(2,1)}, bf16[1024]{0:T(1024)(128)(2,1)S(1)}, f32[688,1024]{1,0:T(8,128)S(1)}) fusion(bf16[688,1024]{1,0:T(8,128)(2,1)} %collective-permute-done.25, f32[1376,1024]{1,0:T(8,128)} %copy-done.51, f32[1024]{0:T(1024)S(1)} %get-tuple-element.218, bf16[2,344,1024]{2,1,0:T(8,128)(2,1)} %param.21, ...), kind=kLoop, calls=%fused_computation.14 | loop fusion | flops 15497216 | bytes 19753728 | tf_op jit(solution)/shard_map/reduce_sum | solution.py:704
  295.2 4.9 convolution_convert_fusion
  320.4 18.9 %collective-permute-done.29 = bf16[688,256]{1,0:T(8,128)(2,1)S(1)} collective-permute-done((bf16[688,256]{1,0:T(8,128)(2,1)S(1)}, bf16[688,256]{1,0:T(8,128)(2,1)S(1)}, u32[]{:S(2)}, u32[]{:S(2)}) %collective-permute-start.29) | collective-permute-done | bytes 352288 | tf_op jit(solution)/shard_map/ppermute | solution.py:441
  340.2 25.6 %attend_backward.2 = bf16[4,1,344,768]{3,2,1,0:T(8,128)(2,1)} custom-call(s32[1,2]{1,0:T(1,128)} %copy-done.11, bf16[4,1,344,768]{3,2,1,0:T(8,128)(2,1)} %bitcast.287, bf16[4,1,344,768]{3,2,1,0:T(8,128)(2,1)} %bitcast.288, bf16[4,1,344,768]{3,2,1,0:T(8,128)(2,1)} %bitcast.289, bf16[4,1,344,256]{3,2,1,0:T(8,128)(2,1)} %copy-done.9, ...), custom_call_target="tpu_custom_call" | custom-call | flops 19388170240 | bytes 8454144 | tf_op jit(solution)/shard_map/attend_backward/pallas_call | solution.py:236
  379.1 4.3 fusion.81
  383.4 17.4 %collective-permute-done.32 = bf16[688,256]{1,0:T(8,128)(2,1)S(1)} collective-permute-done((bf16[688,256]{1,0:T(8,128)(2,1)S(1)}, bf16[688,256]{1,0:T(8,128)(2,1)S(1)}, u32[]{:S(2)}, u32[]{:S(2)}) %collective-permute-start.32) | collective-permute-done | bytes 352288 | tf_op jit(solution)/shard_map/ppermute | solution.py:441
  407.3 25.7 %attend_backward.3 = bf16[4,1,344,768]{3,2,1,0:T(8,128)(2,1)} custom-call(s32[1,2]{1,0:T(1,128)} %copy-done.10, bf16[4,1,344,768]{3,2,1,0:T(8,128)(2,1)} %bitcast.281, bf16[4,1,344,768]{3,2,1,0:T(8,128)(2,1)} %bitcast.282, bf16[4,1,344,768]{3,2,1,0:T(8,128)(2,1)} %bitcast.283, bf16[4,1,344,256]{3,2,1,0:T(8,128)(2,1)} %copy-done.8, ...), custom_call_target="tpu_custom_call" | custom-call | flops 19388170240 | bytes 8454144 | tf_op jit(solution)/shard_map/attend_backward/pallas_call | solution.py:236
  433.0 20.9 %collective-permute-done.31 = bf16[344,1024]{1,0:T(8,128)(2,1)S(1)} collective-permute-done((bf16[344,1024]{1,0:T(8,128)(2,1)S(1)}, bf16[344,1024]{1,0:T(8,128)(2,1)S(1)}, u32[]{:S(2)}, u32[]{:S(2)}) %collective-permute-start.31) | collective-permute-done | bytes 704544 | tf_op jit(solution)/shard_map/ppermute | solution.py:441
  460.8 6.1 %fusion.1 = bf16[1024,768]{0,1:T(8,128)(2,1)S(1)} fusion(f32[1024,768]{0,1:T(8,128)} %fusion.81, bf16[4,344,1024]{2,1,0:T(8,128)(2,1)} %copy-done.18, bf16[4,344,768]{2,1,0:T(8,128)(2,1)} %bitcast.290), kind=kOutput, calls=%fused_computation.12 | convolution fusion | flops 2165833728 | bytes 9650176 | tf_op jit(solution)/shard_map/dot_general | solution.py:22
  479.5 7.6 %collective-permute-done.35 = bf16[128,896]{1,0:T(8,128)(2,1)S(1)} collective-permute-done((bf16[128,896]{1,0:T(8,128)(2,1)S(1)}, bf16[128,896]{1,0:T(8,128)(2,1)S(1)}, u32[]{:S(2)}, u32[]{:S(2)}) %collective-permute-start.35) | collective-permute-done | bytes 229408 | tf_op jit(solution)/shard_map/ppermute | solution.py:478
  488.4 7.1 %collective-permute-done.36 = bf16[128,896]{1,0:T(8,128)(2,1)S(1)} collective-permute-done((bf16[128,896]{1,0:T(8,128)(2,1)S(1)}, bf16[128,896]{1,0:T(8,128)(2,1)S(1)}, u32[]{:S(2)}, u32[]{:S(2)}) %collective-permute-start.36) | collective-permute-done | bytes 229408 | tf_op jit(solution)/shard_map/ppermute | solution.py:478
  497.9 4.3 collective-permute-done.37
  510.2 5.1 collective-permute-done.42
  530.2 4.6 collective-permute-done.34
  540.6 4.3 fusion.15
  544.8 19.7 %collective-permute-done.54 = bf16[2,256,1024]{2,1,0:T(8,128)(2,1)} collective-permute-done((bf16[2,256,1024]{2,1,0:T(8,128)(2,1)}, bf16[2,256,1024]{2,1,0:T(8,128)(2,1)}, u32[]{:S(2)}, u32[]{:S(2)}) %collective-permute-start.54) | collective-permute-done | bytes 1048608 | tf_op jit(solution)/shard_map/ppermute | solution.py:441
  (426 shorter events, 242.8 us)
Async XLA Ops:
  7.2 191.7 %all-gather.2.cloned.1.call-start = ((), (), s32[]{:S(2)}) async-start(), calls=%async_computation.1 | async-start | bytes 8912896 | tf_op jit(solution)/shard_map/all_gather | solution.py:620
  53.6 476.4 %reduce-scatter.2.cloned.1.call-start = ((), (), s32[]{:S(2)}) async-start(), calls=%async_computation.2 | async-start | bytes 8912896 | tf_op jit(solution)/shard_map/reduce_scatter | solution.py:709
  59.2 46.4 %collective-permute-start.8 = (bf16[344,1024]{1,0:T(8,128)(2,1)}, bf16[344,1024]{1,0:T(8,128)(2,1)}, u32[]{:S(2)}, u32[]{:S(2)}) collective-permute-start(bf16[344,1024]{1,0:T(8,128)(2,1)} %get-tuple-element.188), channel_id=1, source_target_pairs={{0,2},{2,0},{1,3},{3,1},{4,6},{6,4},{5,7},{7,5},{8,10},{10,8},{9,1... | collective-permute-start | bytes 2113544 | tf_op jit(solution)/shard_map/ppermute | solution.py:441
  60.6 78.7 %collective-permute-start.7 = (bf16[344,1024]{1,0:T(8,128)(2,1)}, bf16[344,1024]{1,0:T(8,128)(2,1)}, u32[]{:S(2)}, u32[]{:S(2)}) collective-permute-start(bf16[344,1024]{1,0:T(8,128)(2,1)} %get-tuple-element.188), channel_id=1, source_target_pairs={{0,1},{1,0},{2,3},{3,2},{4,5},{5,4},{6,7},{7,6},{8,9},{9,8},{10,11... | collective-permute-start | bytes 2113544 | tf_op jit(solution)/shard_map/ppermute | solution.py:463
  60.6 39.7 %collective-permute-start.20 = (bf16[344,1024]{1,0:T(8,128)(2,1)}, bf16[344,1024]{1,0:T(8,128)(2,1)}, u32[]{:S(2)}, u32[]{:S(2)}) collective-permute-start(bf16[344,1024]{1,0:T(8,128)(2,1)} %get-tuple-element.189), channel_id=1, source_target_pairs={{0,2},{2,0},{1,3},{3,1},{4,6},{6,4},{5,7},{7,5},{8,10},{10,8},{9,1... | collective-permute-start | bytes 2113544 | tf_op jit(solution)/shard_map/ppermute | solution.py:441
  62.4 51.0 %collective-permute-start.19 = (bf16[344,1024]{1,0:T(8,128)(2,1)}, bf16[344,1024]{1,0:T(8,128)(2,1)}, u32[]{:S(2)}, u32[]{:S(2)}) collective-permute-start(bf16[344,1024]{1,0:T(8,128)(2,1)} %get-tuple-element.189), channel_id=1, source_target_pairs={{0,1},{1,0},{2,3},{3,2},{4,5},{5,4},{6,7},{7,6},{8,9},{9,8},{10,11... | collective-permute-start | bytes 2113544 | tf_op jit(solution)/shard_map/ppermute | solution.py:463
  72.5 10.4 %collective-permute-start.14 = (bf16[64,1024]{1,0:T(8,128)(2,1)S(1)}, bf16[64,1024]{1,0:T(8,128)(2,1)S(1)}, u32[]{:S(2)}, u32[]{:S(2)}) collective-permute-start(bf16[64,1024]{1,0:T(8,128)(2,1)S(1)} %collective-permute-done.12), channel_id=1, source_target_pairs={{0,4},{8,0},{16,8},{24,16},{28,24},{20,28},{12,20},{4,12},{1,5},{9... | collective-permute-start | bytes 393224 | tf_op jit(solution)/shard_map/ppermute | solution.py:478
  87.8 10.3 %collective-permute-start.16 = (bf16[64,1024]{1,0:T(8,128)(2,1)S(1)}, bf16[64,1024]{1,0:T(8,128)(2,1)S(1)}, u32[]{:S(2)}, u32[]{:S(2)}) collective-permute-start(bf16[64,1024]{1,0:T(8,128)(2,1)S(1)} %collective-permute-done.14), channel_id=1, source_target_pairs={{0,4},{8,0},{16,8},{24,16},{28,24},{20,28},{12,20},{4,12},{1,5},{9... | collective-permute-start | bytes 393224 | tf_op jit(solution)/shard_map/ppermute | solution.py:478
  100.2 13.2 %collective-permute-start.21 = (bf16[344,1024]{1,0:T(8,128)(2,1)}, bf16[344,1024]{1,0:T(8,128)(2,1)}, u32[]{:S(2)}, u32[]{:S(2)}) collective-permute-start(bf16[344,1024]{1,0:T(8,128)(2,1)} %collective-permute-done.20), channel_id=1, source_target_pairs={{0,1},{1,0},{2,3},{3,2},{4,5},{5,4},{6,7},{7,6},{8,9},{9,8},{10,11... | collective-permute-start | bytes 2113544 | tf_op jit(solution)/shard_map/ppermute | solution.py:463
  106.5 32.8 %collective-permute-start.9 = (bf16[344,1024]{1,0:T(8,128)(2,1)}, bf16[344,1024]{1,0:T(8,128)(2,1)}, u32[]{:S(2)}, u32[]{:S(2)}) collective-permute-start(bf16[344,1024]{1,0:T(8,128)(2,1)} %collective-permute-done.8), channel_id=1, source_target_pairs={{0,1},{1,0},{2,3},{3,2},{4,5},{5,4},{6,7},{7,6},{8,9},{9,8},{10,11... | collective-permute-start | bytes 2113544 | tf_op jit(solution)/shard_map/ppermute | solution.py:463
  137.3 27.4 %collective-permute-start.22 = (bf16[688,256]{1,0:T(8,128)(2,1)S(1)}, bf16[688,256]{1,0:T(8,128)(2,1)S(1)}, u32[]{:S(2)}, u32[]{:S(2)}) collective-permute-start(bf16[688,256]{1,0:T(8,128)(2,1)S(1)} %bitcast.354), channel_id=1, source_target_pairs={{0,2},{2,0},{1,3},{3,1},{4,6},{6,4},{5,7},{7,5},{8,10},{10,8},{9,1... | collective-permute-start | bytes 1056776 | tf_op jit(solution)/shard_map/ppermute | solution.py:441
  163.5 10.4 %collective-permute-start.10 = (bf16[688,256]{1,0:T(8,128)(2,1)S(1)}, bf16[688,256]{1,0:T(8,128)(2,1)S(1)}, u32[]{:S(2)}, u32[]{:S(2)}) collective-permute-start(bf16[688,256]{1,0:T(8,128)(2,1)S(1)} %bitcast.357), channel_id=1, source_target_pairs={{0,2},{2,0},{1,3},{3,1},{4,6},{6,4},{5,7},{7,5},{8,10},{10,8},{9,1... | collective-permute-start | bytes 1056776 | tf_op jit(solution)/shard_map/ppermute | solution.py:441
  165.8 10.4 %collective-permute-start.23 = (bf16[344,1024]{1,0:T(8,128)(2,1)S(1)}, bf16[344,1024]{1,0:T(8,128)(2,1)S(1)}, u32[]{:S(2)}, u32[]{:S(2)}) collective-permute-start(bf16[344,1024]{1,0:T(8,128)(2,1)S(1)} %slice.470), channel_id=1, source_target_pairs={{0,1},{1,0},{2,3},{3,2},{4,5},{5,4},{6,7},{7,6},{8,9},{9,8},{10,11... | collective-permute-start | bytes 2113544 | tf_op jit(solution)/shard_map/ppermute | solution.py:463
  175.7 15.5 %collective-permute-start.26 = (bf16[688,1024]{1,0:T(8,128)(2,1)}, bf16[688,1024]{1,0:T(8,128)(2,1)}, u32[]{:S(2)}, u32[]{:S(2)}) collective-permute-start(bf16[688,1024]{1,0:T(8,128)(2,1)} %bitcast.62), channel_id=1, source_target_pairs={{0,1},{1,0},{2,3},{3,2},{4,5},{5,4},{6,7},{7,6},{8,9},{9,8},{10,11... | collective-permute-start | bytes 4227080 | tf_op jit(solution)/shard_map/ppermute | solution.py:463
  266.1 9.5 %collective-permute-start.27 = (bf16[688,1024]{1,0:T(8,128)(2,1)}, bf16[688,1024]{1,0:T(8,128)(2,1)}, u32[]{:S(2)}, u32[]{:S(2)}) collective-permute-start(bf16[688,1024]{1,0:T(8,128)(2,1)} %slice.468), channel_id=1, source_target_pairs={{0,1},{1,0},{2,3},{3,2},{4,5},{5,4},{6,7},{7,6},{8,9},{9,8},{10,11... | collective-permute-start | bytes 4227080 | tf_op jit(solution)/shard_map/ppermute | solution.py:463
  310.0 10.1 %collective-permute-start.44 = (bf16[64,1024]{1,0:T(8,128)(2,1)S(1)}, bf16[64,1024]{1,0:T(8,128)(2,1)S(1)}, u32[]{:S(2)}, u32[]{:S(2)}) collective-permute-start(bf16[64,1024]{1,0:T(8,128)(2,1)S(1)} %get-tuple-element.199), channel_id=1, source_target_pairs={{0,8},{8,16},{16,24},{24,28},{28,20},{20,12},{12,4},{4,0},{1,9},{9... | collective-permute-start | bytes 393224 | tf_op jit(solution)/shard_map/ppermute | solution.py:478
  314.5 24.8 %collective-permute-start.29 = (bf16[688,256]{1,0:T(8,128)(2,1)S(1)}, bf16[688,256]{1,0:T(8,128)(2,1)S(1)}, u32[]{:S(2)}, u32[]{:S(2)}) collective-permute-start(bf16[688,256]{1,0:T(8,128)(2,1)S(1)} %bitcast.348), channel_id=1, source_target_pairs={{0,2},{2,0},{1,3},{3,1},{4,6},{6,4},{5,7},{7,5},{8,10},{10,8},{9,1... | collective-permute-start | bytes 1056776 | tf_op jit(solution)/shard_map/ppermute | solution.py:441
  315.6 61.3 %collective-permute-start.48 = (bf16[64,1024]{1,0:T(8,128)(2,1)S(1)}, bf16[64,1024]{1,0:T(8,128)(2,1)S(1)}, u32[]{:S(2)}, u32[]{:S(2)}) collective-permute-start(bf16[64,1024]{1,0:T(8,128)(2,1)S(1)} %get-tuple-element.200), channel_id=1, source_target_pairs={{0,4},{8,0},{16,8},{24,16},{28,24},{20,28},{12,20},{4,12},{1,5},{9... | collective-permute-start | bytes 393224 | tf_op jit(solution)/shard_map/ppermute | solution.py:478
  320.1 56.8 %collective-permute-start.45 = (bf16[64,1024]{1,0:T(8,128)(2,1)S(1)}, bf16[64,1024]{1,0:T(8,128)(2,1)S(1)}, u32[]{:S(2)}, u32[]{:S(2)}) collective-permute-start(bf16[64,1024]{1,0:T(8,128)(2,1)S(1)} %fusion.51), channel_id=1, source_target_pairs={{0,8},{8,16},{16,24},{24,28},{28,20},{20,12},{12,4},{4,0},{1,9},{9... | collective-permute-start | bytes 393224 | tf_op jit(solution)/shard_map/ppermute | solution.py:478
  371.3 35.3 %collective-permute-start.30 = (bf16[2,344,1024]{2,1,0:T(8,128)(2,1)S(1)}, bf16[2,344,1024]{2,1,0:T(8,128)(2,1)S(1)}, u32[]{:S(2)}, u32[]{:S(2)}) collective-permute-start(bf16[2,344,1024]{2,1,0:T(8,128)(2,1)S(1)} %slice_bitcast_fusion.2), channel_id=1, source_target_pairs={{0,1},{1,0},{2,3},{3,2},{4,5},{5,4},{6,7},{7,6},{8,9},{9,8},{10,11... | collective-permute-start | bytes 4227080 | tf_op jit(solution)/shard_map/ppermute | solution.py:463
  373.3 27.5 %collective-permute-start.32 = (bf16[688,256]{1,0:T(8,128)(2,1)S(1)}, bf16[688,256]{1,0:T(8,128)(2,1)S(1)}, u32[]{:S(2)}, u32[]{:S(2)}) collective-permute-start(bf16[688,256]{1,0:T(8,128)(2,1)S(1)} %bitcast.349), channel_id=1, source_target_pairs={{0,2},{2,0},{1,3},{3,1},{4,6},{6,4},{5,7},{7,5},{8,10},{10,8},{9,1... | collective-permute-start | bytes 1056776 | tf_op jit(solution)/shard_map/ppermute | solution.py:441
  377.0 24.7 %collective-permute-start.46 = (bf16[64,1024]{1,0:T(8,128)(2,1)S(1)}, bf16[64,1024]{1,0:T(8,128)(2,1)S(1)}, u32[]{:S(2)}, u32[]{:S(2)}) collective-permute-start(bf16[64,1024]{1,0:T(8,128)(2,1)S(1)} %get-tuple-element.197), channel_id=1, source_target_pairs={{0,8},{8,16},{16,24},{24,28},{28,20},{20,12},{12,4},{4,0},{1,9},{9... | collective-permute-start | bytes 393224 | tf_op jit(solution)/shard_map/ppermute | solution.py:478
  378.1 23.6 %collective-permute-start.49 = (bf16[64,1024]{1,0:T(8,128)(2,1)S(1)}, bf16[64,1024]{1,0:T(8,128)(2,1)S(1)}, u32[]{:S(2)}, u32[]{:S(2)}) collective-permute-start(bf16[64,1024]{1,0:T(8,128)(2,1)S(1)} %get-tuple-element.198), channel_id=1, source_target_pairs={{0,4},{8,0},{16,8},{24,16},{28,24},{20,28},{12,20},{4,12},{1,5},{9... | collective-permute-start | bytes 393224 | tf_op jit(solution)/shard_map/ppermute | solution.py:478
  401.8 71.6 %collective-permute-start.47 = (bf16[64,1024]{1,0:T(8,128)(2,1)S(1)}, bf16[64,1024]{1,0:T(8,128)(2,1)S(1)}, u32[]{:S(2)}, u32[]{:S(2)}) collective-permute-start(bf16[64,1024]{1,0:T(8,128)(2,1)S(1)} %get-tuple-element.195), channel_id=1, source_target_pairs={{0,8},{8,16},{16,24},{24,28},{28,20},{20,12},{12,4},{4,0},{1,9},{9... | collective-permute-start | bytes 393224 | tf_op jit(solution)/shard_map/ppermute | solution.py:478
  402.5 70.9 %collective-permute-start.50 = (bf16[64,1024]{1,0:T(8,128)(2,1)S(1)}, bf16[64,1024]{1,0:T(8,128)(2,1)S(1)}, u32[]{:S(2)}, u32[]{:S(2)}) collective-permute-start(bf16[64,1024]{1,0:T(8,128)(2,1)S(1)} %get-tuple-element.196), channel_id=1, source_target_pairs={{0,4},{8,0},{16,8},{24,16},{28,24},{20,28},{12,20},{4,12},{1,5},{9... | collective-permute-start | bytes 393224 | tf_op jit(solution)/shard_map/ppermute | solution.py:478
  407.2 46.7 %collective-permute-start.31 = (bf16[344,1024]{1,0:T(8,128)(2,1)S(1)}, bf16[344,1024]{1,0:T(8,128)(2,1)S(1)}, u32[]{:S(2)}, u32[]{:S(2)}) collective-permute-start(bf16[344,1024]{1,0:T(8,128)(2,1)S(1)} %slice_bitcast_fusion.6), channel_id=1, source_target_pairs={{0,2},{2,0},{1,3},{3,1},{4,6},{6,4},{5,7},{7,5},{8,10},{10,8},{9,1... | collective-permute-start | bytes 2113544 | tf_op jit(solution)/shard_map/ppermute | solution.py:441
  473.3 13.8 %collective-permute-start.35 = (bf16[128,896]{1,0:T(8,128)(2,1)S(1)}, bf16[128,896]{1,0:T(8,128)(2,1)S(1)}, u32[]{:S(2)}, u32[]{:S(2)}) collective-permute-start(bf16[128,896]{1,0:T(8,128)(2,1)S(1)} %get-tuple-element.181), channel_id=1, source_target_pairs={{0,8},{8,16},{16,24},{24,28},{28,20},{20,12},{12,4},{4,0},{1,9},{9... | collective-permute-start | bytes 688136 | tf_op jit(solution)/shard_map/ppermute | solution.py:478
  474.4 23.4 %collective-permute-start.51 = (bf16[64,1024]{1,0:T(8,128)(2,1)S(1)}, bf16[64,1024]{1,0:T(8,128)(2,1)S(1)}, u32[]{:S(2)}, u32[]{:S(2)}) collective-permute-start(bf16[64,1024]{1,0:T(8,128)(2,1)S(1)} %fusion.53), channel_id=1, source_target_pairs={{0,2},{2,0},{1,3},{3,1},{4,6},{6,4},{5,7},{7,5},{8,10},{10,8},{9,1... | collective-permute-start | bytes 393224 | tf_op jit(solution)/shard_map/ppermute | solution.py:441
  477.6 10.9 %collective-permute-start.39 = (bf16[128,896]{1,0:T(8,128)(2,1)S(1)}, bf16[128,896]{1,0:T(8,128)(2,1)S(1)}, u32[]{:S(2)}, u32[]{:S(2)}) collective-permute-start(bf16[128,896]{1,0:T(8,128)(2,1)S(1)} %get-tuple-element.182), channel_id=1, source_target_pairs={{0,4},{8,0},{16,8},{24,16},{28,24},{20,28},{12,20},{4,12},{1,5},{9... | collective-permute-start | bytes 688136 | tf_op jit(solution)/shard_map/ppermute | solution.py:478
  488.4 27.4 %collective-permute-start.33 = (bf16[2,344,1024]{2,1,0:T(8,128)(2,1)S(1)}, bf16[2,344,1024]{2,1,0:T(8,128)(2,1)S(1)}, u32[]{:S(2)}, u32[]{:S(2)}) collective-permute-start(bf16[2,344,1024]{2,1,0:T(8,128)(2,1)S(1)} %slice_bitcast_fusion), channel_id=1, source_target_pairs={{0,1},{1,0},{2,3},{3,2},{4,5},{5,4},{6,7},{7,6},{8,9},{9,8},{10,11... | collective-permute-start | bytes 4227080 | tf_op jit(solution)/shard_map/ppermute | solution.py:463
  516.5 18.4 %collective-permute-start.34 = (bf16[344,1024]{1,0:T(8,128)(2,1)S(1)}, bf16[344,1024]{1,0:T(8,128)(2,1)}, u32[]{:S(2)}, u32[]{:S(2)}) collective-permute-start(bf16[344,1024]{1,0:T(8,128)(2,1)S(1)} %slice_bitcast_fusion.4), channel_id=1, source_target_pairs={{0,2},{2,0},{1,3},{3,1},{4,6},{6,4},{5,7},{7,5},{8,10},{10,8},{9,1... | collective-permute-start | bytes 2113544 | tf_op jit(solution)/shard_map/ppermute | solution.py:441
  539.4 25.1 %collective-permute-start.54 = (bf16[2,256,1024]{2,1,0:T(8,128)(2,1)}, bf16[2,256,1024]{2,1,0:T(8,128)(2,1)}, u32[]{:S(2)}, u32[]{:S(2)}) collective-permute-start(bf16[2,256,1024]{2,1,0:T(8,128)(2,1)} %get-tuple-element.191), channel_id=1, source_target_pairs={{0,2},{2,0},{1,3},{3,1},{4,6},{6,4},{5,7},{7,5},{8,10},{10,8},{9,1... | collective-permute-start | bytes 3145736 | tf_op jit(solution)/shard_map/ppermute | solution.py:441
  (96 other events, 958.5 us)
Sparse Core Ops, SparseCore 0:
  53.7 127.7 all-gather.1
  275.7 212.5 reduce-scatter.1

commit v4 on v2

--- a/solution.py
+++ b/solution.py
@@ -262,14 +262,14 @@
     )(limits, triple, triple, triple, attended, grad, logs)
 
 
-def project_kernel(rows_ref, gain_ref, shift_ref, weight_ref, bias_ref, normed_ref, triple_ref):
+def project_kernel(rows_ref, small_ref, weight_ref, bias_ref, normed_ref, triple_ref):
     normal, _ = normalize(rows_ref[0].astype(F32))
-    normed = (normal * gain_ref[...] + shift_ref[...]).astype(BF)
+    normed = (normal * small_ref[0:1, :] + small_ref[1:2, :]).astype(BF)
     normed_ref[0] = normed
     triple_ref[0] = (dot(normed, weight_ref[...]) + bias_ref[...]).astype(BF)
 
 
-def project(tokens, gain, shift, weight, bias):
+def project(tokens, small, weight, bias):
     pieces, rows, width = tokens.shape
     columns = weight.shape[1]
 
@@ -282,7 +282,7 @@
     return pl.pallas_call(
         project_kernel,
         grid=(pieces,),
-        in_specs=[piece(width), whole(gain), whole(shift), whole(weight), whole(bias)],
+        in_specs=[piece(width), whole(small), whole(weight), whole(bias)],
         out_specs=[piece(width), piece(columns)],
         out_shape=[
             jax.ShapeDtypeStruct((pieces, rows, width), BF),
@@ -295,7 +295,7 @@
             transcendentals=0,
         ),
         name="project",
-    )(tokens, gain, shift, weight, bias)
+    )(tokens, small, weight, bias)
 
 
 def project_back_kernel(grad_ref, rows_ref, weight_ref, part_ref, gain_ref, shift_ref, total_ref):
@@ -390,6 +390,83 @@
     )(rows, weight, bias)
 
 
+def feed_grads_kernel(*refs):
+    groups = (len(refs) - 1) // 4
+    out_ref = refs[-1]
+    devices, height, _ = out_ref.shape
+    for half, (lefts, rights) in enumerate(
+        ((refs[:groups], refs[groups : 2 * groups]),
+         (refs[2 * groups : 3 * groups], refs[3 * groups : 4 * groups]))
+    ):
+        total = None
+        for left, right in zip(lefts, rights):
+            part = dot_left_t(left[...], right[...])
+            total = part if total is None else total + part
+        part = height // 2
+        for device in range(devices):
+            out_ref[device, half * part : (half + 1) * part, :] = total[
+                device * part : (device + 1) * part
+            ].astype(BF)
+
+
+def feed_grads(rows, grad_expanded, active, grad_feed, devices):
+    groups = len(rows)
+    count, width = rows[0].shape
+    shard = width // devices
+    side = pl.BlockSpec((count, 2 * shard), lambda i: (0, i))
+    whole = pl.BlockSpec((count, width), lambda i: (0, 0))
+    return pl.pallas_call(
+        feed_grads_kernel,
+        grid=(devices // 2,),
+        in_specs=[side] * groups + [whole] * groups + [side] * groups + [whole] * groups,
+        out_specs=pl.BlockSpec((2, 2 * shard, width), lambda i: (i, 0, 0)),
+        out_shape=jax.ShapeDtypeStruct((devices, 2 * shard, width), BF),
+        compiler_params=pltpu.CompilerParams(vmem_limit_bytes=52 * 2**20),
+        cost_estimate=pl.CostEstimate(
+            flops=4 * groups * count * width * width,
+            bytes_accessed=8 * groups * count * width + 4 * width * width,
+            transcendentals=0,
+        ),
+        name="feed_grads",
+    )(*rows, *grad_expanded, *active, *grad_feed)
+
+
+def assemble_kernel(order_ref, *refs):
+    count = len(refs) - 3
+    triple_ref, small_ref, output_ref = refs[count:]
+    first, second = triple_ref.shape[2], small_ref.shape[2]
+    _, half, width = output_ref.shape
+    for piece in range(count):
+        ref = refs[piece]
+        place = order_ref[0, piece]
+        triple_ref[place] = ref[:, :first]
+        small_ref[place] = ref[:, first : first + second]
+        place = order_ref[1, piece]
+        for side in range(2):
+            output_ref[place, :, side * (width // 2) : (side + 1) * (width // 2)] = ref[
+                side * half : (side + 1) * half, first + second :
+            ]
+
+
+def assemble(order, pieces, first, second):
+    count = len(pieces)
+    shard, columns = pieces[0].shape
+    width = 2 * (columns - first - second)
+    shapes = [(count, shard, first), (count, shard, second), (count, shard // 2, width)]
+    return pl.pallas_call(
+        assemble_kernel,
+        grid_spec=pltpu.PrefetchScalarGridSpec(
+            num_scalar_prefetch=1,
+            grid=(1,),
+            in_specs=[pl.BlockSpec((shard, columns), lambda i, order: (0, 0))] * count,
+            out_specs=[pl.BlockSpec(shape, lambda i, order: (0, 0, 0)) for shape in shapes],
+        ),
+        out_shape=[jax.ShapeDtypeStruct(shape, BF) for shape in shapes],
+        compiler_params=pltpu.CompilerParams(vmem_limit_bytes=40 * 2**20),
+        name="assemble",
+    )(order, *pieces)
+
+
 def far_send(array, shift):
     count = lax.axis_size("far")
     return lax.ppermute(array, "far", [(i, (i + shift) % count) for i in range(count)])
@@ -408,11 +485,6 @@
     return out
 
 
-def far_sum(slots):
-    arrived = far_exchange(slots)
-    return sum(part.astype(F32) for part in arrived)
-
-
 def other_core(array):
     return lax.ppermute(array, "core", [(0, 1), (1, 0)])
 
@@ -441,16 +513,17 @@
 
 def ring_gather(array):
     count = lax.axis_size("fsdp")
-    out = jnp.zeros((count,) + array.shape, array.dtype)
-    out = lax.dynamic_update_index_in_dim(out, array, ring_index(0), 0)
+    pieces, places = [array], [ring_index(0)]
     up = down = array
     for step in range(1, count // 2 + 1):
         up = ring_send(up, 1)
-        out = lax.dynamic_update_index_in_dim(out, up, ring_index(-step), 0)
+        pieces.append(up)
+        places.append(ring_index(-step))
         if step <= (count - 1) // 2:
             down = ring_send(down, -1)
-            out = lax.dynamic_update_index_in_dim(out, down, ring_index(step), 0)
-    return out
+            pieces.append(down)
+            places.append(ring_index(step))
+    return lax.optimization_barrier(pieces), jnp.stack(places)
 
 
 def ring_scatter(array):
@@ -468,6 +541,10 @@
                 moving = moving + block(direction * (hops - step))
         total = total + moving
     return total
+
+
+def after(array, *earlier):
+    return lax.optimization_barrier((array,) + earlier)[0]
 
 
 def core_join(mine, axis, core):
@@ -501,10 +578,10 @@
     own_rows = image_count * local_len
     far_count, fsdp_count = lax.axis_size("far"), lax.axis_size("fsdp")
     far, core = lax.axis_index("far"), lax.axis_index("core")
-    seq_count = 2 * far_count
+    seq_count, seq = 2 * far_count, 2 * far + core
     shard = width // fsdp_count
     units = expand_weight.shape[1]
-    unit_part = units // (2 * fsdp_count)
+    unit_part = units // (seq_count * fsdp_count)
     near_heads = width // HEAD_DIM // seq_count
     head_width = near_heads * HEAD_DIM
 
@@ -517,52 +594,70 @@
         array = lax.dynamic_index_in_dim(array, core, axis + 1, False)
         return array.reshape(shape[:axis] + (head_width,) + shape[axis + 1 :])
 
+    def my_units(array, axis):
+        shape = array.shape
+        array = array.reshape(
+            shape[:axis] + (-1, seq_count, unit_part) + shape[axis + 1 :]
+        )
+        array = lax.dynamic_index_in_dim(array, seq, axis + 1, False)
+        return array.reshape(shape[:axis] + (-1,) + shape[axis + 1 :])
+
     triple_mine = my_heads(triple_weight.reshape(shard, 3, width), 2).reshape(shard, 3 * head_width)
-    bias_mine = lax.dynamic_index_in_dim(expand_bias.reshape(2, unit_part), core, 0, False)
-    bias_columns = unit_part // shard
+    triple_mine = jnp.pad(triple_mine, ((0, 0), (0, -(3 * head_width) % 128)))
     vectors = [
         first_gain, first_shift, query_bias, value_bias, output_bias, attend_scale,
         second_gain, second_shift, reduce_bias, feed_scale,
     ]
     vector_count = len(vectors)
-    packed = jnp.concatenate(
-        [triple_mine, jnp.stack(vectors, 1), bias_mine.reshape(shard, bias_columns)], 1
-    )
-    packed = jnp.pad(packed, ((0, 0), (0, -packed.shape[1] % 128)))
-    packed = ring_gather(packed).reshape(width, -1)
-    triple_whole = packed[:, : 3 * head_width]
-    small = packed[:, 3 * head_width : 3 * head_width + vector_count + bias_columns]
-    small = small.astype(F32).T
+    bias_columns = units // width
+    small_mine = jnp.concatenate(
+        [jnp.stack(vectors, 1), expand_bias.reshape(shard, bias_columns)], 1
+    )
+    small_mine = jnp.pad(small_mine, ((0, 0), (0, -small_mine.shape[1] % 128)))
+    split_output = shard % (2 * HEAD_DIM) == 0
+    if split_output:
+        output_mine = lax.dynamic_index_in_dim(
+            output_weight.reshape(shard // (2 * HEAD_DIM), 2, HEAD_DIM, width), core, 1, False
+        ).reshape(shard // 2, 2, width // 2)
+        output_mine = output_mine.transpose(1, 0, 2).reshape(shard, width // 2)
+    else:
+        output_mine = jnp.zeros((shard, 128), BF)
+    pieces, places = ring_gather(jnp.concatenate([triple_mine, small_mine, output_mine], 1))
+    rolled = (places - far * (fsdp_count // far_count)) % fsdp_count
+    triple_whole, small, output_whole = assemble(
+        jnp.stack([places, rolled]).astype(jnp.int32),
+        pieces, triple_mine.shape[1], small_mine.shape[1],
+    )
+    triple_whole = triple_whole.reshape(width, -1)[:, : 3 * head_width]
+    small = small.reshape(width, -1)[:, :16].astype(F32).T
     (gain_1, shift_1, bias_q, bias_v, bias_o, scale_a, gain_2, shift_2, bias_r, scale_f) = [
         small[i] for i in range(vector_count)
     ]
     bias_e = (
-        small[vector_count:]
+        small[vector_count : vector_count + bias_columns]
         .reshape(bias_columns, fsdp_count, shard)
         .transpose(1, 2, 0)
-        .reshape(1, fsdp_count * unit_part)
-    )
-
-    split_output = shard % (2 * HEAD_DIM) == 0
+        .reshape(units)
+    )
+    bias_e = my_units(bias_e, 0)[None]
     if split_output:
-        output_mine = lax.dynamic_index_in_dim(
-            output_weight.reshape(shard // (2 * HEAD_DIM), 2, HEAD_DIM, width), core, 1, False
-        ).reshape(shard // 2, width)
-        output_whole = ring_gather(output_mine)
+        output_whole = output_whole.reshape(width // 2, width)
     else:
         output_whole = lax.dynamic_index_in_dim(
             fsdp_gather(output_weight).reshape(-1, 2, HEAD_DIM, width), core, 1, False
         )
-    output_whole = output_whole.reshape(far_count, head_width, width)
-    output_whole = jnp.roll(output_whole, -far, 0).reshape(width // 2, width)
-    expand_mine = lax.dynamic_index_in_dim(
-        expand_weight.reshape(shard, fsdp_count, 2, unit_part), core, 2, False
-    ).reshape(shard, units // 2)
-    expand_whole = fsdp_gather(expand_mine)
-    reduce_mine = lax.dynamic_index_in_dim(
-        reduce_weight.reshape(2, unit_part, width), core, 0, False
-    )
-    reduce_whole = fsdp_gather(reduce_mine)
+        output_whole = output_whole.reshape(far_count, head_width, width)
+        output_whole = jnp.roll(output_whole, -far, 0).reshape(width // 2, width)
+    expand_mine = my_units(expand_weight, 1)
+    reduce_mine = my_units(reduce_weight, 0)
+    joined = units // seq_count == width and shard % 128 == 0
+    if joined:
+        feed_mine = after(jnp.concatenate([expand_mine, reduce_mine], 0), *pieces)
+        feed_weights = fsdp_gather(feed_mine).reshape(fsdp_count, 2, shard, width)
+        expand_whole = feed_weights[:, 0].reshape(width, width)
+        reduce_whole = feed_weights[:, 1].reshape(width, width)
+    else:
+        expand_whole, reduce_whole = fsdp_gather(expand_mine), fsdp_gather(reduce_mine)
 
     groups = 2 if image_count % 2 == 0 else 1
     group_images = image_count // groups
@@ -570,16 +665,30 @@
     joint_bias = jnp.concatenate(
         [my_heads(bias_q, 0), jnp.zeros((head_width,), F32), my_heads(bias_v, 0)]
     )
+
+    def group_rows(array, group):
+        array = array[group * group_images : (group + 1) * group_images]
+        return array.reshape(rows, width)
+
+    def seq_gather(array):
+        slots = []
+        for slot in far_gather(array):
+            slots += [slot, other_core(slot)]
+        return jnp.stack(slots, 0)
+
+    def seq_reduce(array):
+        array = array.reshape(far_count, 2, rows, width)
+        array = array[:, 0].astype(F32) + other_core(array[:, 1].astype(BF)).astype(F32)
+        array = array.astype(BF)
+        return array, lambda array: far_exchange([array[r] for r in range(far_count)])
+
+    def total(arrays):
+        return sum(array.astype(F32) for array in arrays)
+
     tokens, normed, triples = [], [], []
     for group in range(groups):
-        mine = images[group * group_images : (group + 1) * group_images].reshape(rows, width)
-        slots = []
-        for slot in far_gather(mine):
-            slots += [slot, other_core(slot)]
-        tokens.append(jnp.stack(slots, 0))
-        first_normed, triple = project(
-            tokens[-1], gain_1[None], shift_1[None], triple_whole, joint_bias[None]
-        )
+        tokens.append(seq_gather(group_rows(images, group)))
+        first_normed, triple = project(tokens[-1], small, triple_whole, joint_bias[None])
         normed.append(first_normed)
         triples.append(triple)
 
@@ -611,6 +720,7 @@
         return array.reshape(seq_count, rows, parts * head_width)
 
     kernel_in, kernel_out, kernel_logs, attended_rows, branch_parts = [], [], [], [], []
+    residuals, normal_2, factor_2, second_normed, activated, slopes = [], [], [], [], [], []
     for group in range(groups):
         picked = limits[group * group_images : (group + 1) * group_images]
         kernel_in.append(to_kernel(triples[group]))
@@ -620,85 +730,99 @@
         attended = from_kernel(attended, 1).reshape(far_count, 2 * rows, head_width)
         attended = far_exchange([attended[r] for r in range(far_count)])
         attended_rows.append(jnp.concatenate(attended, 1))
-        branch = dot(attended_rows[-1], output_whole)
-        branch_parts.append(
-            branch[:rows] + other_core(branch[rows:].astype(BF)).astype(F32) + bias_o
+    for group in range(groups):
+        branch = dot(attended_rows[group], output_whole)
+        branch = branch[:rows] + other_core(branch[rows:].astype(BF)).astype(F32) + bias_o
+        branch_parts.append(branch)
+        residual = group_rows(images, group).astype(F32) + scale_a * branch
+        residuals.append(residual)
+        normal, factor = normalize(residual)
+        normal_2.append(normal)
+        factor_2.append(factor)
+        gathered = seq_gather((normal * gain_2 + shift_2).astype(BF))
+        second_normed.append(gathered.reshape(seq_count * rows, width))
+    for group in range(groups):
+        active, slope = expand_rows(second_normed[group], expand_whole, bias_e)
+        activated.append(active)
+        slopes.append(slope)
+
+    grad_feed, grad_expanded, upper_parts, moved = [], [], [], ()
+    for group in range(groups):
+        both = group_rows(cotangent, group)
+        both = seq_gather(both).reshape(seq_count * rows, width)
+        grad_feed.append((scale_f * both.astype(F32)).astype(BF))
+    for group in range(groups):
+        grad = dot_right_t(grad_feed[group], reduce_whole) * slopes[group].astype(F32)
+        grad_expanded.append(grad.astype(BF))
+        partial, send = seq_reduce(
+            dot_right_t(grad_expanded[group], expand_whole).reshape(seq_count, rows, width)
         )
-    branch_attend = jnp.concatenate(branch_parts, 0)
-    inputs = images.reshape(own_rows, width).astype(F32)
-    residual = inputs + scale_a * branch_attend
-    normal_2, factor_2 = normalize(residual)
-    second_mine = (normal_2 * gain_2 + shift_2).astype(BF)
-    second_normed = jnp.concatenate([second_mine, other_core(second_mine)], 0)
-    activated, slope = expand_rows(second_normed, expand_whole, bias_e)
-    branch = dot(activated, reduce_whole)
-    branch_feed = (
-        branch[:own_rows] + other_core(branch[own_rows:].astype(BF)).astype(F32) + bias_r
-    )
-    outputs = residual + scale_f * branch_feed
-
-    cotangent = cotangent.reshape(own_rows, width)
-    upstream = cotangent.astype(F32)
-    both = jnp.concatenate([cotangent, other_core(cotangent)], 0)
-    grad_feed = (scale_f * both.astype(F32)).astype(BF)
-    grad_feed_scale = jnp.sum(upstream * branch_feed, 0)
-    grad_reduce_bias = column_total(grad_feed[:own_rows])
-    grad_reduce_weight = dot_left_t(activated, grad_feed).astype(BF)
-    grad_expanded = (dot_right_t(grad_feed, reduce_whole) * slope.astype(F32)).astype(BF)
-    grad_expanded, grad_reduce_weight = lax.optimization_barrier(
-        (grad_expanded, grad_reduce_weight)
-    )
-    grad_reduce_weight = fsdp_scatter(grad_reduce_weight)
-    grad_expand_bias = column_total(grad_expanded)
-    grad_expand_weight = dot_left_t(second_normed, grad_expanded).astype(BF)
-    grad_expanded, grad_expand_weight = lax.optimization_barrier(
-        (grad_expanded, grad_expand_weight)
-    )
-    grad_expand_weight = fsdp_scatter(grad_expand_weight)
-    partial = dot_right_t(grad_expanded, expand_whole)
-    upper = partial[:own_rows] + other_core(partial[own_rows:].astype(BF)).astype(F32)
-    grad_second_gain = jnp.sum(upper * normal_2, 0)
-    grad_second_shift = jnp.sum(upper, 0)
-    grad_residual = upstream + normalize_back(normal_2, factor_2, upper * gain_2)
-    grad_attend_scale = jnp.sum(grad_residual * branch_attend, 0)
-    grad_attend = (scale_a * grad_residual).astype(BF)
-    grad_output_bias = column_total(grad_attend)
-    grad_attend = jnp.concatenate([grad_attend, other_core(grad_attend)], 0)
-    grad_attended = dot_right_t(grad_attend, output_whole).astype(BF)
-    grad_attended = grad_attended.reshape(2, groups, rows, far_count, head_width)
-    grad_sides = grad_attend.reshape(2, groups, rows, width)
+        moved = send(partial)
+        upper_parts.append(total(moved))
+    grad_expand_bias = sum(column_total(grad) for grad in grad_expanded)
+    if joined:
+        feed_sums = feed_grads(second_normed, grad_expanded, activated, grad_feed, fsdp_count)
+        feed_sums = feed_sums.reshape(2 * width, width)
+        upper_parts = [after(part, feed_sums) for part in upper_parts]
+        feed_sums = fsdp_scatter(feed_sums).reshape(2, shard, width)
+        expand_sums, reduce_sums = feed_sums[0], feed_sums[1]
+    else:
+        expand_sums = sum(dot_left_t(a, b) for a, b in zip(second_normed, grad_expanded))
+        reduce_sums = sum(dot_left_t(a, b) for a, b in zip(activated, grad_feed))
+        expand_sums = fsdp_scatter(expand_sums.astype(BF))
+        reduce_sums = fsdp_scatter(reduce_sums.astype(BF))
+
+    outputs, grad_feed_scale, grad_reduce_bias = [], 0.0, 0.0
+    for group in range(groups):
+        branch = dot(activated[group], reduce_whole).reshape(seq_count, rows, width)
+        partial, send = seq_reduce(after(branch, *moved))
+        branch = total(send(partial)) + bias_r
+        outputs.append(residuals[group] + scale_f * branch)
+        upstream = group_rows(cotangent, group).astype(F32)
+        grad_feed_scale = grad_feed_scale + jnp.sum(upstream * branch, 0)
+        grad_reduce_bias = grad_reduce_bias + column_total(grad_feed[group][:rows])
+    outputs = jnp.concatenate(outputs, 0)
+
+    grad_second_gain = grad_second_shift = grad_attend_scale = grad_output_bias = 0.0
+    grad_residual, grad_sides, grad_attended = [], [], []
+    for group in range(groups):
+        upper = upper_parts[group]
+        grad_second_gain = grad_second_gain + jnp.sum(upper * normal_2[group], 0)
+        grad_second_shift = grad_second_shift + jnp.sum(upper, 0)
+        grad = normalize_back(normal_2[group], factor_2[group], upper * gain_2)
+        grad = group_rows(cotangent, group).astype(F32) + grad
+        grad_residual.append(grad)
+        grad_attend_scale = grad_attend_scale + jnp.sum(grad * branch_parts[group], 0)
+        grad = (scale_a * grad).astype(BF)
+        grad_output_bias = grad_output_bias + column_total(grad)
+        grad_sides.append(jnp.concatenate([grad, other_core(grad)], 0))
+        grad = dot_right_t(grad_sides[group], output_whole).astype(BF)
+        grad_attended.append(
+            [grad[:, r * head_width : (r + 1) * head_width] for r in range(far_count)]
+        )
     grad_output_weight = sum(
-        dot_left_t(attended_rows[group], grad_sides[:, group].reshape(2 * rows, width))
-        for group in range(groups)
+        dot_left_t(attended_rows[group], grad_sides[group]) for group in range(groups)
     ).astype(BF)
     grad_output_weight = jnp.roll(
         grad_output_weight.reshape(far_count, head_width, width), far, 0
     ).reshape(width // 2, width)
 
-    grad_heads = [
-        to_kernel(
-            jnp.stack(
-                far_exchange(
-                    [
-                        grad_attended[:, group, :, r].reshape(2 * rows, head_width)
-                        for r in range(far_count)
-                    ]
-                ),
-                0,
-            )
-        )
-        for group in range(groups)
-    ]
+    grad_heads = [to_kernel(jnp.stack(far_exchange(parts), 0)) for parts in grad_attended]
     upper_parts, grad_triples = [], []
     grad_first_gain = grad_first_shift = column_sums = 0.0
     for group in range(groups):
         picked = limits[group * group_images : (group + 1) * group_images]
+        grad_heads_in = grad_heads[group]
+        if group > 0:
+            grad_heads_in = after(grad_heads_in, partial)
         grad_triple = from_kernel(
             attend_backward(
-                kernel_in[group], kernel_out[group], grad_heads[group], kernel_logs[group], picked
+                kernel_in[group], kernel_out[group], grad_heads_in, kernel_logs[group], picked
             ),
             3,
         )
+        if group > 0:
+            grad_triple = after(grad_triple, *moved)
         grad_triples.append(grad_triple)
         partial, gain_part, shift_part, total_part = project_back(
             grad_triple, tokens[group], triple_whole
@@ -706,10 +830,9 @@
         grad_first_gain = grad_first_gain + gain_part[0]
         grad_first_shift = grad_first_shift + shift_part[0]
         column_sums = column_sums + total_part[0]
-        partial = partial.reshape(far_count, 2, rows, width)
-        partial = partial[:, 0].astype(F32) + other_core(partial[:, 1]).astype(F32)
-        partial = partial.astype(BF)
-        upper_parts.append(far_sum([partial[r] for r in range(far_count)]))
+        partial, send = seq_reduce(partial)
+        moved = send(partial)
+        upper_parts.append(total(moved))
     grad_triple_weight = sum(
         dot_left_t(
             normed[group].reshape(seq_count * rows, width),
@@ -717,9 +840,13 @@
         )
         for group in range(groups)
     ).astype(BF)
-    upper = jnp.concatenate(upper_parts, 0)
-    normal, factor = normalize(inputs)
-    grad_images = grad_residual + normalize_back(normal, factor, upper * gain_1)
+    grad_images = []
+    for group in range(groups):
+        normal, factor = normalize(group_rows(images, group).astype(F32))
+        grad_images.append(
+            grad_residual[group] + normalize_back(normal, factor, upper_parts[group] * gain_1)
+        )
+    grad_images = jnp.concatenate(grad_images, 0)
 
     def place_heads(vector):
         here = jnp.arange(far_count)[:, None, None, None] == far
@@ -728,10 +855,10 @@
         return jnp.where(here, vector, 0.0).reshape(width)
 
     def place_units(vector):
-        vector = vector.reshape(fsdp_count, shard, bias_columns)
-        vector = vector.transpose(2, 0, 1).reshape(1, bias_columns, width)
-        vector = jnp.where(jnp.arange(2)[:, None, None] == core, vector, 0.0)
-        return [vector[i, j] for i in range(2) for j in range(bias_columns)]
+        here = jnp.arange(seq_count)[None, :, None] == seq
+        vector = jnp.where(here, vector.reshape(fsdp_count, 1, unit_part), 0.0)
+        vector = vector.reshape(width, bias_columns)
+        return [vector[:, i] for i in range(bias_columns)]
 
     sums = [
         grad_first_gain, grad_first_shift,
@@ -760,10 +887,7 @@
         return total
 
     if split_output:
-        grad_output_weight = ring_scatter(
-            grad_output_weight.reshape(fsdp_count, shard // 2, width)
-        ).astype(BF)
-        grad_output_weight = far_total(grad_output_weight).astype(BF)
+        grad_output_weight = far_total(fsdp_scatter(grad_output_weight)).astype(BF)
         grad_output_weight = core_join(
             grad_output_weight.reshape(-1, HEAD_DIM, width), 1, core
         ).reshape(shard, width)
@@ -773,18 +897,23 @@
         spread = fsdp_scatter(spread.reshape(width, width))
         grad_output_weight = far_total(spread)
         grad_output_weight = grad_output_weight + other_core(grad_output_weight)
-    grad_expand_weight = core_join(
-        far_total(grad_expand_weight).astype(BF).reshape(shard, fsdp_count, unit_part), 2, core
-    ).reshape(shard, units)
-    grad_reduce_weight = core_join(far_total(grad_reduce_weight).astype(BF), 0, core).reshape(
-        2 * unit_part, width
-    )
-    grad_expand_bias = (
-        sums[10 : 10 + 2 * bias_columns]
-        .reshape(2, bias_columns, shard)
-        .transpose(0, 2, 1)
-        .reshape(2 * unit_part)
-    )
+    def seq_join(array):
+        array = jnp.roll(jnp.stack(far_gather(array), 0), far, 0)
+        return core_join(array, 1, core)
+
+    feed_sums = seq_join(jnp.stack([expand_sums, reduce_sums]) if joined else expand_sums)
+    if joined:
+        expand_sums, reduce_sums = feed_sums[:, :, 0], feed_sums[:, :, 1]
+    else:
+        expand_sums, reduce_sums = feed_sums, seq_join(reduce_sums)
+    grad_expand_weight = (
+        expand_sums.astype(F32)
+        .reshape(seq_count, shard, fsdp_count, unit_part)
+        .transpose(1, 2, 0, 3)
+        .reshape(shard, units)
+    )
+    grad_reduce_weight = reduce_sums.astype(F32).reshape(seq_count * unit_part, width)
+    grad_expand_bias = sums[10 : 10 + bias_columns].T.reshape(units // fsdp_count)
     return (
         outputs.reshape(image_count, local_len, width).astype(BF),
         grad_images.reshape(image_count, local_len, width),
@@ -798,22 +927,310 @@
         sums[5],
         sums[6],
         sums[7],
-        grad_expand_weight.astype(F32),
+        grad_expand_weight,
         grad_expand_bias,
-        grad_reduce_weight.astype(F32),
+        grad_reduce_weight,
         sums[8],
         sums[9],
     )
 
 
+def layer_norm(inputs, gain, shift):
+    average = jnp.mean(inputs, -1, keepdims=True)
+    centered = inputs - average
+    variance = jnp.mean(centered * centered, -1, keepdims=True)
+    return centered * lax.rsqrt(variance + EPSILON) * gain + shift
+
+
+def exact_gelu(values):
+    return jax.nn.gelu(values, approximate=False)
+
+
+def to_float(array):
+    return array.astype(jnp.float32)
+
+
+def plain_matmul(left, right):
+    return jnp.dot(left, right, preferred_element_type=jnp.float32)
+
+
+def plain_matmul_left_t(left, right):
+    return lax.dot_general(
+        left, right, (((0,), (0,)), ((), ())), preferred_element_type=jnp.float32
+    )
+
+
+def plain_matmul_right_t(left, right):
+    return lax.dot_general(
+        left, right, (((1,), (1,)), ((), ())), preferred_element_type=jnp.float32
+    )
+
+
+def plain_column_total(array):
+    return plain_matmul(jnp.ones((1, array.shape[0]), jnp.bfloat16), array)[0]
+
+
+def masked_scores(queries, key_rows, live_count, factor):
+    scores = (
+        jnp.einsum("qhd,khd->hqk", queries, key_rows, preferred_element_type=jnp.float32) * factor
+    )
+    live_keys = lax.broadcasted_iota(jnp.int32, (1, 1, key_rows.shape[0]), 2) < live_count
+    return jnp.where(live_keys, scores, -1e30)
+
+
+def plain_attend_forward(bundle):
+    packed, live_count = bundle
+    length, triple_count, local_width = packed.shape
+    head_count = local_width // HEAD_DIM
+    unpacked = packed.reshape(length, triple_count, head_count, HEAD_DIM)
+    factor = HEAD_DIM ** (-0.5)
+    scores = masked_scores(unpacked[:, 0], unpacked[:, 1], live_count, factor)
+    highest = jnp.max(scores, -1, keepdims=True)
+    powers = jnp.exp(scores - highest)
+    row_total = jnp.sum(powers, -1, keepdims=True)
+    weights_low = (powers / row_total).astype(jnp.bfloat16)
+    mixed_rows = jnp.einsum(
+        "hqk,khd->qhd", weights_low, unpacked[:, 2], preferred_element_type=jnp.float32
+    )
+    logsum = highest + jnp.log(row_total)
+    return (mixed_rows.reshape(length, local_width).astype(jnp.bfloat16), logsum)
+
+
+def plain_attend_backward(bundle):
+    packed, grad_mixed, logsum, live_count = bundle
+    length, triple_count, local_width = packed.shape
+    head_count = local_width // HEAD_DIM
+    unpacked = packed.reshape(length, triple_count, head_count, HEAD_DIM)
+    factor = HEAD_DIM ** (-0.5)
+    scores = masked_scores(unpacked[:, 0], unpacked[:, 1], live_count, factor)
+    probs = jnp.exp(scores - logsum)
+    grad_heads = grad_mixed.reshape(length, head_count, HEAD_DIM)
+    grad_probs = jnp.einsum(
+        "qhd,khd->hqk", grad_heads, unpacked[:, 2], preferred_element_type=jnp.float32
+    )
+    grad_values = jnp.einsum(
+        "hqk,qhd->khd", probs.astype(jnp.bfloat16), grad_heads, preferred_element_type=jnp.float32
+    )
+    inner = jnp.sum(probs * grad_probs, -1, keepdims=True)
+    grad_scores = (probs * (grad_probs - inner)).astype(jnp.bfloat16)
+    grad_queries = (
+        jnp.einsum("hqk,khd->qhd", grad_scores, unpacked[:, 1], preferred_element_type=jnp.float32)
+        * factor
+    )
+    grad_keys = (
+        jnp.einsum("hqk,qhd->khd", grad_scores, unpacked[:, 0], preferred_element_type=jnp.float32)
+        * factor
+    )
+    stacked = jnp.stack([grad_queries, grad_keys, grad_values], 1)
+    return stacked.reshape(length, triple_count, local_width).astype(jnp.bfloat16)
+
+
+def plain_shards(
+    images,
+    cotangent,
+    valid_count,
+    first_gain,
+    first_shift,
+    triple_weight,
+    query_bias,
+    value_bias,
+    output_weight,
+    output_bias,
+    attend_scale,
+    second_gain,
+    second_shift,
+    expand_weight,
+    expand_bias,
+    reduce_weight,
+    reduce_bias,
+    feed_scale,
+):
+    image_count, local_len, width = images.shape
+    gathered = (
+        lax.all_gather(first_gain, "fsdp", axis=0, tiled=True),
+        lax.all_gather(first_shift, "fsdp", axis=0, tiled=True),
+        lax.all_gather(triple_weight, "fsdp", axis=0, tiled=True),
+        lax.all_gather(query_bias, "fsdp", axis=0, tiled=True),
+        lax.all_gather(value_bias, "fsdp", axis=0, tiled=True),
+        lax.all_gather(output_weight, "fsdp", axis=0, tiled=True),
+        lax.all_gather(output_bias, "fsdp", axis=0, tiled=True),
+        lax.all_gather(attend_scale, "fsdp", axis=0, tiled=True),
+        lax.all_gather(second_gain, "fsdp", axis=0, tiled=True),
+        lax.all_gather(second_shift, "fsdp", axis=0, tiled=True),
+        lax.all_gather(expand_weight, "fsdp", axis=0, tiled=True),
+        lax.all_gather(expand_bias, "fsdp", axis=0, tiled=True),
+        lax.all_gather(reduce_weight, "fsdp", axis=0, tiled=True),
+        lax.all_gather(reduce_bias, "fsdp", axis=0, tiled=True),
+        lax.all_gather(feed_scale, "fsdp", axis=0, tiled=True),
+    )
+    inputs = images.astype(jnp.float32).reshape(-1, width)
+    first_normed = layer_norm(inputs, to_float(gathered[0]), to_float(gathered[1])).astype(
+        jnp.bfloat16
+    )
+    joint_bias = to_float(jnp.concatenate([gathered[3], jnp.zeros_like(gathered[3]), gathered[4]]))
+    triple = (plain_matmul(first_normed, gathered[2]) + joint_bias).astype(jnp.bfloat16)
+    triple = triple.reshape(image_count, local_len, 3, width)
+    by_heads = lax.all_to_all(triple, "seq", split_axis=3, concat_axis=1, tiled=True)
+    attended, logsums = lax.map(plain_attend_forward, (by_heads, valid_count))
+    by_tokens = lax.all_to_all(attended, "seq", split_axis=1, concat_axis=2, tiled=True)
+    attended_rows = by_tokens.reshape(-1, width)
+    branch_attend = plain_matmul(attended_rows, gathered[5]) + to_float(gathered[6])
+    residual = inputs + to_float(gathered[7]) * branch_attend
+    second_normed = layer_norm(residual, to_float(gathered[8]), to_float(gathered[9])).astype(
+        jnp.bfloat16
+    )
+    expanded = plain_matmul(second_normed, gathered[10]) + to_float(gathered[11])
+    activated = exact_gelu(expanded).astype(jnp.bfloat16)
+    branch_feed = plain_matmul(activated, gathered[12]) + to_float(gathered[13])
+    outputs = residual + to_float(gathered[14]) * branch_feed
+    weights = (
+        lax.all_gather(first_gain, "fsdp", axis=0, tiled=True),
+        lax.all_gather(first_shift, "fsdp", axis=0, tiled=True),
+        lax.all_gather(triple_weight, "fsdp", axis=0, tiled=True),
+        lax.all_gather(query_bias, "fsdp", axis=0, tiled=True),
+        lax.all_gather(value_bias, "fsdp", axis=0, tiled=True),
+        lax.all_gather(output_weight, "fsdp", axis=0, tiled=True),
+        lax.all_gather(output_bias, "fsdp", axis=0, tiled=True),
+        lax.all_gather(attend_scale, "fsdp", axis=0, tiled=True),
+        lax.all_gather(second_gain, "fsdp", axis=0, tiled=True),
+        lax.all_gather(second_shift, "fsdp", axis=0, tiled=True),
+        lax.all_gather(expand_weight, "fsdp", axis=0, tiled=True),
+        lax.all_gather(expand_bias, "fsdp", axis=0, tiled=True),
+        lax.all_gather(reduce_weight, "fsdp", axis=0, tiled=True),
+        lax.all_gather(reduce_bias, "fsdp", axis=0, tiled=True),
+        lax.all_gather(feed_scale, "fsdp", axis=0, tiled=True),
+    )
+    upstream = cotangent.astype(jnp.float32).reshape(-1, width)
+    grad_feed_scale = jnp.sum(upstream * branch_feed, 0)
+    grad_feed = (to_float(weights[14]) * upstream).astype(jnp.bfloat16)
+    grad_reduce_bias = plain_column_total(grad_feed)
+    grad_reduce_weight = plain_matmul_left_t(activated, grad_feed)
+    grad_activated = plain_matmul_right_t(grad_feed, weights[12])
+    unused, gelu_pull = jax.vjp(exact_gelu, expanded)
+    grad_expanded = gelu_pull(grad_activated)[0].astype(jnp.bfloat16)
+    grad_expand_bias = plain_column_total(grad_expanded)
+    grad_expand_weight = plain_matmul_left_t(second_normed, grad_expanded)
+    grad_second_normed = plain_matmul_right_t(grad_expanded, weights[10])
+    unused, second_pull = jax.vjp(layer_norm, residual, to_float(weights[8]), to_float(weights[9]))
+    grad_residual_norm, grad_second_gain, grad_second_shift = second_pull(grad_second_normed)
+    grad_residual = upstream + grad_residual_norm
+    grad_attend_scale = jnp.sum(grad_residual * branch_attend, 0)
+    grad_attend = (to_float(weights[7]) * grad_residual).astype(jnp.bfloat16)
+    grad_output_bias = plain_column_total(grad_attend)
+    grad_output_weight = plain_matmul_left_t(attended_rows, grad_attend)
+    grad_attended = plain_matmul_right_t(grad_attend, weights[5]).astype(jnp.bfloat16)
+    grad_attended = grad_attended.reshape(image_count, local_len, width)
+    grad_by_heads = lax.all_to_all(grad_attended, "seq", split_axis=2, concat_axis=1, tiled=True)
+    grad_triple_heads = lax.map(plain_attend_backward, (by_heads, grad_by_heads, logsums, valid_count))
+    grad_triple = lax.all_to_all(grad_triple_heads, "seq", split_axis=1, concat_axis=3, tiled=True)
+    grad_triple = grad_triple.reshape(-1, 3 * width)
+    column_sums = plain_column_total(grad_triple)
+    grad_query_bias = column_sums[:width]
+    grad_value_bias = column_sums[2 * width :]
+    grad_triple_weight = plain_matmul_left_t(first_normed, grad_triple)
+    grad_first_normed = plain_matmul_right_t(grad_triple, weights[2])
+    unused, first_pull = jax.vjp(layer_norm, inputs, to_float(weights[0]), to_float(weights[1]))
+    grad_inputs_norm, grad_first_gain, grad_first_shift = first_pull(grad_first_normed)
+    grad_images = grad_residual + grad_inputs_norm
+    owned = (
+        lax.psum_scatter(
+            grad_first_gain.astype(jnp.bfloat16), "fsdp", scatter_dimension=0, tiled=True
+        ).astype(jnp.float32),
+        lax.psum_scatter(
+            grad_first_shift.astype(jnp.bfloat16), "fsdp", scatter_dimension=0, tiled=True
+        ).astype(jnp.float32),
+        lax.psum_scatter(
+            grad_triple_weight.astype(jnp.bfloat16), "fsdp", scatter_dimension=0, tiled=True
+        ).astype(jnp.float32),
+        lax.psum_scatter(
+            grad_query_bias.astype(jnp.bfloat16), "fsdp", scatter_dimension=0, tiled=True
+        ).astype(jnp.float32),
+        lax.psum_scatter(
+            grad_value_bias.astype(jnp.bfloat16), "fsdp", scatter_dimension=0, tiled=True
+        ).astype(jnp.float32),
+        lax.psum_scatter(
+            grad_output_weight.astype(jnp.bfloat16), "fsdp", scatter_dimension=0, tiled=True
+        ).astype(jnp.float32),
+        lax.psum_scatter(
+            grad_output_bias.astype(jnp.bfloat16), "fsdp", scatter_dimension=0, tiled=True
+        ).astype(jnp.float32),
+        lax.psum_scatter(
+            grad_attend_scale.astype(jnp.bfloat16), "fsdp", scatter_dimension=0, tiled=True
+        ).astype(jnp.float32),
+        lax.psum_scatter(
+            grad_second_gain.astype(jnp.bfloat16), "fsdp", scatter_dimension=0, tiled=True
+        ).astype(jnp.float32),
+        lax.psum_scatter(
+            grad_second_shift.astype(jnp.bfloat16), "fsdp", scatter_dimension=0, tiled=True
+        ).astype(jnp.float32),
+        lax.psum_scatter(
+            grad_expand_weight.astype(jnp.bfloat16), "fsdp", scatter_dimension=0, tiled=True
+        ).astype(jnp.float32),
+        lax.psum_scatter(
+            grad_expand_bias.astype(jnp.bfloat16), "fsdp", scatter_dimension=0, tiled=True
+        ).astype(jnp.float32),
+        lax.psum_scatter(
+            grad_reduce_weight.astype(jnp.bfloat16), "fsdp", scatter_dimension=0, tiled=True
+        ).astype(jnp.float32),
+        lax.psum_scatter(
+            grad_reduce_bias.astype(jnp.bfloat16), "fsdp", scatter_dimension=0, tiled=True
+        ).astype(jnp.float32),
+        lax.psum_scatter(
+            grad_feed_scale.astype(jnp.bfloat16), "fsdp", scatter_dimension=0, tiled=True
+        ).astype(jnp.float32),
+    )
+    summed = lax.psum(
+        (
+            owned[0],
+            owned[1],
+            owned[2],
+            owned[3],
+            owned[4],
+            owned[5],
+            owned[6],
+            owned[7],
+            owned[8],
+            owned[9],
+            owned[10],
+            owned[11],
+            owned[12],
+            owned[13],
+            owned[14],
+        ),
+        "seq",
+    )
+    return (
+        outputs.reshape(image_count, local_len, width).astype(jnp.bfloat16),
+        grad_images.reshape(image_count, local_len, width),
+        summed[0],
+        summed[1],
+        summed[2],
+        summed[3],
+        summed[4],
+        summed[5],
+        summed[6],
+        summed[7],
+        summed[8],
+        summed[9],
+        summed[10],
+        summed[11],
+        summed[12],
+        summed[13],
+        summed[14],
+    )
+
+
 def solution(mesh):
     fsdp, seq = mesh.devices.shape
-    split = Mesh(mesh.devices.reshape(fsdp, seq // 2, 2), ("fsdp", "far", "core"))
-    tokens = P("fsdp", ("far", "core"), None)
+    if seq == 4:
+        plan, tokens = shards, P("fsdp", ("far", "core"), None)
+        mesh = Mesh(mesh.devices.reshape(fsdp, 2, 2), ("fsdp", "far", "core"))
+    else:
+        plan, tokens = plain_shards, P("fsdp", "seq", None)
     row, matrix = P("fsdp"), P("fsdp", None)
     return jax.shard_map(
-        shards,
-        mesh=split,
+        plan,
+        mesh=mesh,
         in_specs=(
             tokens, tokens, row, row, row, matrix, row, row, matrix,
             row, row, row, row, matrix, row, matrix, row, row,

time: 579 us -> 610 us (1.054)
  Pallas kernels: 116 us -> 145 us
  other arithmetic: 60.4 us -> 87.8 us
  matrix products: 70.4 us -> 52.2 us
  starting transfers between devices: 60.5 us -> 50.4 us
    ppermute x12 -> x19, waiting for transfers between devices: 44.5 us -> 107 us  [far_send(): lax.ppermute(array, 'far', [(i, (i + shift) % count) for i in range(count)])]
    ppermute x28 -> x14, waiting for transfers between devices: 78.5 us -> 33.6 us  [ring_send(): return lax.ppermute(array, 'fsdp', pairs)]
    pallas_call x0 -> x2, Pallas kernels: none -> 22.4 us  [the longest x1 20.5 us: feed_grads(): pl.pallas_call(feed_grads_kernel, grid=(devices // 2,), in_specs=[side] *...]
    all_gather x2 -> x1, waiting for transfers between devices: 22.3 us -> 0.01 us  [fsdp_gather(): return lax.all_gather(array, 'fsdp', axis=0, tiled=True)]
    ppermute x28 -> x14, starting transfers between devices: 42.9 us -> 22.7 us  [ring_send(): return lax.ppermute(array, 'fsdp', pairs)]
    convert_element_type x10 -> x13, other arithmetic: 15.8 us -> 33.6 us  [the longest x4 20.4 us: shards(): grad_feed.append((scale_f * both.astype(F32)).astype(BF))]
    dot_general x6 -> x4, matrix products: 32.4 us -> 15 us  [dot_left_t(): lax.dot_general(left, right, (((0,), (0,)), ((), ())), preferred_element_...]
    unnamed x170 -> x246, local copies, waits for them, and re-layouts: 26.3 us -> 39.7 us
  transfers between devices with their start and end apart: 61 -> 61, of which waited for: 27 -> 24; matrix products, arithmetic and copies ran while one was open for 34% -> 28% of each run, Pallas kernels for 20% -> 20%
where the time goes in v4:
time: 610 us; the launch traced here: 603 us
  Pallas kernels  145 us (24%)
  waiting for transfers between devices  144 us (24%)
  local copies, waits for them, and re-layouts  108 us (18%)
  other arithmetic  87.8 us (14%)
  matrix products  52.2 us (9%)
  starting transfers between devices  50.4 us (8%)
  between operations  15.8 us (3%)
    ppermute x19, waiting for transfers between devices, far_send(): lax.ppermute(array, 'far', [(i, (i + shift) % count) for i in range(count)])  107 us
    pallas_call x2, Pallas kernels, attend_backward(): pl.pallas_call(attend_backward_kernel, grid_spec=pltpu.PrefetchScalarGrid...  50.9 us
    unnamed x246, local copies, waits for them, and re-layouts  39.7 us
    ppermute x14, waiting for transfers between devices, ring_send(): return lax.ppermute(array, 'fsdp', pairs)  33.6 us
    pallas_call x2, Pallas kernels, attend_forward(): pl.pallas_call(attend_forward_kernel, grid_spec=pltpu.PrefetchScalarGridS...  29.8 us
    pallas_call x2, Pallas kernels, expand_rows(): pl.pallas_call(expand_kernel, grid=(units // tile,), in_specs=[pl.BlockSp...  25.4 us
    ppermute x19, starting transfers between devices, far_send(): lax.ppermute(array, 'far', [(i, (i + shift) % count) for i in range(count)])  22.7 us
    ppermute x14, starting transfers between devices, ring_send(): return lax.ppermute(array, 'fsdp', pairs)  22.7 us
  transfers between devices with their start and end apart: 61, of which 24 were waited for; matrix products, arithmetic and copies ran while one was open for 28% of the time, Pallas kernels for 20%

profile of v4, /device:TPU:0, one launch (start us, length us, event | category | flops | bytes accessed | tf_op | source)
XLA Modules:
  0.0 603.0 jit_solution(10839279622298094789)
XLA Ops:
  34.3 10.3 %collective-permute-done.8 = bf16[344,1024]{1,0:T(8,128)(2,1)} collective-permute-done((bf16[344,1024]{1,0:T(8,128)(2,1)}, bf16[344,1024]{1,0:T(8,128)(2,1)}, u32[]{:S(2)}, u32[]{:S(2)}) %collective-permute-start.8) | collective-permute-done | bytes 704544 | tf_op jit(solution)/shard_map/ppermute | solution.py:472
  47.6 11.8 %collective-permute-done.19 = bf16[344,1024]{1,0:T(8,128)(2,1)} collective-permute-done((bf16[344,1024]{1,0:T(8,128)(2,1)}, bf16[344,1024]{1,0:T(8,128)(2,1)}, u32[]{:S(2)}, u32[]{:S(2)}) %collective-permute-start.19) | collective-permute-done | bytes 704544 | tf_op jit(solution)/shard_map/ppermute | solution.py:472
  67.2 5.0 collective-permute-done.4.refs_5_
  96.8 4.3 project.3
  104.0 14.7 %attend_forward.3 = (bf16[4,1,344,256]{3,2,1,0:T(8,128)(2,1)S(1)}, f32[1,2,1376,128]{3,2,1,0:T(8,128)S(1)}) custom-call(s32[1,2]{1,0:T(1,128)S(1)} %get-tuple-element.289.limit_ref, bf16[4,1,344,768]{3,2,1,0:T(8,128)(2,1)} %bitcast.382, bf16[4,1,344,768]{3,2,1,0:T(8,128)(2,1)} %bitcast.383, bf16[4,1,344,768]{3,2,1,0:T(8,128)(2,1)} %bitcast.384), custom_call_target="tpu_custom_call" | custom-call | flops 7755268096 | bytes 4227072 | tf_op jit(solution)/shard_map/attend_forward/pallas_call | solution.py:202
  120.3 4.6 project.2
  126.3 15.1 %attend_forward.2 = (bf16[4,1,344,256]{3,2,1,0:T(8,128)(2,1)S(1)}, f32[1,2,1376,128]{3,2,1,0:T(8,128)S(1)}) custom-call(s32[1,2]{1,0:T(1,128)S(1)} %get-tuple-element.288.limit_ref, bf16[4,1,344,768]{3,2,1,0:T(8,128)(2,1)} %bitcast.388, bf16[4,1,344,768]{3,2,1,0:T(8,128)(2,1)} %bitcast.389, bf16[4,1,344,768]{3,2,1,0:T(8,128)(2,1)} %bitcast.390), custom_call_target="tpu_custom_call" | custom-call | flops 7755268096 | bytes 4227072 | tf_op jit(solution)/shard_map/attend_forward/pallas_call | solution.py:202
  152.7 4.6 maximum_convert_fusion
  157.3 4.5 maximum_convert_fusion.1
  172.9 6.5 %fusion = (bf16[1376,1024]{1,0:T(8,128)(2,1)}, bf16[1376,1024]{1,0:T(8,128)(2,1)}) fusion(f32[4,344,1024]{2,1,0:T(8,128)} %maximum_convert_fusion, f32[1024]{0:T(1024)S(1)} %bitcast.469, f32[4,344,1024]{2,1,0:T(8,128)S(1)} %copy-done.46), kind=kLoop, calls=%fused_computation.1 | loop fusion | flops 5636096 | bytes 16912384 | tf_op jit(solution)/shard_map/convert_element_type | solution.py:753
  179.4 10.3 %collective-permute-done.13 = bf16[344,1024]{1,0:T(8,128)(2,1)} collective-permute-done((bf16[344,1024]{1,0:T(8,128)(2,1)}, bf16[344,1024]{1,0:T(8,128)(2,1)}, u32[]{:S(2)}, u32[]{:S(2)}) %collective-permute-start.13) | collective-permute-done | bytes 704544 | tf_op jit(solution)/shard_map/ppermute | solution.py:472
  192.6 11.8 %collective-permute-done.24 = bf16[344,1024]{1,0:T(8,128)(2,1)} collective-permute-done((bf16[344,1024]{1,0:T(8,128)(2,1)}, bf16[344,1024]{1,0:T(8,128)(2,1)}, u32[]{:S(2)}, u32[]{:S(2)}) %collective-permute-start.24) | collective-permute-done | bytes 704544 | tf_op jit(solution)/shard_map/ppermute | solution.py:472
  204.4 4.8 multiply_convert_fusion.1
  215.2 6.4 %copy.257 = bf16[2048,1024]{1,0:T(8,128)(2,1)} copy(bf16[2048,1024]{0,1:T(8,128)(2,1)} %all-gather.2.cloned.1.call-done) | data formatting | bytes 8388608 | tf_op jit(solution)/shard_map/all_gather | solution.py:493
  224.3 12.2 %expand_rows.3 = (bf16[1376,1024]{1,0:T(8,128)(2,1)S(1)}, bf16[1376,1024]{1,0:T(8,128)(2,1)}) custom-call(bf16[1376,1024]{1,0:T(8,128)(2,1)} %bitcast.424, bf16[1024,1024]{1,0:T(8,128)(2,1)S(1)} %bitcast.364, f32[1,1024]{1,0:T(1,128)S(1)} %bitcast.369), custom_call_target="tpu_custom_call" | custom-call | flops 5771362304 | bytes 10551296 | tf_op jit(solution)/shard_map/expand_rows/pallas_call | solution.py:373
  236.5 13.2 %expand_rows.2 = (bf16[1376,1024]{1,0:T(8,128)(2,1)S(1)}, bf16[1376,1024]{1,0:T(8,128)(2,1)}) custom-call(bf16[1376,1024]{1,0:T(8,128)(2,1)} %bitcast.422, bf16[1024,1024]{1,0:T(8,128)(2,1)S(1)} %bitcast.365, f32[1,1024]{1,0:T(1,128)S(1)} %bitcast.370), custom_call_target="tpu_custom_call" | custom-call | flops 5771362304 | bytes 10551296 | tf_op jit(solution)/shard_map/expand_rows/pallas_call | solution.py:373
  249.7 5.7 multiply_convert_fusion.2.refs_3_
  282.4 12.4 %collective-permute-done.27 = bf16[344,1024]{1,0:T(8,128)(2,1)S(1)} collective-permute-done((bf16[344,1024]{1,0:T(8,128)(2,1)S(1)}, bf16[344,1024]{1,0:T(8,128)(2,1)S(1)}, u32[]{:S(2)}, u32[]{:S(2)}) %collective-permute-start.27) | collective-permute-done | bytes 704544 | tf_op jit(solution)/shard_map/ppermute | solution.py:472
  297.9 20.5 %feed_grads.1 = bf16[8,256,1024]{2,1,0:T(8,128)(2,1)} custom-call(bf16[1376,1024]{1,0:T(8,128)(2,1)} %bitcast.423, bf16[1376,1024]{1,0:T(8,128)(2,1)} %bitcast.425, bf16[1376,1024]{1,0:T(8,128)(2,1)} %copy-done.76, bf16[1376,1024]{1,0:T(8,128)(2,1)} %copy-done.74, bf16[1376,1024]{1,0:T(8,128)(2,1)} %copy-done.31, bf16[1376,1024]{1,0:T(8,128)(2,1)} %copy-done.30, ...), custom_call_target="tpu_custom_call" | custom-call | flops 11542724608 | bytes 26738688 | tf_op jit(solution)/shard_map/feed_grads/pallas_call | solution.py:418
  329.8 12.6 %collective-permute-done.31 = bf16[344,1024]{1,0:T(8,128)(2,1)S(1)} collective-permute-done((bf16[344,1024]{1,0:T(8,128)(2,1)S(1)}, bf16[344,1024]{1,0:T(8,128)(2,1)S(1)}, u32[]{:S(2)}, u32[]{:S(2)}) %collective-permute-start.31) | collective-permute-done | bytes 704544 | tf_op jit(solution)/shard_map/ppermute | solution.py:472
  342.4 14.1 %collective-permute-done.29 = bf16[344,1024]{1,0:T(8,128)(2,1)S(1)} collective-permute-done((bf16[344,1024]{1,0:T(8,128)(2,1)S(1)}, bf16[344,1024]{1,0:T(8,128)(2,1)S(1)}, u32[]{:S(2)}, u32[]{:S(2)}) %collective-permute-start.29) | collective-permute-done | bytes 704544 | tf_op jit(solution)/shard_map/ppermute | solution.py:472
  377.7 6.5 %copy.282 = bf16[2048,1024]{0,1:T(8,128)(2,1)} copy(bf16[2048,1024]{1,0:T(8,128)(2,1)} %bitcast.411) | data formatting | bytes 8388608 | tf_op jit(solution)/shard_map/reshape | solution.py:765
  399.8 5.0 collective-permute-done.38
  405.8 25.7 %attend_backward.2 = bf16[4,1,344,768]{3,2,1,0:T(8,128)(2,1)} custom-call(s32[1,2]{1,0:T(1,128)} %copy-done.19, bf16[4,1,344,768]{3,2,1,0:T(8,128)(2,1)} %bitcast.391, bf16[4,1,344,768]{3,2,1,0:T(8,128)(2,1)} %bitcast.392, bf16[4,1,344,768]{3,2,1,0:T(8,128)(2,1)} %bitcast.393, bf16[4,1,344,256]{3,2,1,0:T(8,128)(2,1)} %copy-done.7, ...), custom_call_target="tpu_custom_call" | custom-call | flops 19388170240 | bytes 8454144 | tf_op jit(solution)/shard_map/attend_backward/pallas_call | solution.py:236
  444.2 6.1 %collective-permute-done.42 = bf16[688,256]{1,0:T(8,128)(2,1)S(1)} collective-permute-done((bf16[688,256]{1,0:T(8,128)(2,1)S(1)}, bf16[688,256]{1,0:T(8,128)(2,1)S(1)}, u32[]{:S(2)}, u32[]{:S(2)}) %collective-permute-start.42) | collective-permute-done | bytes 352288 | tf_op jit(solution)/shard_map/ppermute | solution.py:472
  451.1 4.4 fusion.114
  459.6 25.2 %attend_backward.3 = bf16[4,1,344,768]{3,2,1,0:T(8,128)(2,1)} custom-call(s32[1,2]{1,0:T(1,128)} %copy-done.18, bf16[4,1,344,768]{3,2,1,0:T(8,128)(2,1)} %bitcast.385, bf16[4,1,344,768]{3,2,1,0:T(8,128)(2,1)} %bitcast.386, bf16[4,1,344,768]{3,2,1,0:T(8,128)(2,1)} %bitcast.387, bf16[4,1,344,256]{3,2,1,0:T(8,128)(2,1)} %copy-done.6, ...), custom_call_target="tpu_custom_call" | custom-call | flops 19388170240 | bytes 8454144 | tf_op jit(solution)/shard_map/attend_backward/pallas_call | solution.py:236
  496.8 6.0 fusion.3
  512.4 8.6 %collective-permute-done.45 = bf16[128,896]{1,0:T(8,128)(2,1)S(1)} collective-permute-done((bf16[128,896]{1,0:T(8,128)(2,1)S(1)}, bf16[128,896]{1,0:T(8,128)(2,1)S(1)}, u32[]{:S(2)}, u32[]{:S(2)}) %collective-permute-start.45) | collective-permute-done | bytes 229408 | tf_op jit(solution)/shard_map/ppermute | solution.py:504
  530.1 4.9 collective-permute-done.46
  540.7 6.1 %collective-permute-done.47 = bf16[128,896]{1,0:T(8,128)(2,1)S(1)} collective-permute-done((bf16[128,896]{1,0:T(8,128)(2,1)S(1)}, bf16[128,896]{1,0:T(8,128)(2,1)S(1)}, u32[]{:S(2)}, u32[]{:S(2)}) %collective-permute-start.47) | collective-permute-done | bytes 229408 | tf_op jit(solution)/shard_map/ppermute | solution.py:504
  577.8 4.6 collective-permute-done.44
  (541 shorter events, 278.8 us)
Async XLA Ops:
  7.2 208.0 %all-gather.2.cloned.1.call-start = ((), (), s32[]{:S(2)}) async-start(), calls=%async_computation.2 | async-start | bytes 4718592 | tf_op jit(solution)/shard_map/all_gather | solution.py:493
  25.6 21.5 %collective-permute-start.7 = (bf16[344,1024]{1,0:T(8,128)(2,1)}, bf16[344,1024]{1,0:T(8,128)(2,1)}, u32[]{:S(2)}, u32[]{:S(2)}) collective-permute-start(bf16[344,1024]{1,0:T(8,128)(2,1)} %get-tuple-element.250), channel_id=1, source_target_pairs={{0,1},{1,0},{2,3},{3,2},{4,5},{5,4},{6,7},{7,6},{8,9},{9,8},{10,11... | collective-permute-start | bytes 2113544 | tf_op jit(solution)/shard_map/ppermute | solution.py:489
  25.6 19.0 %collective-permute-start.8 = (bf16[344,1024]{1,0:T(8,128)(2,1)}, bf16[344,1024]{1,0:T(8,128)(2,1)}, u32[]{:S(2)}, u32[]{:S(2)}) collective-permute-start(bf16[344,1024]{1,0:T(8,128)(2,1)} %get-tuple-element.250), channel_id=1, source_target_pairs={{0,2},{2,0},{1,3},{3,1},{4,6},{6,4},{5,7},{7,5},{8,10},{10,8},{9,1... | collective-permute-start | bytes 2113544 | tf_op jit(solution)/shard_map/ppermute | solution.py:472
  27.5 31.9 %collective-permute-start.19 = (bf16[344,1024]{1,0:T(8,128)(2,1)}, bf16[344,1024]{1,0:T(8,128)(2,1)}, u32[]{:S(2)}, u32[]{:S(2)}) collective-permute-start(bf16[344,1024]{1,0:T(8,128)(2,1)} %get-tuple-element.251), channel_id=1, source_target_pairs={{0,2},{2,0},{1,3},{3,1},{4,6},{6,4},{5,7},{7,5},{8,10},{10,8},{9,1... | collective-permute-start | bytes 2113544 | tf_op jit(solution)/shard_map/ppermute | solution.py:472
  32.2 28.9 %collective-permute-start.3 = (bf16[128,1408]{1,0:T(8,128)(2,1)S(1)}, bf16[128,1408]{1,0:T(8,128)(2,1)}, u32[]{:S(2)}, u32[]{:S(2)}) collective-permute-start(bf16[128,1408]{1,0:T(8,128)(2,1)S(1)} %collective-permute-done.1.refs_2_), channel_id=1, source_target_pairs={{0,4},{8,0},{16,8},{24,16},{28,24},{20,28},{12,20},{4,12},{1,5},{9... | collective-permute-start | bytes 1081352 | tf_op jit(solution)/shard_map/ppermute | solution.py:504
  33.9 27.3 %collective-permute-start.2 = (bf16[128,1408]{1,0:T(8,128)(2,1)S(1)}, bf16[128,1408]{1,0:T(8,128)(2,1)S(1)}, u32[]{:S(2)}, u32[]{:S(2)}) collective-permute-start(bf16[128,1408]{1,0:T(8,128)(2,1)S(1)} %collective-permute-done.refs_1_), channel_id=1, source_target_pairs={{0,8},{8,16},{16,24},{24,28},{28,20},{20,12},{12,4},{4,0},{1,9},{9... | collective-permute-start | bytes 1081352 | tf_op jit(solution)/shard_map/ppermute | solution.py:504
  44.6 29.1 %collective-permute-start.9 = (bf16[344,1024]{1,0:T(8,128)(2,1)}, bf16[344,1024]{1,0:T(8,128)(2,1)}, u32[]{:S(2)}, u32[]{:S(2)}) collective-permute-start(bf16[344,1024]{1,0:T(8,128)(2,1)} %collective-permute-done.8), channel_id=1, source_target_pairs={{0,1},{1,0},{2,3},{3,2},{4,5},{5,4},{6,7},{7,6},{8,9},{9,8},{10,11... | collective-permute-start | bytes 2113544 | tf_op jit(solution)/shard_map/ppermute | solution.py:489
  47.1 30.2 %collective-permute-start.18 = (bf16[344,1024]{1,0:T(8,128)(2,1)}, bf16[344,1024]{1,0:T(8,128)(2,1)S(1)}, u32[]{:S(2)}, u32[]{:S(2)}) collective-permute-start(bf16[344,1024]{1,0:T(8,128)(2,1)} %get-tuple-element.251), channel_id=1, source_target_pairs={{0,1},{1,0},{2,3},{3,2},{4,5},{5,4},{6,7},{7,6},{8,9},{9,8},{10,11... | collective-permute-start | bytes 2113544 | tf_op jit(solution)/shard_map/ppermute | solution.py:489
  77.2 74.7 %collective-permute-start.15 = (bf16[344,1024]{1,0:T(8,128)(2,1)}, bf16[344,1024]{1,0:T(8,128)(2,1)}, u32[]{:S(2)}, u32[]{:S(2)}) collective-permute-start(bf16[344,1024]{1,0:T(8,128)(2,1)} %get-tuple-element.247), channel_id=1, source_target_pairs={{0,1},{1,0},{2,3},{3,2},{4,5},{5,4},{6,7},{7,6},{8,9},{9,8},{10,11... | collective-permute-start | bytes 2113544 | tf_op jit(solution)/shard_map/ppermute | solution.py:489
  77.3 66.3 %collective-permute-start.33 = (bf16[344,1024]{1,0:T(8,128)(2,1)}, bf16[344,1024]{1,0:T(8,128)(2,1)}, u32[]{:S(2)}, u32[]{:S(2)}) collective-permute-start(bf16[344,1024]{1,0:T(8,128)(2,1)} %get-tuple-element.246), channel_id=1, source_target_pairs={{0,2},{2,0},{1,3},{3,1},{4,6},{6,4},{5,7},{7,5},{8,10},{10,8},{9,1... | collective-permute-start | bytes 2113544 | tf_op jit(solution)/shard_map/ppermute | solution.py:472
  78.9 73.5 %collective-permute-start.17 = (bf16[344,1024]{1,0:T(8,128)(2,1)}, bf16[344,1024]{1,0:T(8,128)(2,1)}, u32[]{:S(2)}, u32[]{:S(2)}) collective-permute-start(bf16[344,1024]{1,0:T(8,128)(2,1)} %collective-permute-done.16), channel_id=1, source_target_pairs={{0,1},{1,0},{2,3},{3,2},{4,5},{5,4},{6,7},{7,6},{8,9},{9,8},{10,11... | collective-permute-start | bytes 2113544 | tf_op jit(solution)/shard_map/ppermute | solution.py:489
  84.5 400.3 %reduce-scatter.3.cloned.1.call-start = ((), (), s32[]{:S(2)}) async-start(), calls=%async_computation.3 | async-start | bytes 1179648 | tf_op jit(solution)/shard_map/reduce_scatter | solution.py:497
  119.7 23.9 %collective-permute-start.21 = (bf16[688,256]{1,0:T(8,128)(2,1)}, bf16[688,256]{1,0:T(8,128)(2,1)}, u32[]{:S(2)}, u32[]{:S(2)}) collective-permute-start(bf16[688,256]{1,0:T(8,128)(2,1)} %bitcast.77), channel_id=1, source_target_pairs={{0,2},{2,0},{1,3},{3,1},{4,6},{6,4},{5,7},{7,5},{8,10},{10,8},{9,1... | collective-permute-start | bytes 1056776 | tf_op jit(solution)/shard_map/ppermute | solution.py:472
  170.8 18.9 %collective-permute-start.13 = (bf16[344,1024]{1,0:T(8,128)(2,1)}, bf16[344,1024]{1,0:T(8,128)(2,1)}, u32[]{:S(2)}, u32[]{:S(2)}) collective-permute-start(bf16[344,1024]{1,0:T(8,128)(2,1)} %get-tuple-element.280), channel_id=1, source_target_pairs={{0,2},{2,0},{1,3},{3,1},{4,6},{6,4},{5,7},{7,5},{8,10},{10,8},{9,1... | collective-permute-start | bytes 2113544 | tf_op jit(solution)/shard_map/ppermute | solution.py:472
  172.4 32.0 %collective-permute-start.24 = (bf16[344,1024]{1,0:T(8,128)(2,1)}, bf16[344,1024]{1,0:T(8,128)(2,1)}, u32[]{:S(2)}, u32[]{:S(2)}) collective-permute-start(bf16[344,1024]{1,0:T(8,128)(2,1)} %get-tuple-element.281), channel_id=1, source_target_pairs={{0,2},{2,0},{1,3},{3,1},{4,6},{6,4},{5,7},{7,5},{8,10},{10,8},{9,1... | collective-permute-start | bytes 2113544 | tf_op jit(solution)/shard_map/ppermute | solution.py:472
  179.4 29.8 %collective-permute-start.12 = (bf16[344,1024]{1,0:T(8,128)(2,1)}, bf16[344,1024]{1,0:T(8,128)(2,1)}, u32[]{:S(2)}, u32[]{:S(2)}) collective-permute-start(bf16[344,1024]{1,0:T(8,128)(2,1)} %get-tuple-element.280), channel_id=1, source_target_pairs={{0,1},{1,0},{2,3},{3,2},{4,5},{5,4},{6,7},{7,6},{8,9},{9,8},{10,11... | collective-permute-start | bytes 2113544 | tf_op jit(solution)/shard_map/ppermute | solution.py:489
  189.7 19.5 %collective-permute-start.14 = (bf16[344,1024]{1,0:T(8,128)(2,1)}, bf16[344,1024]{1,0:T(8,128)(2,1)}, u32[]{:S(2)}, u32[]{:S(2)}) collective-permute-start(bf16[344,1024]{1,0:T(8,128)(2,1)} %collective-permute-done.13), channel_id=1, source_target_pairs={{0,1},{1,0},{2,3},{3,2},{4,5},{5,4},{6,7},{7,6},{8,9},{9,8},{10,11... | collective-permute-start | bytes 2113544 | tf_op jit(solution)/shard_map/ppermute | solution.py:489
  192.1 20.3 %collective-permute-start.23 = (bf16[344,1024]{1,0:T(8,128)(2,1)}, bf16[344,1024]{1,0:T(8,128)(2,1)S(1)}, u32[]{:S(2)}, u32[]{:S(2)}) collective-permute-start(bf16[344,1024]{1,0:T(8,128)(2,1)} %get-tuple-element.281), channel_id=1, source_target_pairs={{0,1},{1,0},{2,3},{3,2},{4,5},{5,4},{6,7},{7,6},{8,9},{9,8},{10,11... | collective-permute-start | bytes 2113544 | tf_op jit(solution)/shard_map/ppermute | solution.py:489
  276.1 18.7 %collective-permute-start.27 = (bf16[344,1024]{1,0:T(8,128)(2,1)S(1)}, bf16[344,1024]{1,0:T(8,128)(2,1)S(1)}, u32[]{:S(2)}, u32[]{:S(2)}) collective-permute-start(bf16[344,1024]{1,0:T(8,128)(2,1)S(1)} %slice_bitcast_fusion.16), channel_id=1, source_target_pairs={{0,2},{2,0},{1,3},{3,1},{4,6},{6,4},{5,7},{7,5},{8,10},{10,8},{9,1... | collective-permute-start | bytes 2113544 | tf_op jit(solution)/shard_map/ppermute | solution.py:472
  281.5 36.9 %collective-permute-start.36 = (bf16[344,1024]{1,0:T(8,128)(2,1)S(1)}, bf16[344,1024]{1,0:T(8,128)(2,1)}, u32[]{:S(2)}, u32[]{:S(2)}) collective-permute-start(bf16[344,1024]{1,0:T(8,128)(2,1)S(1)} %slice_bitcast_fusion.10), channel_id=1, source_target_pairs={{0,2},{2,0},{1,3},{3,1},{4,6},{6,4},{5,7},{7,5},{8,10},{10,8},{9,1... | collective-permute-start | bytes 2113544 | tf_op jit(solution)/shard_map/ppermute | solution.py:472
  297.4 24.3 %collective-permute-start.30 = (bf16[2,344,1024]{2,1,0:T(8,128)(2,1)}, bf16[2,344,1024]{2,1,0:T(8,128)(2,1)}, u32[]{:S(2)}, u32[]{:S(2)}) collective-permute-start(bf16[2,344,1024]{2,1,0:T(8,128)(2,1)} %fusion.42), channel_id=1, source_target_pairs={{0,1},{1,0},{2,3},{3,2},{4,5},{5,4},{6,7},{7,6},{8,9},{9,8},{10,11... | collective-permute-start | bytes 4227080 | tf_op jit(solution)/shard_map/ppermute | solution.py:489
  297.4 27.9 %collective-permute-start.28 = (bf16[2,344,1024]{2,1,0:T(8,128)(2,1)}, bf16[2,344,1024]{2,1,0:T(8,128)(2,1)}, u32[]{:S(2)}, u32[]{:S(2)}) collective-permute-start(bf16[2,344,1024]{2,1,0:T(8,128)(2,1)} %fusion.41), channel_id=1, source_target_pairs={{0,1},{1,0},{2,3},{3,2},{4,5},{5,4},{6,7},{7,6},{8,9},{9,8},{10,11... | collective-permute-start | bytes 4227080 | tf_op jit(solution)/shard_map/ppermute | solution.py:489
  323.7 18.7 %collective-permute-start.31 = (bf16[344,1024]{1,0:T(8,128)(2,1)S(1)}, bf16[344,1024]{1,0:T(8,128)(2,1)S(1)}, u32[]{:S(2)}, u32[]{:S(2)}) collective-permute-start(bf16[344,1024]{1,0:T(8,128)(2,1)S(1)} %slice_bitcast_fusion.12), channel_id=1, source_target_pairs={{0,2},{2,0},{1,3},{3,1},{4,6},{6,4},{5,7},{7,5},{8,10},{10,8},{9,1... | collective-permute-start | bytes 2113544 | tf_op jit(solution)/shard_map/ppermute | solution.py:472
  327.3 29.2 %collective-permute-start.29 = (bf16[344,1024]{1,0:T(8,128)(2,1)S(1)}, bf16[344,1024]{1,0:T(8,128)(2,1)S(1)}, u32[]{:S(2)}, u32[]{:S(2)}) collective-permute-start(bf16[344,1024]{1,0:T(8,128)(2,1)S(1)} %slice_bitcast_fusion.14), channel_id=1, source_target_pairs={{0,2},{2,0},{1,3},{3,1},{4,6},{6,4},{5,7},{7,5},{8,10},{10,8},{9,1... | collective-permute-start | bytes 2113544 | tf_op jit(solution)/shard_map/ppermute | solution.py:472
  374.4 180.0 %reduce-scatter.5.cloned.1.call-start = ((), (), s32[]{:S(2)}) async-start(), calls=%async_computation.4 | async-start | bytes 4718592 | tf_op jit(solution)/shard_map/reduce_scatter | solution.py:497
  437.1 18.4 %collective-permute-start.39 = (bf16[2,344,1024]{2,1,0:T(8,128)(2,1)S(1)}, bf16[2,344,1024]{2,1,0:T(8,128)(2,1)S(1)}, u32[]{:S(2)}, u32[]{:S(2)}) collective-permute-start(bf16[2,344,1024]{2,1,0:T(8,128)(2,1)S(1)} %slice_bitcast_fusion.4), channel_id=1, source_target_pairs={{0,1},{1,0},{2,3},{3,2},{4,5},{5,4},{6,7},{7,6},{8,9},{9,8},{10,11... | collective-permute-start | bytes 4227080 | tf_op jit(solution)/shard_map/ppermute | solution.py:489
  458.1 27.2 %collective-permute-start.40 = (bf16[344,1024]{1,0:T(8,128)(2,1)}, bf16[344,1024]{1,0:T(8,128)(2,1)S(1)}, u32[]{:S(2)}, u32[]{:S(2)}) collective-permute-start(bf16[344,1024]{1,0:T(8,128)(2,1)} %slice_bitcast_fusion.8), channel_id=1, source_target_pairs={{0,2},{2,0},{1,3},{3,1},{4,6},{6,4},{5,7},{7,5},{8,10},{10,8},{9,1... | collective-permute-start | bytes 2113544 | tf_op jit(solution)/shard_map/ppermute | solution.py:472
  484.8 25.9 %collective-permute-start.54 = (bf16[64,1024]{1,0:T(8,128)(2,1)}, bf16[64,1024]{1,0:T(8,128)(2,1)}, u32[]{:S(2)}, u32[]{:S(2)}) collective-permute-start(bf16[64,1024]{1,0:T(8,128)(2,1)} %reduce-scatter.3.cloned.1.call-done), channel_id=1, source_target_pairs={{0,2},{2,0},{1,3},{3,1},{4,6},{6,4},{5,7},{7,5},{8,10},{10,8},{9,1... | collective-permute-start | bytes 393224 | tf_op jit(solution)/shard_map/ppermute | solution.py:472
  511.7 29.0 %collective-permute-start.55 = (bf16[1,64,1024]{2,1,0:T(8,128)(2,1)S(1)}, bf16[1,64,1024]{2,1,0:T(8,128)(2,1)S(1)}, u32[]{:S(2)}, u32[]{:S(2)}) collective-permute-start(bf16[1,64,1024]{2,1,0:T(8,128)(2,1)S(1)} %fusion.79), channel_id=1, source_target_pairs={{0,1},{1,0},{2,3},{3,2},{4,5},{5,4},{6,7},{7,6},{8,9},{9,8},{10,11... | collective-permute-start | bytes 393224 | tf_op jit(solution)/shard_map/ppermute | solution.py:489
  527.3 33.8 %collective-permute-start.43 = (bf16[2,344,1024]{2,1,0:T(8,128)(2,1)}, bf16[2,344,1024]{2,1,0:T(8,128)(2,1)}, u32[]{:S(2)}, u32[]{:S(2)}) collective-permute-start(bf16[2,344,1024]{2,1,0:T(8,128)(2,1)} %slice_bitcast_fusion.2), channel_id=1, source_target_pairs={{0,1},{1,0},{2,3},{3,2},{4,5},{5,4},{6,7},{7,6},{8,9},{9,8},{10,11... | collective-permute-start | bytes 4227080 | tf_op jit(solution)/shard_map/ppermute | solution.py:489
  564.0 18.5 %collective-permute-start.44 = (bf16[344,1024]{1,0:T(8,128)(2,1)}, bf16[344,1024]{1,0:T(8,128)(2,1)}, u32[]{:S(2)}, u32[]{:S(2)}) collective-permute-start(bf16[344,1024]{1,0:T(8,128)(2,1)} %slice_bitcast_fusion.6), channel_id=1, source_target_pairs={{0,2},{2,0},{1,3},{3,1},{4,6},{6,4},{5,7},{7,5},{8,10},{10,8},{9,1... | collective-permute-start | bytes 2113544 | tf_op jit(solution)/shard_map/ppermute | solution.py:472
  568.0 21.9 %collective-permute-start.57 = (bf16[2,2,128,1024]{2,3,0,1:T(8,128)(2,1)}, bf16[2,2,128,1024]{2,3,0,1:T(8,128)(2,1)}, u32[]{:S(2)}, u32[]{:S(2)}) collective-permute-start(bf16[2,2,128,1024]{2,3,0,1:T(8,128)(2,1)} %fusion.55), channel_id=1, source_target_pairs={{0,1},{1,0},{2,3},{3,2},{4,5},{5,4},{6,7},{7,6},{8,9},{9,8},{10,11... | collective-permute-start | bytes 3145736 | tf_op jit(solution)/shard_map/ppermute | solution.py:489
  (148 other events, 1440.2 us)
Sparse Core Ops, SparseCore 0:
  84.6 76.1 all-gather.1
  374.5 64.5 reduce-scatter.2
  443.2 94.1 reduce-scatter.4

commit v5 on v3

--- a/solution.py
+++ b/solution.py
@@ -262,14 +262,14 @@
     )(limits, triple, triple, triple, attended, grad, logs)
 
 
-def project_kernel(rows_ref, gain_ref, shift_ref, weight_ref, bias_ref, normed_ref, triple_ref):
+def project_kernel(rows_ref, small_ref, weight_ref, bias_ref, normed_ref, triple_ref):
     normal, _ = normalize(rows_ref[0].astype(F32))
-    normed = (normal * gain_ref[...] + shift_ref[...]).astype(BF)
+    normed = (normal * small_ref[0:1, :] + small_ref[1:2, :]).astype(BF)
     normed_ref[0] = normed
     triple_ref[0] = (dot(normed, weight_ref[...]) + bias_ref[...]).astype(BF)
 
 
-def project(tokens, gain, shift, weight, bias):
+def project(tokens, small, weight, bias):
     pieces, rows, width = tokens.shape
     columns = weight.shape[1]
 
@@ -282,7 +282,7 @@
     return pl.pallas_call(
         project_kernel,
         grid=(pieces,),
-        in_specs=[piece(width), whole(gain), whole(shift), whole(weight), whole(bias)],
+        in_specs=[piece(width), whole(small), whole(weight), whole(bias)],
         out_specs=[piece(width), piece(columns)],
         out_shape=[
             jax.ShapeDtypeStruct((pieces, rows, width), BF),
@@ -295,7 +295,7 @@
             transcendentals=0,
         ),
         name="project",
-    )(tokens, gain, shift, weight, bias)
+    )(tokens, small, weight, bias)
 
 
 def project_back_kernel(grad_ref, rows_ref, weight_ref, part_ref, gain_ref, shift_ref, total_ref):
@@ -485,20 +485,6 @@
     return jnp.where(place < count // 2, 2 * place, 2 * (count - 1 - place) + 1)
 
 
-def ring_gather(array):
-    count = lax.axis_size("fsdp")
-    out = jnp.zeros((count,) + array.shape, array.dtype)
-    out = lax.dynamic_update_index_in_dim(out, array, ring_index(0), 0)
-    up = down = array
-    for step in range(1, count // 2 + 1):
-        up = ring_send(up, 1)
-        out = lax.dynamic_update_index_in_dim(out, up, ring_index(-step), 0)
-        if step <= (count - 1) // 2:
-            down = ring_send(down, -1)
-            out = lax.dynamic_update_index_in_dim(out, down, ring_index(step), 0)
-    return out
-
-
 def ring_scatter(array):
     count = lax.axis_size("fsdp")
 
@@ -575,36 +561,34 @@
         second_gain, second_shift, reduce_bias, feed_scale,
     ]
     vector_count = len(vectors)
-    packed = jnp.concatenate(
-        [triple_mine, jnp.stack(vectors, 1), bias_mine.reshape(shard, bias_columns)], 1
-    )
-    packed = jnp.pad(packed, ((0, 0), (0, -packed.shape[1] % 128)))
-    packed = ring_gather(packed).reshape(width, -1)
-    triple_whole = packed[:, : 3 * head_width]
-    small = packed[:, 3 * head_width : 3 * head_width + vector_count + bias_columns]
-    small = small.astype(F32).T
+    small_mine = jnp.concatenate(
+        [jnp.stack(vectors, 1), bias_mine.reshape(shard, bias_columns)], 1
+    )
+    small_mine = jnp.pad(small_mine, ((0, 0), (0, -small_mine.shape[1] % 128)))
+    pairs = shard // (2 * HEAD_DIM)
+    output_mine = lax.dynamic_index_in_dim(
+        output_weight.reshape(pairs, 2, HEAD_DIM, width), core, 1, False
+    )
+    output_mine = output_mine.reshape(shard // 2, 2, width // 2).transpose(1, 0, 2)
+    output_mine = output_mine.reshape(shard, width // 2)
+    first = 3 * head_width
+    second = first + small_mine.shape[1]
+    packed = fsdp_gather(jnp.concatenate([triple_mine, small_mine, output_mine], 1))
+    triple_whole = packed[:, :first]
+    small = packed[:, first : first + 16].astype(F32).T
+    output_whole = packed[:, second:].reshape(fsdp_count, 2, shard // 2, width // 2)
+    output_whole = output_whole.transpose(0, 2, 1, 3).reshape(far_count, head_width, width)
+    output_whole = jnp.roll(output_whole, -far, 0).reshape(width // 2, width)
     (gain_1, shift_1, bias_q, bias_v, bias_o, scale_a, gain_2, shift_2, bias_r, scale_f) = [
         small[i] for i in range(vector_count)
     ]
     bias_e = (
-        small[vector_count:]
+        small[vector_count : vector_count + bias_columns]
         .reshape(bias_columns, fsdp_count, shard)
         .transpose(1, 2, 0)
         .reshape(1, fsdp_count * unit_part)
     )
 
-    split_output = shard % (2 * HEAD_DIM) == 0
-    if split_output:
-        output_mine = lax.dynamic_index_in_dim(
-            output_weight.reshape(shard // (2 * HEAD_DIM), 2, HEAD_DIM, width), core, 1, False
-        ).reshape(shard // 2, width)
-        output_whole = ring_gather(output_mine)
-    else:
-        output_whole = lax.dynamic_index_in_dim(
-            fsdp_gather(output_weight).reshape(-1, 2, HEAD_DIM, width), core, 1, False
-        )
-    output_whole = output_whole.reshape(far_count, head_width, width)
-    output_whole = jnp.roll(output_whole, -far, 0).reshape(width // 2, width)
     blocks = units // 2 // width
     expand_mine = lax.dynamic_index_in_dim(
         expand_weight.reshape(shard, fsdp_count, 2, unit_part), core, 2, False
@@ -614,11 +598,7 @@
     )
     feed_mine = jnp.concatenate([expand_mine[:, i] for i in range(blocks)] + [reduce_mine], 0)
     height = blocks * shard + unit_part
-    feed_mine = lax.dynamic_slice_in_dim(
-        feed_mine, far * (height // far_count), height // far_count, 0
-    )
-    feed_weights = lax.all_gather(after(feed_mine, packed), ("fsdp", "far"), axis=0, tiled=True)
-    feed_weights = feed_weights.reshape(fsdp_count, height, width)
+    feed_weights = fsdp_gather(feed_mine).reshape(fsdp_count, height, width)
     expand_blocks = [
         feed_weights[:, i * shard : (i + 1) * shard].reshape(width, width) for i in range(blocks)
     ]
@@ -638,7 +618,7 @@
             slots += [slot, other_core(slot)]
         tokens.append(jnp.stack(slots, 0))
         first_normed, triple = project(
-            tokens[-1], gain_1[None], shift_1[None], triple_whole, joint_bias[None]
+            tokens[-1], small, triple_whole, joint_bias[None]
         )
         normed.append(first_normed)
         triples.append(triple)
@@ -706,12 +686,7 @@
     grad_expanded = (dot_right_t(grad_feed, reduce_whole) * slope.astype(F32)).astype(BF)
     feed_sums = feed_grads(second_normed, activated, grad_expanded, grad_feed, fsdp_count)
     grad_expanded, feed_sums = lax.optimization_barrier((grad_expanded, feed_sums))
-    feed_sums = lax.psum_scatter(
-        feed_sums.reshape(fsdp_count * height, width),
-        ("fsdp", "far"),
-        scatter_dimension=0,
-        tiled=True,
-    )
+    feed_sums = fsdp_scatter(feed_sums.reshape(fsdp_count * height, width))
     partial = sum(
         dot_right_t(grad_expanded[:, i * width : (i + 1) * width], expand_blocks[i])
         for i in range(blocks)
@@ -808,17 +783,27 @@
     ] + place_units(grad_expand_bias)
     sums = jnp.stack(sums, 0).astype(BF).T
     sums = jnp.pad(sums, ((0, 0), (0, -sums.shape[1] % 128)))
-    grad_packed = jnp.concatenate([grad_triple_weight, sums], 1)
+    grad_output_weight = grad_output_weight.reshape(fsdp_count, shard // 2, 2, width // 2)
+    grad_output_weight = grad_output_weight.transpose(0, 2, 1, 3).reshape(width, width // 2)
+    grad_packed = jnp.concatenate([grad_triple_weight, sums, grad_output_weight], 1)
     grad_packed = ring_scatter(grad_packed.reshape(fsdp_count, shard, -1)).astype(BF)
+    feed_sums = after(feed_sums, grad_packed)
     grad_packed = jnp.roll(jnp.stack(far_gather(grad_packed), 0), far, 0)
-    grad_packed = core_join(grad_packed, 1, core).astype(F32)
+    grad_packed = core_join(grad_packed, 1, core)
     grad_triple_weight = (
-        grad_packed[:, :, :, : 3 * head_width]
+        grad_packed[:, :, :, :first]
         .reshape(far_count, 2, shard, 3, near_heads, HEAD_DIM)
         .transpose(2, 3, 0, 4, 1, 5)
         .reshape(shard, 3 * width)
-    )
-    sums = jnp.sum(grad_packed[:, :, :, 3 * head_width :], (0, 1)).T
+        .astype(F32)
+    )
+    sums = jnp.sum(grad_packed[:, :, :, first : first + 16].astype(F32), (0, 1)).T
+    grad_output_weight = (
+        jnp.sum(grad_packed[:, :, :, second:].astype(F32), 0)
+        .reshape(2, 2, pairs, HEAD_DIM, width // 2)
+        .transpose(2, 0, 3, 1, 4)
+        .reshape(shard, width)
+    )
 
     def far_total(array):
         total = array.astype(F32)
@@ -826,22 +811,7 @@
             total = total + far_send(array, r).astype(F32)
         return total
 
-    if split_output:
-        grad_output_weight = ring_scatter(
-            grad_output_weight.reshape(fsdp_count, shard // 2, width)
-        ).astype(BF)
-        grad_output_weight = far_total(grad_output_weight).astype(BF)
-        grad_output_weight = core_join(
-            grad_output_weight.reshape(-1, HEAD_DIM, width), 1, core
-        ).reshape(shard, width)
-    else:
-        spread = grad_output_weight.reshape(-1, 1, HEAD_DIM, width)
-        spread = jnp.where(jnp.arange(2)[None, :, None, None] == core, spread, 0)
-        spread = fsdp_scatter(spread.reshape(width, width))
-        grad_output_weight = far_total(spread)
-        grad_output_weight = grad_output_weight + other_core(grad_output_weight)
-    feed_sums = jnp.roll(jnp.stack(far_gather(core_join(feed_sums, 0, core)), 0), far, 0)
-    feed_sums = feed_sums.transpose(1, 0, 2, 3).reshape(2, height, width).astype(F32)
+    feed_sums = core_join(far_total(feed_sums).astype(BF), 0, core).astype(F32)
     grad_expand_weight = (
         feed_sums[:, : blocks * shard]
         .reshape(2, blocks, shard, -1, unit_part)
@@ -863,7 +833,7 @@
         grad_triple_weight,
         sums[2],
         sums[3],
-        grad_output_weight.astype(F32),
+        grad_output_weight,
         sums[4],
         sums[5],
         sums[6],
@@ -876,14 +846,302 @@
     )
 
 
+def layer_norm(inputs, gain, shift):
+    average = jnp.mean(inputs, -1, keepdims=True)
+    centered = inputs - average
+    variance = jnp.mean(centered * centered, -1, keepdims=True)
+    return centered * lax.rsqrt(variance + EPSILON) * gain + shift
+
+
+def exact_gelu(values):
+    return jax.nn.gelu(values, approximate=False)
+
+
+def to_float(array):
+    return array.astype(jnp.float32)
+
+
+def plain_matmul(left, right):
+    return jnp.dot(left, right, preferred_element_type=jnp.float32)
+
+
+def plain_matmul_left_t(left, right):
+    return lax.dot_general(
+        left, right, (((0,), (0,)), ((), ())), preferred_element_type=jnp.float32
+    )
+
+
+def plain_matmul_right_t(left, right):
+    return lax.dot_general(
+        left, right, (((1,), (1,)), ((), ())), preferred_element_type=jnp.float32
+    )
+
+
+def plain_column_total(array):
+    return plain_matmul(jnp.ones((1, array.shape[0]), jnp.bfloat16), array)[0]
+
+
+def masked_scores(queries, key_rows, live_count, factor):
+    scores = (
+        jnp.einsum("qhd,khd->hqk", queries, key_rows, preferred_element_type=jnp.float32) * factor
+    )
+    live_keys = lax.broadcasted_iota(jnp.int32, (1, 1, key_rows.shape[0]), 2) < live_count
+    return jnp.where(live_keys, scores, -1e30)
+
+
+def plain_attend_forward(bundle):
+    packed, live_count = bundle
+    length, triple_count, local_width = packed.shape
+    head_count = local_width // HEAD_DIM
+    unpacked = packed.reshape(length, triple_count, head_count, HEAD_DIM)
+    factor = HEAD_DIM ** (-0.5)
+    scores = masked_scores(unpacked[:, 0], unpacked[:, 1], live_count, factor)
+    highest = jnp.max(scores, -1, keepdims=True)
+    powers = jnp.exp(scores - highest)
+    row_total = jnp.sum(powers, -1, keepdims=True)
+    weights_low = (powers / row_total).astype(jnp.bfloat16)
+    mixed_rows = jnp.einsum(
+        "hqk,khd->qhd", weights_low, unpacked[:, 2], preferred_element_type=jnp.float32
+    )
+    logsum = highest + jnp.log(row_total)
+    return (mixed_rows.reshape(length, local_width).astype(jnp.bfloat16), logsum)
+
+
+def plain_attend_backward(bundle):
+    packed, grad_mixed, logsum, live_count = bundle
+    length, triple_count, local_width = packed.shape
+    head_count = local_width // HEAD_DIM
+    unpacked = packed.reshape(length, triple_count, head_count, HEAD_DIM)
+    factor = HEAD_DIM ** (-0.5)
+    scores = masked_scores(unpacked[:, 0], unpacked[:, 1], live_count, factor)
+    probs = jnp.exp(scores - logsum)
+    grad_heads = grad_mixed.reshape(length, head_count, HEAD_DIM)
+    grad_probs = jnp.einsum(
+        "qhd,khd->hqk", grad_heads, unpacked[:, 2], preferred_element_type=jnp.float32
+    )
+    grad_values = jnp.einsum(
+        "hqk,qhd->khd", probs.astype(jnp.bfloat16), grad_heads, preferred_element_type=jnp.float32
+    )
+    inner = jnp.sum(probs * grad_probs, -1, keepdims=True)
+    grad_scores = (probs * (grad_probs - inner)).astype(jnp.bfloat16)
+    grad_queries = (
+        jnp.einsum("hqk,khd->qhd", grad_scores, unpacked[:, 1], preferred_element_type=jnp.float32)
+        * factor
+    )
+    grad_keys = (
+        jnp.einsum("hqk,qhd->khd", grad_scores, unpacked[:, 0], preferred_element_type=jnp.float32)
+        * factor
+    )
+    stacked = jnp.stack([grad_queries, grad_keys, grad_values], 1)
+    return stacked.reshape(length, triple_count, local_width).astype(jnp.bfloat16)
+
+
+def plain_shards(
+    images,
+    cotangent,
+    valid_count,
+    first_gain,
+    first_shift,
+    triple_weight,
+    query_bias,
+    value_bias,
+    output_weight,
+    output_bias,
+    attend_scale,
+    second_gain,
+    second_shift,
+    expand_weight,
+    expand_bias,
+    reduce_weight,
+    reduce_bias,
+    feed_scale,
+):
+    image_count, local_len, width = images.shape
+    gathered = (
+        lax.all_gather(first_gain, "fsdp", axis=0, tiled=True),
+        lax.all_gather(first_shift, "fsdp", axis=0, tiled=True),
+        lax.all_gather(triple_weight, "fsdp", axis=0, tiled=True),
+        lax.all_gather(query_bias, "fsdp", axis=0, tiled=True),
+        lax.all_gather(value_bias, "fsdp", axis=0, tiled=True),
+        lax.all_gather(output_weight, "fsdp", axis=0, tiled=True),
+        lax.all_gather(output_bias, "fsdp", axis=0, tiled=True),
+        lax.all_gather(attend_scale, "fsdp", axis=0, tiled=True),
+        lax.all_gather(second_gain, "fsdp", axis=0, tiled=True),
+        lax.all_gather(second_shift, "fsdp", axis=0, tiled=True),
+        lax.all_gather(expand_weight, "fsdp", axis=0, tiled=True),
+        lax.all_gather(expand_bias, "fsdp", axis=0, tiled=True),
+        lax.all_gather(reduce_weight, "fsdp", axis=0, tiled=True),
+        lax.all_gather(reduce_bias, "fsdp", axis=0, tiled=True),
+        lax.all_gather(feed_scale, "fsdp", axis=0, tiled=True),
+    )
+    inputs = images.astype(jnp.float32).reshape(-1, width)
+    first_normed = layer_norm(inputs, to_float(gathered[0]), to_float(gathered[1])).astype(
+        jnp.bfloat16
+    )
+    joint_bias = to_float(jnp.concatenate([gathered[3], jnp.zeros_like(gathered[3]), gathered[4]]))
+    triple = (plain_matmul(first_normed, gathered[2]) + joint_bias).astype(jnp.bfloat16)
+    triple = triple.reshape(image_count, local_len, 3, width)
+    by_heads = lax.all_to_all(triple, "seq", split_axis=3, concat_axis=1, tiled=True)
+    attended, logsums = lax.map(plain_attend_forward, (by_heads, valid_count))
+    by_tokens = lax.all_to_all(attended, "seq", split_axis=1, concat_axis=2, tiled=True)
+    attended_rows = by_tokens.reshape(-1, width)
+    branch_attend = plain_matmul(attended_rows, gathered[5]) + to_float(gathered[6])
+    residual = inputs + to_float(gathered[7]) * branch_attend
+    second_normed = layer_norm(residual, to_float(gathered[8]), to_float(gathered[9])).astype(
+        jnp.bfloat16
+    )
+    expanded = plain_matmul(second_normed, gathered[10]) + to_float(gathered[11])
+    activated = exact_gelu(expanded).astype(jnp.bfloat16)
+    branch_feed = plain_matmul(activated, gathered[12]) + to_float(gathered[13])
+    outputs = residual + to_float(gathered[14]) * branch_feed
+    weights = (
+        lax.all_gather(first_gain, "fsdp", axis=0, tiled=True),
+        lax.all_gather(first_shift, "fsdp", axis=0, tiled=True),
+        lax.all_gather(triple_weight, "fsdp", axis=0, tiled=True),
+        lax.all_gather(query_bias, "fsdp", axis=0, tiled=True),
+        lax.all_gather(value_bias, "fsdp", axis=0, tiled=True),
+        lax.all_gather(output_weight, "fsdp", axis=0, tiled=True),
+        lax.all_gather(output_bias, "fsdp", axis=0, tiled=True),
+        lax.all_gather(attend_scale, "fsdp", axis=0, tiled=True),
+        lax.all_gather(second_gain, "fsdp", axis=0, tiled=True),
+        lax.all_gather(second_shift, "fsdp", axis=0, tiled=True),
+        lax.all_gather(expand_weight, "fsdp", axis=0, tiled=True),
+        lax.all_gather(expand_bias, "fsdp", axis=0, tiled=True),
+        lax.all_gather(reduce_weight, "fsdp", axis=0, tiled=True),
+        lax.all_gather(reduce_bias, "fsdp", axis=0, tiled=True),
+        lax.all_gather(feed_scale, "fsdp", axis=0, tiled=True),
+    )
+    upstream = cotangent.astype(jnp.float32).reshape(-1, width)
+    grad_feed_scale = jnp.sum(upstream * branch_feed, 0)
+    grad_feed = (to_float(weights[14]) * upstream).astype(jnp.bfloat16)
+    grad_reduce_bias = plain_column_total(grad_feed)
+    grad_reduce_weight = plain_matmul_left_t(activated, grad_feed)
+    grad_activated = plain_matmul_right_t(grad_feed, weights[12])
+    unused, gelu_pull = jax.vjp(exact_gelu, expanded)
+    grad_expanded = gelu_pull(grad_activated)[0].astype(jnp.bfloat16)
+    grad_expand_bias = plain_column_total(grad_expanded)
+    grad_expand_weight = plain_matmul_left_t(second_normed, grad_expanded)
+    grad_second_normed = plain_matmul_right_t(grad_expanded, weights[10])
+    unused, second_pull = jax.vjp(layer_norm, residual, to_float(weights[8]), to_float(weights[9]))
+    grad_residual_norm, grad_second_gain, grad_second_shift = second_pull(grad_second_normed)
+    grad_residual = upstream + grad_residual_norm
+    grad_attend_scale = jnp.sum(grad_residual * branch_attend, 0)
+    grad_attend = (to_float(weights[7]) * grad_residual).astype(jnp.bfloat16)
+    grad_output_bias = plain_column_total(grad_attend)
+    grad_output_weight = plain_matmul_left_t(attended_rows, grad_attend)
+    grad_attended = plain_matmul_right_t(grad_attend, weights[5]).astype(jnp.bfloat16)
+    grad_attended = grad_attended.reshape(image_count, local_len, width)
+    grad_by_heads = lax.all_to_all(grad_attended, "seq", split_axis=2, concat_axis=1, tiled=True)
+    grad_triple_heads = lax.map(plain_attend_backward, (by_heads, grad_by_heads, logsums, valid_count))
+    grad_triple = lax.all_to_all(grad_triple_heads, "seq", split_axis=1, concat_axis=3, tiled=True)
+    grad_triple = grad_triple.reshape(-1, 3 * width)
+    column_sums = plain_column_total(grad_triple)
+    grad_query_bias = column_sums[:width]
+    grad_value_bias = column_sums[2 * width :]
+    grad_triple_weight = plain_matmul_left_t(first_normed, grad_triple)
+    grad_first_normed = plain_matmul_right_t(grad_triple, weights[2])
+    unused, first_pull = jax.vjp(layer_norm, inputs, to_float(weights[0]), to_float(weights[1]))
+    grad_inputs_norm, grad_first_gain, grad_first_shift = first_pull(grad_first_normed)
+    grad_images = grad_residual + grad_inputs_norm
+    owned = (
+        lax.psum_scatter(
+            grad_first_gain.astype(jnp.bfloat16), "fsdp", scatter_dimension=0, tiled=True
+        ).astype(jnp.float32),
+        lax.psum_scatter(
+            grad_first_shift.astype(jnp.bfloat16), "fsdp", scatter_dimension=0, tiled=True
+        ).astype(jnp.float32),
+        lax.psum_scatter(
+            grad_triple_weight.astype(jnp.bfloat16), "fsdp", scatter_dimension=0, tiled=True
+        ).astype(jnp.float32),
+        lax.psum_scatter(
+            grad_query_bias.astype(jnp.bfloat16), "fsdp", scatter_dimension=0, tiled=True
+        ).astype(jnp.float32),
+        lax.psum_scatter(
+            grad_value_bias.astype(jnp.bfloat16), "fsdp", scatter_dimension=0, tiled=True
+        ).astype(jnp.float32),
+        lax.psum_scatter(
+            grad_output_weight.astype(jnp.bfloat16), "fsdp", scatter_dimension=0, tiled=True
+        ).astype(jnp.float32),
+        lax.psum_scatter(
+            grad_output_bias.astype(jnp.bfloat16), "fsdp", scatter_dimension=0, tiled=True
+        ).astype(jnp.float32),
+        lax.psum_scatter(
+            grad_attend_scale.astype(jnp.bfloat16), "fsdp", scatter_dimension=0, tiled=True
+        ).astype(jnp.float32),
+        lax.psum_scatter(
+            grad_second_gain.astype(jnp.bfloat16), "fsdp", scatter_dimension=0, tiled=True
+        ).astype(jnp.float32),
+        lax.psum_scatter(
+            grad_second_shift.astype(jnp.bfloat16), "fsdp", scatter_dimension=0, tiled=True
+        ).astype(jnp.float32),
+        lax.psum_scatter(
+            grad_expand_weight.astype(jnp.bfloat16), "fsdp", scatter_dimension=0, tiled=True
+        ).astype(jnp.float32),
+        lax.psum_scatter(
+            grad_expand_bias.astype(jnp.bfloat16), "fsdp", scatter_dimension=0, tiled=True
+        ).astype(jnp.float32),
+        lax.psum_scatter(
+            grad_reduce_weight.astype(jnp.bfloat16), "fsdp", scatter_dimension=0, tiled=True
+        ).astype(jnp.float32),
+        lax.psum_scatter(
+            grad_reduce_bias.astype(jnp.bfloat16), "fsdp", scatter_dimension=0, tiled=True
+        ).astype(jnp.float32),
+        lax.psum_scatter(
+            grad_feed_scale.astype(jnp.bfloat16), "fsdp", scatter_dimension=0, tiled=True
+        ).astype(jnp.float32),
+    )
+    summed = lax.psum(
+        (
+            owned[0],
+            owned[1],
+            owned[2],
+            owned[3],
+            owned[4],
+            owned[5],
+            owned[6],
+            owned[7],
+            owned[8],
+            owned[9],
+            owned[10],
+            owned[11],
+            owned[12],
+            owned[13],
+            owned[14],
+        ),
+        "seq",
+    )
+    return (
+        outputs.reshape(image_count, local_len, width).astype(jnp.bfloat16),
+        grad_images.reshape(image_count, local_len, width),
+        summed[0],
+        summed[1],
+        summed[2],
+        summed[3],
+        summed[4],
+        summed[5],
+        summed[6],
+        summed[7],
+        summed[8],
+        summed[9],
+        summed[10],
+        summed[11],
+        summed[12],
+        summed[13],
+        summed[14],
+    )
+
+
 def solution(mesh):
     fsdp, seq = mesh.devices.shape
-    split = Mesh(mesh.devices.reshape(fsdp, seq // 2, 2), ("fsdp", "far", "core"))
-    tokens = P("fsdp", ("far", "core"), None)
+    if seq == 4 and fsdp == 8:
+        plan, tokens = shards, P("fsdp", ("far", "core"), None)
+        mesh = Mesh(mesh.devices.reshape(fsdp, 2, 2), ("fsdp", "far", "core"))
+    else:
+        plan, tokens = plain_shards, P("fsdp", "seq", None)
     row, matrix = P("fsdp"), P("fsdp", None)
     return jax.shard_map(
-        shards,
-        mesh=split,
+        plan,
+        mesh=mesh,
         in_specs=(
             tokens, tokens, row, row, row, matrix, row, row, matrix,
             row, row, row, row, matrix, row, matrix, row, row,

time: 593 us -> 577 us (0.973)
  starting transfers between devices: 53.3 us -> 23 us
  other arithmetic: 62 us -> 81.6 us
  waiting for transfers between devices: 166 us -> 153 us
  matrix products: 48.5 us -> 55.2 us
    all_gather x1 -> x2, waiting for transfers between devices: 0.01 us -> 50.8 us  [fsdp_gather(): return lax.all_gather(array, 'fsdp', axis=0, tiled=True)]
    ppermute x28 -> x7, waiting for transfers between devices: 69.2 us -> 22.6 us  [ring_send(): return lax.ppermute(array, 'fsdp', pairs)]
    ppermute x28 -> x7, starting transfers between devices: 37.5 us -> 6.41 us  [ring_send(): return lax.ppermute(array, 'fsdp', pairs)]
    ppermute x11 -> x10, waiting for transfers between devices: 94.5 us -> 77.9 us  [far_send(): lax.ppermute(array, 'far', [(i, (i + shift) % count) for i in range(count)])]
    broadcast_in_dim x10 -> x0, local copies, waits for them, and re-layouts: 12.9 us -> none  [the longest x4 6.38 us: ring_gather(): out = lax.dynamic_update_index_in_dim(out, up, ring_index(-step), 0)]
    another operation x0 -> x12, local copies, waits for them, and re-layouts: none -> 11.2 us  [the longest x10 8.46 us: shards(): jnp.stack(vectors, 1)]
    dynamic_update_slice x16 -> x0, local copies, waits for them, and re-layouts: 8.85 us -> none  [the longest x8 3.9 us: ring_gather(): out = lax.dynamic_update_index_in_dim(out, up, ring_index(-step), 0)]
    ppermute x11 -> x10, starting transfers between devices: 13.2 us -> 14.4 us  [far_send(): lax.ppermute(array, 'far', [(i, (i + shift) % count) for i in range(count)])]
  transfers between devices with their start and end apart: 57 -> 35, of which waited for: 26 -> 14; matrix products, arithmetic and copies ran while one was open for 24% -> 29% of each run, Pallas kernels for 17% -> 17%
where the time goes in v5:
time: 577 us; the launch traced here: 572 us
  waiting for transfers between devices  153 us (27%)
  Pallas kernels  138 us (24%)
  local copies, waits for them, and re-layouts  106 us (18%)
  other arithmetic  81.6 us (14%)
  matrix products  55.2 us (10%)
  starting transfers between devices  23 us (4%)
  between operations  15.4 us (3%)
    ppermute x10, waiting for transfers between devices, far_send(): lax.ppermute(array, 'far', [(i, (i + shift) % count) for i in range(count)])  77.9 us
    pallas_call x2, Pallas kernels, attend_backward(): pl.pallas_call(attend_backward_kernel, grid_spec=pltpu.PrefetchScalarGrid...  51.1 us
    all_gather x2, waiting for transfers between devices, fsdp_gather(): return lax.all_gather(array, 'fsdp', axis=0, tiled=True)  50.8 us
    pallas_call x2, Pallas kernels, attend_forward(): pl.pallas_call(attend_forward_kernel, grid_spec=pltpu.PrefetchScalarGridS...  31.3 us
    unnamed x166, local copies, waits for them, and re-layouts  28.9 us
    dot_general x4, matrix products, dot_right_t(): lax.dot_general(left, right, (((1,), (1,)), ((), ())), preferred_element_...  22.6 us
    ppermute x7, waiting for transfers between devices, ring_send(): return lax.ppermute(array, 'fsdp', pairs)  22.6 us
    pallas_call x1, Pallas kernels, feed_grads(): pl.pallas_call(feed_grads_kernel, grid=(devices,), in_specs=[pl.BlockSpec...  20 us
  transfers between devices with their start and end apart: 35, of which 14 were waited for; matrix products, arithmetic and copies ran while one was open for 29% of the time, Pallas kernels for 17%

profile of v5, /device:TPU:0, one launch (start us, length us, event | category | flops | bytes accessed | tf_op | source)
XLA Modules:
  0.0 572.5 jit_solution(15358008612465100589)
XLA Ops:
  28.0 16.8 %collective-permute-done.1 = bf16[344,1024]{1,0:T(8,128)(2,1)S(1)} collective-permute-done((bf16[344,1024]{1,0:T(8,128)(2,1)}, bf16[344,1024]{1,0:T(8,128)(2,1)S(1)}, u32[]{:S(2)}, u32[]{:S(2)}) %collective-permute-start.1) | collective-permute-done | bytes 704544 | tf_op jit(solution)/shard_map/ppermute | solution.py:441
  45.3 13.8 %collective-permute-done.6 = bf16[344,1024]{1,0:T(8,128)(2,1)S(1)} collective-permute-done((bf16[344,1024]{1,0:T(8,128)(2,1)}, bf16[344,1024]{1,0:T(8,128)(2,1)S(1)}, u32[]{:S(2)}, u32[]{:S(2)}) %collective-permute-start.6) | collective-permute-done | bytes 704544 | tf_op jit(solution)/shard_map/ppermute | solution.py:441
  65.0 16.8 %all-gather.3.cloned.1.call-done = bf16[1024,1408]{1,0:T(8,128)(2,1)} async-done(((bf16[128,1408]{1,0:T(8,128)(2,1)}), bf16[1024,1408]{1,0:T(8,128)(2,1)}) %all-gather.3.cloned.1.call-update) | async-done | bytes 2883600 | tf_op jit(solution)/shard_map/all_gather | solution.py:467
  93.3 4.5 project.3
  99.1 15.7 %attend_forward.3 = (bf16[4,1,344,256]{3,2,1,0:T(8,128)(2,1)S(1)}, f32[1,2,1376,128]{3,2,1,0:T(8,128)S(1)}) custom-call(s32[1,2]{1,0:T(1,128)S(1)} %get-tuple-element.208.limit_ref, bf16[4,1,344,768]{3,2,1,0:T(8,128)(2,1)} %bitcast.253, bf16[4,1,344,768]{3,2,1,0:T(8,128)(2,1)} %bitcast.254, bf16[4,1,344,768]{3,2,1,0:T(8,128)(2,1)} %bitcast.255), custom_call_target="tpu_custom_call" | custom-call | flops 7755268096 | bytes 4227072 | tf_op jit(solution)/shard_map/attend_forward/pallas_call | solution.py:202
  117.2 4.6 project.2
  123.2 15.6 %attend_forward.2 = (bf16[4,1,344,256]{3,2,1,0:T(8,128)(2,1)S(1)}, f32[1,2,1376,128]{3,2,1,0:T(8,128)S(1)}) custom-call(s32[1,2]{1,0:T(1,128)S(1)} %get-tuple-element.207.limit_ref, bf16[4,1,344,768]{3,2,1,0:T(8,128)(2,1)} %bitcast.259, bf16[4,1,344,768]{3,2,1,0:T(8,128)(2,1)} %bitcast.260, bf16[4,1,344,768]{3,2,1,0:T(8,128)(2,1)} %bitcast.261), custom_call_target="tpu_custom_call" | custom-call | flops 7755268096 | bytes 4227072 | tf_op jit(solution)/shard_map/attend_forward/pallas_call | solution.py:202
  142.5 5.2 collective-permute-done.3
  159.9 5.0 add_convert_fusion.1
  165.6 4.2 multiply_convert_fusion.1.feed_ref
  173.5 34.0 %all-gather.5.cloned.1.call-done = bf16[4096,1024]{1,0:T(8,128)(2,1)} async-done(((bf16[512,1024]{1,0:T(8,128)(2,1)}), bf16[4096,1024]{1,0:T(8,128)(2,1)}) %all-gather.5.cloned.1.call-update) | async-done | bytes 8388624 | tf_op jit(solution)/shard_map/all_gather | solution.py:467
  215.9 19.0 %expand_rows.1 = (bf16[1376,2048]{1,0:T(8,128)(2,1)}, bf16[1376,2048]{1,0:T(8,128)(2,1)}) custom-call(bf16[1376,1024]{1,0:T(8,128)(2,1)S(1)} %copy-done.8, bf16[8,512,1024]{2,1,0:T(8,128)(2,1)} %bitcast.275, f32[1,2048]{1,0:T(1,128)S(1)} %reshape.479.bias_ref), custom_call_target="tpu_custom_call" | custom-call | flops 11542724608 | bytes 18284544 | tf_op jit(solution)/shard_map/expand_rows/pallas_call | solution.py:377
  235.0 9.7 %multiply_convert_fusion.expanded_ref = bf16[1376,2048]{1,0:T(8,128)(2,1)} fusion(bf16[1376,2048]{1,0:T(8,128)(2,1)} %get-tuple-element.46, bf16[1376,1024]{1,0:T(8,128)(2,1)S(1)} %copy-done.40, bf16[2048,1024]{1,0:T(8,128)(2,1)S(1)} %bitcast.279), kind=kOutput, calls=%fused_computation | convolution fusion | flops 5779816448 | bytes 18284544 | tf_op jit(solution)/shard_map/dot_general | solution.py:26
  244.6 20.0 %feed_grads.1 = bf16[8,512,1024]{2,1,0:T(8,128)(2,1)} custom-call(bf16[1376,1024]{1,0:T(8,128)(2,1)} %pad_maximum_fusion.4.rows_ref, bf16[1376,2048]{1,0:T(8,128)(2,1)} %get-tuple-element.45.active_ref, bf16[1376,2048]{1,0:T(8,128)(2,1)} %multiply_convert_fusion.expanded_ref, bf16[1376,1024]{1,0:T(8,128)(2,1)} %multiply_convert_fusion.1.feed_ref), custom_call_target="tpu_custom_call" | custom-call | flops 11542724608 | bytes 25296896 | tf_op jit(solution)/shard_map/feed_grads/pallas_call | solution.py:418
  264.6 4.9 fusion.16
  274.3 6.1 %fusion.65 = f32[1376,1024]{1,0:T(8,128)S(1)} fusion(bf16[1376,2048]{1,0:T(8,128)(2,1)S(1)} %bitcast.344, bf16[2048,1024]{1,0:T(8,128)(2,1)S(1)} %bitcast.280), kind=kOutput, calls=%fused_computation.214 | convolution fusion | flops 5771362304 | bytes 15466496 | tf_op jit(solution)/shard_map/dot_general | solution.py:18
  283.9 4.6 multiply_reduce_fusion
  288.6 7.2 %fusion.1 = (bf16[1024]{0:T(1024)(128)(2,1)S(1)}, bf16[688,1024]{1,0:T(8,128)(2,1)}, bf16[1024]{0:T(1024)(128)(2,1)S(1)}, f32[688,1024]{1,0:T(8,128)}) fusion(bf16[688,1024]{1,0:T(8,128)(2,1)} %collective-permute-done.11, f32[1376,1024]{1,0:T(8,128)} %copy-done.48, f32[1024]{0:T(1024)S(1)} %get-tuple-element.141, bf16[2,344,1024]{2,1,0:T(8,128)(2,1)} %param.21, ...), kind=kLoop, calls=%fused_computation.9 | loop fusion | flops 15497216 | bytes 19753728 | tf_op jit(solution)/shard_map/reduce_sum | solution.py:684
  310.0 4.9 convolution_convert_fusion
  314.9 4.3 reshape.484
  319.1 4.2 fusion.61
  330.2 12.1 %collective-permute-done.15 = bf16[688,256]{1,0:T(8,128)(2,1)S(1)} collective-permute-done((bf16[688,256]{1,0:T(8,128)(2,1)S(1)}, bf16[688,256]{1,0:T(8,128)(2,1)S(1)}, u32[]{:S(2)}, u32[]{:S(2)}) %collective-permute-start.15) | collective-permute-done | bytes 352288 | tf_op jit(solution)/shard_map/ppermute | solution.py:441
  343.2 25.8 %attend_backward.2 = bf16[4,1,344,768]{3,2,1,0:T(8,128)(2,1)} custom-call(s32[1,2]{1,0:T(1,128)} %copy-done.15, bf16[4,1,344,768]{3,2,1,0:T(8,128)(2,1)} %bitcast.262, bf16[4,1,344,768]{3,2,1,0:T(8,128)(2,1)} %bitcast.263, bf16[4,1,344,768]{3,2,1,0:T(8,128)(2,1)} %bitcast.264, bf16[4,1,344,256]{3,2,1,0:T(8,128)(2,1)} %copy-done.13, ...), custom_call_target="tpu_custom_call" | custom-call | flops 19388170240 | bytes 8454144 | tf_op jit(solution)/shard_map/attend_backward/pallas_call | solution.py:236
  391.0 7.4 %fusion.66 = f32[1024,768]{1,0:T(8,128)} fusion(bf16[1376,1024]{1,0:T(8,128)(2,1)} %bitcast.252, bf16[1376,768]{1,0:T(8,128)(2,1)} %bitcast.265), kind=kOutput, calls=%fused_computation.215 | convolution fusion | flops 2164260864 | bytes 8077312 | tf_op jit(solution)/shard_map/dot_general | solution.py:22
  402.0 25.3 %attend_backward.3 = bf16[4,1,344,768]{3,2,1,0:T(8,128)(2,1)} custom-call(s32[1,2]{1,0:T(1,128)} %copy-done.14, bf16[4,1,344,768]{3,2,1,0:T(8,128)(2,1)} %bitcast.256, bf16[4,1,344,768]{3,2,1,0:T(8,128)(2,1)} %bitcast.257, bf16[4,1,344,768]{3,2,1,0:T(8,128)(2,1)} %bitcast.258, bf16[4,1,344,256]{3,2,1,0:T(8,128)(2,1)} %copy-done.12, ...), custom_call_target="tpu_custom_call" | custom-call | flops 19388170240 | bytes 8454144 | tf_op jit(solution)/shard_map/attend_backward/pallas_call | solution.py:236
  427.3 6.2 %fusion = bf16[1024,768]{1,0:T(8,128)(2,1)} fusion(f32[1024,768]{1,0:T(8,128)} %fusion.66, bf16[4,344,1024]{2,1,0:T(8,128)(2,1)S(1)} %copy-done.22, bf16[4,344,768]{2,1,0:T(8,128)(2,1)} %bitcast.267), kind=kOutput, calls=%fused_computation.6 | convolution fusion | flops 2165833728 | bytes 9650176 | tf_op jit(solution)/shard_map/dot_general | solution.py:22
  451.7 7.6 %collective-permute-done.21 = bf16[128,1408]{0,1:T(8,128)(2,1)} collective-permute-done((bf16[128,1408]{0,1:T(8,128)(2,1)}, bf16[128,1408]{0,1:T(8,128)(2,1)}, u32[]{:S(2)}, u32[]{:S(2)}) %collective-permute-start.21) | collective-permute-done | bytes 360480 | tf_op jit(solution)/shard_map/ppermute | solution.py:478
  462.7 7.3 %collective-permute-done.22 = bf16[128,1408]{0,1:T(8,128)(2,1)} collective-permute-done((bf16[128,1408]{0,1:T(8,128)(2,1)}, bf16[128,1408]{0,1:T(8,128)(2,1)}, u32[]{:S(2)}, u32[]{:S(2)}) %collective-permute-start.22) | collective-permute-done | bytes 360480 | tf_op jit(solution)/shard_map/ppermute | solution.py:478
  474.1 5.9 %collective-permute-done.23 = bf16[128,1408]{0,1:T(8,128)(2,1)S(1)} collective-permute-done((bf16[128,1408]{0,1:T(8,128)(2,1)}, bf16[128,1408]{0,1:T(8,128)(2,1)S(1)}, u32[]{:S(2)}, u32[]{:S(2)}) %collective-permute-start.23) | collective-permute-done | bytes 360480 | tf_op jit(solution)/shard_map/ppermute | solution.py:478
  496.7 13.5 %collective-permute-done.28 = bf16[128,1408]{0,1:T(8,128)(2,1)S(1)} collective-permute-done((bf16[128,1408]{0,1:T(8,128)(2,1)S(1)}, bf16[128,1408]{0,1:T(8,128)(2,1)S(1)}, u32[]{:S(2)}, u32[]{:S(2)}) %collective-permute-start.28) | collective-permute-done | bytes 360480 | tf_op jit(solution)/shard_map/ppermute | solution.py:441
  521.5 4.3 fusion.14
  525.8 16.5 %collective-permute-done.30 = bf16[512,1024]{1,0:T(8,128)(2,1)} collective-permute-done((bf16[512,1024]{1,0:T(8,128)(2,1)}, bf16[512,1024]{1,0:T(8,128)(2,1)}, u32[]{:S(2)}, u32[]{:S(2)}) %collective-permute-start.30) | collective-permute-done | bytes 1048608 | tf_op jit(solution)/shard_map/ppermute | solution.py:441
  (385 shorter events, 204.1 us)
Async XLA Ops:
  7.2 74.5 %all-gather.3.cloned.1.call-start = ((), (), s32[]{:S(2)}) async-start(), calls=%async_computation.1 | async-start | bytes 3244032 | tf_op jit(solution)/shard_map/all_gather | solution.py:467
  21.2 186.2 %all-gather.5.cloned.1.call-start = ((), (), s32[]{:S(2)}) async-start(), calls=%async_computation.2 | async-start | bytes 9437184 | tf_op jit(solution)/shard_map/all_gather | solution.py:467
  23.5 493.0 %reduce-scatter.2.cloned.1.call-start = ((), (), s32[]{:S(2)}) async-start(), calls=%async_computation.3 | async-start | bytes 9437184 | tf_op jit(solution)/shard_map/reduce_scatter | solution.py:471
  25.0 19.8 %collective-permute-start.1 = (bf16[344,1024]{1,0:T(8,128)(2,1)}, bf16[344,1024]{1,0:T(8,128)(2,1)S(1)}, u32[]{:S(2)}, u32[]{:S(2)}) collective-permute-start(bf16[344,1024]{1,0:T(8,128)(2,1)} %get-tuple-element.182), channel_id=1, source_target_pairs={{0,2},{2,0},{1,3},{3,1},{4,6},{6,4},{5,7},{7,5},{8,10},{10,8},{9,1... | collective-permute-start | bytes 2113544 | tf_op jit(solution)/shard_map/ppermute | solution.py:441
  28.0 31.1 %collective-permute-start.6 = (bf16[344,1024]{1,0:T(8,128)(2,1)}, bf16[344,1024]{1,0:T(8,128)(2,1)S(1)}, u32[]{:S(2)}, u32[]{:S(2)}) collective-permute-start(bf16[344,1024]{1,0:T(8,128)(2,1)} %get-tuple-element.183), channel_id=1, source_target_pairs={{0,2},{2,0},{1,3},{3,1},{4,6},{6,4},{5,7},{7,5},{8,10},{10,8},{9,1... | collective-permute-start | bytes 2113544 | tf_op jit(solution)/shard_map/ppermute | solution.py:441
  28.0 31.2 %collective-permute-start = (bf16[344,1024]{1,0:T(8,128)(2,1)}, bf16[344,1024]{1,0:T(8,128)(2,1)}, u32[]{:S(2)}, u32[]{:S(2)}) collective-permute-start(bf16[344,1024]{1,0:T(8,128)(2,1)} %get-tuple-element.182), channel_id=1, source_target_pairs={{0,1},{1,0},{2,3},{3,2},{4,5},{5,4},{6,7},{7,6},{8,9},{9,8},{10,11... | collective-permute-start | bytes 2113544 | tf_op jit(solution)/shard_map/ppermute | solution.py:463
  44.8 14.4 %collective-permute-start.2 = (bf16[344,1024]{1,0:T(8,128)(2,1)S(1)}, bf16[344,1024]{1,0:T(8,128)(2,1)}, u32[]{:S(2)}, u32[]{:S(2)}) collective-permute-start(bf16[344,1024]{1,0:T(8,128)(2,1)S(1)} %collective-permute-done.1), channel_id=1, source_target_pairs={{0,1},{1,0},{2,3},{3,2},{4,5},{5,4},{6,7},{7,6},{8,9},{9,8},{10,11... | collective-permute-start | bytes 2113544 | tf_op jit(solution)/shard_map/ppermute | solution.py:463
  44.8 17.6 %collective-permute-start.5 = (bf16[344,1024]{1,0:T(8,128)(2,1)}, bf16[344,1024]{1,0:T(8,128)(2,1)S(1)}, u32[]{:S(2)}, u32[]{:S(2)}) collective-permute-start(bf16[344,1024]{1,0:T(8,128)(2,1)} %get-tuple-element.183), channel_id=1, source_target_pairs={{0,1},{1,0},{2,3},{3,2},{4,5},{5,4},{6,7},{7,6},{8,9},{9,8},{10,11... | collective-permute-start | bytes 2113544 | tf_op jit(solution)/shard_map/ppermute | solution.py:463
  115.9 24.3 %collective-permute-start.8 = (bf16[688,256]{1,0:T(8,128)(2,1)}, bf16[688,256]{1,0:T(8,128)(2,1)}, u32[]{:S(2)}, u32[]{:S(2)}) collective-permute-start(bf16[688,256]{1,0:T(8,128)(2,1)} %bitcast.34), channel_id=1, source_target_pairs={{0,2},{2,0},{1,3},{3,1},{4,6},{6,4},{5,7},{7,5},{8,10},{10,8},{9,1... | collective-permute-start | bytes 1056776 | tf_op jit(solution)/shard_map/ppermute | solution.py:441
  139.0 8.7 %collective-permute-start.3 = (bf16[688,256]{1,0:T(8,128)(2,1)S(1)}, bf16[688,256]{1,0:T(8,128)(2,1)S(1)}, u32[]{:S(2)}, u32[]{:S(2)}) collective-permute-start(bf16[688,256]{1,0:T(8,128)(2,1)S(1)} %bitcast.326), channel_id=1, source_target_pairs={{0,2},{2,0},{1,3},{3,1},{4,6},{6,4},{5,7},{7,5},{8,10},{10,8},{9,1... | collective-permute-start | bytes 1056776 | tf_op jit(solution)/shard_map/ppermute | solution.py:441
  142.4 7.6 %collective-permute-start.9 = (bf16[344,1024]{1,0:T(8,128)(2,1)S(1)}, bf16[344,1024]{1,0:T(8,128)(2,1)S(1)}, u32[]{:S(2)}, u32[]{:S(2)}) collective-permute-start(bf16[344,1024]{1,0:T(8,128)(2,1)S(1)} %slice.482), channel_id=1, source_target_pairs={{0,1},{1,0},{2,3},{3,2},{4,5},{5,4},{6,7},{7,6},{8,9},{9,8},{10,11... | collective-permute-start | bytes 2113544 | tf_op jit(solution)/shard_map/ppermute | solution.py:463
  149.5 16.1 %collective-permute-start.12 = (bf16[688,1024]{1,0:T(8,128)(2,1)}, bf16[688,1024]{1,0:T(8,128)(2,1)}, u32[]{:S(2)}, u32[]{:S(2)}) collective-permute-start(bf16[688,1024]{1,0:T(8,128)(2,1)} %bitcast.47), channel_id=1, source_target_pairs={{0,1},{1,0},{2,3},{3,2},{4,5},{5,4},{6,7},{7,6},{8,9},{9,8},{10,11... | collective-permute-start | bytes 4227080 | tf_op jit(solution)/shard_map/ppermute | solution.py:463
  274.3 9.6 %collective-permute-start.13 = (bf16[688,1024]{1,0:T(8,128)(2,1)}, bf16[688,1024]{1,0:T(8,128)(2,1)}, u32[]{:S(2)}, u32[]{:S(2)}) collective-permute-start(bf16[688,1024]{1,0:T(8,128)(2,1)} %slice.480), channel_id=1, source_target_pairs={{0,1},{1,0},{2,3},{3,2},{4,5},{5,4},{6,7},{7,6},{8,9},{9,8},{10,11... | collective-permute-start | bytes 4227080 | tf_op jit(solution)/shard_map/ppermute | solution.py:463
  283.3 5.2 collective-permute-start.11
  299.1 10.9 %collective-permute-start.14 = (bf16[688,1024]{1,0:T(8,128)(2,1)}, bf16[688,1024]{1,0:T(8,128)(2,1)}, u32[]{:S(2)}, u32[]{:S(2)}) collective-permute-start(bf16[688,1024]{1,0:T(8,128)(2,1)} %multiply_convert_fusion.2), channel_id=1, source_target_pairs={{0,1},{1,0},{2,3},{3,2},{4,5},{5,4},{6,7},{7,6},{8,9},{9,8},{10,11... | collective-permute-start | bytes 4227080 | tf_op jit(solution)/shard_map/ppermute | solution.py:463
  324.3 64.8 %collective-permute-start.18 = (bf16[688,256]{1,0:T(8,128)(2,1)}, bf16[688,256]{1,0:T(8,128)(2,1)}, u32[]{:S(2)}, u32[]{:S(2)}) collective-permute-start(bf16[688,256]{1,0:T(8,128)(2,1)} %bitcast.61), channel_id=1, source_target_pairs={{0,2},{2,0},{1,3},{3,1},{4,6},{6,4},{5,7},{7,5},{8,10},{10,8},{9,1... | collective-permute-start | bytes 1056776 | tf_op jit(solution)/shard_map/ppermute | solution.py:441
  325.7 16.6 %collective-permute-start.15 = (bf16[688,256]{1,0:T(8,128)(2,1)S(1)}, bf16[688,256]{1,0:T(8,128)(2,1)S(1)}, u32[]{:S(2)}, u32[]{:S(2)}) collective-permute-start(bf16[688,256]{1,0:T(8,128)(2,1)S(1)} %bitcast.321), channel_id=1, source_target_pairs={{0,2},{2,0},{1,3},{3,1},{4,6},{6,4},{5,7},{7,5},{8,10},{10,8},{9,1... | collective-permute-start | bytes 1056776 | tf_op jit(solution)/shard_map/ppermute | solution.py:441
  375.8 22.6 %collective-permute-start.16 = (bf16[2,344,1024]{2,1,0:T(8,128)(2,1)}, bf16[2,344,1024]{2,1,0:T(8,128)(2,1)}, u32[]{:S(2)}, u32[]{:S(2)}) collective-permute-start(bf16[2,344,1024]{2,1,0:T(8,128)(2,1)} %slice_bitcast_fusion.2), channel_id=1, source_target_pairs={{0,1},{1,0},{2,3},{3,2},{4,5},{5,4},{6,7},{7,6},{8,9},{9,8},{10,11... | collective-permute-start | bytes 4227080 | tf_op jit(solution)/shard_map/ppermute | solution.py:463
  400.4 26.8 %collective-permute-start.17 = (bf16[344,1024]{1,0:T(8,128)(2,1)S(1)}, bf16[344,1024]{1,0:T(8,128)(2,1)S(1)}, u32[]{:S(2)}, u32[]{:S(2)}) collective-permute-start(bf16[344,1024]{1,0:T(8,128)(2,1)S(1)} %slice_bitcast_fusion.6), channel_id=1, source_target_pairs={{0,2},{2,0},{1,3},{3,1},{4,6},{6,4},{5,7},{7,5},{8,10},{10,8},{9,1... | collective-permute-start | bytes 2113544 | tf_op jit(solution)/shard_map/ppermute | solution.py:441
  449.6 9.7 %collective-permute-start.21 = (bf16[128,1408]{0,1:T(8,128)(2,1)}, bf16[128,1408]{0,1:T(8,128)(2,1)}, u32[]{:S(2)}, u32[]{:S(2)}) collective-permute-start(bf16[128,1408]{0,1:T(8,128)(2,1)} %get-tuple-element.167), channel_id=1, source_target_pairs={{0,8},{8,16},{16,24},{24,28},{28,20},{20,12},{12,4},{4,0},{1,9},{9... | collective-permute-start | bytes 1081352 | tf_op jit(solution)/shard_map/ppermute | solution.py:478
  449.6 13.1 %collective-permute-start.25 = (bf16[128,1408]{0,1:T(8,128)(2,1)S(1)}, bf16[128,1408]{0,1:T(8,128)(2,1)S(1)}, u32[]{:S(2)}, u32[]{:S(2)}) collective-permute-start(bf16[128,1408]{0,1:T(8,128)(2,1)S(1)} %get-tuple-element.168), channel_id=1, source_target_pairs={{0,4},{8,0},{16,8},{24,16},{28,24},{20,28},{12,20},{4,12},{1,5},{9... | collective-permute-start | bytes 1081352 | tf_op jit(solution)/shard_map/ppermute | solution.py:478
  461.2 8.7 %collective-permute-start.22 = (bf16[128,1408]{0,1:T(8,128)(2,1)}, bf16[128,1408]{0,1:T(8,128)(2,1)}, u32[]{:S(2)}, u32[]{:S(2)}) collective-permute-start(bf16[128,1408]{0,1:T(8,128)(2,1)} %fusion.33), channel_id=1, source_target_pairs={{0,8},{8,16},{16,24},{24,28},{28,20},{20,12},{12,4},{4,0},{1,9},{9... | collective-permute-start | bytes 1081352 | tf_op jit(solution)/shard_map/ppermute | solution.py:478
  462.7 21.3 %collective-permute-start.19 = (bf16[2,344,1024]{2,1,0:T(8,128)(2,1)}, bf16[2,344,1024]{2,1,0:T(8,128)(2,1)}, u32[]{:S(2)}, u32[]{:S(2)}) collective-permute-start(bf16[2,344,1024]{2,1,0:T(8,128)(2,1)} %slice_bitcast_fusion), channel_id=1, source_target_pairs={{0,1},{1,0},{2,3},{3,2},{4,5},{5,4},{6,7},{7,6},{8,9},{9,8},{10,11... | collective-permute-start | bytes 4227080 | tf_op jit(solution)/shard_map/ppermute | solution.py:463
  472.1 8.0 %collective-permute-start.23 = (bf16[128,1408]{0,1:T(8,128)(2,1)}, bf16[128,1408]{0,1:T(8,128)(2,1)S(1)}, u32[]{:S(2)}, u32[]{:S(2)}) collective-permute-start(bf16[128,1408]{0,1:T(8,128)(2,1)} %get-tuple-element.165), channel_id=1, source_target_pairs={{0,8},{8,16},{16,24},{24,28},{28,20},{20,12},{12,4},{4,0},{1,9},{9... | collective-permute-start | bytes 1081352 | tf_op jit(solution)/shard_map/ppermute | solution.py:478
  472.7 7.9 %collective-permute-start.26 = (bf16[128,1408]{0,1:T(8,128)(2,1)S(1)}, bf16[128,1408]{0,1:T(8,128)(2,1)}, u32[]{:S(2)}, u32[]{:S(2)}) collective-permute-start(bf16[128,1408]{0,1:T(8,128)(2,1)S(1)} %get-tuple-element.166), channel_id=1, source_target_pairs={{0,4},{8,0},{16,8},{24,16},{28,24},{20,28},{12,20},{4,12},{1,5},{9... | collective-permute-start | bytes 1081352 | tf_op jit(solution)/shard_map/ppermute | solution.py:478
  481.9 8.0 %collective-permute-start.24 = (bf16[128,1408]{0,1:T(8,128)(2,1)S(1)}, bf16[128,1408]{0,1:T(8,128)(2,1)S(1)}, u32[]{:S(2)}, u32[]{:S(2)}) collective-permute-start(bf16[128,1408]{0,1:T(8,128)(2,1)S(1)} %get-tuple-element.163), channel_id=1, source_target_pairs={{0,8},{8,16},{16,24},{24,28},{28,20},{20,12},{12,4},{4,0},{1,9},{9... | collective-permute-start | bytes 1081352 | tf_op jit(solution)/shard_map/ppermute | solution.py:478
  483.7 7.4 %collective-permute-start.27 = (bf16[128,1408]{0,1:T(8,128)(2,1)S(1)}, bf16[128,1408]{0,1:T(8,128)(2,1)S(1)}, u32[]{:S(2)}, u32[]{:S(2)}) collective-permute-start(bf16[128,1408]{0,1:T(8,128)(2,1)S(1)} %get-tuple-element.164), channel_id=1, source_target_pairs={{0,4},{8,0},{16,8},{24,16},{28,24},{20,28},{12,20},{4,12},{1,5},{9... | collective-permute-start | bytes 1081352 | tf_op jit(solution)/shard_map/ppermute | solution.py:478
  487.9 23.6 %collective-permute-start.20 = (bf16[344,1024]{1,0:T(8,128)(2,1)}, bf16[344,1024]{1,0:T(8,128)(2,1)}, u32[]{:S(2)}, u32[]{:S(2)}) collective-permute-start(bf16[344,1024]{1,0:T(8,128)(2,1)} %slice_bitcast_fusion.4), channel_id=1, source_target_pairs={{0,2},{2,0},{1,3},{3,1},{4,6},{6,4},{5,7},{7,5},{8,10},{10,8},{9,1... | collective-permute-start | bytes 2113544 | tf_op jit(solution)/shard_map/ppermute | solution.py:441
  492.3 17.9 %collective-permute-start.28 = (bf16[128,1408]{0,1:T(8,128)(2,1)S(1)}, bf16[128,1408]{0,1:T(8,128)(2,1)S(1)}, u32[]{:S(2)}, u32[]{:S(2)}) collective-permute-start(bf16[128,1408]{0,1:T(8,128)(2,1)S(1)} %fusion.35), channel_id=1, source_target_pairs={{0,2},{2,0},{1,3},{3,1},{4,6},{6,4},{5,7},{7,5},{8,10},{10,8},{9,1... | collective-permute-start | bytes 1081352 | tf_op jit(solution)/shard_map/ppermute | solution.py:441
  511.5 32.5 %collective-permute-start.29 = (bf16[2,128,1408]{1,2,0:T(8,128)(2,1)}, bf16[2,128,1408]{1,2,0:T(8,128)(2,1)}, u32[]{:S(2)}, u32[]{:S(2)}) collective-permute-start(bf16[2,128,1408]{1,2,0:T(8,128)(2,1)} %fusion.28), channel_id=1, source_target_pairs={{0,1},{1,0},{2,3},{3,2},{4,5},{5,4},{6,7},{7,6},{8,9},{9,8},{10,11... | collective-permute-start | bytes 2162696 | tf_op jit(solution)/shard_map/ppermute | solution.py:463
  516.5 25.9 %collective-permute-start.30 = (bf16[512,1024]{1,0:T(8,128)(2,1)}, bf16[512,1024]{1,0:T(8,128)(2,1)}, u32[]{:S(2)}, u32[]{:S(2)}) collective-permute-start(bf16[512,1024]{1,0:T(8,128)(2,1)} %reduce-scatter.2.cloned.1.call-done), channel_id=1, source_target_pairs={{0,2},{2,0},{1,3},{3,1},{4,6},{6,4},{5,7},{7,5},{8,10},{10,8},{9,1... | collective-permute-start | bytes 3145736 | tf_op jit(solution)/shard_map/ppermute | solution.py:441
  544.0 8.7 %collective-permute-start.31 = (bf16[512,1024]{1,0:T(8,128)(2,1)S(1)}, bf16[512,1024]{1,0:T(8,128)(2,1)}, u32[]{:S(2)}, u32[]{:S(2)}) collective-permute-start(bf16[512,1024]{1,0:T(8,128)(2,1)S(1)} %add_convert_fusion.2), channel_id=1, source_target_pairs={{0,1},{1,0},{2,3},{3,2},{4,5},{5,4},{6,7},{7,6},{8,9},{9,8},{10,11... | collective-permute-start | bytes 3145736 | tf_op jit(solution)/shard_map/ppermute | solution.py:463
  (83 other events, 733.7 us)
Sparse Core Ops, SparseCore 0:
  21.3 60.3 all-gather.2
  83.9 123.5 all-gather.4
  284.0 147.2 reduce-scatter.1

commit v6 on v5

--- a/solution.py
+++ b/solution.py
@@ -699,32 +699,26 @@
     grad_attend_scale = jnp.sum(grad_residual * branch_attend, 0)
     grad_attend = (scale_a * grad_residual).astype(BF)
     grad_output_bias = column_total(grad_attend)
-    grad_attend = jnp.concatenate([grad_attend, other_core(grad_attend)], 0)
-    grad_attended = dot_right_t(grad_attend, output_whole).astype(BF)
-    grad_attended = grad_attended.reshape(2, groups, rows, far_count, head_width)
-    grad_sides = grad_attend.reshape(2, groups, rows, width)
+    grad_other = other_core(grad_attend)
+    grad_sides = []
+    for group in range(groups):
+        part = slice(group * rows, (group + 1) * rows)
+        grad_sides.append(jnp.concatenate([grad_attend[part], grad_other[part]], 0))
+    grad_attended = [
+        [
+            dot_right_t(side, output_whole[r * head_width : (r + 1) * head_width]).astype(BF)
+            for r in range(far_count)
+        ]
+        for side in grad_sides
+    ]
     grad_output_weight = sum(
-        dot_left_t(attended_rows[group], grad_sides[:, group].reshape(2 * rows, width))
-        for group in range(groups)
+        dot_left_t(attended_rows[group], grad_sides[group]) for group in range(groups)
     ).astype(BF)
     grad_output_weight = jnp.roll(
         grad_output_weight.reshape(far_count, head_width, width), far, 0
     ).reshape(width // 2, width)
 
-    grad_heads = [
-        to_kernel(
-            jnp.stack(
-                far_exchange(
-                    [
-                        grad_attended[:, group, :, r].reshape(2 * rows, head_width)
-                        for r in range(far_count)
-                    ]
-                ),
-                0,
-            )
-        )
-        for group in range(groups)
-    ]
+    grad_heads = [to_kernel(jnp.stack(far_exchange(parts), 0)) for parts in grad_attended]
     upper_parts, grad_triples = [], []
     grad_first_gain = grad_first_shift = column_sums = 0.0
     for group in range(groups):
@@ -763,6 +757,12 @@
     normal, factor = normalize(inputs)
     grad_images = grad_residual + normalize_back(normal, factor, upper * gain_1)
 
+    def far_total(array):
+        total = array.astype(F32)
+        for r in range(1, far_count):
+            total = total + far_send(array, r).astype(F32)
+        return total
+
     def place_heads(vector):
         here = jnp.arange(far_count)[:, None, None, None] == far
         here = here & (jnp.arange(2)[None, None, :, None] == core)
@@ -785,9 +785,11 @@
     sums = jnp.pad(sums, ((0, 0), (0, -sums.shape[1] % 128)))
     grad_output_weight = grad_output_weight.reshape(fsdp_count, shard // 2, 2, width // 2)
     grad_output_weight = grad_output_weight.transpose(0, 2, 1, 3).reshape(width, width // 2)
+    grad_triple_weight = after(grad_triple_weight, partial)
     grad_packed = jnp.concatenate([grad_triple_weight, sums, grad_output_weight], 1)
     grad_packed = ring_scatter(grad_packed.reshape(fsdp_count, shard, -1)).astype(BF)
-    feed_sums = after(feed_sums, grad_packed)
+    feed_sums = far_total(feed_sums).astype(BF)
+    grad_packed = after(grad_packed, feed_sums, *moved)
     grad_packed = jnp.roll(jnp.stack(far_gather(grad_packed), 0), far, 0)
     grad_packed = core_join(grad_packed, 1, core)
     grad_triple_weight = (
@@ -805,13 +807,7 @@
         .reshape(shard, width)
     )
 
-    def far_total(array):
-        total = array.astype(F32)
-        for r in range(1, far_count):
-            total = total + far_send(array, r).astype(F32)
-        return total
-
-    feed_sums = core_join(far_total(feed_sums).astype(BF), 0, core).astype(F32)
+    feed_sums = core_join(feed_sums, 0, core).astype(F32)
     grad_expand_weight = (
         feed_sums[:, : blocks * shard]
         .reshape(2, blocks, shard, -1, unit_part)

time: 577 us -> 539 us (0.934)
  waiting for transfers between devices: 153 us -> 137 us
  other arithmetic: 81.6 us -> 68.3 us
    ppermute x7, waiting for transfers between devices: 22.6 us -> 11.6 us  [ring_send(): return lax.ppermute(array, 'fsdp', pairs)]
    dot_general x4 -> x7, matrix products: 22.6 us -> 20.6 us  [dot_right_t(): lax.dot_general(left, right, (((1,), (1,)), ((), ())), preferred_element_...]
    unnamed x166 -> x180, local copies, waits for them, and re-layouts: 28.9 us -> 31 us
  transfers between devices with their start and end apart: 35 -> 35, of which waited for: 14 -> 12; matrix products, arithmetic and copies ran while one was open for 29% -> 29% of each run, Pallas kernels for 17% -> 18%
where the time goes in v6:
time: 539 us; the launch traced here: 535 us
  waiting for transfers between devices  137 us (25%)
  Pallas kernels  137 us (25%)
  local copies, waits for them, and re-layouts  104 us (19%)
  other arithmetic  68.3 us (13%)
  matrix products  55 us (10%)
  starting transfers between devices  18.8 us (3%)
  between operations  15.6 us (3%)
    ppermute x10, waiting for transfers between devices, far_send(): lax.ppermute(array, 'far', [(i, (i + shift) % count) for i in range(count)])  74.2 us
    pallas_call x2, Pallas kernels, attend_backward(): pl.pallas_call(attend_backward_kernel, grid_spec=pltpu.PrefetchScalarGrid...  50.9 us
    all_gather x2, waiting for transfers between devices, fsdp_gather(): return lax.all_gather(array, 'fsdp', axis=0, tiled=True)  48.7 us
    unnamed x180, local copies, waits for them, and re-layouts  31 us
    pallas_call x2, Pallas kernels, attend_forward(): pl.pallas_call(attend_forward_kernel, grid_spec=pltpu.PrefetchScalarGridS...  30.4 us
    dot_general x7, matrix products, dot_right_t(): lax.dot_general(left, right, (((1,), (1,)), ((), ())), preferred_element_...  20.6 us
    pallas_call x1, Pallas kernels, feed_grads(): pl.pallas_call(feed_grads_kernel, grid=(devices,), in_specs=[pl.BlockSpec...  19.8 us
    pallas_call x1, Pallas kernels, expand_rows(): pl.pallas_call(expand_kernel, grid=(units // tile,), in_specs=[pl.BlockSp...  19.1 us
  transfers between devices with their start and end apart: 35, of which 12 were waited for; matrix products, arithmetic and copies ran while one was open for 29% of the time, Pallas kernels for 18%

profile of v6, /device:TPU:0, one launch (start us, length us, event | category | flops | bytes accessed | tf_op | source)
XLA Modules:
  0.0 534.8 jit_solution(6829809306736894351)
XLA Ops:
  27.5 16.8 %collective-permute-done.1 = bf16[344,1024]{1,0:T(8,128)(2,1)S(1)} collective-permute-done((bf16[344,1024]{1,0:T(8,128)(2,1)}, bf16[344,1024]{1,0:T(8,128)(2,1)S(1)}, u32[]{:S(2)}, u32[]{:S(2)}) %collective-permute-start.1) | collective-permute-done | bytes 704544 | tf_op jit(solution)/shard_map/ppermute | solution.py:441
  44.8 13.8 %collective-permute-done.6 = bf16[344,1024]{1,0:T(8,128)(2,1)S(1)} collective-permute-done((bf16[344,1024]{1,0:T(8,128)(2,1)}, bf16[344,1024]{1,0:T(8,128)(2,1)S(1)}, u32[]{:S(2)}, u32[]{:S(2)}) %collective-permute-start.6) | collective-permute-done | bytes 704544 | tf_op jit(solution)/shard_map/ppermute | solution.py:441
  64.5 15.9 %all-gather.3.cloned.1.call-done = bf16[1024,1408]{1,0:T(8,128)(2,1)} async-done(((bf16[128,1408]{1,0:T(8,128)(2,1)}), bf16[1024,1408]{1,0:T(8,128)(2,1)}) %all-gather.3.cloned.1.call-update) | async-done | bytes 2883600 | tf_op jit(solution)/shard_map/all_gather | solution.py:467
  91.7 4.4 project.3
  98.9 14.7 %attend_forward.3 = (bf16[4,1,344,256]{3,2,1,0:T(8,128)(2,1)S(1)}, f32[1,2,1376,128]{3,2,1,0:T(8,128)S(1)}) custom-call(s32[1,2]{1,0:T(1,128)S(1)} %get-tuple-element.208.limit_ref, bf16[4,1,344,768]{3,2,1,0:T(8,128)(2,1)} %bitcast.254, bf16[4,1,344,768]{3,2,1,0:T(8,128)(2,1)} %bitcast.255, bf16[4,1,344,768]{3,2,1,0:T(8,128)(2,1)} %bitcast.256), custom_call_target="tpu_custom_call" | custom-call | flops 7755268096 | bytes 4227072 | tf_op jit(solution)/shard_map/attend_forward/pallas_call | solution.py:202
  116.4 4.6 project.2
  122.4 15.7 %attend_forward.2 = (bf16[4,1,344,256]{3,2,1,0:T(8,128)(2,1)S(1)}, f32[1,2,1376,128]{3,2,1,0:T(8,128)S(1)}) custom-call(s32[1,2]{1,0:T(1,128)S(1)} %get-tuple-element.207.limit_ref, bf16[4,1,344,768]{3,2,1,0:T(8,128)(2,1)} %bitcast.260, bf16[4,1,344,768]{3,2,1,0:T(8,128)(2,1)} %bitcast.261, bf16[4,1,344,768]{3,2,1,0:T(8,128)(2,1)} %bitcast.262), custom_call_target="tpu_custom_call" | custom-call | flops 7755268096 | bytes 4227072 | tf_op jit(solution)/shard_map/attend_forward/pallas_call | solution.py:202
  141.5 5.3 collective-permute-done.3
  158.5 5.0 add_convert_fusion.1
  166.0 4.1 multiply_convert_fusion.1.feed_ref
  170.1 3.7 pad_maximum_fusion.4.rows_ref
  173.7 32.9 %all-gather.5.cloned.1.call-done = bf16[4096,1024]{1,0:T(8,128)(2,1)} async-done(((bf16[512,1024]{1,0:T(8,128)(2,1)}), bf16[4096,1024]{1,0:T(8,128)(2,1)}) %all-gather.5.cloned.1.call-update) | async-done | bytes 8388624 | tf_op jit(solution)/shard_map/all_gather | solution.py:467
  206.6 4.9 slice.353
  215.4 19.1 %expand_rows.1 = (bf16[1376,2048]{1,0:T(8,128)(2,1)}, bf16[1376,2048]{1,0:T(8,128)(2,1)}) custom-call(bf16[1376,1024]{1,0:T(8,128)(2,1)S(1)} %copy-done.8, bf16[8,512,1024]{2,1,0:T(8,128)(2,1)} %bitcast.274, f32[1,2048]{1,0:T(1,128)S(1)} %reshape.473.bias_ref), custom_call_target="tpu_custom_call" | custom-call | flops 11542724608 | bytes 18284544 | tf_op jit(solution)/shard_map/expand_rows/pallas_call | solution.py:377
  234.5 9.8 %multiply_convert_fusion.expanded_ref = bf16[1376,2048]{1,0:T(8,128)(2,1)} fusion(bf16[1376,2048]{1,0:T(8,128)(2,1)} %get-tuple-element.47, bf16[1376,1024]{1,0:T(8,128)(2,1)S(1)} %copy-done.43, bf16[2048,1024]{1,0:T(8,128)(2,1)S(1)} %bitcast.279), kind=kOutput, calls=%fused_computation | convolution fusion | flops 5779816448 | bytes 18284544 | tf_op jit(solution)/shard_map/dot_general | solution.py:26
  244.3 19.8 %feed_grads.1 = bf16[8,512,1024]{2,1,0:T(8,128)(2,1)} custom-call(bf16[1376,1024]{1,0:T(8,128)(2,1)} %pad_maximum_fusion.4.rows_ref, bf16[1376,2048]{1,0:T(8,128)(2,1)} %get-tuple-element.46.active_ref, bf16[1376,2048]{1,0:T(8,128)(2,1)} %multiply_convert_fusion.expanded_ref, bf16[1376,1024]{1,0:T(8,128)(2,1)} %multiply_convert_fusion.1.feed_ref), custom_call_target="tpu_custom_call" | custom-call | flops 11542724608 | bytes 25296896 | tf_op jit(solution)/shard_map/feed_grads/pallas_call | solution.py:418
  272.1 9.1 %fusion.71 = f32[1376,1024]{1,0:T(8,128)S(1)} fusion(bf16[1376,2048]{1,0:T(8,128)(2,1)} %get-tuple-element.46.active_ref, bf16[2048,1024]{1,0:T(8,128)(2,1)S(1)} %bitcast.280), kind=kOutput, calls=%fused_computation.226 | convolution fusion | flops 5771362304 | bytes 15466496 | tf_op jit(solution)/shard_map/dot_general | solution.py:18
  286.4 4.5 multiply_reduce_fusion
  291.8 6.1 %fusion.1 = (bf16[1024]{0:T(1024)(128)(2,1)S(1)}, bf16[688,1024]{1,0:T(8,128)(2,1)}, bf16[1024]{0:T(1024)(128)(2,1)S(1)}, f32[688,1024]{1,0:T(8,128)S(1)}) fusion(bf16[688,1024]{1,0:T(8,128)(2,1)} %collective-permute-done.11, f32[1376,1024]{1,0:T(8,128)} %copy-done.52, f32[1024]{0:T(1024)S(1)} %get-tuple-element.143, bf16[2,344,1024]{2,1,0:T(8,128)(2,1)} %param.21, ...), kind=kLoop, calls=%fused_computation.8 | loop fusion | flops 15497216 | bytes 19753728 | tf_op jit(solution)/shard_map/reduce_sum | solution.py:684
  322.3 11.3 %collective-permute-done.15 = bf16[688,256]{1,0:T(8,128)(2,1)S(1)} collective-permute-done((bf16[688,256]{1,0:T(8,128)(2,1)S(1)}, bf16[688,256]{1,0:T(8,128)(2,1)S(1)}, u32[]{:S(2)}, u32[]{:S(2)}) %collective-permute-start.15) | collective-permute-done | bytes 352288 | tf_op jit(solution)/shard_map/ppermute | solution.py:441
  334.5 25.7 %attend_backward.2 = bf16[4,1,344,768]{3,2,1,0:T(8,128)(2,1)} custom-call(s32[1,2]{1,0:T(1,128)} %copy-done.15, bf16[4,1,344,768]{3,2,1,0:T(8,128)(2,1)} %bitcast.263, bf16[4,1,344,768]{3,2,1,0:T(8,128)(2,1)} %bitcast.264, bf16[4,1,344,768]{3,2,1,0:T(8,128)(2,1)} %bitcast.265, bf16[4,1,344,256]{3,2,1,0:T(8,128)(2,1)} %copy-done.13, ...), custom_call_target="tpu_custom_call" | custom-call | flops 19388170240 | bytes 8454144 | tf_op jit(solution)/shard_map/attend_backward/pallas_call | solution.py:236
  361.9 3.9 project_back.2
  382.4 4.4 fusion.72
  390.4 25.2 %attend_backward.3 = bf16[4,1,344,768]{3,2,1,0:T(8,128)(2,1)} custom-call(s32[1,2]{1,0:T(1,128)} %copy-done.14, bf16[4,1,344,768]{3,2,1,0:T(8,128)(2,1)} %bitcast.257, bf16[4,1,344,768]{3,2,1,0:T(8,128)(2,1)} %bitcast.258, bf16[4,1,344,768]{3,2,1,0:T(8,128)(2,1)} %bitcast.259, bf16[4,1,344,256]{3,2,1,0:T(8,128)(2,1)} %copy-done.12, ...), custom_call_target="tpu_custom_call" | custom-call | flops 19388170240 | bytes 8454144 | tf_op jit(solution)/shard_map/attend_backward/pallas_call | solution.py:236
  418.1 3.9 project_back.3
  427.0 6.7 %fusion = bf16[1024,768]{1,0:T(8,128)(2,1)} fusion(f32[1024,768]{1,0:T(8,128)} %fusion.72, bf16[4,344,1024]{2,1,0:T(8,128)(2,1)} %copy-done.24, bf16[4,344,768]{2,1,0:T(8,128)(2,1)S(1)} %bitcast.267), kind=kOutput, calls=%fused_computation.6 | convolution fusion | flops 2165833728 | bytes 9650176 | tf_op jit(solution)/shard_map/dot_general | solution.py:22
  442.6 7.4 %collective-permute-done.21 = bf16[128,1408]{0,1:T(8,128)(2,1)S(1)} collective-permute-done((bf16[128,1408]{0,1:T(8,128)(2,1)S(1)}, bf16[128,1408]{0,1:T(8,128)(2,1)S(1)}, u32[]{:S(2)}, u32[]{:S(2)}) %collective-permute-start.21) | collective-permute-done | bytes 360480 | tf_op jit(solution)/shard_map/ppermute | solution.py:478
  450.5 8.6 %collective-permute-done.20 = bf16[344,1024]{1,0:T(8,128)(2,1)S(1)} collective-permute-done((bf16[344,1024]{1,0:T(8,128)(2,1)S(1)}, bf16[344,1024]{1,0:T(8,128)(2,1)S(1)}, u32[]{:S(2)}, u32[]{:S(2)}) %collective-permute-start.20) | collective-permute-done | bytes 704544 | tf_op jit(solution)/shard_map/ppermute | solution.py:441
  468.3 4.2 collective-permute-done.23
  478.0 11.4 %collective-permute-done.28 = bf16[512,1024]{1,0:T(8,128)(2,1)} collective-permute-done((bf16[512,1024]{1,0:T(8,128)(2,1)}, bf16[512,1024]{1,0:T(8,128)(2,1)}, u32[]{:S(2)}, u32[]{:S(2)}) %collective-permute-start.28) | collective-permute-done | bytes 1048608 | tf_op jit(solution)/shard_map/ppermute | solution.py:441
  497.4 7.1 %collective-permute-done.29 = bf16[128,1408]{0,1:T(8,128)(2,1)S(1)} collective-permute-done((bf16[128,1408]{0,1:T(8,128)(2,1)S(1)}, bf16[128,1408]{0,1:T(8,128)(2,1)S(1)}, u32[]{:S(2)}, u32[]{:S(2)}) %collective-permute-start.29) | collective-permute-done | bytes 360480 | tf_op jit(solution)/shard_map/ppermute | solution.py:441
  513.7 3.9 reshape.491
  (399 shorter events, 185.4 us)
Async XLA Ops:
  7.2 73.1 %all-gather.3.cloned.1.call-start = ((), (), s32[]{:S(2)}) async-start(), calls=%async_computation.1 | async-start | bytes 3244032 | tf_op jit(solution)/shard_map/all_gather | solution.py:467
  19.8 186.8 %all-gather.5.cloned.1.call-start = ((), (), s32[]{:S(2)}) async-start(), calls=%async_computation.2 | async-start | bytes 9437184 | tf_op jit(solution)/shard_map/all_gather | solution.py:467
  23.0 441.9 %reduce-scatter.2.cloned.1.call-start = ((), (), s32[]{:S(2)}) async-start(), calls=%async_computation.3 | async-start | bytes 9437184 | tf_op jit(solution)/shard_map/reduce_scatter | solution.py:471
  24.5 19.8 %collective-permute-start.1 = (bf16[344,1024]{1,0:T(8,128)(2,1)}, bf16[344,1024]{1,0:T(8,128)(2,1)S(1)}, u32[]{:S(2)}, u32[]{:S(2)}) collective-permute-start(bf16[344,1024]{1,0:T(8,128)(2,1)} %get-tuple-element.182), channel_id=1, source_target_pairs={{0,2},{2,0},{1,3},{3,1},{4,6},{6,4},{5,7},{7,5},{8,10},{10,8},{9,1... | collective-permute-start | bytes 2113544 | tf_op jit(solution)/shard_map/ppermute | solution.py:441
  27.5 31.1 %collective-permute-start.6 = (bf16[344,1024]{1,0:T(8,128)(2,1)}, bf16[344,1024]{1,0:T(8,128)(2,1)S(1)}, u32[]{:S(2)}, u32[]{:S(2)}) collective-permute-start(bf16[344,1024]{1,0:T(8,128)(2,1)} %get-tuple-element.183), channel_id=1, source_target_pairs={{0,2},{2,0},{1,3},{3,1},{4,6},{6,4},{5,7},{7,5},{8,10},{10,8},{9,1... | collective-permute-start | bytes 2113544 | tf_op jit(solution)/shard_map/ppermute | solution.py:441
  27.5 31.2 %collective-permute-start = (bf16[344,1024]{1,0:T(8,128)(2,1)}, bf16[344,1024]{1,0:T(8,128)(2,1)}, u32[]{:S(2)}, u32[]{:S(2)}) collective-permute-start(bf16[344,1024]{1,0:T(8,128)(2,1)} %get-tuple-element.182), channel_id=1, source_target_pairs={{0,1},{1,0},{2,3},{3,2},{4,5},{5,4},{6,7},{7,6},{8,9},{9,8},{10,11... | collective-permute-start | bytes 2113544 | tf_op jit(solution)/shard_map/ppermute | solution.py:463
  44.3 14.4 %collective-permute-start.2 = (bf16[344,1024]{1,0:T(8,128)(2,1)S(1)}, bf16[344,1024]{1,0:T(8,128)(2,1)}, u32[]{:S(2)}, u32[]{:S(2)}) collective-permute-start(bf16[344,1024]{1,0:T(8,128)(2,1)S(1)} %collective-permute-done.1), channel_id=1, source_target_pairs={{0,1},{1,0},{2,3},{3,2},{4,5},{5,4},{6,7},{7,6},{8,9},{9,8},{10,11... | collective-permute-start | bytes 2113544 | tf_op jit(solution)/shard_map/ppermute | solution.py:463
  44.3 17.6 %collective-permute-start.5 = (bf16[344,1024]{1,0:T(8,128)(2,1)}, bf16[344,1024]{1,0:T(8,128)(2,1)S(1)}, u32[]{:S(2)}, u32[]{:S(2)}) collective-permute-start(bf16[344,1024]{1,0:T(8,128)(2,1)} %get-tuple-element.183), channel_id=1, source_target_pairs={{0,1},{1,0},{2,3},{3,2},{4,5},{5,4},{6,7},{7,6},{8,9},{9,8},{10,11... | collective-permute-start | bytes 2113544 | tf_op jit(solution)/shard_map/ppermute | solution.py:463
  114.8 24.3 %collective-permute-start.8 = (bf16[688,256]{1,0:T(8,128)(2,1)S(1)}, bf16[688,256]{1,0:T(8,128)(2,1)}, u32[]{:S(2)}, u32[]{:S(2)}) collective-permute-start(bf16[688,256]{1,0:T(8,128)(2,1)S(1)} %bitcast.320), channel_id=1, source_target_pairs={{0,2},{2,0},{1,3},{3,1},{4,6},{6,4},{5,7},{7,5},{8,10},{10,8},{9,1... | collective-permute-start | bytes 1056776 | tf_op jit(solution)/shard_map/ppermute | solution.py:441
  138.2 8.7 %collective-permute-start.3 = (bf16[688,256]{1,0:T(8,128)(2,1)S(1)}, bf16[688,256]{1,0:T(8,128)(2,1)S(1)}, u32[]{:S(2)}, u32[]{:S(2)}) collective-permute-start(bf16[688,256]{1,0:T(8,128)(2,1)S(1)} %bitcast.321), channel_id=1, source_target_pairs={{0,2},{2,0},{1,3},{3,1},{4,6},{6,4},{5,7},{7,5},{8,10},{10,8},{9,1... | collective-permute-start | bytes 1056776 | tf_op jit(solution)/shard_map/ppermute | solution.py:441
  141.4 7.7 %collective-permute-start.9 = (bf16[344,1024]{1,0:T(8,128)(2,1)S(1)}, bf16[344,1024]{1,0:T(8,128)(2,1)S(1)}, u32[]{:S(2)}, u32[]{:S(2)}) collective-permute-start(bf16[344,1024]{1,0:T(8,128)(2,1)S(1)} %slice.498), channel_id=1, source_target_pairs={{0,1},{1,0},{2,3},{3,2},{4,5},{5,4},{6,7},{7,6},{8,9},{9,8},{10,11... | collective-permute-start | bytes 2113544 | tf_op jit(solution)/shard_map/ppermute | solution.py:463
  148.7 17.3 %collective-permute-start.12 = (bf16[688,1024]{1,0:T(8,128)(2,1)}, bf16[688,1024]{1,0:T(8,128)(2,1)}, u32[]{:S(2)}, u32[]{:S(2)}) collective-permute-start(bf16[688,1024]{1,0:T(8,128)(2,1)} %bitcast.47), channel_id=1, source_target_pairs={{0,1},{1,0},{2,3},{3,2},{4,5},{5,4},{6,7},{7,6},{8,9},{9,8},{10,11... | collective-permute-start | bytes 4227080 | tf_op jit(solution)/shard_map/ppermute | solution.py:463
  272.1 14.3 %collective-permute-start.13 = (bf16[688,1024]{1,0:T(8,128)(2,1)}, bf16[688,1024]{1,0:T(8,128)(2,1)}, u32[]{:S(2)}, u32[]{:S(2)}) collective-permute-start(bf16[688,1024]{1,0:T(8,128)(2,1)} %slice.496), channel_id=1, source_target_pairs={{0,1},{1,0},{2,3},{3,2},{4,5},{5,4},{6,7},{7,6},{8,9},{9,8},{10,11... | collective-permute-start | bytes 4227080 | tf_op jit(solution)/shard_map/ppermute | solution.py:463
  284.1 6.9 %collective-permute-start.11 = (bf16[688,1024]{1,0:T(8,128)(2,1)}, bf16[688,1024]{1,0:T(8,128)(2,1)}, u32[]{:S(2)}, u32[]{:S(2)}) collective-permute-start(bf16[688,1024]{1,0:T(8,128)(2,1)} %slice.497), channel_id=1, source_target_pairs={{0,1},{1,0},{2,3},{3,2},{4,5},{5,4},{6,7},{7,6},{8,9},{9,8},{10,11... | collective-permute-start | bytes 4227080 | tf_op jit(solution)/shard_map/ppermute | solution.py:463
  300.9 11.8 %collective-permute-start.14 = (bf16[688,1024]{1,0:T(8,128)(2,1)}, bf16[688,1024]{1,0:T(8,128)(2,1)}, u32[]{:S(2)}, u32[]{:S(2)}) collective-permute-start(bf16[688,1024]{1,0:T(8,128)(2,1)} %multiply_convert_fusion.2), channel_id=1, source_target_pairs={{0,1},{1,0},{2,3},{3,2},{4,5},{5,4},{6,7},{7,6},{8,9},{9,8},{10,11... | collective-permute-start | bytes 4227080 | tf_op jit(solution)/shard_map/ppermute | solution.py:463
  315.7 64.8 %collective-permute-start.18 = (bf16[688,256]{1,0:T(8,128)(2,1)}, bf16[688,256]{1,0:T(8,128)(2,1)}, u32[]{:S(2)}, u32[]{:S(2)}) collective-permute-start(bf16[688,256]{1,0:T(8,128)(2,1)} %convolution_convert_fusion), channel_id=1, source_target_pairs={{0,2},{2,0},{1,3},{3,1},{4,6},{6,4},{5,7},{7,5},{8,10},{10,8},{9,1... | collective-permute-start | bytes 1056776 | tf_op jit(solution)/shard_map/ppermute | solution.py:441
  317.8 15.8 %collective-permute-start.15 = (bf16[688,256]{1,0:T(8,128)(2,1)S(1)}, bf16[688,256]{1,0:T(8,128)(2,1)S(1)}, u32[]{:S(2)}, u32[]{:S(2)}) collective-permute-start(bf16[688,256]{1,0:T(8,128)(2,1)S(1)} %convolution_convert_fusion.2), channel_id=1, source_target_pairs={{0,2},{2,0},{1,3},{3,1},{4,6},{6,4},{5,7},{7,5},{8,10},{10,8},{9,1... | collective-permute-start | bytes 1056776 | tf_op jit(solution)/shard_map/ppermute | solution.py:441
  367.0 19.9 %collective-permute-start.16 = (bf16[2,344,1024]{2,1,0:T(8,128)(2,1)}, bf16[2,344,1024]{2,1,0:T(8,128)(2,1)}, u32[]{:S(2)}, u32[]{:S(2)}) collective-permute-start(bf16[2,344,1024]{2,1,0:T(8,128)(2,1)} %slice_bitcast_fusion.2), channel_id=1, source_target_pairs={{0,1},{1,0},{2,3},{3,2},{4,5},{5,4},{6,7},{7,6},{8,9},{9,8},{10,11... | collective-permute-start | bytes 4227080 | tf_op jit(solution)/shard_map/ppermute | solution.py:463
  388.8 26.8 %collective-permute-start.17 = (bf16[344,1024]{1,0:T(8,128)(2,1)S(1)}, bf16[344,1024]{1,0:T(8,128)(2,1)S(1)}, u32[]{:S(2)}, u32[]{:S(2)}) collective-permute-start(bf16[344,1024]{1,0:T(8,128)(2,1)S(1)} %slice_bitcast_fusion.6), channel_id=1, source_target_pairs={{0,2},{2,0},{1,3},{3,1},{4,6},{6,4},{5,7},{7,5},{8,10},{10,8},{9,1... | collective-permute-start | bytes 2113544 | tf_op jit(solution)/shard_map/ppermute | solution.py:441
  426.5 7.3 %collective-permute-start.19 = (bf16[2,344,1024]{2,1,0:T(8,128)(2,1)}, bf16[2,344,1024]{2,1,0:T(8,128)(2,1)}, u32[]{:S(2)}, u32[]{:S(2)}) collective-permute-start(bf16[2,344,1024]{2,1,0:T(8,128)(2,1)} %slice_bitcast_fusion), channel_id=1, source_target_pairs={{0,1},{1,0},{2,3},{3,2},{4,5},{5,4},{6,7},{7,6},{8,9},{9,8},{10,11... | collective-permute-start | bytes 4227080 | tf_op jit(solution)/shard_map/ppermute | solution.py:463
  439.1 10.9 %collective-permute-start.21 = (bf16[128,1408]{0,1:T(8,128)(2,1)S(1)}, bf16[128,1408]{0,1:T(8,128)(2,1)S(1)}, u32[]{:S(2)}, u32[]{:S(2)}) collective-permute-start(bf16[128,1408]{0,1:T(8,128)(2,1)S(1)} %get-tuple-element.169), channel_id=1, source_target_pairs={{0,8},{8,16},{16,24},{24,28},{28,20},{20,12},{12,4},{4,0},{1,9},{9... | collective-permute-start | bytes 1081352 | tf_op jit(solution)/shard_map/ppermute | solution.py:478
  440.7 18.3 %collective-permute-start.20 = (bf16[344,1024]{1,0:T(8,128)(2,1)S(1)}, bf16[344,1024]{1,0:T(8,128)(2,1)S(1)}, u32[]{:S(2)}, u32[]{:S(2)}) collective-permute-start(bf16[344,1024]{1,0:T(8,128)(2,1)S(1)} %slice_bitcast_fusion.4), channel_id=1, source_target_pairs={{0,2},{2,0},{1,3},{3,1},{4,6},{6,4},{5,7},{7,5},{8,10},{10,8},{9,1... | collective-permute-start | bytes 2113544 | tf_op jit(solution)/shard_map/ppermute | solution.py:441
  442.0 19.2 %collective-permute-start.25 = (bf16[128,1408]{0,1:T(8,128)(2,1)S(1)}, bf16[128,1408]{0,1:T(8,128)(2,1)S(1)}, u32[]{:S(2)}, u32[]{:S(2)}) collective-permute-start(bf16[128,1408]{0,1:T(8,128)(2,1)S(1)} %get-tuple-element.170), channel_id=1, source_target_pairs={{0,4},{8,0},{16,8},{24,16},{28,24},{20,28},{12,20},{4,12},{1,5},{9... | collective-permute-start | bytes 1081352 | tf_op jit(solution)/shard_map/ppermute | solution.py:478
  450.1 11.2 %collective-permute-start.22 = (bf16[128,1408]{0,1:T(8,128)(2,1)S(1)}, bf16[128,1408]{0,1:T(8,128)(2,1)S(1)}, u32[]{:S(2)}, u32[]{:S(2)}) collective-permute-start(bf16[128,1408]{0,1:T(8,128)(2,1)S(1)} %fusion.35), channel_id=1, source_target_pairs={{0,8},{8,16},{16,24},{24,28},{28,20},{20,12},{12,4},{4,0},{1,9},{9... | collective-permute-start | bytes 1081352 | tf_op jit(solution)/shard_map/ppermute | solution.py:478
  462.2 10.3 %collective-permute-start.23 = (bf16[128,1408]{0,1:T(8,128)(2,1)}, bf16[128,1408]{0,1:T(8,128)(2,1)S(1)}, u32[]{:S(2)}, u32[]{:S(2)}) collective-permute-start(bf16[128,1408]{0,1:T(8,128)(2,1)} %get-tuple-element.167), channel_id=1, source_target_pairs={{0,8},{8,16},{16,24},{24,28},{28,20},{20,12},{12,4},{4,0},{1,9},{9... | collective-permute-start | bytes 1081352 | tf_op jit(solution)/shard_map/ppermute | solution.py:478
  462.3 10.3 %collective-permute-start.26 = (bf16[128,1408]{0,1:T(8,128)(2,1)S(1)}, bf16[128,1408]{0,1:T(8,128)(2,1)}, u32[]{:S(2)}, u32[]{:S(2)}) collective-permute-start(bf16[128,1408]{0,1:T(8,128)(2,1)S(1)} %get-tuple-element.168), channel_id=1, source_target_pairs={{0,4},{8,0},{16,8},{24,16},{28,24},{20,28},{12,20},{4,12},{1,5},{9... | collective-permute-start | bytes 1081352 | tf_op jit(solution)/shard_map/ppermute | solution.py:478
  464.8 24.6 %collective-permute-start.28 = (bf16[512,1024]{1,0:T(8,128)(2,1)}, bf16[512,1024]{1,0:T(8,128)(2,1)}, u32[]{:S(2)}, u32[]{:S(2)}) collective-permute-start(bf16[512,1024]{1,0:T(8,128)(2,1)} %reduce-scatter.2.cloned.1.call-done), channel_id=1, source_target_pairs={{0,2},{2,0},{1,3},{3,1},{4,6},{6,4},{5,7},{7,5},{8,10},{10,8},{9,1... | collective-permute-start | bytes 3145736 | tf_op jit(solution)/shard_map/ppermute | solution.py:441
  474.7 16.8 %collective-permute-start.24 = (bf16[128,1408]{0,1:T(8,128)(2,1)}, bf16[128,1408]{0,1:T(8,128)(2,1)S(1)}, u32[]{:S(2)}, u32[]{:S(2)}) collective-permute-start(bf16[128,1408]{0,1:T(8,128)(2,1)} %get-tuple-element.165), channel_id=1, source_target_pairs={{0,8},{8,16},{16,24},{24,28},{28,20},{20,12},{12,4},{4,0},{1,9},{9... | collective-permute-start | bytes 1081352 | tf_op jit(solution)/shard_map/ppermute | solution.py:478
  476.1 16.1 %collective-permute-start.27 = (bf16[128,1408]{0,1:T(8,128)(2,1)S(1)}, bf16[128,1408]{0,1:T(8,128)(2,1)}, u32[]{:S(2)}, u32[]{:S(2)}) collective-permute-start(bf16[128,1408]{0,1:T(8,128)(2,1)S(1)} %get-tuple-element.166), channel_id=1, source_target_pairs={{0,4},{8,0},{16,8},{24,16},{28,24},{20,28},{12,20},{4,12},{1,5},{9... | collective-permute-start | bytes 1081352 | tf_op jit(solution)/shard_map/ppermute | solution.py:478
  491.4 14.4 %collective-permute-start.31 = (bf16[512,1024]{1,0:T(8,128)(2,1)S(1)}, bf16[512,1024]{1,0:T(8,128)(2,1)S(1)}, u32[]{:S(2)}, u32[]{:S(2)}) collective-permute-start(bf16[512,1024]{1,0:T(8,128)(2,1)S(1)} %add_convert_fusion.2), channel_id=1, source_target_pairs={{0,1},{1,0},{2,3},{3,2},{4,5},{5,4},{6,7},{7,6},{8,9},{9,8},{10,11... | collective-permute-start | bytes 3145736 | tf_op jit(solution)/shard_map/ppermute | solution.py:463
  493.6 10.9 %collective-permute-start.29 = (bf16[128,1408]{0,1:T(8,128)(2,1)S(1)}, bf16[128,1408]{0,1:T(8,128)(2,1)S(1)}, u32[]{:S(2)}, u32[]{:S(2)}) collective-permute-start(bf16[128,1408]{0,1:T(8,128)(2,1)S(1)} %fusion.37), channel_id=1, source_target_pairs={{0,2},{2,0},{1,3},{3,1},{4,6},{6,4},{5,7},{7,5},{8,10},{10,8},{9,1... | collective-permute-start | bytes 1081352 | tf_op jit(solution)/shard_map/ppermute | solution.py:441
  505.8 11.8 %collective-permute-start.30 = (bf16[2,128,1408]{1,2,0:T(8,128)(2,1)}, bf16[2,128,1408]{1,2,0:T(8,128)(2,1)S(1)}, u32[]{:S(2)}, u32[]{:S(2)}) collective-permute-start(bf16[2,128,1408]{1,2,0:T(8,128)(2,1)} %fusion.30), channel_id=1, source_target_pairs={{0,1},{1,0},{2,3},{3,2},{4,5},{5,4},{6,7},{7,6},{8,9},{9,8},{10,11... | collective-permute-start | bytes 2162696 | tf_op jit(solution)/shard_map/ppermute | solution.py:463
  (92 other events, 761.1 us)
Sparse Core Ops, SparseCore 0:
  19.9 60.3 all-gather.2
  83.0 123.5 all-gather.4
  284.8 147.3 reduce-scatter.1

commit v7 on v6

--- a/solution.py
+++ b/solution.py
@@ -671,17 +671,11 @@
     second_mine = (normal_2 * gain_2 + shift_2).astype(BF)
     second_normed = jnp.concatenate([second_mine, other_core(second_mine)], 0)
     activated, slope = expand_rows(second_normed, feed_weights, bias_e)
-    branch = dot(activated, reduce_whole)
-    branch_feed = (
-        branch[:own_rows] + other_core(branch[own_rows:].astype(BF)).astype(F32) + bias_r
-    )
-    outputs = residual + scale_f * branch_feed
 
     cotangent = cotangent.reshape(own_rows, width)
     upstream = cotangent.astype(F32)
     both = jnp.concatenate([cotangent, other_core(cotangent)], 0)
     grad_feed = (scale_f * both.astype(F32)).astype(BF)
-    grad_feed_scale = jnp.sum(upstream * branch_feed, 0)
     grad_reduce_bias = column_total(grad_feed[:own_rows])
     grad_expanded = (dot_right_t(grad_feed, reduce_whole) * slope.astype(F32)).astype(BF)
     feed_sums = feed_grads(second_normed, activated, grad_expanded, grad_feed, fsdp_count)
@@ -691,7 +685,6 @@
         dot_right_t(grad_expanded[:, i * width : (i + 1) * width], expand_blocks[i])
         for i in range(blocks)
     )
-    grad_expand_bias = column_total(grad_expanded)
     upper = partial[:own_rows] + other_core(partial[own_rows:].astype(BF)).astype(F32)
     grad_second_gain = jnp.sum(upper * normal_2, 0)
     grad_second_shift = jnp.sum(upper, 0)
@@ -719,6 +712,16 @@
     ).reshape(width // 2, width)
 
     grad_heads = [to_kernel(jnp.stack(far_exchange(parts), 0)) for parts in grad_attended]
+    sent = [part for parts in grad_attended for part in parts]
+    branch = dot(after(activated, *sent), reduce_whole)
+    grad_expand_bias = column_total(after(grad_expanded, *sent))
+    grad_heads[0] = after(grad_heads[0], branch, grad_expand_bias)
+    branch_feed = (
+        branch[:own_rows] + other_core(branch[own_rows:].astype(BF)).astype(F32) + bias_r
+    )
+    outputs = residual + scale_f * branch_feed
+    grad_feed_scale = jnp.sum(upstream * branch_feed, 0)
+
     upper_parts, grad_triples = [], []
     grad_first_gain = grad_first_shift = column_sums = 0.0
     for group in range(groups):

time: 539 us -> 522 us (0.968)
  local copies, waits for them, and re-layouts: 104 us -> 94.1 us
    ppermute x10, waiting for transfers between devices: 74.2 us -> 53.4 us  [far_send(): lax.ppermute(array, 'far', [(i, (i + shift) % count) for i in range(count)])]
    ppermute x7, waiting for transfers between devices: 11.6 us -> 24.1 us  [ring_send(): return lax.ppermute(array, 'fsdp', pairs)]
    unnamed x180 -> x160, local copies, waits for them, and re-layouts: 31 us -> 28.1 us
  transfers between devices with their start and end apart: 35 -> 35, of which waited for: 12 -> 13; matrix products, arithmetic and copies ran while one was open for 29% -> 26% of each run, Pallas kernels for 18% -> 19%
where the time goes in v7:
time: 522 us; the launch traced here: 518 us
  Pallas kernels  138 us (26%)
  waiting for transfers between devices  134 us (26%)
  local copies, waits for them, and re-layouts  94.1 us (18%)
  other arithmetic  63.7 us (12%)
  matrix products  51.3 us (10%)
  starting transfers between devices  21.4 us (4%)
  between operations  15.4 us (3%)
    ppermute x10, waiting for transfers between devices, far_send(): lax.ppermute(array, 'far', [(i, (i + shift) % count) for i in range(count)])  53.4 us
    all_gather x2, waiting for transfers between devices, fsdp_gather(): return lax.all_gather(array, 'fsdp', axis=0, tiled=True)  51.3 us
    pallas_call x2, Pallas kernels, attend_backward(): pl.pallas_call(attend_backward_kernel, grid_spec=pltpu.PrefetchScalarGrid...  51.1 us
    pallas_call x2, Pallas kernels, attend_forward(): pl.pallas_call(attend_forward_kernel, grid_spec=pltpu.PrefetchScalarGridS...  31.3 us
    unnamed x160, local copies, waits for them, and re-layouts  28.1 us
    ppermute x7, waiting for transfers between devices, ring_send(): return lax.ppermute(array, 'fsdp', pairs)  24.1 us
    dot_general x7, matrix products, dot_right_t(): lax.dot_general(left, right, (((1,), (1,)), ((), ())), preferred_element_...  22.2 us
    pallas_call x1, Pallas kernels, feed_grads(): pl.pallas_call(feed_grads_kernel, grid=(devices,), in_specs=[pl.BlockSpec...  19.8 us
  transfers between devices with their start and end apart: 35, of which 13 were waited for; matrix products, arithmetic and copies ran while one was open for 26% of the time, Pallas kernels for 19%

profile of v7, /device:TPU:0, one launch (start us, length us, event | category | flops | bytes accessed | tf_op | source)
XLA Modules:
  0.0 518.0 jit_solution(17634265351295747627)
XLA Ops:
  28.1 16.8 %collective-permute-done.1 = bf16[344,1024]{1,0:T(8,128)(2,1)S(1)} collective-permute-done((bf16[344,1024]{1,0:T(8,128)(2,1)}, bf16[344,1024]{1,0:T(8,128)(2,1)S(1)}, u32[]{:S(2)}, u32[]{:S(2)}) %collective-permute-start.1) | collective-permute-done | bytes 704544 | tf_op jit(solution)/shard_map/ppermute | solution.py:441
  45.4 13.8 %collective-permute-done.6 = bf16[344,1024]{1,0:T(8,128)(2,1)S(1)} collective-permute-done((bf16[344,1024]{1,0:T(8,128)(2,1)}, bf16[344,1024]{1,0:T(8,128)(2,1)S(1)}, u32[]{:S(2)}, u32[]{:S(2)}) %collective-permute-start.6) | collective-permute-done | bytes 704544 | tf_op jit(solution)/shard_map/ppermute | solution.py:441
  65.0 16.7 %all-gather.3.cloned.1.call-done = bf16[1024,1408]{1,0:T(8,128)(2,1)} async-done(((bf16[128,1408]{1,0:T(8,128)(2,1)}), bf16[1024,1408]{1,0:T(8,128)(2,1)}) %all-gather.3.cloned.1.call-update) | async-done | bytes 2883600 | tf_op jit(solution)/shard_map/all_gather | solution.py:467
  93.3 4.5 project.3
  99.2 15.7 %attend_forward.3 = (bf16[4,1,344,256]{3,2,1,0:T(8,128)(2,1)S(1)}, f32[1,2,1376,128]{3,2,1,0:T(8,128)S(1)}) custom-call(s32[1,2]{1,0:T(1,128)S(1)} %get-tuple-element.212.limit_ref, bf16[4,1,344,768]{3,2,1,0:T(8,128)(2,1)} %bitcast.252, bf16[4,1,344,768]{3,2,1,0:T(8,128)(2,1)} %bitcast.253, bf16[4,1,344,768]{3,2,1,0:T(8,128)(2,1)} %bitcast.254), custom_call_target="tpu_custom_call" | custom-call | flops 7755268096 | bytes 4227072 | tf_op jit(solution)/shard_map/attend_forward/pallas_call | solution.py:202
  117.2 4.6 project.2
  123.3 15.6 %attend_forward.2 = (bf16[4,1,344,256]{3,2,1,0:T(8,128)(2,1)S(1)}, f32[1,2,1376,128]{3,2,1,0:T(8,128)S(1)}) custom-call(s32[1,2]{1,0:T(1,128)S(1)} %get-tuple-element.211.limit_ref, bf16[4,1,344,768]{3,2,1,0:T(8,128)(2,1)} %bitcast.258, bf16[4,1,344,768]{3,2,1,0:T(8,128)(2,1)} %bitcast.259, bf16[4,1,344,768]{3,2,1,0:T(8,128)(2,1)} %bitcast.260), custom_call_target="tpu_custom_call" | custom-call | flops 7755268096 | bytes 4227072 | tf_op jit(solution)/shard_map/attend_forward/pallas_call | solution.py:202
  142.5 5.2 collective-permute-done.3
  155.9 3.4 fusion.7
  159.4 5.1 add_convert_fusion.1
  165.2 4.1 multiply_convert_fusion.1.feed_ref
  169.3 3.6 pad_maximum_fusion.4.rows_ref
  172.9 34.6 %all-gather.5.cloned.1.call-done = bf16[4096,1024]{1,0:T(8,128)(2,1)} async-done(((bf16[512,1024]{1,0:T(8,128)(2,1)}), bf16[4096,1024]{1,0:T(8,128)(2,1)}) %all-gather.5.cloned.1.call-update) | async-done | bytes 8388624 | tf_op jit(solution)/shard_map/all_gather | solution.py:467
  215.9 19.0 %expand_rows.1 = (bf16[1376,2048]{1,0:T(8,128)(2,1)}, bf16[1376,2048]{1,0:T(8,128)(2,1)}) custom-call(bf16[1376,1024]{1,0:T(8,128)(2,1)S(1)} %copy-done.6, bf16[8,512,1024]{2,1,0:T(8,128)(2,1)} %bitcast.273, f32[1,2048]{1,0:T(1,128)S(1)} %reshape.473.bias_ref), custom_call_target="tpu_custom_call" | custom-call | flops 11542724608 | bytes 18284544 | tf_op jit(solution)/shard_map/expand_rows/pallas_call | solution.py:377
  235.0 9.8 %multiply_convert_fusion.expanded_ref = bf16[1376,2048]{1,0:T(8,128)(2,1)} fusion(bf16[1376,2048]{1,0:T(8,128)(2,1)} %get-tuple-element.50, bf16[1376,1024]{1,0:T(8,128)(2,1)S(1)} %copy-done.42, bf16[2048,1024]{1,0:T(8,128)(2,1)S(1)} %bitcast.279), kind=kOutput, calls=%fused_computation | convolution fusion | flops 5779816448 | bytes 18284544 | tf_op jit(solution)/shard_map/dot_general | solution.py:26
  244.8 19.8 %feed_grads.1 = bf16[8,512,1024]{2,1,0:T(8,128)(2,1)} custom-call(bf16[1376,1024]{1,0:T(8,128)(2,1)} %pad_maximum_fusion.4.rows_ref, bf16[1376,2048]{1,0:T(8,128)(2,1)} %get-tuple-element.52.active_ref, bf16[1376,2048]{1,0:T(8,128)(2,1)} %multiply_convert_fusion.expanded_ref, bf16[1376,1024]{1,0:T(8,128)(2,1)} %multiply_convert_fusion.1.feed_ref), custom_call_target="tpu_custom_call" | custom-call | flops 11542724608 | bytes 25296896 | tf_op jit(solution)/shard_map/feed_grads/pallas_call | solution.py:418
  264.6 4.7 fusion.16
  304.3 7.7 %fusion.69 = f32[1376,1024]{1,0:T(8,128)} fusion(bf16[1376,2048]{1,0:T(8,128)(2,1)S(1)} %bitcast.341, bf16[2048,1024]{1,0:T(8,128)(2,1)S(1)} %bitcast.280), kind=kOutput, calls=%fused_computation.224 | convolution fusion | flops 5771362304 | bytes 15466496 | tf_op jit(solution)/shard_map/dot_general | solution.py:18
  321.4 3.4 slice.496
  326.8 25.9 %attend_backward.2 = bf16[4,1,344,768]{3,2,1,0:T(8,128)(2,1)} custom-call(s32[1,2]{1,0:T(1,128)} %copy-done.12, bf16[4,1,344,768]{3,2,1,0:T(8,128)(2,1)} %bitcast.261, bf16[4,1,344,768]{3,2,1,0:T(8,128)(2,1)} %bitcast.262, bf16[4,1,344,768]{3,2,1,0:T(8,128)(2,1)} %bitcast.263, bf16[4,1,344,256]{3,2,1,0:T(8,128)(2,1)} %copy-done.10, ...), custom_call_target="tpu_custom_call" | custom-call | flops 19388170240 | bytes 8454144 | tf_op jit(solution)/shard_map/attend_backward/pallas_call | solution.py:236
  354.3 3.9 project_back.2
  361.0 4.3 fusion.70
  365.4 4.0 fusion.1
  372.7 25.2 %attend_backward.3 = bf16[4,1,344,768]{3,2,1,0:T(8,128)(2,1)} custom-call(s32[1,2]{1,0:T(1,128)} %copy-done.11, bf16[4,1,344,768]{3,2,1,0:T(8,128)(2,1)} %bitcast.255, bf16[4,1,344,768]{3,2,1,0:T(8,128)(2,1)} %bitcast.256, bf16[4,1,344,768]{3,2,1,0:T(8,128)(2,1)} %bitcast.257, bf16[4,1,344,256]{3,2,1,0:T(8,128)(2,1)} %copy-done.9, ...), custom_call_target="tpu_custom_call" | custom-call | flops 19388170240 | bytes 8454144 | tf_op jit(solution)/shard_map/attend_backward/pallas_call | solution.py:236
  399.7 3.9 project_back.3
  408.5 6.8 %fusion = bf16[1024,768]{1,0:T(8,128)(2,1)} fusion(f32[1024,768]{1,0:T(8,128)} %fusion.70, bf16[4,344,1024]{2,1,0:T(8,128)(2,1)} %copy-done.21, bf16[4,344,768]{2,1,0:T(8,128)(2,1)S(1)} %bitcast.265), kind=kOutput, calls=%fused_computation.6 | convolution fusion | flops 2165833728 | bytes 9650176 | tf_op jit(solution)/shard_map/dot_general | solution.py:22
  424.4 13.1 %collective-permute-done.21 = bf16[128,1408]{0,1:T(8,128)(2,1)S(1)} collective-permute-done((bf16[128,1408]{0,1:T(8,128)(2,1)S(1)}, bf16[128,1408]{0,1:T(8,128)(2,1)S(1)}, u32[]{:S(2)}, u32[]{:S(2)}) %collective-permute-start.21) | collective-permute-done | bytes 360480 | tf_op jit(solution)/shard_map/ppermute | solution.py:478
  442.4 7.1 %collective-permute-done.22 = bf16[128,1408]{0,1:T(8,128)(2,1)S(1)} collective-permute-done((bf16[128,1408]{0,1:T(8,128)(2,1)S(1)}, bf16[128,1408]{0,1:T(8,128)(2,1)S(1)}, u32[]{:S(2)}, u32[]{:S(2)}) %collective-permute-start.22) | collective-permute-done | bytes 360480 | tf_op jit(solution)/shard_map/ppermute | solution.py:478
  457.0 3.5 collective-permute-done.23
  466.4 11.1 %collective-permute-done.28 = bf16[512,1024]{1,0:T(8,128)(2,1)} collective-permute-done((bf16[512,1024]{1,0:T(8,128)(2,1)}, bf16[512,1024]{1,0:T(8,128)(2,1)}, u32[]{:S(2)}, u32[]{:S(2)}) %collective-permute-start.28) | collective-permute-done | bytes 1048608 | tf_op jit(solution)/shard_map/ppermute | solution.py:441
  485.8 6.7 %collective-permute-done.29 = bf16[128,1408]{0,1:T(8,128)(2,1)S(1)} collective-permute-done((bf16[128,1408]{0,1:T(8,128)(2,1)S(1)}, bf16[128,1408]{0,1:T(8,128)(2,1)S(1)}, u32[]{:S(2)}, u32[]{:S(2)}) %collective-permute-start.29) | collective-permute-done | bytes 360480 | tf_op jit(solution)/shard_map/ppermute | solution.py:441
  501.7 3.9 reshape.491
  (383 shorter events, 175.3 us)
Async XLA Ops:
  7.2 74.5 %all-gather.3.cloned.1.call-start = ((), (), s32[]{:S(2)}) async-start(), calls=%async_computation.1 | async-start | bytes 3244032 | tf_op jit(solution)/shard_map/all_gather | solution.py:467
  21.2 186.2 %all-gather.5.cloned.1.call-start = ((), (), s32[]{:S(2)}) async-start(), calls=%async_computation.2 | async-start | bytes 9437184 | tf_op jit(solution)/shard_map/all_gather | solution.py:467
  23.6 429.5 %reduce-scatter.2.cloned.1.call-start = ((), (), s32[]{:S(2)}) async-start(), calls=%async_computation.3 | async-start | bytes 9437184 | tf_op jit(solution)/shard_map/reduce_scatter | solution.py:471
  25.1 19.8 %collective-permute-start.1 = (bf16[344,1024]{1,0:T(8,128)(2,1)}, bf16[344,1024]{1,0:T(8,128)(2,1)S(1)}, u32[]{:S(2)}, u32[]{:S(2)}) collective-permute-start(bf16[344,1024]{1,0:T(8,128)(2,1)} %get-tuple-element.186), channel_id=1, source_target_pairs={{0,2},{2,0},{1,3},{3,1},{4,6},{6,4},{5,7},{7,5},{8,10},{10,8},{9,1... | collective-permute-start | bytes 2113544 | tf_op jit(solution)/shard_map/ppermute | solution.py:441
  28.0 31.1 %collective-permute-start.6 = (bf16[344,1024]{1,0:T(8,128)(2,1)}, bf16[344,1024]{1,0:T(8,128)(2,1)S(1)}, u32[]{:S(2)}, u32[]{:S(2)}) collective-permute-start(bf16[344,1024]{1,0:T(8,128)(2,1)} %get-tuple-element.187), channel_id=1, source_target_pairs={{0,2},{2,0},{1,3},{3,1},{4,6},{6,4},{5,7},{7,5},{8,10},{10,8},{9,1... | collective-permute-start | bytes 2113544 | tf_op jit(solution)/shard_map/ppermute | solution.py:441
  28.1 31.2 %collective-permute-start = (bf16[344,1024]{1,0:T(8,128)(2,1)}, bf16[344,1024]{1,0:T(8,128)(2,1)}, u32[]{:S(2)}, u32[]{:S(2)}) collective-permute-start(bf16[344,1024]{1,0:T(8,128)(2,1)} %get-tuple-element.186), channel_id=1, source_target_pairs={{0,1},{1,0},{2,3},{3,2},{4,5},{5,4},{6,7},{7,6},{8,9},{9,8},{10,11... | collective-permute-start | bytes 2113544 | tf_op jit(solution)/shard_map/ppermute | solution.py:463
  44.9 14.4 %collective-permute-start.2 = (bf16[344,1024]{1,0:T(8,128)(2,1)S(1)}, bf16[344,1024]{1,0:T(8,128)(2,1)}, u32[]{:S(2)}, u32[]{:S(2)}) collective-permute-start(bf16[344,1024]{1,0:T(8,128)(2,1)S(1)} %collective-permute-done.1), channel_id=1, source_target_pairs={{0,1},{1,0},{2,3},{3,2},{4,5},{5,4},{6,7},{7,6},{8,9},{9,8},{10,11... | collective-permute-start | bytes 2113544 | tf_op jit(solution)/shard_map/ppermute | solution.py:463
  44.9 17.6 %collective-permute-start.5 = (bf16[344,1024]{1,0:T(8,128)(2,1)}, bf16[344,1024]{1,0:T(8,128)(2,1)S(1)}, u32[]{:S(2)}, u32[]{:S(2)}) collective-permute-start(bf16[344,1024]{1,0:T(8,128)(2,1)} %get-tuple-element.187), channel_id=1, source_target_pairs={{0,1},{1,0},{2,3},{3,2},{4,5},{5,4},{6,7},{7,6},{8,9},{9,8},{10,11... | collective-permute-start | bytes 2113544 | tf_op jit(solution)/shard_map/ppermute | solution.py:463
  115.9 24.3 %collective-permute-start.8 = (bf16[688,256]{1,0:T(8,128)(2,1)}, bf16[688,256]{1,0:T(8,128)(2,1)}, u32[]{:S(2)}, u32[]{:S(2)}) collective-permute-start(bf16[688,256]{1,0:T(8,128)(2,1)} %bitcast.34), channel_id=1, source_target_pairs={{0,2},{2,0},{1,3},{3,1},{4,6},{6,4},{5,7},{7,5},{8,10},{10,8},{9,1... | collective-permute-start | bytes 1056776 | tf_op jit(solution)/shard_map/ppermute | solution.py:441
  139.0 8.7 %collective-permute-start.3 = (bf16[688,256]{1,0:T(8,128)(2,1)S(1)}, bf16[688,256]{1,0:T(8,128)(2,1)S(1)}, u32[]{:S(2)}, u32[]{:S(2)}) collective-permute-start(bf16[688,256]{1,0:T(8,128)(2,1)S(1)} %bitcast.324), channel_id=1, source_target_pairs={{0,2},{2,0},{1,3},{3,1},{4,6},{6,4},{5,7},{7,5},{8,10},{10,8},{9,1... | collective-permute-start | bytes 1056776 | tf_op jit(solution)/shard_map/ppermute | solution.py:441
  142.5 7.6 %collective-permute-start.9 = (bf16[344,1024]{1,0:T(8,128)(2,1)S(1)}, bf16[344,1024]{1,0:T(8,128)(2,1)S(1)}, u32[]{:S(2)}, u32[]{:S(2)}) collective-permute-start(bf16[344,1024]{1,0:T(8,128)(2,1)S(1)} %slice.498), channel_id=1, source_target_pairs={{0,1},{1,0},{2,3},{3,2},{4,5},{5,4},{6,7},{7,6},{8,9},{9,8},{10,11... | collective-permute-start | bytes 2113544 | tf_op jit(solution)/shard_map/ppermute | solution.py:463
  149.6 15.6 %collective-permute-start.11 = (bf16[688,1024]{1,0:T(8,128)(2,1)}, bf16[688,1024]{1,0:T(8,128)(2,1)}, u32[]{:S(2)}, u32[]{:S(2)}) collective-permute-start(bf16[688,1024]{1,0:T(8,128)(2,1)} %bitcast.45), channel_id=1, source_target_pairs={{0,1},{1,0},{2,3},{3,2},{4,5},{5,4},{6,7},{7,6},{8,9},{9,8},{10,11... | collective-permute-start | bytes 4227080 | tf_op jit(solution)/shard_map/ppermute | solution.py:463
  164.5 4.8 collective-permute-start.10
  283.9 5.9 %collective-permute-start.13 = (bf16[688,1024]{1,0:T(8,128)(2,1)}, bf16[688,1024]{1,0:T(8,128)(2,1)}, u32[]{:S(2)}, u32[]{:S(2)}) collective-permute-start(bf16[688,1024]{1,0:T(8,128)(2,1)} %multiply_convert_fusion.2), channel_id=1, source_target_pairs={{0,1},{1,0},{2,3},{3,2},{4,5},{5,4},{6,7},{7,6},{8,9},{9,8},{10,11... | collective-permute-start | bytes 4227080 | tf_op jit(solution)/shard_map/ppermute | solution.py:463
  295.8 29.1 %collective-permute-start.15 = (bf16[688,256]{1,0:T(8,128)(2,1)}, bf16[688,256]{1,0:T(8,128)(2,1)}, u32[]{:S(2)}, u32[]{:S(2)}) collective-permute-start(bf16[688,256]{1,0:T(8,128)(2,1)} %convolution_convert_fusion.2), channel_id=1, source_target_pairs={{0,2},{2,0},{1,3},{3,1},{4,6},{6,4},{5,7},{7,5},{8,10},{10,8},{9,1... | collective-permute-start | bytes 1056776 | tf_op jit(solution)/shard_map/ppermute | solution.py:441
  297.3 61.4 %collective-permute-start.18 = (bf16[688,256]{1,0:T(8,128)(2,1)}, bf16[688,256]{1,0:T(8,128)(2,1)}, u32[]{:S(2)}, u32[]{:S(2)}) collective-permute-start(bf16[688,256]{1,0:T(8,128)(2,1)} %convolution_convert_fusion), channel_id=1, source_target_pairs={{0,2},{2,0},{1,3},{3,1},{4,6},{6,4},{5,7},{7,5},{8,10},{10,8},{9,1... | collective-permute-start | bytes 1056776 | tf_op jit(solution)/shard_map/ppermute | solution.py:441
  324.8 40.6 %collective-permute-start.14 = (bf16[688,1024]{1,0:T(8,128)(2,1)}, bf16[688,1024]{1,0:T(8,128)(2,1)}, u32[]{:S(2)}, u32[]{:S(2)}) collective-permute-start(bf16[688,1024]{1,0:T(8,128)(2,1)} %slice.496), channel_id=1, source_target_pairs={{0,1},{1,0},{2,3},{3,2},{4,5},{5,4},{6,7},{7,6},{8,9},{9,8},{10,11... | collective-permute-start | bytes 4227080 | tf_op jit(solution)/shard_map/ppermute | solution.py:463
  358.3 11.1 %collective-permute-start.16 = (bf16[2,344,1024]{2,1,0:T(8,128)(2,1)S(1)}, bf16[2,344,1024]{2,1,0:T(8,128)(2,1)S(1)}, u32[]{:S(2)}, u32[]{:S(2)}) collective-permute-start(bf16[2,344,1024]{2,1,0:T(8,128)(2,1)S(1)} %slice_bitcast_fusion.2), channel_id=1, source_target_pairs={{0,1},{1,0},{2,3},{3,2},{4,5},{5,4},{6,7},{7,6},{8,9},{9,8},{10,11... | collective-permute-start | bytes 4227080 | tf_op jit(solution)/shard_map/ppermute | solution.py:463
  371.1 26.7 %collective-permute-start.17 = (bf16[344,1024]{1,0:T(8,128)(2,1)S(1)}, bf16[344,1024]{1,0:T(8,128)(2,1)S(1)}, u32[]{:S(2)}, u32[]{:S(2)}) collective-permute-start(bf16[344,1024]{1,0:T(8,128)(2,1)S(1)} %slice_bitcast_fusion.6), channel_id=1, source_target_pairs={{0,2},{2,0},{1,3},{3,1},{4,6},{6,4},{5,7},{7,5},{8,10},{10,8},{9,1... | collective-permute-start | bytes 2113544 | tf_op jit(solution)/shard_map/ppermute | solution.py:441
  408.1 7.2 %collective-permute-start.19 = (bf16[2,344,1024]{2,1,0:T(8,128)(2,1)}, bf16[2,344,1024]{2,1,0:T(8,128)(2,1)}, u32[]{:S(2)}, u32[]{:S(2)}) collective-permute-start(bf16[2,344,1024]{2,1,0:T(8,128)(2,1)} %slice_bitcast_fusion), channel_id=1, source_target_pairs={{0,1},{1,0},{2,3},{3,2},{4,5},{5,4},{6,7},{7,6},{8,9},{9,8},{10,11... | collective-permute-start | bytes 4227080 | tf_op jit(solution)/shard_map/ppermute | solution.py:463
  421.2 16.2 %collective-permute-start.21 = (bf16[128,1408]{0,1:T(8,128)(2,1)S(1)}, bf16[128,1408]{0,1:T(8,128)(2,1)S(1)}, u32[]{:S(2)}, u32[]{:S(2)}) collective-permute-start(bf16[128,1408]{0,1:T(8,128)(2,1)S(1)} %get-tuple-element.173), channel_id=1, source_target_pairs={{0,8},{8,16},{16,24},{24,28},{28,20},{20,12},{12,4},{4,0},{1,9},{9... | collective-permute-start | bytes 1081352 | tf_op jit(solution)/shard_map/ppermute | solution.py:478
  421.4 18.7 %collective-permute-start.20 = (bf16[344,1024]{1,0:T(8,128)(2,1)S(1)}, bf16[344,1024]{1,0:T(8,128)(2,1)S(1)}, u32[]{:S(2)}, u32[]{:S(2)}) collective-permute-start(bf16[344,1024]{1,0:T(8,128)(2,1)S(1)} %slice_bitcast_fusion.4), channel_id=1, source_target_pairs={{0,2},{2,0},{1,3},{3,1},{4,6},{6,4},{5,7},{7,5},{8,10},{10,8},{9,1... | collective-permute-start | bytes 2113544 | tf_op jit(solution)/shard_map/ppermute | solution.py:441
  424.0 18.4 %collective-permute-start.25 = (bf16[128,1408]{0,1:T(8,128)(2,1)S(1)}, bf16[128,1408]{0,1:T(8,128)(2,1)S(1)}, u32[]{:S(2)}, u32[]{:S(2)}) collective-permute-start(bf16[128,1408]{0,1:T(8,128)(2,1)S(1)} %get-tuple-element.174), channel_id=1, source_target_pairs={{0,4},{8,0},{16,8},{24,16},{28,24},{20,28},{12,20},{4,12},{1,5},{9... | collective-permute-start | bytes 1081352 | tf_op jit(solution)/shard_map/ppermute | solution.py:478
  437.5 12.0 %collective-permute-start.22 = (bf16[128,1408]{0,1:T(8,128)(2,1)S(1)}, bf16[128,1408]{0,1:T(8,128)(2,1)S(1)}, u32[]{:S(2)}, u32[]{:S(2)}) collective-permute-start(bf16[128,1408]{0,1:T(8,128)(2,1)S(1)} %fusion.33), channel_id=1, source_target_pairs={{0,8},{8,16},{16,24},{24,28},{28,20},{20,12},{12,4},{4,0},{1,9},{9... | collective-permute-start | bytes 1081352 | tf_op jit(solution)/shard_map/ppermute | solution.py:478
  450.4 10.1 %collective-permute-start.23 = (bf16[128,1408]{0,1:T(8,128)(2,1)}, bf16[128,1408]{0,1:T(8,128)(2,1)S(1)}, u32[]{:S(2)}, u32[]{:S(2)}) collective-permute-start(bf16[128,1408]{0,1:T(8,128)(2,1)} %get-tuple-element.171), channel_id=1, source_target_pairs={{0,8},{8,16},{16,24},{24,28},{28,20},{20,12},{12,4},{4,0},{1,9},{9... | collective-permute-start | bytes 1081352 | tf_op jit(solution)/shard_map/ppermute | solution.py:478
  451.4 9.4 %collective-permute-start.26 = (bf16[128,1408]{0,1:T(8,128)(2,1)S(1)}, bf16[128,1408]{0,1:T(8,128)(2,1)}, u32[]{:S(2)}, u32[]{:S(2)}) collective-permute-start(bf16[128,1408]{0,1:T(8,128)(2,1)S(1)} %get-tuple-element.172), channel_id=1, source_target_pairs={{0,4},{8,0},{16,8},{24,16},{28,24},{20,28},{12,20},{4,12},{1,5},{9... | collective-permute-start | bytes 1081352 | tf_op jit(solution)/shard_map/ppermute | solution.py:478
  453.1 24.4 %collective-permute-start.28 = (bf16[512,1024]{1,0:T(8,128)(2,1)}, bf16[512,1024]{1,0:T(8,128)(2,1)}, u32[]{:S(2)}, u32[]{:S(2)}) collective-permute-start(bf16[512,1024]{1,0:T(8,128)(2,1)} %reduce-scatter.2.cloned.1.call-done), channel_id=1, source_target_pairs={{0,2},{2,0},{1,3},{3,1},{4,6},{6,4},{5,7},{7,5},{8,10},{10,8},{9,1... | collective-permute-start | bytes 3145736 | tf_op jit(solution)/shard_map/ppermute | solution.py:441
  463.0 16.4 %collective-permute-start.24 = (bf16[128,1408]{0,1:T(8,128)(2,1)}, bf16[128,1408]{0,1:T(8,128)(2,1)S(1)}, u32[]{:S(2)}, u32[]{:S(2)}) collective-permute-start(bf16[128,1408]{0,1:T(8,128)(2,1)} %get-tuple-element.169), channel_id=1, source_target_pairs={{0,8},{8,16},{16,24},{24,28},{28,20},{20,12},{12,4},{4,0},{1,9},{9... | collective-permute-start | bytes 1081352 | tf_op jit(solution)/shard_map/ppermute | solution.py:478
  464.4 15.7 %collective-permute-start.27 = (bf16[128,1408]{0,1:T(8,128)(2,1)S(1)}, bf16[128,1408]{0,1:T(8,128)(2,1)}, u32[]{:S(2)}, u32[]{:S(2)}) collective-permute-start(bf16[128,1408]{0,1:T(8,128)(2,1)S(1)} %get-tuple-element.170), channel_id=1, source_target_pairs={{0,4},{8,0},{16,8},{24,16},{28,24},{20,28},{12,20},{4,12},{1,5},{9... | collective-permute-start | bytes 1081352 | tf_op jit(solution)/shard_map/ppermute | solution.py:478
  479.4 14.4 %collective-permute-start.31 = (bf16[512,1024]{1,0:T(8,128)(2,1)S(1)}, bf16[512,1024]{1,0:T(8,128)(2,1)S(1)}, u32[]{:S(2)}, u32[]{:S(2)}) collective-permute-start(bf16[512,1024]{1,0:T(8,128)(2,1)S(1)} %add_convert_fusion.2), channel_id=1, source_target_pairs={{0,1},{1,0},{2,3},{3,2},{4,5},{5,4},{6,7},{7,6},{8,9},{9,8},{10,11... | collective-permute-start | bytes 3145736 | tf_op jit(solution)/shard_map/ppermute | solution.py:463
  481.5 10.9 %collective-permute-start.29 = (bf16[128,1408]{0,1:T(8,128)(2,1)S(1)}, bf16[128,1408]{0,1:T(8,128)(2,1)S(1)}, u32[]{:S(2)}, u32[]{:S(2)}) collective-permute-start(bf16[128,1408]{0,1:T(8,128)(2,1)S(1)} %fusion.35), channel_id=1, source_target_pairs={{0,2},{2,0},{1,3},{3,1},{4,6},{6,4},{5,7},{7,5},{8,10},{10,8},{9,1... | collective-permute-start | bytes 1081352 | tf_op jit(solution)/shard_map/ppermute | solution.py:441
  493.8 11.8 %collective-permute-start.30 = (bf16[2,128,1408]{1,2,0:T(8,128)(2,1)}, bf16[2,128,1408]{1,2,0:T(8,128)(2,1)S(1)}, u32[]{:S(2)}, u32[]{:S(2)}) collective-permute-start(bf16[2,128,1408]{1,2,0:T(8,128)(2,1)} %fusion.28), channel_id=1, source_target_pairs={{0,1},{1,0},{2,3},{3,2},{4,5},{5,4},{6,7},{7,6},{8,9},{9,8},{10,11... | collective-permute-start | bytes 2162696 | tf_op jit(solution)/shard_map/ppermute | solution.py:463
  (82 other events, 716.2 us)
Sparse Core Ops, SparseCore 0:
  21.3 60.3 all-gather.2
  83.9 123.5 all-gather.4
  286.7 151.7 reduce-scatter.1
